TPU v7x, 128 devices: a whole 4x4x4 slice. The times are simulated.
128 devices in a mesh: tm: 32 (over z, y, core), head: 4 (over x).
Axes of the slice: x: 4, y: 4, z: 4, core: 2. Of those that a mesh axis runs over, the one named last changes fastest.
Arguments:
- tokens: bfloat16 [100352, 1024], P('tm'), may hold values from -11 to 11
- w_query: bfloat16 [1024, 1024], P(None, 'head'), may hold values from -1 to 1
- w_key: bfloat16 [1024, 1024], P(None, 'head'), may hold values from -1 to 1
- w_value: bfloat16 [1024, 1024], P(None, 'head'), may hold values from -0.1875 to 0.1875
- w_out: bfloat16 [1024, 1024], P('head'), may hold values from -3 to 3
- pattern: int32 [512, 512], P('tm'), may hold values 0 or 1
- visible: int32 [512, 20], P('tm'), may hold values from 0 to 195, as said below
- slot: int32 [10240], replicated, may hold values from 0 to 10239, as said below
- pred: bfloat16 [10240, 1024], P('tm', 'head'), may hold values from -6 to 6
Outputs:
- target: bfloat16 [10240, 1024], P('tm', 'head')
- row_loss: float32 [10240], P('tm')
Inputs may be any that keep to these rules, and one draw needn't show every extreme that they name: `visible`: each row holds 20 different positions in rising order; frames 2 t and 2 t + 1 have the same row. `slot`: A permutation of the visible rows. Of the 320 visible rows of one tm index, at most 41 have student rows of any one tm index (student rows 320 o to 320 o + 319 belong to tm index o), exactly 41 for one of them and at least 9 for every one.
All inputs are finite; a program needn't handle non-finite values. No bound on the sum of `pattern` on one device may be relied on, other than what follows from the above.
Results may differ from a plain program's by a relative error of at most 0.0085.
Values may be sent and summed in bfloat16 or wider, within the bound.
No kernel may reach another device: no remote copies, remote signals or barrier semaphores. Data moves between devices by JAX's collectives and lax.ppermute only.
A program may use at most 128 MiB of HBM per device.

v0:
```python
import math

import jax
import jax.numpy as jnp
from jax import lax
from jax.sharding import PartitionSpec as P

HEAD_DIM = 64
PATCHES = 196


epsilon = 1e-06


def pool_quadrants(field_rows, frame_count):
    columns = field_rows.shape[1]
    tile_grid = field_rows.reshape(frame_count, 2, 7, 2, 7, columns)
    pooled = jnp.sum(tile_grid, axis=(2, 4), dtype=jnp.float32) / 7.0
    return pooled.reshape(frame_count * 4, columns).astype(jnp.bfloat16)


def pack_rows(rows_in, places, slots_total, n_peers):
    head_cols = rows_in.shape[1]
    packed = jnp.zeros((slots_total * n_peers, head_cols), jnp.bfloat16).at[places].set(rows_in)
    return packed.reshape(n_peers, slots_total, head_cols)


def body(tokens, w_query, w_key, w_value, w_out, pattern, visible, slot, pred):
    n_peers = lax.axis_size("tm")
    my_block = lax.axis_index("tm")
    my_heads = lax.axis_index("head")
    frame_count = visible.shape[0]
    model_width = tokens.shape[1]
    head_cols = w_query.shape[1]
    local_heads = head_cols // HEAD_DIM
    queries = jnp.dot(tokens, w_query, preferred_element_type=jnp.float32).astype(jnp.bfloat16)
    keys_local = jnp.dot(tokens, w_key, preferred_element_type=jnp.float32).astype(jnp.bfloat16)
    values_local = jnp.dot(tokens, w_value, preferred_element_type=jnp.float32).astype(jnp.bfloat16)
    summary_keys, summary_values = (
        lax.all_gather(pool_quadrants(keys_local, frame_count), "tm", axis=0, tiled=True),
        lax.all_gather(pool_quadrants(values_local, frame_count), "tm", axis=0, tiled=True),
    )
    far_count = summary_keys.shape[0]
    summary_keys = summary_keys.reshape(far_count, local_heads, HEAD_DIM)
    summary_values = summary_values.reshape(far_count, local_heads, HEAD_DIM)
    allowed = jnp.repeat(pattern, 4, axis=1)
    group_frames = math.gcd(frame_count, 4)
    blocks = frame_count // group_frames
    shape_q = (blocks, group_frames, PATCHES, local_heads, HEAD_DIM)
    score_scale = HEAD_DIM ** (-0.5)

    def attend(inputs):
        block_q, block_k, block_v, block_allow = inputs
        local_scores = (
            jnp.einsum("fqhd,fkhd->fhqk", block_q, block_k, preferred_element_type=jnp.float32)
            * score_scale
        )
        far_scores = (
            jnp.einsum("fqhd,shd->fhqs", block_q, summary_keys, preferred_element_type=jnp.float32)
            * score_scale
        )
        far_scores = jnp.where(block_allow[:, None, None, :] > 0, far_scores, -jnp.inf)
        row_top = jnp.maximum(jnp.max(local_scores, axis=3), jnp.max(far_scores, axis=3))[..., None]
        local_exp = jnp.exp(local_scores - row_top)
        far_exp = jnp.exp(far_scores - row_top)
        row_total = jnp.sum(local_exp, axis=3, keepdims=True) + jnp.sum(
            far_exp, axis=3, keepdims=True
        )
        local_weights = (local_exp / row_total).astype(jnp.bfloat16)
        far_weights = (far_exp / row_total).astype(jnp.bfloat16)
        mixed_out = jnp.einsum(
            "fhqk,fkhd->fqhd", local_weights, block_v, preferred_element_type=jnp.float32
        )
        mixed_out = mixed_out + jnp.einsum(
            "fhqs,shd->fqhd", far_weights, summary_values, preferred_element_type=jnp.float32
        )
        return mixed_out.astype(jnp.bfloat16)

    attended = lax.map(
        attend,
        (
            queries.reshape(shape_q),
            keys_local.reshape(shape_q),
            values_local.reshape(shape_q),
            allowed.reshape(blocks, group_frames, far_count),
        ),
    )
    attended = attended.reshape(frame_count * PATCHES, head_cols)
    positions = (jnp.arange(frame_count, dtype=jnp.int32)[:, None] * PATCHES + visible).reshape(-1)
    own_rows = positions.shape[0]
    token_cols = lax.dynamic_slice_in_dim(tokens, my_heads * head_cols, head_cols, 1)
    send_heads = attended[positions]
    send_tokens = token_cols[positions]
    total_rows = slot.shape[0]
    owner_all = slot // own_rows
    inverse = (
        jnp.zeros((total_rows,), jnp.int32).at[slot].set(jnp.arange(total_rows, dtype=jnp.int32))
    )
    my_start = my_block * own_rows
    wanted = lax.dynamic_slice_in_dim(inverse, my_start, own_rows)
    wanted_source = wanted // own_rows
    my_owners = lax.dynamic_slice_in_dim(owner_all, my_start, own_rows)
    my_slots = lax.dynamic_slice_in_dim(slot, my_start, own_rows)
    place_send = my_owners * own_rows + my_slots % own_rows
    packed_heads = pack_rows(send_heads, place_send, own_rows, n_peers)
    packed_tokens = pack_rows(send_tokens, place_send, own_rows, n_peers)
    got_heads, got_tokens = (
        lax.all_to_all(packed_heads, "tm", split_axis=0, concat_axis=0, tiled=True),
        lax.all_to_all(packed_tokens, "tm", split_axis=0, concat_axis=0, tiled=True),
    )
    place_recv = wanted_source * own_rows + jnp.arange(own_rows, dtype=jnp.int32)
    recv_heads = got_heads.reshape(-1, head_cols)[place_recv]
    recv_tokens = got_tokens.reshape(-1, head_cols)[place_recv]
    projected = lax.psum_scatter(
        lax.dot_general(
            w_out, recv_heads, (((0,), (1,)), ((), ())), preferred_element_type=jnp.float32
        ),
        "head",
        scatter_dimension=0,
        tiled=True,
    )
    raw_rows = recv_tokens.astype(jnp.float32) + projected.T
    pred_rows = pred.astype(jnp.float32)
    row_sum, row_square = lax.psum(
        (jnp.sum(raw_rows, axis=1), jnp.sum(raw_rows * raw_rows, axis=1)), "head"
    )
    row_mean = row_sum / model_width
    row_var = row_square / model_width - row_mean * row_mean
    normed = (raw_rows - row_mean[:, None]) * lax.rsqrt(row_var + epsilon)[:, None]
    loss_part = jnp.sum((pred_rows - normed) ** 2, axis=1)
    row_loss = lax.psum(loss_part, "head") / model_width
    return (normed.astype(jnp.bfloat16), row_loss)


def solution(mesh):
    return jax.shard_map(
        body,
        mesh=mesh,
        in_specs=(
            P("tm", None),
            P(None, "head"),
            P(None, "head"),
            P(None, "head"),
            P("head", None),
            P("tm", None),
            P("tm", None),
            P(),
            P("tm", "head"),
        ),
        out_specs=(P("tm", "head"), P("tm")),
        check_vma=False,
    )
```

profile of v0, /device:TPU:0, one launch (start us, length us, event | category | flops | bytes accessed | tf_op | source)
XLA Modules:
  0.0 454.4 jit_solution(10381426109654608463)
XLA Ops:
  40.3 6.7 %copy.77 = bf16[4,4,196,4,64]{2,4,3,1,0:T(8,128)(2,1)} copy(bf16[4,4,196,4,64]{4,3,2,1,0:T(4,128)(2,1)} %reshape.185) | data formatting | bytes 3211264 | tf_op jit(solution)/shard_map/while | solution.py:79
  54.5 6.6 %copy.78 = bf16[4,4,196,4,64]{2,4,3,1,0:T(8,128)(2,1)} copy(bf16[4,4,196,4,64]{4,3,2,1,0:T(4,128)(2,1)} %reshape.186) | data formatting | bytes 3211264 | tf_op jit(solution)/shard_map/while | solution.py:79
  61.1 6.6 %copy.79 = bf16[4,4,196,4,64]{2,4,3,1,0:T(8,128)(2,1)} copy(bf16[4,4,196,4,64]{4,3,2,1,0:T(4,128)(2,1)} %reshape.187) | data formatting | bytes 3211264 | tf_op jit(solution)/shard_map/while | solution.py:79
  79.4 28.8 %all-gather.5.cloned.1.call-done = bf16[2048,256]{1,0:T(8,128)(2,1)} async-done(((bf16[64,256]{1,0:T(8,128)(2,1)}), bf16[2048,256]{1,0:T(8,128)(2,1)}) %all-gather.5.cloned.1.call-update) | async-done | bytes 1048592 | tf_op jit(solution)/shard_map/all_gather | solution.py:41
  109.7 152.1 %while.10 = (s32[]{:T(128)}, bf16[4,4,196,4,64]{2,4,3,1,0:T(8,128)(2,1)}, bf16[4,4,196,4,64]{2,4,3,1,0:T(8,128)(2,1)}, bf16[4,4,196,4,64]{2,4,3,1,0:T(8,128)(2,1...) while((s32[]{:T(128)}, ...), condition=%wide.region_9.10_spmd, body=%wide.region_4.9_spmd.sunk | while | flops 1884524672 | bytes 91089008 | solution.py:79
  110.0 11.6 %bitcast_reduce_fusion.2 = (f32[4,4,196]{2,0,1:T(4,128)S(1)}, f32[4,4,196,2048]{3,2,1,0:T(8,128)}) fusion(pred[4,2048]{1,0:T(4,128)(4,1)S(1)} %fusion.60, bf16[2048,4,64]{0,2,1:T(8,128)(2,1)S(1)} %get-tuple-element.194, bf16[4,4,196,4,64]{2,4,3,1,0:T(8,128)(2,1)} %get-tuple-element.191, s32[]{:T(128)S(6)} %copy.117), kind=kOutput, calls=%fused_computation.8.clone.1 | convolution fusion | flops 841348032 | bytes 27283716 | tf_op jit(solution)/shard_map/while/body/eval_jaxpr/fqhd,shd->fhqs/dot_general | solution.py:59
  124.1 9.7 %fusion.62 = f32[4,4,196]{2,0,1:T(4,128)S(1)} fusion(f32[4,4,196,2048]{3,2,1,0:T(8,128)} %get-tuple-element.166, f32[4,4,196]{2,0,1:T(4,128)S(1)} %copy.112, pred[4,2048]{1,0:T(4,128)(4,1)S(1)} %fusion.60), kind=kLoop, calls=%fused_computation.12.clone.1 | loop fusion | flops 25686976 | bytes 25723392 | tf_op jit(solution)/shard_map/while/body/eval_jaxpr/reduce_sum | solution.py:66
  133.8 11.4 %fusion.63 = f32[4,196,4,64]{1,3,2,0:T(8,128)S(1)} fusion(bf16[2048,4,64]{0,2,1:T(8,128)(2,1)S(1)} %get-tuple-element.195, f32[4,4,196,2048]{3,2,1,0:T(8,128)} %get-tuple-element.166, f32[4,4,196]{2,0,1:T(4,128)S(1)} %copy.113, f32[4,4,196]{2,0,1:T(4,128)S(1)} %copy.112, pred[4,2048]{1,0:T(4,128)(4,1)S(1)} %fusion.60), kind=kOutput, calls=%fused_computation.21.clone.1 | convolution fusion | flops 854196224 | bytes 27574784 | tf_op jit(solution)/shard_map/while/body/eval_jaxpr/fhqs,shd->fqhd/dot_general | solution.py:74
  147.9 11.6 %bitcast_reduce_fusion.2 = (f32[4,4,196]{2,0,1:T(4,128)S(1)}, f32[4,4,196,2048]{3,2,1,0:T(8,128)}) fusion(pred[4,2048]{1,0:T(4,128)(4,1)S(1)} %fusion.60, bf16[2048,4,64]{0,2,1:T(8,128)(2,1)S(1)} %get-tuple-element.194, bf16[4,4,196,4,64]{2,4,3,1,0:T(8,128)(2,1)} %get-tuple-element.191, s32[]{:T(128)S(6)} %copy.117), kind=kOutput, calls=%fused_computation.8.clone.1 | convolution fusion | flops 841348032 | bytes 27283716 | tf_op jit(solution)/shard_map/while/body/eval_jaxpr/fqhd,shd->fhqs/dot_general | solution.py:59
  162.0 9.7 %fusion.62 = f32[4,4,196]{2,0,1:T(4,128)S(1)} fusion(f32[4,4,196,2048]{3,2,1,0:T(8,128)} %get-tuple-element.166, f32[4,4,196]{2,0,1:T(4,128)S(1)} %copy.112, pred[4,2048]{1,0:T(4,128)(4,1)S(1)} %fusion.60), kind=kLoop, calls=%fused_computation.12.clone.1 | loop fusion | flops 25686976 | bytes 25723392 | tf_op jit(solution)/shard_map/while/body/eval_jaxpr/reduce_sum | solution.py:66
  171.7 11.4 %fusion.63 = f32[4,196,4,64]{1,3,2,0:T(8,128)S(1)} fusion(bf16[2048,4,64]{0,2,1:T(8,128)(2,1)S(1)} %get-tuple-element.195, f32[4,4,196,2048]{3,2,1,0:T(8,128)} %get-tuple-element.166, f32[4,4,196]{2,0,1:T(4,128)S(1)} %copy.113, f32[4,4,196]{2,0,1:T(4,128)S(1)} %copy.112, pred[4,2048]{1,0:T(4,128)(4,1)S(1)} %fusion.60), kind=kOutput, calls=%fused_computation.21.clone.1 | convolution fusion | flops 854196224 | bytes 27574784 | tf_op jit(solution)/shard_map/while/body/eval_jaxpr/fhqs,shd->fqhd/dot_general | solution.py:74
  185.9 11.6 %bitcast_reduce_fusion.2 = (f32[4,4,196]{2,0,1:T(4,128)S(1)}, f32[4,4,196,2048]{3,2,1,0:T(8,128)}) fusion(pred[4,2048]{1,0:T(4,128)(4,1)S(1)} %fusion.60, bf16[2048,4,64]{0,2,1:T(8,128)(2,1)S(1)} %get-tuple-element.194, bf16[4,4,196,4,64]{2,4,3,1,0:T(8,128)(2,1)} %get-tuple-element.191, s32[]{:T(128)S(6)} %copy.117), kind=kOutput, calls=%fused_computation.8.clone.1 | convolution fusion | flops 841348032 | bytes 27283716 | tf_op jit(solution)/shard_map/while/body/eval_jaxpr/fqhd,shd->fhqs/dot_general | solution.py:59
  200.0 9.7 %fusion.62 = f32[4,4,196]{2,0,1:T(4,128)S(1)} fusion(f32[4,4,196,2048]{3,2,1,0:T(8,128)} %get-tuple-element.166, f32[4,4,196]{2,0,1:T(4,128)S(1)} %copy.112, pred[4,2048]{1,0:T(4,128)(4,1)S(1)} %fusion.60), kind=kLoop, calls=%fused_computation.12.clone.1 | loop fusion | flops 25686976 | bytes 25723392 | tf_op jit(solution)/shard_map/while/body/eval_jaxpr/reduce_sum | solution.py:66
  209.7 11.4 %fusion.63 = f32[4,196,4,64]{1,3,2,0:T(8,128)S(1)} fusion(bf16[2048,4,64]{0,2,1:T(8,128)(2,1)S(1)} %get-tuple-element.195, f32[4,4,196,2048]{3,2,1,0:T(8,128)} %get-tuple-element.166, f32[4,4,196]{2,0,1:T(4,128)S(1)} %copy.113, f32[4,4,196]{2,0,1:T(4,128)S(1)} %copy.112, pred[4,2048]{1,0:T(4,128)(4,1)S(1)} %fusion.60), kind=kOutput, calls=%fused_computation.21.clone.1 | convolution fusion | flops 854196224 | bytes 27574784 | tf_op jit(solution)/shard_map/while/body/eval_jaxpr/fhqs,shd->fqhd/dot_general | solution.py:74
  223.8 11.6 %bitcast_reduce_fusion.2 = (f32[4,4,196]{2,0,1:T(4,128)S(1)}, f32[4,4,196,2048]{3,2,1,0:T(8,128)}) fusion(pred[4,2048]{1,0:T(4,128)(4,1)S(1)} %fusion.60, bf16[2048,4,64]{0,2,1:T(8,128)(2,1)S(1)} %get-tuple-element.194, bf16[4,4,196,4,64]{2,4,3,1,0:T(8,128)(2,1)} %get-tuple-element.191, s32[]{:T(128)S(6)} %copy.117), kind=kOutput, calls=%fused_computation.8.clone.1 | convolution fusion | flops 841348032 | bytes 27283716 | tf_op jit(solution)/shard_map/while/body/eval_jaxpr/fqhd,shd->fhqs/dot_general | solution.py:59
  237.9 9.7 %fusion.62 = f32[4,4,196]{2,0,1:T(4,128)S(1)} fusion(f32[4,4,196,2048]{3,2,1,0:T(8,128)} %get-tuple-element.166, f32[4,4,196]{2,0,1:T(4,128)S(1)} %copy.112, pred[4,2048]{1,0:T(4,128)(4,1)S(1)} %fusion.60), kind=kLoop, calls=%fused_computation.12.clone.1 | loop fusion | flops 25686976 | bytes 25723392 | tf_op jit(solution)/shard_map/while/body/eval_jaxpr/reduce_sum | solution.py:66
  247.6 11.4 %fusion.63 = f32[4,196,4,64]{1,3,2,0:T(8,128)S(1)} fusion(bf16[2048,4,64]{0,2,1:T(8,128)(2,1)S(1)} %get-tuple-element.195, f32[4,4,196,2048]{3,2,1,0:T(8,128)} %get-tuple-element.166, f32[4,4,196]{2,0,1:T(4,128)S(1)} %copy.113, f32[4,4,196]{2,0,1:T(4,128)S(1)} %copy.112, pred[4,2048]{1,0:T(4,128)(4,1)S(1)} %fusion.60), kind=kOutput, calls=%fused_computation.21.clone.1 | convolution fusion | flops 854196224 | bytes 27574784 | tf_op jit(solution)/shard_map/while/body/eval_jaxpr/fhqs,shd->fqhd/dot_general | solution.py:74
  261.8 6.7 %copy.90 = bf16[4,4,196,4,64]{4,3,2,1,0:T(4,128)(2,1)} copy(bf16[4,4,196,4,64]{2,4,3,1,0:T(8,128)(2,1)} %get-tuple-element.44) | data formatting | bytes 3211264 | tf_op jit(solution)/shard_map/reshape | solution.py:88
  273.3 6.2 %scatter_custom_fusion.2 = bf16[10240,256]{1,0:T(8,128)(2,1)} fusion(s32[320]{0:T(512)} %compare_select_fusion.3, bf16[]{:T(256)} %constant.42.clone.1, bf16[3136,256]{1,0:T(8,128)(2,1)S(1)} %reshape.188, s32[1024]{0:T(1024)} %pad_clamp_fusion.1), kind=kCustom, calls=%fused_computation.46 | custom fusion | bytes 5243392 | tf_op jit(solution)/shard_map/scatter | solution.py:24
  292.5 58.1 %all-to-all-done.1 = bf16[32,320,256]{2,1,0:T(8,128)(2,1)} async-done(((bf16[32,320,256]{2,1,0:T(8,128)(2,1)}), bf16[32,320,256]{2,1,0:T(8,128)(2,1)}, u32[]{:S(2)}, u32[]{:S(2)}) %all-to-all-start.1) | async-done | bytes 5242912 | tf_op jit(solution)/shard_map/all_to_all | solution.py:108
  355.7 37.9 %scatter_custom_fusion.1 = s32[10240]{0:T(1024)S(1)} fusion(s32[10240]{0:T(1024)S(1)} %compare_select_fusion, s32[10240]{0:T(1024)S(1)} %iota.12, s32[]{:T(128)} %constant.49.clone.1), kind=kCustom, calls=%fused_computation.62 | custom fusion | bytes 40964 | tf_op jit(solution)/shard_map/scatter | solution.py:97
  400.1 21.3 %all-to-all-done = bf16[32,320,256]{2,1,0:T(8,128)(2,1)} async-done(((bf16[32,320,256]{2,1,0:T(8,128)(2,1)}), bf16[32,320,256]{2,1,0:T(8,128)(2,1)}, u32[]{:S(2)}, u32[]{:S(2)}) %all-to-all-start) | async-done | bytes 5242912 | tf_op jit(solution)/shard_map/all_to_all | solution.py:109
  427.3 10.5 %all-reduce = (f32[320]{0:T(512)S(1)}, f32[320]{0:T(512)S(1)}) all-reduce(f32[320]{0:T(512)S(1)} %get-tuple-element.86, f32[320]{0:T(512)S(1)} %get-tuple-element.85), channel_id=1, replica_groups=mesh['tm'=32,'head'=4] {'head'}, use_global_device_ids=true, to_apply=%region_15.16 | all-reduce | flops 640 | bytes 5120 | tf_op jit(solution)/shard_map/psum | solution.py:124
  439.6 7.7 %psum.23 = f32[320]{0:T(512)S(1)} all-reduce(f32[320]{0:T(512)S(1)} %get-tuple-element.109), channel_id=1, replica_groups=mesh['tm'=32,'head'=4] {'head'}, use_global_device_ids=true, to_apply=%region_17.18 | all-reduce | flops 320 | bytes 2560 | tf_op jit(solution)/shard_map/psum | solution.py:131
  (99 shorter events, 112.4 us)
Async XLA Ops:
  7.2 1.1 copy-start
  7.2 70.7 %all-gather.3.cloned.1.call-start = ((), (), s32[]{:S(2)}) async-start(), calls=%async_computation.3 | async-start | bytes 1081344 | tf_op jit(solution)/shard_map/all_gather | solution.py:40
  14.9 3.6 copy-start.7
  18.3 89.9 %all-gather.5.cloned.1.call-start = ((), (), s32[]{:S(2)}) async-start(), calls=%async_computation.4 | async-start | bytes 1081344 | tf_op jit(solution)/shard_map/all_gather | solution.py:41
  40.3 6.7 %copy-start.8 = (bf16[1024,256]{1,0:T(8,128)(2,1)S(1)}, bf16[1024,256]{1,0:T(8,128)(2,1)}, u32[]{:S(2)}) copy-start(bf16[1024,256]{1,0:T(8,128)(2,1)} %param.12) | copy-start | bytes 1572868
  61.1 6.6 %copy-start.5 = (s32[16,512]{1,0:T(8,128)S(1)}, s32[16,512]{1,0:T(8,128)}, u32[]{:S(2)}) copy-start(s32[16,512]{1,0:T(8,128)} %param.16) | copy-start | bytes 98308
  67.8 8.0 %copy-start.6 = (s32[16,20]{1,0:T(8,128)S(1)}, s32[16,20]{1,0:T(8,128)}, u32[]{:S(2)}) copy-start(s32[16,20]{1,0:T(8,128)} %param.17) | copy-start | bytes 3844
  279.5 71.1 %all-to-all-start.1 = ((bf16[32,320,256]{2,1,0:T(8,128)(2,1)}), bf16[32,320,256]{2,1,0:T(8,128)(2,1)}, u32[]{:S(2)}, u32[]{:S(2)}) async-start(bf16[32,320,256]{2,1,0:T(8,128)(2,1)} %bitcast.108), calls=%async_computation.1 | async-start | bytes 10485760 | tf_op jit(solution)/shard_map/all_to_all | solution.py:108
  350.6 5.1 %copy-start.4 = (s32[10240]{0:T(1024)S(1)}, s32[10240]{0:T(1024)}, u32[]{:S(2)}) copy-start(s32[10240]{0:T(1024)} %param.18) | copy-start | bytes 122884
  350.6 48.0 %copy-start.2 = (bf16[256,1024]{1,0:T(8,128)(2,1)S(1)}, bf16[256,1024]{1,0:T(8,128)(2,1)}, u32[]{:S(2)}) copy-start(bf16[256,1024]{1,0:T(8,128)(2,1)} %param.15) | copy-start | bytes 1572868
  350.6 70.8 %all-to-all-start = ((bf16[32,320,256]{2,1,0:T(8,128)(2,1)}), bf16[32,320,256]{2,1,0:T(8,128)(2,1)}, u32[]{:S(2)}, u32[]{:S(2)}) async-start(bf16[32,320,256]{2,1,0:T(8,128)(2,1)} %bitcast.107), calls=%async_computation | async-start | bytes 10485760 | tf_op jit(solution)/shard_map/all_to_all | solution.py:109
  355.6 70.6 %reduce-scatter.2.cloned.1.call-start = ((), (), s32[]{:S(2)}) async-start(), calls=%async_computation.5 | async-start | bytes 1638400 | tf_op jit(solution)/shard_map/reduce_scatter | solution.py:114
  393.7 44.1 %copy-start.3 = (bf16[320,256]{1,0:T(8,128)(2,1)S(1)}, bf16[320,256]{1,0:T(8,128)(2,1)}, u32[]{:S(2)}) copy-start(bf16[320,256]{1,0:T(8,128)(2,1)} %param.19) | copy-start | bytes 491524
  393.7 54.2 %copy-start.1 = (bf16[1024,256]{1,0:T(8,128)(2,1)S(1)}, bf16[1024,256]{1,0:T(8,128)(2,1)}, u32[]{:S(2)}) copy-start(bf16[1024,256]{1,0:T(8,128)(2,1)} %param.13) | copy-start | bytes 1572868
Sparse Core Ops, SparseCore 0:
  18.4 45.3 all-gather.2
  66.1 42.0 all-gather.4
  400.2 25.7 reduce-scatter.1
where the time goes:
time: 457 us; the launch traced here: 454 us
  matrix products  127 us (28%)
  local copies, waits for them, and re-layouts  124 us (27%)
  waiting for transfers between devices  108 us (24%)
  other arithmetic  52.4 us (11%)
  blocking collectives  18.2 us (4%)
  between operations  14 us (3%)
  starting transfers between devices  10.6 us (2%)
    all_to_all x1, waiting for transfers between devices, body(): lax.all_to_all(packed_heads, 'tm', split_axis=0, concat_axis=0, tiled=True)  58.1 us
    dot_general x4, matrix products, attend(): jnp.einsum('fqhd,shd->fhqs', block_q, summary_keys, preferred_element_typ...  46.4 us
    dot_general x4, matrix products, attend(): jnp.einsum('fhqs,shd->fqhd', far_weights, summary_values, preferred_eleme...  45.5 us
    reduce_sum x4, other arithmetic, attend(): jnp.sum(far_exp, axis=3, keepdims=True)  38.6 us
    scatter x1, local copies, waits for them, and re-layouts, body(): jnp.zeros((total_rows,), jnp.int32).at[slot]  37.9 us
    all_gather x1, waiting for transfers between devices, body(): lax.all_gather(pool_quadrants(values_local, frame_count), 'tm', axis=0, t...  28.8 us
    all_to_all x1, waiting for transfers between devices, body(): lax.all_to_all(packed_tokens, 'tm', split_axis=0, concat_axis=0, tiled=True)  21.3 us
    while x3, local copies, waits for them, and re-layouts, body(): lax.map(attend, (queries.reshape(shape_q), keys_local.reshape(shape_q), v...  19.9 us
  transfers between devices with their start and end apart: 5, of which 3 were waited for; matrix products, arithmetic and copies ran while one was open for 26% of the time, Pallas kernels for 0%

commit v1 on v0

v1 whole, which is shorter than its diff:
```python
import numpy as np

import jax
import jax.numpy as jnp
from jax import lax
from jax.experimental import pallas as pl
from jax.experimental.pallas import tpu as pltpu
from jax.sharding import PartitionSpec as P

HEAD_DIM = 64
PATCHES = 196
CAP = 48
NEG = -1e30
EPS = 1e-06
BF = jnp.bfloat16
F32 = jnp.float32


def nt(a, b):
    return lax.dot_general(a, b, (((1,), (1,)), ((), ())), preferred_element_type=F32)


def nn(a, b):
    return lax.dot_general(a, b, (((1,), (0,)), ((), ())), preferred_element_type=F32)


def project_kernel(x_ref, wq_ref, wk_ref, wv_ref, pool_ref, pos_ref, k_ref, v_ref, s_ref, q_ref, vis_ref):
    x = x_ref[...]
    rows = x.shape[0]
    keep = pos_ref.shape[0]
    cols = wk_ref.shape[1]
    k = nn(x, wk_ref[...]).astype(BF)
    v = nn(x, wv_ref[...]).astype(BF)
    k_ref[...] = k
    v_ref[...] = v
    pool = pool_ref[...]
    s_ref[:, :, :cols] = (nn(pool, k) / 7.0).astype(BF).reshape(4, 4, cols)
    s_ref[:, :, cols:] = (nn(pool, v) / 7.0).astype(BF).reshape(4, 4, cols)
    pick = (pos_ref[...] == lax.broadcasted_iota(jnp.int32, (keep, rows), 1)).astype(F32).astype(BF)
    vis = nn(pick, x).astype(BF)
    vis_ref[...] = vis
    q_ref[...] = (nn(vis, wq_ref[...]).astype(BF).astype(F32) * HEAD_DIM ** -0.5).astype(BF)


def local_kernel(q_ref, k_ref, v_ref, o_ref, ml_ref):
    q = q_ref[...]
    k = k_ref[...]
    v = v_ref[...]
    rows, cols = q.shape
    keep = rows // 4
    heads = cols // HEAD_DIM
    r = lax.broadcasted_iota(jnp.int32, (rows, 1), 0)
    frame = sum((r >= keep * i).astype(jnp.int32) for i in (1, 2, 3))
    c = lax.broadcasted_iota(jnp.int32, (rows, k.shape[0]), 1) - frame * PATCHES
    inside = (c >= 0) & (c < PATCHES)
    lane = lax.broadcasted_iota(jnp.int32, (rows, cols), 1)
    lane2 = lax.broadcasted_iota(jnp.int32, (rows, 128), 1)
    out = jnp.zeros((rows, cols), F32)
    ml = jnp.zeros((rows, 128), F32)
    for h in range(heads):
        mine = (lane >= h * HEAD_DIM) & (lane < (h + 1) * HEAD_DIM)
        qh = jnp.where(mine, q, jnp.zeros_like(q))
        s = jnp.where(inside, nt(qh, k), NEG)
        m = jnp.max(s, axis=1, keepdims=True)
        e = jnp.exp(s - m)
        total = jnp.sum(e, axis=1, keepdims=True)
        out = jnp.where(mine, nn(e.astype(BF), v), out)
        ml = jnp.where(lane2 == h, m, jnp.where(lane2 == heads + h, total, ml))
    o_ref[...] = out
    ml_ref[...] = ml


def far_kernel(q_ref, sa_ref, sb_ref, pa_ref, pb_ref, pick_ref, o_ref, ml_ref, out_ref):
    q = q_ref[...]
    rows, cols = q.shape
    heads = cols // HEAD_DIM
    lane = lax.broadcasted_iota(jnp.int32, (rows, cols), 1)
    pick = pick_ref[...]
    bias = [nn(pick, p[...]) for p in (pa_ref, pb_ref)]
    count = sa_ref.shape[0] * 16
    out = jnp.zeros((rows, cols), F32)
    for h in range(heads):
        mine = (lane >= h * HEAD_DIM) & (lane < (h + 1) * HEAD_DIM)
        qh = jnp.where(mine, q, jnp.zeros_like(q))
        scores = []
        top = ml_ref[:, h : h + 1]
        for part, ref in enumerate((sa_ref, sb_ref)):
            for u in range(4):
                key = ref[:, u, :, :cols].reshape(count, cols)
                s = nt(qh, key) + bias[part]
                top = jnp.maximum(top, jnp.max(s, axis=1, keepdims=True))
                scores.append(s)
        near = jnp.exp(ml_ref[:, h : h + 1] - top)
        total = near * ml_ref[:, heads + h : heads + h + 1]
        acc = near * o_ref[...]
        for part, ref in enumerate((sa_ref, sb_ref)):
            for u in range(4):
                e = jnp.exp(scores[part * 4 + u] - top)
                total = total + jnp.sum(e, axis=1, keepdims=True)
                acc = acc + nn(e.astype(BF), ref[:, u, :, cols:].reshape(count, cols))
        out = jnp.where(mine, acc / total, out)
    out_ref[...] = out.astype(BF)


def whole(n):
    return [pl.BlockSpec(memory_space=pltpu.VMEM) for _ in range(n)]


def params(mib):
    return pltpu.CompilerParams(vmem_limit_bytes=mib * 2**20)


def tm_index(z, y, c):
    return ((z % 4) * 4 + y % 4) * 2 + c


SAME_CORE = [[tm_index(z, y, c) for z in range(4) for y in range(4)] for c in range(2)]


def body(tokens, w_query, w_key, w_value, w_out, pattern, visible, slot, pred):
    n_peers = lax.axis_size("tm")
    me = lax.axis_index("tm")
    core = me % 2
    head = lax.axis_index("head")
    n_heads = lax.axis_size("head")
    frames, keep = visible.shape
    width = tokens.shape[1]
    cols = w_query.shape[1]
    own = frames * keep
    steps = frames // 4
    block = 4 * PATCHES
    chunk = 4 * keep

    r = np.arange(block)
    p = r % PATCHES
    quadrant = 2 * (p // 14 >= 7) + (p % 14 >= 7)
    pool = np.zeros((16, block), np.float32)
    pool[quadrant * 4 + r // PATCHES, r] = 1.0
    pos = (jnp.arange(frames, dtype=jnp.int32)[:, None] % 4 * PATCHES + visible).reshape(own, 1)

    fixed = lambda i: (0, 0)
    k, v, summary, q, vis = pl.pallas_call(
        project_kernel,
        grid=(steps,),
        in_specs=[
            pl.BlockSpec((block, width), lambda i: (i, 0)),
            pl.BlockSpec((width, cols), fixed),
            pl.BlockSpec((width, cols), fixed),
            pl.BlockSpec((width, cols), fixed),
            pl.BlockSpec((16, block), fixed),
            pl.BlockSpec((chunk, 1), lambda i: (i, 0)),
        ],
        out_specs=[
            pl.BlockSpec((block, cols), lambda i: (i, 0)),
            pl.BlockSpec((block, cols), lambda i: (i, 0)),
            pl.BlockSpec((4, None, 4, 2 * cols), lambda i: (0, i, 0, 0)),
            pl.BlockSpec((chunk, cols), lambda i: (i, 0)),
            pl.BlockSpec((chunk, width), lambda i: (i, 0)),
        ],
        out_shape=[
            jax.ShapeDtypeStruct((frames * PATCHES, cols), BF),
            jax.ShapeDtypeStruct((frames * PATCHES, cols), BF),
            jax.ShapeDtypeStruct((4, steps, 4, 2 * cols), BF),
            jax.ShapeDtypeStruct((own, cols), BF),
            jax.ShapeDtypeStruct((own, width), BF),
        ],
        compiler_params=params(40),
        cost_estimate=pl.CostEstimate(flops=4 * 10**9, bytes_accessed=10**7, transcendentals=0),
        name="project",
    )(tokens, w_query, w_key, w_value, jnp.asarray(pool, BF), pos)
    summary = summary.reshape(4, frames, 2 * cols)

    gathered = lax.all_to_all(
        jnp.broadcast_to(summary[None], (n_peers // 2,) + summary.shape),
        "tm", 0, 0, axis_index_groups=SAME_CORE, tiled=True,
    )
    gathered_b = lax.ppermute(gathered, "tm", [(t, t ^ 1) for t in range(n_peers)])

    owner_all = slot // own
    my_slots = lax.dynamic_slice_in_dim(slot, me * own, own)
    my_owner = my_slots // own
    before = np.tril(np.ones((own, own), np.float32), -1)
    same = (my_owner[:, None] == my_owner[None, :]) & (before > 0)
    place = my_owner * CAP + jnp.sum(same, axis=1, dtype=jnp.int32)
    pack = (jnp.arange(n_peers * CAP, dtype=jnp.int32)[:, None] == place[None, :]).astype(BF)
    coming = (owner_all == me).reshape(n_peers, own)
    rank = jnp.dot(coming.astype(BF), jnp.asarray(before.T, BF), preferred_element_type=F32).astype(jnp.int32)
    rank = jnp.where(coming, rank, -1)
    hit = rank[:, None, :] == jnp.arange(CAP, dtype=jnp.int32)[None, :, None]
    student = jnp.max(jnp.where(hit, (slot % own).reshape(n_peers, 1, own), -1), axis=2)
    unpack = (jnp.arange(own, dtype=jnp.int32)[:, None] == student.reshape(1, -1)).astype(BF)

    def route(x):
        packed = jnp.dot(pack, x, preferred_element_type=F32).astype(BF).reshape(n_peers, CAP, -1)
        got = lax.all_to_all(packed, "tm", 0, 0, tiled=True)
        return jnp.dot(unpack, got.reshape(n_peers * CAP, -1), preferred_element_type=F32).astype(BF)

    token_rows = route(lax.dynamic_slice_in_dim(vis, head * cols, cols, 1))

    o_near, ml = pl.pallas_call(
        local_kernel,
        grid=(steps,),
        in_specs=[
            pl.BlockSpec((chunk, cols), lambda i: (i, 0)),
            pl.BlockSpec((block, cols), lambda i: (i, 0)),
            pl.BlockSpec((block, cols), lambda i: (i, 0)),
        ],
        out_specs=[
            pl.BlockSpec((chunk, cols), lambda i: (i, 0)),
            pl.BlockSpec((chunk, 128), lambda i: (i, 0)),
        ],
        out_shape=[
            jax.ShapeDtypeStruct((own, cols), F32),
            jax.ShapeDtypeStruct((own, 128), F32),
        ],
        compiler_params=params(40),
        cost_estimate=pl.CostEstimate(flops=10**9, bytes_accessed=4 * 10**6, transcendentals=10**6),
        name="near",
    )(q, k, v)

    banned = jnp.where(pattern > 0, 0.0, NEG).astype(BF).reshape(frames, n_peers // 2, 2, frames)
    ban_a = lax.dynamic_index_in_dim(banned, core, 2, keepdims=False).reshape(frames, -1)
    ban_b = lax.dynamic_index_in_dim(banned, 1 - core, 2, keepdims=False).reshape(frames, -1)
    pick = jnp.asarray(np.arange(own)[:, None] // keep == np.arange(frames)[None, :], BF)
    attended = pl.pallas_call(
        far_kernel,
        in_specs=whole(8),
        out_specs=pl.BlockSpec(memory_space=pltpu.VMEM),
        out_shape=jax.ShapeDtypeStruct((own, cols), BF),
        compiler_params=params(48),
        cost_estimate=pl.CostEstimate(flops=3 * 10**9, bytes_accessed=3 * 10**6, transcendentals=3 * 10**6),
        name="far",
    )(q, gathered, gathered_b, ban_a, ban_b, pick, o_near, ml)

    rows = route(attended)
    partial = jnp.dot(rows, w_out, preferred_element_type=F32)

    def column_block(h):
        return lax.dynamic_slice_in_dim(partial, (h % n_heads) * cols, cols, 1)

    def to(d):
        return [(h, (h + d) % n_heads) for h in range(n_heads)]

    raw = token_rows.astype(F32) + column_block(head)
    for d in (1, 3, 2):
        raw = raw + lax.ppermute(column_block(head + d).astype(BF), "head", to(d)).astype(F32)
    guess = pred.astype(F32)
    stats = jnp.stack([
        jnp.sum(raw, axis=1),
        jnp.sum(raw * raw, axis=1),
        jnp.sum(guess * raw, axis=1),
        jnp.sum(guess, axis=1),
        jnp.sum(guess * guess, axis=1),
    ])
    total = stats
    for d in (1, 3, 2):
        total = total + lax.ppermute(stats, "head", to(d))
    mean = total[0] / width
    var = total[1] / width - mean * mean
    scale = lax.rsqrt(var + EPS)
    normed = (raw - mean[:, None]) * scale[:, None]
    cross = (total[2] - mean * total[3]) * scale
    square = (total[1] - 2.0 * mean * total[0] + width * mean * mean) * scale * scale
    row_loss = (total[4] - 2.0 * cross + square) / width
    return normed.astype(BF), row_loss


def solution(mesh):
    return jax.shard_map(
        body,
        mesh=mesh,
        in_specs=(
            P("tm", None),
            P(None, "head"),
            P(None, "head"),
            P(None, "head"),
            P("head", None),
            P("tm", None),
            P("tm", None),
            P(),
            P("tm", "head"),
        ),
        out_specs=(P("tm", "head"), P("tm")),
        check_vma=False,
    )
```

time: 457 us -> 115 us (0.25)
  matrix products: 127 us -> 5.78 us
  local copies, waits for them, and re-layouts: 124 us -> 16.9 us
  waiting for transfers between devices: 108 us -> 23.7 us
  other arithmetic: 52.4 us -> 4.77 us
  Pallas kernels: 0 us -> 19.2 us
  between operations: 14 us -> 0.92 us
  starting transfers between devices: 10.6 us -> 18.2 us
  blocking collectives: 18.2 us -> 25.1 us
    dot_general x20 -> x5, matrix products: 127 us -> 5.78 us  [the longest x2 2.92 us: route(): jnp.dot(pack, x, preferred_element_type=F32).astype(BF)]
    all_to_all x2, waiting for transfers between devices: 79.4 us -> 20.3 us  [route(): got = lax.all_to_all(packed, 'tm', 0, 0, tiled=True)]
    scatter x3 -> x0, local copies, waits for them, and re-layouts: 50.2 us -> none  [the longest x1 37.9 us: body(): jnp.zeros((total_rows,), jnp.int32).at[slot]]
    reduce_sum x12 -> x1, other arithmetic: 49.5 us -> 0.25 us  [body(): place = my_owner * CAP + jnp.sum(same, axis=1, dtype=jnp.int32)]
    all_gather x2 -> x0, waiting for transfers between devices: 28.8 us -> none  [the longest x1 28.8 us: body(): lax.all_gather(pool_quadrants(values_local, frame_count), 'tm', axis=0, t...]
    all_to_all x0 -> x1, blocking collectives: none -> 25.1 us  [body(): lax.all_to_all(jnp.broadcast_to(summary[None], (n_peers // 2,) + summary....]
    reshape x6 -> x5, local copies, waits for them, and re-layouts: 23.3 us -> 2.12 us  [the longest x1 0.99 us: body(): lax.dynamic_index_in_dim(banned, 1 - core, 2, keepdims=False)]
    while x3 -> x0, local copies, waits for them, and re-layouts: 19.9 us -> none  [body(): lax.map(attend, (queries.reshape(shape_q), keys_local.reshape(shape_q), v...]
  transfers between devices with their start and end apart: 5 -> 9, of which waited for: 3 -> 4; matrix products, arithmetic and copies ran while one was open for 26% -> 8% of each run, Pallas kernels for 0% -> 6%
where the time goes in v1:
time: 115 us
  blocking collectives  25.1 us (22%)
  waiting for transfers between devices  23.7 us (21%)
  Pallas kernels  19.2 us (17%)
  starting transfers between devices  18.2 us (16%)
  local copies, waits for them, and re-layouts  16.9 us (15%)
  matrix products  5.78 us (5%)
  other arithmetic  4.77 us (4%)
    all_to_all x1, blocking collectives, body(): lax.all_to_all(jnp.broadcast_to(summary[None], (n_peers // 2,) + summary....  25.1 us
    all_to_all x2, waiting for transfers between devices, route(): got = lax.all_to_all(packed, 'tm', 0, 0, tiled=True)  20.3 us
    unnamed x30, local copies, waits for them, and re-layouts  11.9 us
    all_to_all x2, starting transfers between devices, route(): got = lax.all_to_all(packed, 'tm', 0, 0, tiled=True)  8 us
    pallas_call x1, Pallas kernels, body(): pl.pallas_call(local_kernel, grid=(steps,), in_specs=[pl.BlockSpec((chunk...  6.87 us
    pallas_call x1, Pallas kernels, body(): pl.pallas_call(project_kernel, grid=(steps,), in_specs=[pl.BlockSpec((blo...  6.44 us
    pallas_call x1, Pallas kernels, body(): pl.pallas_call(far_kernel, in_specs=whole(8), out_specs=pl.BlockSpec(memo...  5.84 us
    ppermute x3, starting transfers between devices, body(): lax.ppermute(column_block(head + d).astype(BF), 'head', to(d)).astype(F32)  5.11 us
  transfers between devices with their start and end apart: 9, of which 4 were waited for; matrix products, arithmetic and copies ran while one was open for 8% of the time, Pallas kernels for 6%

profile of v1, /device:TPU:0, one launch (start us, length us, event | category | flops | bytes accessed | tf_op | source)
XLA Modules:
  0.0 114.6 jit_solution(17737872542608211493)
XLA Ops:
  1.6 2.8 %copy-done.1 = bf16[3136,1024]{1,0:T(8,128)(2,1)S(1)} copy-done((bf16[3136,1024]{1,0:T(8,128)(2,1)S(1)}, bf16[3136,1024]{1,0:T(8,128)(2,1)}, u32[]{:S(2)}) %copy-start.1) | copy-done | bytes 6422552
  8.3 6.4 %project.1 = (bf16[3136,256]{1,0:T(8,128)(2,1)S(1)}, bf16[3136,256]{1,0:T(8,128)(2,1)S(1)}, bf16[4,4,4,512]{3,2,1,0:T(4,128)(2,1)S(1)}, bf16[320,256]{1,0:T(8,128)(2,1)S(1)}, bf16[320,1024]{1,0:T(8,128)(2,1)S(1)}) custom-call(bf16[3136,1024]{1,0:T(8,128)(2,1)S(1)} %copy-done.1, bf16[1024,256]{1,0:T(8,128)(2,1)S(1)} %copy-done.2, ...), custom_call_target="tpu_custom_call" | custom-call | flops 4000000000 | bytes 10000000 | tf_op jit(solution)/shard_map/project/pallas_call | solution.py:142
  14.8 1.2 %copy-done.7 = bf16[3136,256]{1,0:T(8,128)(2,1)} copy-done((bf16[3136,256]{1,0:T(8,128)(2,1)}, bf16[3136,256]{1,0:T(8,128)(2,1)S(1)}, u32[]{:S(2)}) %copy-start.7) | copy-done | bytes 1605656
  15.9 1.2 %copy-done.9 = bf16[3136,256]{1,0:T(8,128)(2,1)} copy-done((bf16[3136,256]{1,0:T(8,128)(2,1)}, bf16[3136,256]{1,0:T(8,128)(2,1)S(1)}, u32[]{:S(2)}) %copy-start.9) | copy-done | bytes 1605656
  17.2 25.1 %all_to_all.15.sa_ref = bf16[16,4,16,512]{3,2,1,0:T(8,128)(2,1)S(1)} all-to-all(bf16[16,4,16,512]{3,2,1,0:T(8,128)(2,1)S(1)} %broadcast_in_dim.48), channel_id=1, replica_groups={{0,8,16,24,32,40,48,56,64,72,80,88,96,104,112,120},{4,12,20,28,36,44,52..., dimensions={0} | all-to-all | bytes 2097152 | tf_op jit(solution)/shard_map/all_to_all | solution.py:173
  43.1 2.4 %dynamic-slice_reduce_fusion = (bf16[16,16,16]{2,1,0:T(8,128)(2,1)}, bf16[16,16,16]{2,1,0:T(8,128)(2,1)S(1)}) fusion(bf16[16,16,2,16]{3,2,1,0:T(2,128)(2,1)} %reshape.80, s32[]{:T(128)S(6)} %select_n.98, s32[]{:T(128)S(6)} %select_n.97), kind=kLoop, calls=%fused_computation.32 | loop fusion | bytes 32776 | tf_op jit(solution)/shard_map/jit(dynamic_index_in_dim)/dynamic_slice | solution.py:223
  46.7 1.4 %copy-done.8 = bf16[3136,256]{1,0:T(8,128)(2,1)S(1)} copy-done((bf16[3136,256]{1,0:T(8,128)(2,1)S(1)}, bf16[3136,256]{1,0:T(8,128)(2,1)}, u32[]{:S(2)}) %copy-start.8) | copy-done | bytes 1605656
  48.1 1.4 %copy-done.10 = bf16[3136,256]{1,0:T(8,128)(2,1)S(1)} copy-done((bf16[3136,256]{1,0:T(8,128)(2,1)S(1)}, bf16[3136,256]{1,0:T(8,128)(2,1)}, u32[]{:S(2)}) %copy-start.10) | copy-done | bytes 1605656
  49.5 6.9 %near.1 = (f32[320,256]{1,0:T(8,128)S(1)}, f32[320,128]{1,0:T(8,128)S(1)}) custom-call(bf16[320,256]{1,0:T(8,128)(2,1)S(1)} %get-tuple-element.10.q_ref, bf16[3136,256]{1,0:T(8,128)(2,1)S(1)} %copy-done.8, bf16[3136,256]{1,0:T(8,128)(2,1)S(1)} %copy-done.10), custom_call_target="tpu_custom_call" | custom-call | flops 1000000000 | bytes 4000000 | tf_op jit(solution)/shard_map/near/pallas_call | solution.py:200
  58.3 5.8 %far.1 = bf16[320,256]{1,0:T(8,128)(2,1)S(1)} custom-call(bf16[320,256]{1,0:T(8,128)(2,1)S(1)} %get-tuple-element.10.q_ref, bf16[16,4,16,512]{3,2,1,0:T(8,128)(2,1)S(1)} %all_to_all.15.sa_ref, bf16[16,4,16,512]{3,2,1,0:T(8,128)(2,1)S(1)} %collective-permute-done.sb_ref, bf16[16,256]{1,0:T(8,128)(2,1)S(1)} %reshape.81.pa_ref, ...), custom_call_target="tpu_custom_call" | custom-call | flops 3000000000 | bytes 3000000 | tf_op jit(solution)/shard_map/far/pallas_call | solution.py:225
  64.1 1.5 %convolution_convert_fusion = bf16[1536,256]{1,0:T(8,128)(2,1)} fusion(bf16[320,256]{1,0:T(8,128)(2,1)S(1)} %far.1, s32[320]{0:T(512)S(1)} %multiply_add_fusion), kind=kOutput, calls=%fused_computation | convolution fusion | flops 252542976 | bytes 951552 | tf_op jit(solution)/shard_map/dot_general | solution.py:194
  65.6 3.9 %all-to-all-start.2 = ((bf16[32,48,256]{2,1,0:T(8,128)(2,1)}), bf16[32,48,256]{2,1,0:T(8,128)(2,1)S(1)}, u32[]{:S(2)}, u32[]{:S(2)}) async-start(bf16[32,48,256]{2,1,0:T(8,128)(2,1)} %bitcast.2), calls=%async_computation.2 | async-start | bytes 1572864 | tf_op jit(solution)/shard_map/all_to_all | solution.py:195
  69.7 1.4 %convolution_convert_fusion.1 = bf16[1536,256]{1,0:T(8,128)(2,1)} fusion(s32[320]{0:T(512)S(1)} %multiply_add_fusion, bf16[320,1024]{1,0:T(8,128)(2,1)S(1)} %get-tuple-element.9, s32[]{:T(128)S(6)} %select_n.94), kind=kOutput, calls=%fused_computation.1 | convolution fusion | flops 252542976 | bytes 952324 | tf_op jit(solution)/shard_map/dot_general | solution.py:194
  71.2 12.9 %all-to-all-done.2 = bf16[32,48,256]{2,1,0:T(8,128)(2,1)S(1)} async-done(((bf16[32,48,256]{2,1,0:T(8,128)(2,1)}), bf16[32,48,256]{2,1,0:T(8,128)(2,1)S(1)}, u32[]{:S(2)}, u32[]{:S(2)}) %all-to-all-start.2) | async-done | bytes 786464 | tf_op jit(solution)/shard_map/all_to_all | solution.py:195
  84.1 4.1 %all-to-all-start = ((bf16[32,48,256]{2,1,0:T(8,128)(2,1)}), bf16[32,48,256]{2,1,0:T(8,128)(2,1)S(1)}, u32[]{:S(2)}, u32[]{:S(2)}) async-start(bf16[32,48,256]{2,1,0:T(8,128)(2,1)} %bitcast), calls=%async_computation | async-start | bytes 1572864 | tf_op jit(solution)/shard_map/all_to_all | solution.py:195
  90.2 1.6 %collective-permute-start.1 = (bf16[320,256]{1,0:T(8,128)(2,1)S(1)}, bf16[320,256]{1,0:T(8,128)(2,1)S(1)}, u32[]{:S(2)}, u32[]{:S(2)}) collective-permute-start(bf16[320,256]{1,0:T(8,128)(2,1)S(1)} %get-tuple-element.31), channel_id=1, source_target_pairs={{0,1},{1,2},{2,3},{3,0},{4,5},{5,6},{6,7},{7,4},{8,9},{9,10},{10,1... | collective-permute-start | bytes 491528 | tf_op jit(solution)/shard_map/ppermute | solution.py:246
  91.8 1.7 %collective-permute-start.2 = (bf16[320,256]{1,0:T(8,128)(2,1)S(1)}, bf16[320,256]{1,0:T(8,128)(2,1)}, u32[]{:S(2)}, u32[]{:S(2)}) collective-permute-start(bf16[320,256]{1,0:T(8,128)(2,1)S(1)} %get-tuple-element.33), channel_id=1, source_target_pairs={{0,3},{1,0},{2,1},{3,2},{4,7},{5,4},{6,5},{7,6},{8,11},{9,8},{10,9... | collective-permute-start | bytes 491528 | tf_op jit(solution)/shard_map/ppermute | solution.py:246
  93.5 1.8 %collective-permute-start.3 = (bf16[320,256]{1,0:T(8,128)(2,1)S(1)}, bf16[320,256]{1,0:T(8,128)(2,1)}, u32[]{:S(2)}, u32[]{:S(2)}) collective-permute-start(bf16[320,256]{1,0:T(8,128)(2,1)S(1)} %get-tuple-element.32), channel_id=1, source_target_pairs={{0,2},{1,3},{2,0},{3,1},{4,6},{5,7},{6,4},{7,5},{8,10},{9,11},{10,... | collective-permute-start | bytes 491528 | tf_op jit(solution)/shard_map/ppermute | solution.py:246
  95.3 7.4 %all-to-all-done = bf16[32,48,256]{2,1,0:T(8,128)(2,1)S(1)} async-done(((bf16[32,48,256]{2,1,0:T(8,128)(2,1)}), bf16[32,48,256]{2,1,0:T(8,128)(2,1)S(1)}, u32[]{:S(2)}, u32[]{:S(2)}) %all-to-all-start) | async-done | bytes 786464 | tf_op jit(solution)/shard_map/all_to_all | solution.py:195
  102.8 1.8 %fusion.14 = (f32[320]{0:T(512)S(1)}, f32[320]{0:T(512)S(1)}, f32[320]{0:T(512)S(1)}, f32[320]{0:T(512)S(1)}, f32[320]{0:T(512)S(1)}, /*index=5*/f32[320,256]{1,0:T(8,128)S(1)}) fusion(bf16[320,256]{1,0:T(8,128)(2,1)} %param.21, bf16[320,256]{1,0:T(8,128)(2,1)} %collective-permute-done.3, bf16[320,256]{1,0:T(8,128)(2,1)} %collective-permute-done.2, ...), kind=kOutput, calls=%fused_computation.24 | convolution fusion | flops 253622720 | bytes 2109700 | tf_op jit(solution)/shard_map/dot_general | solution.py:196
  104.6 1.6 %collective-permute-start.4 = (f32[5,320]{1,0:T(8,128)S(1)}, f32[5,320]{1,0:T(8,128)S(1)}, u32[]{:S(2)}, u32[]{:S(2)}) collective-permute-start(f32[5,320]{1,0:T(8,128)S(1)} %stack.23), channel_id=1, source_target_pairs={{0,1},{1,2},{2,3},{3,0},{4,5},{5,6},{6,7},{7,4},{8,9},{9,10},{10,1... | collective-permute-start | bytes 19208 | tf_op jit(solution)/shard_map/ppermute | solution.py:257
  106.2 1.8 %collective-permute-start.5 = (f32[5,320]{1,0:T(8,128)S(1)}, f32[5,320]{1,0:T(8,128)S(1)}, u32[]{:S(2)}, u32[]{:S(2)}) collective-permute-start(f32[5,320]{1,0:T(8,128)S(1)} %stack.23), channel_id=1, source_target_pairs={{0,3},{1,0},{2,1},{3,2},{4,7},{5,4},{6,5},{7,6},{8,11},{9,8},{10,9... | collective-permute-start | bytes 19208 | tf_op jit(solution)/shard_map/ppermute | solution.py:257
  107.9 1.8 %collective-permute-start.6 = (f32[5,320]{1,0:T(8,128)S(1)}, f32[5,320]{1,0:T(8,128)S(1)}, u32[]{:S(2)}, u32[]{:S(2)}) collective-permute-start(f32[5,320]{1,0:T(8,128)S(1)} %stack.23), channel_id=1, source_target_pairs={{0,2},{1,3},{2,0},{3,1},{4,6},{5,7},{6,4},{7,5},{8,10},{9,11},{10,... | collective-permute-start | bytes 19208 | tf_op jit(solution)/shard_map/ppermute | solution.py:257
  109.8 3.3 %collective-permute-done.6 = f32[5,320]{1,0:T(8,128)S(1)} collective-permute-done((f32[5,320]{1,0:T(8,128)S(1)}, f32[5,320]{1,0:T(8,128)S(1)}, u32[]{:S(2)}, u32[]{:S(2)}) %collective-permute-start.6) | collective-permute-done | bytes 6432 | tf_op jit(solution)/shard_map/ppermute | solution.py:257
  (63 shorter events, 12.5 us)
Async XLA Ops:
  0.6 88.6 %copy-start = (bf16[256,1024]{1,0:T(8,128)(2,1)S(1)}, bf16[256,1024]{1,0:T(8,128)(2,1)}, u32[]{:S(2)}) copy-start(bf16[256,1024]{1,0:T(8,128)(2,1)} %param.17) | copy-start | bytes 1572868
  1.6 2.8 %copy-start.1 = (bf16[3136,1024]{1,0:T(8,128)(2,1)S(1)}, bf16[3136,1024]{1,0:T(8,128)(2,1)}, u32[]{:S(2)}) copy-start(bf16[3136,1024]{1,0:T(8,128)(2,1)} %x_ref.1) | copy-start | bytes 19267588
  4.4 1.0 copy-start.2
  5.5 1.0 copy-start.3
  6.5 1.0 copy-start.4
  7.5 0.7 copy-start.6
  14.7 1.2 %copy-start.7 = (bf16[3136,256]{1,0:T(8,128)(2,1)}, bf16[3136,256]{1,0:T(8,128)(2,1)S(1)}, u32[]{:S(2)}) copy-start(bf16[3136,256]{1,0:T(8,128)(2,1)S(1)} %get-tuple-element.12.k_ref) | copy-start | bytes 4816900
  15.9 1.2 %copy-start.9 = (bf16[3136,256]{1,0:T(8,128)(2,1)}, bf16[3136,256]{1,0:T(8,128)(2,1)S(1)}, u32[]{:S(2)}) copy-start(bf16[3136,256]{1,0:T(8,128)(2,1)S(1)} %get-tuple-element.13.v_ref) | copy-start | bytes 4816900
  17.1 25.2 %copy-start.14 = (s32[16,512]{1,0:T(8,128)S(1)}, s32[16,512]{1,0:T(8,128)}, u32[]{:S(2)}) copy-start(s32[16,512]{1,0:T(8,128)} %param.18) | copy-start | bytes 98308
  42.3 15.9 %collective-permute-start = (bf16[16,4,16,512]{3,2,1,0:T(8,128)(2,1)S(1)}, bf16[16,4,16,512]{3,2,1,0:T(8,128)(2,1)S(1)}, u32[]{:S(2)}, u32[]{:S(2)}) collective-permute-start(bf16[16,4,16,512]{3,2,1,0:T(8,128)(2,1)S(1)} %all_to_all.15.sa_ref), channel_id=1, source_target_pairs={{0,4},{4,0},{8,12},{12,8},{16,20},{20,16},{24,28},{28,24},{32,36},... | collective-permute-start | bytes 3145736 | tf_op jit(solution)/shard_map/ppermute | solution.py:177
  45.7 12.6 %copy-start.5 = (bf16[320,16]{1,0:T(8,128)(2,1)S(1)}, bf16[320,16]{1,0:T(8,128)(2,1)}, u32[]{:S(2)}) copy-start(bf16[320,16]{1,0:T(8,128)(2,1)} %constant.127.clone.pick_ref) | copy-start | bytes 30724
  46.7 1.4 %copy-start.8 = (bf16[3136,256]{1,0:T(8,128)(2,1)S(1)}, bf16[3136,256]{1,0:T(8,128)(2,1)}, u32[]{:S(2)}) copy-start(bf16[3136,256]{1,0:T(8,128)(2,1)} %copy-done.7) | copy-start | bytes 4816900
  48.1 1.4 %copy-start.10 = (bf16[3136,256]{1,0:T(8,128)(2,1)S(1)}, bf16[3136,256]{1,0:T(8,128)(2,1)}, u32[]{:S(2)}) copy-start(bf16[3136,256]{1,0:T(8,128)(2,1)} %copy-done.9) | copy-start | bytes 4816900
  49.5 7.7 %copy-start.13 = (pred[320,320]{1,0:T(32,128)(4,1)S(1)}, pred[320,320]{1,0:T(32,128)(4,1)}, u32[]{:S(2)}) copy-start(pred[320,320]{1,0:T(32,128)(4,1)} %constant.125.clone) | copy-start | bytes 307204
  64.1 5.4 %copy-start.12 = (s32[10240]{0:T(1024)S(1)}, s32[10240]{0:T(1024)}, u32[]{:S(2)}) copy-start(s32[10240]{0:T(1024)} %param.20) | copy-start | bytes 122884
  65.6 18.5 %all-to-all-start.2 = ((bf16[32,48,256]{2,1,0:T(8,128)(2,1)}), bf16[32,48,256]{2,1,0:T(8,128)(2,1)S(1)}, u32[]{:S(2)}, u32[]{:S(2)}) async-start(bf16[32,48,256]{2,1,0:T(8,128)(2,1)} %bitcast.2), calls=%async_computation.2 | async-start | bytes 1572864 | tf_op jit(solution)/shard_map/all_to_all | solution.py:195
  69.6 18.6 %copy-start.11 = (bf16[320,320]{1,0:T(8,128)(2,1)S(1)}, bf16[320,320]{1,0:T(8,128)(2,1)}, u32[]{:S(2)}) copy-start(bf16[320,320]{1,0:T(8,128)(2,1)} %constant.126.clone) | copy-start | bytes 614404
  84.1 18.7 %all-to-all-start = ((bf16[32,48,256]{2,1,0:T(8,128)(2,1)}), bf16[32,48,256]{2,1,0:T(8,128)(2,1)S(1)}, u32[]{:S(2)}, u32[]{:S(2)}) async-start(bf16[32,48,256]{2,1,0:T(8,128)(2,1)} %bitcast), calls=%async_computation | async-start | bytes 1572864 | tf_op jit(solution)/shard_map/all_to_all | solution.py:195
  90.2 12.5 %collective-permute-start.1 = (bf16[320,256]{1,0:T(8,128)(2,1)S(1)}, bf16[320,256]{1,0:T(8,128)(2,1)S(1)}, u32[]{:S(2)}, u32[]{:S(2)}) collective-permute-start(bf16[320,256]{1,0:T(8,128)(2,1)S(1)} %get-tuple-element.31), channel_id=1, source_target_pairs={{0,1},{1,2},{2,3},{3,0},{4,5},{5,6},{6,7},{7,4},{8,9},{9,10},{10,1... | collective-permute-start | bytes 491528 | tf_op jit(solution)/shard_map/ppermute | solution.py:246
  91.8 11.0 %collective-permute-start.2 = (bf16[320,256]{1,0:T(8,128)(2,1)S(1)}, bf16[320,256]{1,0:T(8,128)(2,1)}, u32[]{:S(2)}, u32[]{:S(2)}) collective-permute-start(bf16[320,256]{1,0:T(8,128)(2,1)S(1)} %get-tuple-element.33), channel_id=1, source_target_pairs={{0,3},{1,0},{2,1},{3,2},{4,7},{5,4},{6,5},{7,6},{8,11},{9,8},{10,9... | collective-permute-start | bytes 491528 | tf_op jit(solution)/shard_map/ppermute | solution.py:246
  93.5 9.2 %collective-permute-start.3 = (bf16[320,256]{1,0:T(8,128)(2,1)S(1)}, bf16[320,256]{1,0:T(8,128)(2,1)}, u32[]{:S(2)}, u32[]{:S(2)}) collective-permute-start(bf16[320,256]{1,0:T(8,128)(2,1)S(1)} %get-tuple-element.32), channel_id=1, source_target_pairs={{0,2},{1,3},{2,0},{3,1},{4,6},{5,7},{6,4},{7,5},{8,10},{9,11},{10,... | collective-permute-start | bytes 491528 | tf_op jit(solution)/shard_map/ppermute | solution.py:246
  104.6 5.1 %collective-permute-start.4 = (f32[5,320]{1,0:T(8,128)S(1)}, f32[5,320]{1,0:T(8,128)S(1)}, u32[]{:S(2)}, u32[]{:S(2)}) collective-permute-start(f32[5,320]{1,0:T(8,128)S(1)} %stack.23), channel_id=1, source_target_pairs={{0,1},{1,2},{2,3},{3,0},{4,5},{5,6},{6,7},{7,4},{8,9},{9,10},{10,1... | collective-permute-start | bytes 19208 | tf_op jit(solution)/shard_map/ppermute | solution.py:257
  106.2 3.7 %collective-permute-start.5 = (f32[5,320]{1,0:T(8,128)S(1)}, f32[5,320]{1,0:T(8,128)S(1)}, u32[]{:S(2)}, u32[]{:S(2)}) collective-permute-start(f32[5,320]{1,0:T(8,128)S(1)} %stack.23), channel_id=1, source_target_pairs={{0,3},{1,0},{2,1},{3,2},{4,7},{5,4},{6,5},{7,6},{8,11},{9,8},{10,9... | collective-permute-start | bytes 19208 | tf_op jit(solution)/shard_map/ppermute | solution.py:257
  107.9 5.2 %collective-permute-start.6 = (f32[5,320]{1,0:T(8,128)S(1)}, f32[5,320]{1,0:T(8,128)S(1)}, u32[]{:S(2)}, u32[]{:S(2)}) collective-permute-start(f32[5,320]{1,0:T(8,128)S(1)} %stack.23), channel_id=1, source_target_pairs={{0,2},{1,3},{2,0},{3,1},{4,6},{5,7},{6,4},{7,5},{8,10},{9,11},{10,... | collective-permute-start | bytes 19208 | tf_op jit(solution)/shard_map/ppermute | solution.py:257

commit v2 on v1

v2 whole, which is shorter than its diff:
```python
import numpy as np

import jax
import jax.numpy as jnp
from jax import lax
from jax.experimental import pallas as pl
from jax.experimental.pallas import tpu as pltpu
from jax.sharding import PartitionSpec as P

HEAD_DIM = 64
PATCHES = 196
CAP = 48
NEG = -1e30
EPS = 1e-06
BF = jnp.bfloat16
F32 = jnp.float32


def nt(a, b):
    return lax.dot_general(a, b, (((1,), (1,)), ((), ())), preferred_element_type=F32)


def nn(a, b):
    return lax.dot_general(a, b, (((1,), (0,)), ((), ())), preferred_element_type=F32)


def gather_kernel(head_ref, x_ref, wq_ref, wk_ref, wv_ref, pool_ref, pos_ref, order_ref, pat_ref, chunk_ref, qt_ref, sums, rows_in):
    step = pl.program_id(0)
    rows = x_ref.shape[0]
    keep = pos_ref.shape[0]
    cols = wk_ref.shape[1]
    x = x_ref[...]
    pick = (pos_ref[...] == lax.broadcasted_iota(jnp.int32, (keep, rows), 1)).astype(F32).astype(BF)
    both = nn(jnp.concatenate([pool_ref[...], pick], axis=0), x)
    sums[pl.ds(pl.multiple_of(step * 16, 16), 16), :] = both[:16]
    rows_in[pl.ds(pl.multiple_of(step * keep, 16), keep), :] = both[16:].astype(BF)

    @pl.when(step == pl.num_programs(0) - 1)
    def _():
        total = sums[...]
        count = total.shape[0]
        high = total.astype(BF)
        low = (total - high.astype(F32)).astype(BF)
        pair = jnp.concatenate([high, low], axis=0)
        order = order_ref[...]
        for i, w_ref in enumerate((wk_ref, wv_ref)):
            field = nn(pair, w_ref[...])
            pooled = ((field[:count] + field[count:]) / 7.0).astype(BF)
            chunk_ref[:count, i * cols : (i + 1) * cols] = nn(order, pooled).astype(BF)
        chunk_ref[count:, :] = pat_ref[...].astype(F32).astype(BF)
        q = nn(rows_in[...], wq_ref[...]).astype(BF).astype(F32) * HEAD_DIM ** -0.5
        qt_ref[:, :cols] = q.astype(BF)
        qt_ref[:, cols:] = rows_in[:, pl.ds(pl.multiple_of(head_ref[0] * cols, 128), cols)]


def near_kernel(q_ref, x_ref, wk_ref, wv_ref, out_ref):
    x = x_ref[...]
    k = nn(x, wk_ref[...]).astype(BF)
    v = nn(x, wv_ref[...]).astype(BF)
    q = q_ref[...]
    rows, cols = q.shape
    keep = rows // 4
    heads = cols // HEAD_DIM
    lane = lax.broadcasted_iota(jnp.int32, (rows, cols), 1)
    mine = [(lane >= h * HEAD_DIM) & (lane < (h + 1) * HEAD_DIM) for h in range(heads)]
    stack = jnp.concatenate([jnp.where(mine[h], q, jnp.zeros_like(q)) for h in range(heads)], axis=0)
    r = lax.broadcasted_iota(jnp.int32, (rows, 1), 0)
    frame = sum((r >= keep * i).astype(jnp.int32) for i in (1, 2, 3))
    c = lax.broadcasted_iota(jnp.int32, (rows, k.shape[0]), 1) - frame * PATCHES
    wall = jnp.where((c >= 0) & (c < PATCHES), 0.0, NEG)
    s = nt(stack, k) + jnp.concatenate([wall] * heads, axis=0)
    m = jnp.max(s, axis=1, keepdims=True)
    e = jnp.exp(s - m)
    total = jnp.sum(e, axis=1, keepdims=True)
    o = nn(e.astype(BF), v) / total
    level = m + jnp.log(total)
    high = level.astype(BF).astype(F32)
    middle = (level - high).astype(BF).astype(F32)
    low = level - high - middle
    lane2 = lax.broadcasted_iota(jnp.int32, (rows, 128), 1)
    out = jnp.zeros((rows, cols), F32)
    side = jnp.zeros((rows, 128), F32)
    for h in range(heads):
        part = slice(h * rows, (h + 1) * rows)
        out = jnp.where(mine[h], o[part], out)
        for i, piece in enumerate((high, middle, low)):
            side = jnp.where(lane2 == i * heads + h, piece[part], side)
    out_ref[:, :cols] = out.astype(BF)
    out_ref[:, cols:] = side.astype(BF)


def far_kernel(head_ref, qt_ref, near_ref, wo_ref, frame_ref, where_ref, *rest):
    parts, (raw_ref, s1_ref, s2_ref, s3_ref, key, value, pattern) = rest[:8], rest[8:]
    rows = qt_ref.shape[0]
    cols = qt_ref.shape[1] // 2
    heads = cols // HEAD_DIM
    each = parts[0].shape[0] * 16
    count = each * len(parts)
    for i, ref in enumerate(parts):
        spot = slice(i * each, (i + 1) * each)
        for u in range(4):
            key[u, spot, :] = ref[:, u * 16 : (u + 1) * 16, :cols].reshape(each, cols)
            value[u, spot, :] = ref[:, u * 16 : (u + 1) * 16, cols:].reshape(each, cols)
        pattern[spot, :] = ref[:, 64:, :].reshape(each, 2 * cols)
    where = where_ref[...]
    mine = (frame_ref[...] == where).astype(F32).astype(BF)
    allowed = nn(mine, pattern[...]).astype(BF)
    order = (lax.broadcasted_iota(jnp.int32, (allowed.shape[1], count), 0) == where).astype(F32).astype(BF)
    wall = jnp.where(nn(allowed, order) > 0.5, 0.0, NEG)
    q = qt_ref[:, :cols]
    lane = lax.broadcasted_iota(jnp.int32, (rows, cols), 1)
    out = jnp.zeros((rows, cols), F32)
    for h in range(heads):
        mine = (lane >= h * HEAD_DIM) & (lane < (h + 1) * HEAD_DIM)
        qh = jnp.where(mine, q, jnp.zeros_like(q))
        level = sum(near_ref[:, cols + i * heads + h : cols + i * heads + h + 1].astype(F32) for i in range(3))
        top = level
        scores = []
        for u in range(4):
            s = nt(qh, key[u]) + wall
            top = jnp.maximum(top, jnp.max(s, axis=1, keepdims=True))
            scores.append(s)
        total = jnp.exp(level - top)
        acc = total * near_ref[:, :cols].astype(F32)
        for u in range(4):
            e = jnp.exp(scores[u] - top)
            total = total + jnp.sum(e, axis=1, keepdims=True)
            acc = acc + nn(e.astype(BF), value[u])
        out = jnp.where(mine, acc / total, out)
    out = out.astype(BF)
    head = head_ref[0]
    for d, ref in ((1, s1_ref), (2, s2_ref), (3, s3_ref)):
        spot = pl.multiple_of(lax.rem(head + d, 4) * cols, 128)
        ref[...] = nn(out, wo_ref[:, pl.ds(spot, cols)]).astype(BF)
    spot = pl.multiple_of(head * cols, 128)
    raw_ref[...] = nn(out, wo_ref[:, pl.ds(spot, cols)]) + qt_ref[:, cols:].astype(F32)


def whole(n):
    return [pl.BlockSpec(memory_space=pltpu.VMEM) for _ in range(n)]


def params(mib):
    return pltpu.CompilerParams(vmem_limit_bytes=mib * 2**20)


def tm_index(z, y, c):
    return ((z % 4) * 4 + y % 4) * 2 + c


DISTANCES = (0, 1, 3, 2)
PLACES = [(z, y, c) for z in range(4) for y in range(4) for c in range(2)]
SMEM = pl.BlockSpec(memory_space=pltpu.SMEM)


def along_y(d):
    return [(tm_index(z, y, c), tm_index(z, y + d, c)) for z, y, c in PLACES]


def along_z(d):
    return [(tm_index(z, y, c), tm_index(z + d, y, c)) for z, y, c in PLACES]


OTHER_CORE = [(t, t ^ 1) for t in range(32)]


def body(tokens, w_query, w_key, w_value, w_out, pattern, visible, slot, pred):
    n_peers = lax.axis_size("tm")
    me = lax.axis_index("tm")
    head = lax.axis_index("head")
    n_heads = lax.axis_size("head")
    frames, keep = visible.shape
    width = tokens.shape[1]
    cols = w_query.shape[1]
    own = frames * keep
    steps = frames // 4
    block = 4 * PATCHES
    chunk = 4 * keep
    head_at = head.reshape(1).astype(jnp.int32)

    r = np.arange(block)
    p = r % PATCHES
    quadrant = 2 * (p // 14 >= 7) + (p % 14 >= 7)
    pool = np.zeros((16, block), np.float32)
    pool[r // PATCHES * 4 + quadrant, r] = 1.0
    n = np.arange(4 * frames)
    order = np.zeros((4 * frames, 4 * frames), np.float32)
    order[n, n % frames * 4 + n // frames] = 1.0
    pos = (jnp.arange(frames, dtype=jnp.int32)[:, None] % 4 * PATCHES + visible).reshape(own, 1)

    fixed = lambda i: (0, 0)
    mine, qt = pl.pallas_call(
        gather_kernel,
        grid=(steps,),
        in_specs=[
            SMEM,
            pl.BlockSpec((block, width), lambda i: (i, 0)),
            pl.BlockSpec((width, cols), fixed),
            pl.BlockSpec((width, cols), fixed),
            pl.BlockSpec((width, cols), fixed),
            pl.BlockSpec((16, block), fixed),
            pl.BlockSpec((chunk, 1), lambda i: (i, 0)),
            pl.BlockSpec((4 * frames, 4 * frames), fixed),
            pl.BlockSpec((frames, n_peers * frames), fixed),
        ],
        out_specs=[
            pl.BlockSpec((5 * frames, 2 * cols), fixed),
            pl.BlockSpec((own, 2 * cols), fixed),
        ],
        out_shape=[
            jax.ShapeDtypeStruct((5 * frames, 2 * cols), BF),
            jax.ShapeDtypeStruct((own, 2 * cols), BF),
        ],
        scratch_shapes=[pltpu.VMEM((4 * frames, width), F32), pltpu.VMEM((own, width), BF)],
        compiler_params=params(56),
        cost_estimate=pl.CostEstimate(flops=2 * 10**9, bytes_accessed=10**7, transcendentals=0),
        name="gather",
    )(head_at, tokens, w_query, w_key, w_value, jnp.asarray(pool, BF), pos, jnp.asarray(order, BF), pattern)

    plane = jnp.stack([mine] + [lax.ppermute(mine, "tm", along_y(d)) for d in DISTANCES[1:]])
    parts = [plane] + [lax.ppermute(plane, "tm", along_z(d)) for d in DISTANCES[1:]]
    parts = parts + [lax.ppermute(part, "tm", OTHER_CORE) for part in parts]
    my_z, my_y, my_core = me // 8, me // 2 % 4, me % 2
    gap = jnp.asarray(DISTANCES, jnp.int32)
    core_at = jnp.stack([my_core, 1 - my_core])[:, None, None, None]
    z_at = ((my_z - gap) % 4)[None, :, None, None]
    y_at = ((my_y - gap) % 4)[None, None, :, None]
    where = ((z_at * 4 + y_at) * 2 + core_at) * frames + jnp.arange(frames, dtype=jnp.int32)
    where = where.reshape(1, n_peers * frames)

    owner_all = slot // own
    my_slots = lax.dynamic_slice_in_dim(slot, me * own, own)
    my_owner = my_slots // own
    before = np.tril(np.ones((own, own), np.float32), -1)
    same = (my_owner[:, None] == my_owner[None, :]) & (before > 0)
    place = my_owner * CAP + jnp.sum(same, axis=1, dtype=jnp.int32)
    pack = (jnp.arange(n_peers * CAP, dtype=jnp.int32)[:, None] == place[None, :]).astype(BF)
    coming = (owner_all == me).reshape(n_peers, own)
    rank = jnp.dot(coming.astype(BF), jnp.asarray(before.T, BF), preferred_element_type=F32).astype(jnp.int32)
    rank = jnp.where(coming, rank, -1)
    hit = rank[:, None, :] == jnp.arange(CAP, dtype=jnp.int32)[None, :, None]
    code = (slot % own).reshape(n_peers, own) * 512 + jnp.arange(n_peers * own, dtype=jnp.int32).reshape(n_peers, own) // keep
    code = jnp.max(jnp.where(hit, code[:, None, :], -1), axis=2).reshape(1, -1)
    found = jnp.arange(own, dtype=jnp.int32)[:, None] == code >> 9
    unpack = found.astype(BF)
    frame_of = jnp.max(jnp.where(found, code & 511, 0), axis=1, keepdims=True)

    def route(x):
        packed = jnp.dot(pack, x, preferred_element_type=F32).astype(BF).reshape(n_peers, CAP, -1)
        got = lax.all_to_all(packed, "tm", 0, 0, tiled=True)
        return jnp.dot(unpack, got.reshape(n_peers * CAP, -1), preferred_element_type=F32).astype(BF)

    qt_own = route(qt)

    near = pl.pallas_call(
        near_kernel,
        grid=(steps,),
        in_specs=[
            pl.BlockSpec((chunk, cols), lambda i: (i, 0)),
            pl.BlockSpec((block, width), lambda i: (i, 0)),
            pl.BlockSpec((width, cols), fixed),
            pl.BlockSpec((width, cols), fixed),
        ],
        out_specs=pl.BlockSpec((chunk, cols + 128), lambda i: (i, 0)),
        out_shape=jax.ShapeDtypeStruct((own, cols + 128), BF),
        compiler_params=params(56),
        cost_estimate=pl.CostEstimate(flops=5 * 10**9, bytes_accessed=10**7, transcendentals=10**6),
        name="near",
    )(qt, tokens, w_key, w_value)
    near_own = route(near)

    raw, *sends = pl.pallas_call(
        far_kernel,
        in_specs=[SMEM] + whole(13),
        out_specs=whole(4),
        out_shape=[jax.ShapeDtypeStruct((own, cols), F32)] + [jax.ShapeDtypeStruct((own, cols), BF)] * 3,
        scratch_shapes=[
            pltpu.VMEM((4, n_peers * frames, cols), BF),
            pltpu.VMEM((4, n_peers * frames, cols), BF),
            pltpu.VMEM((n_peers * frames, n_peers * frames), BF),
        ],
        compiler_params=params(48),
        cost_estimate=pl.CostEstimate(flops=4 * 10**9, bytes_accessed=4 * 10**6, transcendentals=3 * 10**6),
        name="far",
    )(head_at, qt_own, near_own, w_out, frame_of, where, *parts)

    def to(d):
        return [(h, (h + d) % n_heads) for h in range(n_heads)]

    for d in (1, 3, 2):
        raw = raw + lax.ppermute(sends[d - 1], "head", to(d)).astype(F32)
    guess = pred.astype(F32)
    stats = jnp.stack([
        jnp.sum(raw, axis=1),
        jnp.sum(raw * raw, axis=1),
        jnp.sum(guess * raw, axis=1),
        jnp.sum(guess, axis=1),
        jnp.sum(guess * guess, axis=1),
    ])
    total = stats
    for d in (1, 3, 2):
        total = total + lax.ppermute(stats, "head", to(d))
    mean = total[0] / width
    var = total[1] / width - mean * mean
    scale = lax.rsqrt(var + EPS)
    normed = (raw - mean[:, None]) * scale[:, None]
    cross = (total[2] - mean * total[3]) * scale
    square = (total[1] - 2.0 * mean * total[0] + width * mean * mean) * scale * scale
    row_loss = (total[4] - 2.0 * cross + square) / width
    return normed.astype(BF), row_loss


def solution(mesh):
    return jax.shard_map(
        body,
        mesh=mesh,
        in_specs=(
            P("tm", None),
            P(None, "head"),
            P(None, "head"),
            P(None, "head"),
            P("head", None),
            P("tm", None),
            P("tm", None),
            P(),
            P("tm", "head"),
        ),
        out_specs=(P("tm", "head"), P("tm")),
        check_vma=False,
    )
```

time: 115 us -> 127 us (1.10)
  waiting for transfers between devices: 23.7 us -> 56.1 us
  blocking collectives: 25.1 us -> 0 us
  local copies, waits for them, and re-layouts: 16.9 us -> 1.41 us
  starting transfers between devices: 18.2 us -> 31.4 us
  matrix products: 5.78 us -> 9.97 us
  Pallas kernels: 19.2 us -> 22.5 us
    ppermute x4 -> x13, waiting for transfers between devices: 0.01 us -> 34.8 us  [the longest x3 27.5 us: body(): lax.ppermute(plane, 'tm', along_z(d))]
    all_to_all x1 -> x0, blocking collectives: 25.1 us -> none  [body(): lax.all_to_all(jnp.broadcast_to(summary[None], (n_peers // 2,) + summary....]
    ppermute x4 -> x13, starting transfers between devices: 5.12 us -> 17.5 us  [the longest x3 6.53 us: body(): lax.ppermute(mine, 'tm', along_y(d))]
    unnamed x30 -> x20, local copies, waits for them, and re-layouts: 11.9 us -> 0.04 us
    all_to_all x2, waiting for transfers between devices: 20.3 us -> 16.3 us  [route(): got = lax.all_to_all(packed, 'tm', 0, 0, tiled=True)]
    pallas_call x3, Pallas kernels: 19.2 us -> 22.5 us  [the longest x1 10 us: body(): pl.pallas_call(near_kernel, grid=(steps,), in_specs=[pl.BlockSpec((chunk,...]
    dot_general x1 -> x2, matrix products: 1.75 us -> 4.81 us  [route(): jnp.dot(unpack, got.reshape(n_peers * CAP, -1), preferred_element_type=F32)]
    dynamic_slice x1 -> x0, local copies, waits for them, and re-layouts: 2.43 us -> none  [body(): lax.dynamic_index_in_dim(banned, 1 - core, 2, keepdims=False)]
  transfers between devices with their start and end apart: 9 -> 18, of which waited for: 4 -> 8; matrix products, arithmetic and copies ran while one was open for 8% -> 10% of each run, Pallas kernels for 6% -> 8%
where the time goes in v2:
time: 127 us
  waiting for transfers between devices  56.1 us (44%)
  starting transfers between devices  31.4 us (25%)
  Pallas kernels  22.5 us (18%)
  matrix products  9.97 us (8%)
  other arithmetic  4.43 us (3%)
  local copies, waits for them, and re-layouts  1.41 us (1%)
    ppermute x3, waiting for transfers between devices, body(): lax.ppermute(plane, 'tm', along_z(d))  27.5 us
    all_to_all x2, waiting for transfers between devices, route(): got = lax.all_to_all(packed, 'tm', 0, 0, tiled=True)  16.3 us
    all_to_all x2, starting transfers between devices, route(): got = lax.all_to_all(packed, 'tm', 0, 0, tiled=True)  10.4 us
    pallas_call x1, Pallas kernels, body(): pl.pallas_call(near_kernel, grid=(steps,), in_specs=[pl.BlockSpec((chunk,...  10 us
    ppermute x3, waiting for transfers between devices, body(): raw = raw + lax.ppermute(sends[d - 1], 'head', to(d)).astype(F32)  7.28 us
    pallas_call x1, Pallas kernels, body(): pl.pallas_call(gather_kernel, grid=(steps,), in_specs=[SMEM, pl.BlockSpec...  6.63 us
    ppermute x3, starting transfers between devices, body(): lax.ppermute(mine, 'tm', along_y(d))  6.53 us
    pallas_call x1, Pallas kernels, body(): pl.pallas_call(far_kernel, in_specs=[SMEM] + whole(13), out_specs=whole(4...  5.81 us
  transfers between devices with their start and end apart: 18, of which 8 were waited for; matrix products, arithmetic and copies ran while one was open for 10% of the time, Pallas kernels for 8%

profile of v2, /device:TPU:0, one launch (start us, length us, event | category | flops | bytes accessed | tf_op | source)
XLA Modules:
  0.0 126.8 jit_solution(15277978578470496860)
XLA Ops:
  2.2 6.6 %gather.1 = (bf16[80,512]{1,0:T(8,128)(2,1)}, bf16[320,512]{1,0:T(8,128)(2,1)}) custom-call(s32[1]{0:T(128)} %bitcast.head_ref, bf16[3136,1024]{1,0:T(8,128)(2,1)} %x_ref.3, bf16[1024,256]{1,0:T(8,128)(2,1)} %wq_ref.1, bf16[1024,256]{1,0:T(8,128)(2,1)} %wk_ref.3, bf16[1024,256]{1,0:T(8,128)(2,1)} %wv_ref.3, bf16[16,784]{1,0:T(8,128)(2,1)} %constant.151.clone.pool_ref, ...), custom_call_target="tpu_custom_call" | custom-call | flops 2000000000 | bytes 10000000 | tf_op jit(solution)/shard_map/gather/pallas_call | solution.py:192
  8.8 3.3 %collective-permute-start.2 = (bf16[80,512]{1,0:T(8,128)(2,1)}, bf16[80,512]{1,0:T(8,128)(2,1)S(1)}, u32[]{:S(2)}, u32[]{:S(2)}) collective-permute-start(bf16[80,512]{1,0:T(8,128)(2,1)} %get-tuple-element.9), channel_id=1, source_target_pairs={{0,16},{4,20},{8,24},{12,28},{16,0},{20,4},{24,8},{28,12},{32,48},... | collective-permute-start | bytes 245768 | tf_op jit(solution)/shard_map/ppermute | solution.py:220
  12.8 2.6 %collective-permute-start.1 = (bf16[80,512]{1,0:T(8,128)(2,1)}, bf16[80,512]{1,0:T(8,128)(2,1)S(1)}, u32[]{:S(2)}, u32[]{:S(2)}) collective-permute-start(bf16[80,512]{1,0:T(8,128)(2,1)} %get-tuple-element.9), channel_id=1, source_target_pairs={{0,24},{4,28},{8,0},{12,4},{16,8},{20,12},{24,16},{28,20},{32,56},... | collective-permute-start | bytes 245768 | tf_op jit(solution)/shard_map/ppermute | solution.py:220
  15.8 10.0 %near.1 = bf16[320,384]{1,0:T(8,128)(2,1)} custom-call(bf16[320,512]{1,0:T(8,128)(2,1)} %get-tuple-element.8.q_ref, bf16[3136,1024]{1,0:T(8,128)(2,1)} %x_ref.3, bf16[1024,256]{1,0:T(8,128)(2,1)} %wk_ref.3, bf16[1024,256]{1,0:T(8,128)(2,1)} %wv_ref.3), custom_call_target="tpu_custom_call" | custom-call | flops 5000000000 | bytes 10000000 | tf_op jit(solution)/shard_map/near/pallas_call | solution.py:255
  25.8 2.9 %convolution_convert_fusion.1 = bf16[1536,384]{1,0:T(8,128)(2,1)} fusion(bf16[320,384]{1,0:T(8,128)(2,1)} %near.1, s32[320]{0:T(512)S(1)} %multiply_add_fusion.1), kind=kOutput, calls=%fused_computation.1 | convolution fusion | flops 378568704 | bytes 1426688 | tf_op jit(solution)/shard_map/dot_general | solution.py:249
  28.7 5.7 %all-to-all-start.1 = ((bf16[32,48,384]{2,1,0:T(8,128)(2,1)}), bf16[32,48,384]{2,1,0:T(8,128)(2,1)S(1)}, u32[]{:S(2)}, u32[]{:S(2)}) async-start(bf16[32,48,384]{2,1,0:T(8,128)(2,1)} %bitcast.3), calls=%async_computation.1 | async-start | bytes 2359296 | tf_op jit(solution)/shard_map/all_to_all | solution.py:250
  34.9 2.1 %convolution_convert_fusion = bf16[1536,512]{1,0:T(8,128)(2,1)} fusion(bf16[320,512]{1,0:T(8,128)(2,1)S(1)} %copy-done.9, s32[320]{0:T(512)S(1)} %multiply_add_fusion.1), kind=kOutput, calls=%fused_computation | convolution fusion | flops 504594432 | bytes 1901824 | tf_op jit(solution)/shard_map/dot_general | solution.py:249
  37.1 16.3 %all-to-all-done.1 = bf16[32,48,384]{2,1,0:T(8,128)(2,1)S(1)} async-done(((bf16[32,48,384]{2,1,0:T(8,128)(2,1)}), bf16[32,48,384]{2,1,0:T(8,128)(2,1)S(1)}, u32[]{:S(2)}, u32[]{:S(2)}) %all-to-all-start.1) | async-done | bytes 1179680 | tf_op jit(solution)/shard_map/all_to_all | solution.py:250
  53.4 4.7 %all-to-all-start = ((bf16[32,48,512]{2,1,0:T(8,128)(2,1)}), bf16[32,48,512]{2,1,0:T(8,128)(2,1)}, u32[]{:S(2)}, u32[]{:S(2)}) async-start(bf16[32,48,512]{2,1,0:T(8,128)(2,1)} %bitcast.1), calls=%async_computation | async-start | bytes 3145728 | tf_op jit(solution)/shard_map/all_to_all | solution.py:250
  59.2 1.7 %collective-permute-start.3 = (bf16[4,80,512]{2,1,0:T(8,128)(2,1)S(1)}, bf16[4,80,512]{2,1,0:T(8,128)(2,1)S(1)}, u32[]{:S(2)}, u32[]{:S(2)}) collective-permute-start(bf16[4,80,512]{2,1,0:T(8,128)(2,1)S(1)} %pad_maximum_fusion.rest_0_), channel_id=1, source_target_pairs={{0,32},{4,36},{8,40},{12,44},{16,48},{20,52},{24,56},{28,60},{32,6... | collective-permute-start | bytes 983048 | tf_op jit(solution)/shard_map/ppermute | solution.py:221
  61.0 1.6 %collective-permute-start.4 = (bf16[4,80,512]{2,1,0:T(8,128)(2,1)S(1)}, bf16[4,80,512]{2,1,0:T(8,128)(2,1)S(1)}, u32[]{:S(2)}, u32[]{:S(2)}) collective-permute-start(bf16[4,80,512]{2,1,0:T(8,128)(2,1)S(1)} %pad_maximum_fusion.rest_0_), channel_id=1, source_target_pairs={{0,96},{4,100},{8,104},{12,108},{16,112},{20,116},{24,120},{28,124... | collective-permute-start | bytes 983048 | tf_op jit(solution)/shard_map/ppermute | solution.py:221
  62.5 2.0 %collective-permute-start.5 = (bf16[4,80,512]{2,1,0:T(8,128)(2,1)S(1)}, bf16[4,80,512]{2,1,0:T(8,128)(2,1)S(1)}, u32[]{:S(2)}, u32[]{:S(2)}) collective-permute-start(bf16[4,80,512]{2,1,0:T(8,128)(2,1)S(1)} %pad_maximum_fusion.rest_0_), channel_id=1, source_target_pairs={{0,64},{4,68},{8,72},{12,76},{16,80},{20,84},{24,88},{28,92},{32,9... | collective-permute-start | bytes 983048 | tf_op jit(solution)/shard_map/ppermute | solution.py:221
  65.3 21.0 %collective-permute-done.3.rest_1_ = bf16[4,80,512]{2,1,0:T(8,128)(2,1)S(1)} collective-permute-done((bf16[4,80,512]{2,1,0:T(8,128)(2,1)S(1)}, bf16[4,80,512]{2,1,0:T(8,128)(2,1)S(1)}, u32[]{:S(2)}, u32[]{:S(2)}) %collective-permute-start.3) | collective-permute-done | bytes 327712 | tf_op jit(solution)/shard_map/ppermute | solution.py:221
  86.8 6.5 %collective-permute-done.5.rest_3_ = bf16[4,80,512]{2,1,0:T(8,128)(2,1)S(1)} collective-permute-done((bf16[4,80,512]{2,1,0:T(8,128)(2,1)S(1)}, bf16[4,80,512]{2,1,0:T(8,128)(2,1)S(1)}, u32[]{:S(2)}, u32[]{:S(2)}) %collective-permute-start.5) | collective-permute-done | bytes 327712 | tf_op jit(solution)/shard_map/ppermute | solution.py:221
  93.3 2.7 %fusion.3.near_ref = bf16[320,384]{1,0:T(8,128)(2,1)} fusion(bf16[1536,384]{1,0:T(8,128)(2,1)} %bitcast.17, s32[1536]{0:T(1024)S(1)} %shift_right_arithmetic.16), kind=kOutput, calls=%fused_computation.10 | convolution fusion | flops 378101760 | bytes 1431552 | tf_op jit(solution)/shard_map/dot_general | solution.py:251
  96.0 2.2 %fusion.2.qt_ref = bf16[320,512]{1,0:T(8,128)(2,1)S(1)} fusion(bf16[1536,512]{1,0:T(8,128)(2,1)} %bitcast.2, s32[1536]{0:T(1024)S(1)} %shift_right_arithmetic.16), kind=kOutput, calls=%fused_computation.9 | convolution fusion | flops 503971840 | bytes 1906688 | tf_op jit(solution)/shard_map/dot_general | solution.py:251
  98.2 5.8 %far.1 = (f32[320,256]{1,0:T(8,128)S(1)}, bf16[320,256]{1,0:T(8,128)(2,1)S(1)}, bf16[320,256]{1,0:T(8,128)(2,1)S(1)}, bf16[320,256]{1,0:T(8,128)(2,1)S(1)}) custom-call(s32[1]{0:T(128)} %bitcast.head_ref, bf16[320,512]{1,0:T(8,128)(2,1)S(1)} %fusion.2.qt_ref, bf16[320,384]{1,0:T(8,128)(2,1)S(1)} %copy-done.1, bf16[256,1024]{1,0:T(8,128)(2,1)S(1)} %copy-done, ...), custom_call_target="tpu_custom_call" | custom-call | flops 4000000000 | bytes 4000000 | tf_op jit(solution)/shard_map/far/pallas_call | solution.py:272
  105.5 1.8 %collective-permute-start.11 = (bf16[320,256]{1,0:T(8,128)(2,1)S(1)}, bf16[320,256]{1,0:T(8,128)(2,1)S(1)}, u32[]{:S(2)}, u32[]{:S(2)}) collective-permute-start(bf16[320,256]{1,0:T(8,128)(2,1)S(1)} %get-tuple-element.12), channel_id=1, source_target_pairs={{0,3},{1,0},{2,1},{3,2},{4,7},{5,4},{6,5},{7,6},{8,11},{9,8},{10,9... | collective-permute-start | bytes 491528 | tf_op jit(solution)/shard_map/ppermute | solution.py:291
  107.3 1.8 %collective-permute-start.12 = (bf16[320,256]{1,0:T(8,128)(2,1)S(1)}, bf16[320,256]{1,0:T(8,128)(2,1)S(1)}, u32[]{:S(2)}, u32[]{:S(2)}) collective-permute-start(bf16[320,256]{1,0:T(8,128)(2,1)S(1)} %get-tuple-element.13), channel_id=1, source_target_pairs={{0,2},{1,3},{2,0},{3,1},{4,6},{5,7},{6,4},{7,5},{8,10},{9,11},{10,... | collective-permute-start | bytes 491528 | tf_op jit(solution)/shard_map/ppermute | solution.py:291
  109.1 2.8 %collective-permute-done.10 = bf16[320,256]{1,0:T(8,128)(2,1)S(1)} collective-permute-done((bf16[320,256]{1,0:T(8,128)(2,1)S(1)}, bf16[320,256]{1,0:T(8,128)(2,1)S(1)}, u32[]{:S(2)}, u32[]{:S(2)}) %collective-permute-start.10) | collective-permute-done | bytes 163872 | tf_op jit(solution)/shard_map/ppermute | solution.py:291
  111.9 2.8 %collective-permute-done.11 = bf16[320,256]{1,0:T(8,128)(2,1)S(1)} collective-permute-done((bf16[320,256]{1,0:T(8,128)(2,1)S(1)}, bf16[320,256]{1,0:T(8,128)(2,1)S(1)}, u32[]{:S(2)}, u32[]{:S(2)}) %collective-permute-start.11) | collective-permute-done | bytes 163872 | tf_op jit(solution)/shard_map/ppermute | solution.py:291
  114.7 1.7 %collective-permute-done.12 = bf16[320,256]{1,0:T(8,128)(2,1)S(1)} collective-permute-done((bf16[320,256]{1,0:T(8,128)(2,1)S(1)}, bf16[320,256]{1,0:T(8,128)(2,1)S(1)}, u32[]{:S(2)}, u32[]{:S(2)}) %collective-permute-start.12) | collective-permute-done | bytes 163872 | tf_op jit(solution)/shard_map/ppermute | solution.py:291
  118.0 2.1 %collective-permute-start.14 = (f32[5,320]{1,0:T(8,128)S(1)}, f32[5,320]{1,0:T(8,128)S(1)}, u32[]{:S(2)}, u32[]{:S(2)}) collective-permute-start(f32[5,320]{1,0:T(8,128)S(1)} %stack.55), channel_id=1, source_target_pairs={{0,3},{1,0},{2,1},{3,2},{4,7},{5,4},{6,5},{7,6},{8,11},{9,8},{10,9... | collective-permute-start | bytes 19208 | tf_op jit(solution)/shard_map/ppermute | solution.py:302
  121.8 3.5 %collective-permute-done.15 = f32[5,320]{1,0:T(8,128)S(1)} collective-permute-done((f32[5,320]{1,0:T(8,128)S(1)}, f32[5,320]{1,0:T(8,128)S(1)}, u32[]{:S(2)}, u32[]{:S(2)}) %collective-permute-start.15) | collective-permute-done | bytes 6432 | tf_op jit(solution)/shard_map/ppermute | solution.py:302
  (75 shorter events, 11.7 us)
Async XLA Ops:
  2.2 13.2 %copy-start.4 = (s32[10240]{0:T(1024)S(1)}, s32[10240]{0:T(1024)}, u32[]{:S(2)}) copy-start(s32[10240]{0:T(1024)} %param.21) | copy-start | bytes 122884
  2.2 13.2 %copy-start.6 = (pred[320,320]{1,0:T(32,128)(4,1)S(1)}, pred[320,320]{1,0:T(32,128)(4,1)}, u32[]{:S(2)}) copy-start(pred[320,320]{1,0:T(32,128)(4,1)} %constant.154.clone) | copy-start | bytes 307204
  8.8 50.3 %collective-permute-start.2 = (bf16[80,512]{1,0:T(8,128)(2,1)}, bf16[80,512]{1,0:T(8,128)(2,1)S(1)}, u32[]{:S(2)}, u32[]{:S(2)}) collective-permute-start(bf16[80,512]{1,0:T(8,128)(2,1)} %get-tuple-element.9), channel_id=1, source_target_pairs={{0,16},{4,20},{8,24},{12,28},{16,0},{20,4},{24,8},{28,12},{32,48},... | collective-permute-start | bytes 245768 | tf_op jit(solution)/shard_map/ppermute | solution.py:220
  12.1 47.0 %collective-permute-start = (bf16[80,512]{1,0:T(8,128)(2,1)}, bf16[80,512]{1,0:T(8,128)(2,1)S(1)}, u32[]{:S(2)}, u32[]{:S(2)}) collective-permute-start(bf16[80,512]{1,0:T(8,128)(2,1)} %get-tuple-element.9), channel_id=1, source_target_pairs={{0,8},{4,12},{8,16},{12,20},{16,24},{20,28},{24,0},{28,4},{32,40},... | collective-permute-start | bytes 245768 | tf_op jit(solution)/shard_map/ppermute | solution.py:220
  12.8 46.4 %collective-permute-start.1 = (bf16[80,512]{1,0:T(8,128)(2,1)}, bf16[80,512]{1,0:T(8,128)(2,1)S(1)}, u32[]{:S(2)}, u32[]{:S(2)}) collective-permute-start(bf16[80,512]{1,0:T(8,128)(2,1)} %get-tuple-element.9), channel_id=1, source_target_pairs={{0,24},{4,28},{8,0},{12,4},{16,8},{20,12},{24,16},{28,20},{32,56},... | collective-permute-start | bytes 245768 | tf_op jit(solution)/shard_map/ppermute | solution.py:220
  25.8 9.1 %copy-start.9 = (bf16[320,512]{1,0:T(8,128)(2,1)S(1)}, bf16[320,512]{1,0:T(8,128)(2,1)}, u32[]{:S(2)}) copy-start(bf16[320,512]{1,0:T(8,128)(2,1)} %get-tuple-element.8.q_ref) | copy-start | bytes 983044
  28.7 24.7 %all-to-all-start.1 = ((bf16[32,48,384]{2,1,0:T(8,128)(2,1)}), bf16[32,48,384]{2,1,0:T(8,128)(2,1)S(1)}, u32[]{:S(2)}, u32[]{:S(2)}) async-start(bf16[32,48,384]{2,1,0:T(8,128)(2,1)} %bitcast.3), calls=%async_computation.1 | async-start | bytes 2359296 | tf_op jit(solution)/shard_map/all_to_all | solution.py:250
  37.1 21.2 %copy-start.3 = (bf16[320,320]{1,0:T(8,128)(2,1)S(1)}, bf16[320,320]{1,0:T(8,128)(2,1)}, u32[]{:S(2)}) copy-start(bf16[320,320]{1,0:T(8,128)(2,1)} %constant.155.clone) | copy-start | bytes 614404
  37.1 22.1 %copy-start.7 = (bf16[80,512]{1,0:T(8,128)(2,1)S(1)}, bf16[80,512]{1,0:T(8,128)(2,1)}, u32[]{:S(2)}) copy-start(bf16[80,512]{1,0:T(8,128)(2,1)} %get-tuple-element.9) | copy-start | bytes 245764
  53.4 42.5 %all-to-all-start = ((bf16[32,48,512]{2,1,0:T(8,128)(2,1)}), bf16[32,48,512]{2,1,0:T(8,128)(2,1)}, u32[]{:S(2)}, u32[]{:S(2)}) async-start(bf16[32,48,512]{2,1,0:T(8,128)(2,1)} %bitcast.1), calls=%async_computation | async-start | bytes 3145728 | tf_op jit(solution)/shard_map/all_to_all | solution.py:250
  59.2 27.0 %collective-permute-start.3 = (bf16[4,80,512]{2,1,0:T(8,128)(2,1)S(1)}, bf16[4,80,512]{2,1,0:T(8,128)(2,1)S(1)}, u32[]{:S(2)}, u32[]{:S(2)}) collective-permute-start(bf16[4,80,512]{2,1,0:T(8,128)(2,1)S(1)} %pad_maximum_fusion.rest_0_), channel_id=1, source_target_pairs={{0,32},{4,36},{8,40},{12,44},{16,48},{20,52},{24,56},{28,60},{32,6... | collective-permute-start | bytes 983048 | tf_op jit(solution)/shard_map/ppermute | solution.py:221
  61.0 25.3 %collective-permute-start.4 = (bf16[4,80,512]{2,1,0:T(8,128)(2,1)S(1)}, bf16[4,80,512]{2,1,0:T(8,128)(2,1)S(1)}, u32[]{:S(2)}, u32[]{:S(2)}) collective-permute-start(bf16[4,80,512]{2,1,0:T(8,128)(2,1)S(1)} %pad_maximum_fusion.rest_0_), channel_id=1, source_target_pairs={{0,96},{4,100},{8,104},{12,108},{16,112},{20,116},{24,120},{28,124... | collective-permute-start | bytes 983048 | tf_op jit(solution)/shard_map/ppermute | solution.py:221
  62.5 30.7 %collective-permute-start.5 = (bf16[4,80,512]{2,1,0:T(8,128)(2,1)S(1)}, bf16[4,80,512]{2,1,0:T(8,128)(2,1)S(1)}, u32[]{:S(2)}, u32[]{:S(2)}) collective-permute-start(bf16[4,80,512]{2,1,0:T(8,128)(2,1)S(1)} %pad_maximum_fusion.rest_0_), channel_id=1, source_target_pairs={{0,64},{4,68},{8,72},{12,76},{16,80},{20,84},{24,88},{28,92},{32,9... | collective-permute-start | bytes 983048 | tf_op jit(solution)/shard_map/ppermute | solution.py:221
  65.2 33.0 %collective-permute-start.6 = (bf16[4,80,512]{2,1,0:T(8,128)(2,1)S(1)}, bf16[4,80,512]{2,1,0:T(8,128)(2,1)S(1)}, u32[]{:S(2)}, u32[]{:S(2)}) collective-permute-start(bf16[4,80,512]{2,1,0:T(8,128)(2,1)S(1)} %pad_maximum_fusion.rest_0_), channel_id=1, source_target_pairs={{0,4},{4,0},{8,12},{12,8},{16,20},{20,16},{24,28},{28,24},{32,36},... | collective-permute-start | bytes 983048 | tf_op jit(solution)/shard_map/ppermute | solution.py:222
  86.2 11.9 %collective-permute-start.7 = (bf16[4,80,512]{2,1,0:T(8,128)(2,1)S(1)}, bf16[4,80,512]{2,1,0:T(8,128)(2,1)S(1)}, u32[]{:S(2)}, u32[]{:S(2)}) collective-permute-start(bf16[4,80,512]{2,1,0:T(8,128)(2,1)S(1)} %collective-permute-done.3.rest_1_), channel_id=1, source_target_pairs={{0,4},{4,0},{8,12},{12,8},{16,20},{20,16},{24,28},{28,24},{32,36},... | collective-permute-start | bytes 983048 | tf_op jit(solution)/shard_map/ppermute | solution.py:222
  86.3 11.9 %collective-permute-start.8 = (bf16[4,80,512]{2,1,0:T(8,128)(2,1)S(1)}, bf16[4,80,512]{2,1,0:T(8,128)(2,1)S(1)}, u32[]{:S(2)}, u32[]{:S(2)}) collective-permute-start(bf16[4,80,512]{2,1,0:T(8,128)(2,1)S(1)} %collective-permute-done.4.rest_2_), channel_id=1, source_target_pairs={{0,4},{4,0},{8,12},{12,8},{16,20},{20,16},{24,28},{28,24},{32,36},... | collective-permute-start | bytes 983048 | tf_op jit(solution)/shard_map/ppermute | solution.py:222
  93.3 4.9 %collective-permute-start.9 = (bf16[4,80,512]{2,1,0:T(8,128)(2,1)S(1)}, bf16[4,80,512]{2,1,0:T(8,128)(2,1)S(1)}, u32[]{:S(2)}, u32[]{:S(2)}) collective-permute-start(bf16[4,80,512]{2,1,0:T(8,128)(2,1)S(1)} %collective-permute-done.5.rest_3_), channel_id=1, source_target_pairs={{0,4},{4,0},{8,12},{12,8},{16,20},{20,16},{24,28},{28,24},{32,36},... | collective-permute-start | bytes 983048 | tf_op jit(solution)/shard_map/ppermute | solution.py:222
  98.1 18.3 %copy-start.5 = (bf16[320,256]{1,0:T(8,128)(2,1)S(1)}, bf16[320,256]{1,0:T(8,128)(2,1)}, u32[]{:S(2)}) copy-start(bf16[320,256]{1,0:T(8,128)(2,1)} %param.22) | copy-start | bytes 491524
  104.0 7.9 %collective-permute-start.10 = (bf16[320,256]{1,0:T(8,128)(2,1)S(1)}, bf16[320,256]{1,0:T(8,128)(2,1)S(1)}, u32[]{:S(2)}, u32[]{:S(2)}) collective-permute-start(bf16[320,256]{1,0:T(8,128)(2,1)S(1)} %get-tuple-element.11), channel_id=1, source_target_pairs={{0,1},{1,2},{2,3},{3,0},{4,5},{5,6},{6,7},{7,4},{8,9},{9,10},{10,1... | collective-permute-start | bytes 491528 | tf_op jit(solution)/shard_map/ppermute | solution.py:291
  105.5 9.2 %collective-permute-start.11 = (bf16[320,256]{1,0:T(8,128)(2,1)S(1)}, bf16[320,256]{1,0:T(8,128)(2,1)S(1)}, u32[]{:S(2)}, u32[]{:S(2)}) collective-permute-start(bf16[320,256]{1,0:T(8,128)(2,1)S(1)} %get-tuple-element.12), channel_id=1, source_target_pairs={{0,3},{1,0},{2,1},{3,2},{4,7},{5,4},{6,5},{7,6},{8,11},{9,8},{10,9... | collective-permute-start | bytes 491528 | tf_op jit(solution)/shard_map/ppermute | solution.py:291
  107.3 9.1 %collective-permute-start.12 = (bf16[320,256]{1,0:T(8,128)(2,1)S(1)}, bf16[320,256]{1,0:T(8,128)(2,1)S(1)}, u32[]{:S(2)}, u32[]{:S(2)}) collective-permute-start(bf16[320,256]{1,0:T(8,128)(2,1)S(1)} %get-tuple-element.13), channel_id=1, source_target_pairs={{0,2},{1,3},{2,0},{3,1},{4,6},{5,7},{6,4},{7,5},{8,10},{9,11},{10,... | collective-permute-start | bytes 491528 | tf_op jit(solution)/shard_map/ppermute | solution.py:291
  116.8 5.0 %collective-permute-start.13 = (f32[5,320]{1,0:T(8,128)S(1)}, f32[5,320]{1,0:T(8,128)S(1)}, u32[]{:S(2)}, u32[]{:S(2)}) collective-permute-start(f32[5,320]{1,0:T(8,128)S(1)} %stack.55), channel_id=1, source_target_pairs={{0,1},{1,2},{2,3},{3,0},{4,5},{5,6},{6,7},{7,4},{8,9},{9,10},{10,1... | collective-permute-start | bytes 19208 | tf_op jit(solution)/shard_map/ppermute | solution.py:302
  118.0 3.8 %collective-permute-start.14 = (f32[5,320]{1,0:T(8,128)S(1)}, f32[5,320]{1,0:T(8,128)S(1)}, u32[]{:S(2)}, u32[]{:S(2)}) collective-permute-start(f32[5,320]{1,0:T(8,128)S(1)} %stack.55), channel_id=1, source_target_pairs={{0,3},{1,0},{2,1},{3,2},{4,7},{5,4},{6,5},{7,6},{8,11},{9,8},{10,9... | collective-permute-start | bytes 19208 | tf_op jit(solution)/shard_map/ppermute | solution.py:302
  120.1 5.2 %collective-permute-start.15 = (f32[5,320]{1,0:T(8,128)S(1)}, f32[5,320]{1,0:T(8,128)S(1)}, u32[]{:S(2)}, u32[]{:S(2)}) collective-permute-start(f32[5,320]{1,0:T(8,128)S(1)} %stack.55), channel_id=1, source_target_pairs={{0,2},{1,3},{2,0},{3,1},{4,6},{5,7},{6,4},{7,5},{8,10},{9,11},{10,... | collective-permute-start | bytes 19208 | tf_op jit(solution)/shard_map/ppermute | solution.py:302
  (4 other events, 18.4 us)

commit v3 on v2

v3 whole, which is shorter than its diff:
```python
import numpy as np

import jax
import jax.numpy as jnp
from jax import lax
from jax.experimental import pallas as pl
from jax.experimental.pallas import tpu as pltpu
from jax.sharding import PartitionSpec as P

HEAD_DIM = 64
PATCHES = 196
CAP = 48
NEG = -1e30
EPS = 1e-06
BF = jnp.bfloat16
F32 = jnp.float32


def nt(a, b):
    return lax.dot_general(a, b, (((1,), (1,)), ((), ())), preferred_element_type=F32)


def nn(a, b):
    return lax.dot_general(a, b, (((1,), (0,)), ((), ())), preferred_element_type=F32)


def gather_kernel(head_ref, x_ref, wq_ref, wk_ref, wv_ref, pool_ref, vis_ref, order_ref, chunk_ref, q_ref, t_ref, sums, rows_in):
    step = pl.program_id(0)
    rows = x_ref.shape[0]
    frames, keep = vis_ref.shape
    count = 4 * keep
    cols = wk_ref.shape[1]
    x = x_ref[...]
    r = lax.broadcasted_iota(jnp.int32, (count, 1), 0)
    frame = sum((r >= keep * i).astype(jnp.int32) for i in (1, 2, 3))
    mine = (lax.broadcasted_iota(jnp.int32, (count, frames), 1) == frame + step * 4).astype(F32).astype(BF)
    seen = nn(mine, vis_ref[...].astype(F32).astype(BF))
    spot = lax.broadcasted_iota(jnp.int32, (count, keep), 1) == r - keep * frame
    pos = jnp.sum(jnp.where(spot, seen, 0.0), axis=1, keepdims=True).astype(jnp.int32) + frame * PATCHES
    pick = (pos == lax.broadcasted_iota(jnp.int32, (count, rows), 1)).astype(F32).astype(BF)
    both = nn(jnp.concatenate([pool_ref[...], pick], axis=0), x)
    sums[pl.ds(pl.multiple_of(step * 16, 16), 16), :] = both[:16]
    rows_in[pl.ds(pl.multiple_of(step * count, 16), count), :] = both[16:].astype(BF)

    @pl.when(step == pl.num_programs(0) - 1)
    def _():
        total = sums[...]
        count = total.shape[0]
        high = total.astype(BF)
        low = (total - high.astype(F32)).astype(BF)
        pair = jnp.concatenate([high, low], axis=0)
        order = order_ref[...]
        for i, w_ref in enumerate((wk_ref, wv_ref)):
            field = nn(pair, w_ref[...])
            pooled = ((field[:count] + field[count:]) / 7.0).astype(BF)
            chunk_ref[:, i * cols : (i + 1) * cols] = nn(order, pooled).astype(BF)
        q = nn(rows_in[...], wq_ref[...]).astype(BF).astype(F32) * HEAD_DIM ** -0.5
        q_ref[...] = q.astype(BF)
        t_ref[...] = rows_in[:, pl.ds(pl.multiple_of(head_ref[0] * cols, 128), cols)]


def near_kernel(q_ref, x_ref, wk_ref, wv_ref, spread_ref, q4_ref, o_ref, level_ref):
    x = x_ref[...]
    k = nn(x, wk_ref[...]).astype(BF)
    v = nn(x, wv_ref[...]).astype(BF)
    keep = q_ref.shape[0] // 4
    cols = q_ref.shape[1]
    heads = cols // HEAD_DIM
    rows = keep * heads
    r = lax.broadcasted_iota(jnp.int32, (4 * rows, cols), 0)
    lane = lax.broadcasted_iota(jnp.int32, (4 * rows, cols), 1)
    mine = lane // HEAD_DIM == r // keep % heads
    stack = jnp.where(mine, nn(spread_ref[...], q_ref[...]), 0.0).astype(BF)
    q4_ref[...] = stack
    span = 208
    for f in range(4):
        start = f * PATCHES // 16 * 16
        part = slice(f * rows, (f + 1) * rows)
        c = lax.broadcasted_iota(jnp.int32, (rows, span), 1) + (start - f * PATCHES)
        s = jnp.where((c >= 0) & (c < PATCHES), nt(stack[part], k[start : start + span]), NEG)
        m = jnp.max(s, axis=1, keepdims=True)
        e = jnp.exp(s - m)
        total = jnp.sum(e, axis=1, keepdims=True)
        o_ref[part, :] = nn(e.astype(BF), v[start : start + span]) / total
        level_ref[part, :] = jnp.broadcast_to(m + jnp.log(total), (rows, 128))


def far_kernel(q4_ref, near_ref, level_ref, allow_ref, pick_ref, where_ref, join_ref, pack_ref, *rest):
    parts, (out_ref, key, value, done) = rest[:8], rest[8:]
    cols = q4_ref.shape[1]
    heads = cols // HEAD_DIM
    each = parts[0].shape[0] * 16
    count = each * len(parts)
    for i, ref in enumerate(parts):
        spot = slice(i * each, (i + 1) * each)
        for u in range(4):
            key[u, spot, :] = ref[:, u * 16 : (u + 1) * 16, :cols].reshape(each, cols)
            value[u, spot, :] = ref[:, u * 16 : (u + 1) * 16, cols:].reshape(each, cols)
    allowed = allow_ref[...].astype(F32).astype(BF)
    order = (lax.broadcasted_iota(jnp.int32, (allowed.shape[1], count), 0) == where_ref[...]).astype(F32).astype(BF)
    wall = jnp.where(nn(allowed, order) > 0.5, 0.0, NEG).astype(BF)
    rows = q4_ref.shape[0] // 4
    keep = rows // 4 // heads
    r = lax.broadcasted_iota(jnp.int32, (rows, cols), 0)
    mine = lax.broadcasted_iota(jnp.int32, (rows, cols), 1) // HEAD_DIM == r // keep % heads
    for g in range(4):
        part = slice(g * rows, (g + 1) * rows)
        block = nn(pick_ref[part, :], wall)
        q = q4_ref[part, :]
        level = level_ref[part, :1]
        top = level
        scores = []
        for u in range(4):
            s = nt(q, key[u]) + block
            top = jnp.maximum(top, jnp.max(s, axis=1, keepdims=True))
            scores.append(s)
        total = jnp.exp(level - top)
        acc = total * near_ref[part, :]
        for u in range(4):
            e = jnp.exp(scores[u] - top)
            total = total + jnp.sum(e, axis=1, keepdims=True)
            acc = acc + nn(e.astype(BF), value[u])
        done[part, :] = jnp.where(mine, acc / total, 0.0).astype(BF)
    out = nn(join_ref[...], done[...]).astype(BF)
    out_ref[...] = nn(pack_ref[...], out).astype(BF).reshape(out_ref.shape)


def final_kernel(head_ref, wo_ref, *rest):
    att, side, (target_ref, loss_ref, raw) = rest[:4], rest[4:8], rest[8:]
    head = head_ref[0]
    rows, cols = att[0].shape
    width = raw.shape[1]
    raw[...] = sum(nn(att[i][...], wo_ref[i]) for i in range(4))
    spots = [pl.ds(pl.multiple_of(lax.rem(head + 4 - d, 4) * cols, 128), cols) for d in DISTANCES]
    for i in range(4):
        raw[:, spots[i]] += side[i][:, :cols].astype(F32)
    full = raw[...]
    mean = jnp.sum(full, axis=1, keepdims=True) / width
    var = jnp.sum(full * full, axis=1, keepdims=True) / width - mean * mean
    scale = lax.rsqrt(var + EPS)
    loss = jnp.zeros((rows, 1), F32)
    for i in range(4):
        normed = (raw[:, spots[i]] - mean) * scale
        if i == 0:
            target_ref[...] = normed.astype(BF)
        gap = side[i][:, cols:].astype(F32) - normed
        loss = loss + jnp.sum(gap * gap, axis=1, keepdims=True)
    loss_ref[...] = jnp.broadcast_to(loss / width, (rows, 128)).T[:1]


def whole(n):
    return [pl.BlockSpec(memory_space=pltpu.VMEM) for _ in range(n)]


def params(mib):
    return pltpu.CompilerParams(vmem_limit_bytes=mib * 2**20)


def tm_index(z, y, c):
    return ((z % 4) * 4 + y % 4) * 2 + c


DISTANCES = (0, 1, 3, 2)
PLACES = [(z, y, c) for z in range(4) for y in range(4) for c in range(2)]
SMEM = pl.BlockSpec(memory_space=pltpu.SMEM)


def along_y(d):
    return [(tm_index(z, y, c), tm_index(z, y + d, c)) for z, y, c in PLACES]


def along_z(d):
    return [(tm_index(z, y, c), tm_index(z + d, y, c)) for z, y, c in PLACES]


OTHER_CORE = [(t, t ^ 1) for t in range(32)]


def body(tokens, w_query, w_key, w_value, w_out, pattern, visible, slot, pred):
    n_peers = lax.axis_size("tm")
    me = lax.axis_index("tm")
    head = lax.axis_index("head")
    n_heads = lax.axis_size("head")
    frames, keep = visible.shape
    width = tokens.shape[1]
    cols = w_query.shape[1]
    own = frames * keep
    steps = frames // 4
    block = 4 * PATCHES
    chunk = 4 * keep
    head_at = head.reshape(1).astype(jnp.int32)

    r = np.arange(block)
    p = r % PATCHES
    quadrant = 2 * (p // 14 >= 7) + (p % 14 >= 7)
    pool = np.zeros((16, block), np.float32)
    pool[r // PATCHES * 4 + quadrant, r] = 1.0
    n = np.arange(4 * frames)
    order = np.zeros((4 * frames, 4 * frames), np.float32)
    order[n, n % frames * 4 + n // frames] = 1.0

    fixed = lambda i: (0, 0)
    mine, q, tok = pl.pallas_call(
        gather_kernel,
        grid=(steps,),
        in_specs=[
            SMEM,
            pl.BlockSpec((block, width), lambda i: (i, 0)),
            pl.BlockSpec((width, cols), fixed),
            pl.BlockSpec((width, cols), fixed),
            pl.BlockSpec((width, cols), fixed),
            pl.BlockSpec((16, block), fixed),
            pl.BlockSpec((frames, keep), fixed),
            pl.BlockSpec((4 * frames, 4 * frames), fixed),
        ],
        out_specs=[
            pl.BlockSpec((4 * frames, 2 * cols), fixed),
            pl.BlockSpec((own, cols), fixed),
            pl.BlockSpec((own, cols), fixed),
        ],
        out_shape=[
            jax.ShapeDtypeStruct((4 * frames, 2 * cols), BF),
            jax.ShapeDtypeStruct((own, cols), BF),
            jax.ShapeDtypeStruct((own, cols), BF),
        ],
        scratch_shapes=[pltpu.VMEM((4 * frames, width), F32), pltpu.VMEM((own, width), BF)],
        compiler_params=params(56),
        cost_estimate=pl.CostEstimate(flops=2 * 10**9, bytes_accessed=10**7, transcendentals=0),
        name="gather",
    )(head_at, tokens, w_query, w_key, w_value, jnp.asarray(pool, BF), visible, jnp.asarray(order, BF))

    plane = jnp.stack([mine] + [lax.ppermute(mine, "tm", along_y(d)) for d in DISTANCES[1:]])
    plane, q, tok = lax.optimization_barrier((plane, q, tok))
    parts = [plane] + [lax.ppermute(plane, "tm", along_z(d)) for d in DISTANCES[1:]]
    my_z, my_y, my_core = me // 8, me // 2 % 4, me % 2
    gap = jnp.asarray(DISTANCES, jnp.int32)
    core_at = jnp.stack([my_core, 1 - my_core])[:, None, None, None]
    z_at = ((my_z - gap) % 4)[None, :, None, None]
    y_at = ((my_y - gap) % 4)[None, None, :, None]
    where = ((z_at * 4 + y_at) * 2 + core_at) * frames + jnp.arange(frames, dtype=jnp.int32)
    where = where.reshape(1, n_peers * frames)

    owner_all = slot // own
    my_slots = lax.dynamic_slice_in_dim(slot, me * own, own)
    my_owner = my_slots // own
    before = np.tril(np.ones((own, own), np.float32), -1)
    same = (my_owner[:, None] == my_owner[None, :]) & (before > 0)
    place = my_owner * CAP + jnp.sum(same, axis=1, dtype=jnp.int32)
    pack = (jnp.arange(n_peers * CAP, dtype=jnp.int32)[:, None] == place[None, :]).astype(BF)
    coming = (owner_all == me).reshape(n_peers, own)
    rank = jnp.dot(coming.astype(BF), jnp.asarray(before.T, BF), preferred_element_type=F32).astype(jnp.int32)
    rank = jnp.where(coming, rank, -1)
    hit = rank[:, None, :] == jnp.arange(CAP, dtype=jnp.int32)[None, :, None]
    student = jnp.max(jnp.where(hit, (slot % own).reshape(n_peers, 1, own), -1), axis=2)
    unpack = (jnp.arange(own, dtype=jnp.int32)[:, None] == student.reshape(1, -1)).astype(BF)

    def deliver(packed):
        return lax.all_to_all(packed, "tm", 0, 0, tiled=True)

    def arrange(got):
        return jnp.dot(unpack, got.reshape(n_peers * CAP, -1), preferred_element_type=F32).astype(BF)

    tok_got = deliver(jnp.dot(pack, tok, preferred_element_type=F32).astype(BF).reshape(n_peers, CAP, cols))

    heads = cols // HEAD_DIM
    n = np.arange(own * heads)
    n_frame, n_keep = n // (keep * heads), n % keep
    spread = jnp.asarray(n_frame[: chunk * heads, None] * keep + n_keep[: chunk * heads, None] == np.arange(chunk), BF)
    pick = jnp.asarray(n_frame[:, None] == np.arange(frames), BF)
    join = jnp.asarray(np.arange(own)[:, None] == n_frame * keep + n_keep, BF)
    q4, near, level = pl.pallas_call(
        near_kernel,
        grid=(steps,),
        in_specs=[
            pl.BlockSpec((chunk, cols), lambda i: (i, 0)),
            pl.BlockSpec((block, width), lambda i: (i, 0)),
            pl.BlockSpec((width, cols), fixed),
            pl.BlockSpec((width, cols), fixed),
            pl.BlockSpec((chunk * heads, chunk), fixed),
        ],
        out_specs=[
            pl.BlockSpec((chunk * heads, cols), lambda i: (i, 0)),
            pl.BlockSpec((chunk * heads, cols), lambda i: (i, 0)),
            pl.BlockSpec((chunk * heads, 128), lambda i: (i, 0)),
        ],
        out_shape=[
            jax.ShapeDtypeStruct((own * heads, cols), BF),
            jax.ShapeDtypeStruct((own * heads, cols), F32),
            jax.ShapeDtypeStruct((own * heads, 128), F32),
        ],
        compiler_params=params(56),
        cost_estimate=pl.CostEstimate(flops=5 * 10**9, bytes_accessed=10**7, transcendentals=10**6),
        name="near",
    )(q, tokens, w_key, w_value, spread)

    q4, w_out = lax.optimization_barrier((q4, w_out))
    *parts, q4, near, level, tok_got = lax.optimization_barrier((*parts, q4, near, level, tok_got))
    parts = parts + [lax.ppermute(part, "tm", OTHER_CORE) for part in parts]
    packed = pl.pallas_call(
        far_kernel,
        in_specs=whole(16),
        out_specs=pl.BlockSpec(memory_space=pltpu.VMEM),
        out_shape=jax.ShapeDtypeStruct((n_peers, CAP, cols), BF),
        scratch_shapes=[
            pltpu.VMEM((4, n_peers * frames, cols), BF),
            pltpu.VMEM((4, n_peers * frames, cols), BF),
            pltpu.VMEM((own * heads, cols), BF),
        ],
        compiler_params=params(40),
        cost_estimate=pl.CostEstimate(flops=4 * 10**9, bytes_accessed=4 * 10**6, transcendentals=3 * 10**6),
        name="far",
    )(q4, near, level, pattern, pick, where, join, pack, *parts)
    packed, tok_got = lax.optimization_barrier((packed, tok_got))
    tok_own = arrange(tok_got)
    att = arrange(deliver(packed))

    def to(d):
        return [(h, (h + d) % n_heads) for h in range(n_heads)]

    def over_heads(x):
        return [x] + [lax.ppermute(x, "head", to(d)) for d in DISTANCES[1:]]

    half = cols // 2
    halves = jnp.stack(over_heads(lax.dynamic_slice_in_dim(w_out, my_core * half, half, 0)))
    other = lax.ppermute(halves, "tm", OTHER_CORE)
    first = my_core == 0
    w_all = jnp.concatenate([jnp.where(first, halves, other), jnp.where(first, other, halves)], axis=1)
    side = over_heads(jnp.concatenate([tok_own, pred], axis=1))

    target, row_loss = pl.pallas_call(
        final_kernel,
        in_specs=[SMEM] + whole(9),
        out_specs=whole(2),
        out_shape=[jax.ShapeDtypeStruct((own, cols), BF), jax.ShapeDtypeStruct((1, own), F32)],
        scratch_shapes=[pltpu.VMEM((own, width), F32)],
        compiler_params=params(40),
        cost_estimate=pl.CostEstimate(flops=10**9, bytes_accessed=4 * 10**6, transcendentals=0),
        name="final",
    )(head_at, w_all, *over_heads(att), *side)
    return target, row_loss.reshape(own)


def solution(mesh):
    return jax.shard_map(
        body,
        mesh=mesh,
        in_specs=(
            P("tm", None),
            P(None, "head"),
            P(None, "head"),
            P(None, "head"),
            P("head", None),
            P("tm", None),
            P("tm", None),
            P(),
            P("tm", "head"),
        ),
        out_specs=(P("tm", "head"), P("tm")),
        check_vma=False,
    )
```

time: 127 us -> 111 us (0.87)
  waiting for transfers between devices: 56.1 us -> 26.5 us
  starting transfers between devices: 31.4 us -> 37.4 us
  Pallas kernels: 22.5 us -> 26.7 us
  other arithmetic: 4.43 us -> 8.51 us
  matrix products: 9.97 us -> 6.72 us
  local copies, waits for them, and re-layouts: 1.41 us -> 3.33 us
    ppermute x3, waiting for transfers between devices: 27.5 us -> 0.01 us  [body(): lax.ppermute(plane, 'tm', along_z(d))]
    all_to_all x2, waiting for transfers between devices: 16.3 us -> 5.7 us  [deliver(): return lax.all_to_all(packed, 'tm', 0, 0, tiled=True)]
    ppermute x6 -> x10, waiting for transfers between devices: 12.3 us -> 18.1 us  [the longest x9 18.1 us: over_heads(): return [x] + [lax.ppermute(x, 'head', to(d)) for d in DISTANCES[1:]]]
    ppermute x6 -> x10, starting transfers between devices: 8.61 us -> 12.8 us  [the longest x9 12.8 us: over_heads(): return [x] + [lax.ppermute(x, 'head', to(d)) for d in DISTANCES[1:]]]
    dot_general x4 -> x3, matrix products: 9.82 us -> 5.62 us  [the longest x2 3.22 us: arrange(): jnp.dot(unpack, got.reshape(n_peers * CAP, -1), preferred_element_type=F32)]
    pallas_call x1 -> x2, Pallas kernels: 5.81 us -> 9.43 us  [the longest x1 7.1 us: body(): pl.pallas_call(far_kernel, in_specs=whole(16), out_specs=pl.BlockSpec(mem...]
    ppermute x3, waiting for transfers between devices: 0.01 us -> 2.67 us  [body(): lax.ppermute(mine, 'tm', along_y(d))]
    select_n x0 -> x2, other arithmetic: none -> 2.65 us  [the longest x1 2.62 us: body(): jnp.where(first, halves, other)]
  transfers between devices with their start and end apart: 18 -> 22, of which waited for: 8 -> 9; matrix products, arithmetic and copies ran while one was open for 10% -> 14% of each run, Pallas kernels for 8% -> 16%
where the time goes in v3:
time: 111 us; the launch traced here: 110 us
  starting transfers between devices  37.4 us (34%)
  Pallas kernels  26.7 us (24%)
  waiting for transfers between devices  26.5 us (24%)
  other arithmetic  8.51 us (8%)
  matrix products  6.72 us (6%)
  local copies, waits for them, and re-layouts  3.33 us (3%)
    ppermute x9, waiting for transfers between devices, over_heads(): return [x] + [lax.ppermute(x, 'head', to(d)) for d in DISTANCES[1:]]  18.1 us
    ppermute x9, starting transfers between devices, over_heads(): return [x] + [lax.ppermute(x, 'head', to(d)) for d in DISTANCES[1:]]  12.8 us
    all_to_all x2, starting transfers between devices, deliver(): return lax.all_to_all(packed, 'tm', 0, 0, tiled=True)  12.6 us
    pallas_call x1, Pallas kernels, body(): pl.pallas_call(near_kernel, grid=(steps,), in_specs=[pl.BlockSpec((chunk,...  10.3 us
    pallas_call x1, Pallas kernels, body(): pl.pallas_call(far_kernel, in_specs=whole(16), out_specs=pl.BlockSpec(mem...  7.1 us
    pallas_call x1, Pallas kernels, body(): pl.pallas_call(gather_kernel, grid=(steps,), in_specs=[SMEM, pl.BlockSpec...  6.97 us
    ppermute x3, starting transfers between devices, body(): lax.ppermute(plane, 'tm', along_z(d))  6.05 us
    all_to_all x2, waiting for transfers between devices, deliver(): return lax.all_to_all(packed, 'tm', 0, 0, tiled=True)  5.7 us
  transfers between devices with their start and end apart: 22, of which 9 were waited for; matrix products, arithmetic and copies ran while one was open for 14% of the time, Pallas kernels for 16%

profile of v3, /device:TPU:0, one launch (start us, length us, event | category | flops | bytes accessed | tf_op | source)
XLA Modules:
  0.0 110.1 jit_solution(1080917604082806812)
XLA Ops:
  0.7 7.0 %gather.1 = (bf16[64,512]{1,0:T(8,128)(2,1)}, bf16[320,256]{1,0:T(8,128)(2,1)}, bf16[320,256]{1,0:T(8,128)(2,1)}) custom-call(s32[1]{0:T(128)} %bitcast.head_ref, bf16[3136,1024]{1,0:T(8,128)(2,1)} %x_ref.3, bf16[1024,256]{1,0:T(8,128)(2,1)} %wq_ref.1, bf16[1024,256]{1,0:T(8,128)(2,1)} %wk_ref.3, bf16[1024,256]{1,0:T(8,128)(2,1)} %wv_ref.3, ...), custom_call_target="tpu_custom_call" | custom-call | flops 2000000000 | bytes 10000000 | tf_op jit(solution)/shard_map/gather/pallas_call | solution.py:203
  7.7 1.7 %collective-permute-start = (bf16[64,512]{1,0:T(8,128)(2,1)}, bf16[64,512]{1,0:T(8,128)(2,1)S(1)}, u32[]{:S(2)}, u32[]{:S(2)}) collective-permute-start(bf16[64,512]{1,0:T(8,128)(2,1)} %get-tuple-element.25), channel_id=1, source_target_pairs={{0,8},{4,12},{8,16},{12,20},{16,24},{20,28},{24,0},{28,4},{32,40},... | collective-permute-start | bytes 196616 | tf_op jit(solution)/shard_map/ppermute | solution.py:232
  10.9 2.1 %collective-permute-start.2 = (bf16[64,512]{1,0:T(8,128)(2,1)}, bf16[64,512]{1,0:T(8,128)(2,1)S(1)}, u32[]{:S(2)}, u32[]{:S(2)}) collective-permute-start(bf16[64,512]{1,0:T(8,128)(2,1)} %get-tuple-element.25), channel_id=1, source_target_pairs={{0,16},{4,20},{8,24},{12,28},{16,0},{20,4},{24,8},{28,12},{32,48},... | collective-permute-start | bytes 196616 | tf_op jit(solution)/shard_map/ppermute | solution.py:232
  14.2 2.7 %collective-permute-done.2 = bf16[64,512]{1,0:T(8,128)(2,1)S(1)} collective-permute-done((bf16[64,512]{1,0:T(8,128)(2,1)}, bf16[64,512]{1,0:T(8,128)(2,1)S(1)}, u32[]{:S(2)}, u32[]{:S(2)}) %collective-permute-start.2) | collective-permute-done | bytes 65568 | tf_op jit(solution)/shard_map/ppermute | solution.py:232
  17.8 2.1 %collective-permute-start.7 = (bf16[4,64,512]{2,1,0:T(8,128)(2,1)S(1)}, bf16[4,64,512]{2,1,0:T(8,128)(2,1)S(1)}, u32[]{:S(2)}, u32[]{:S(2)}) collective-permute-start(bf16[4,64,512]{2,1,0:T(8,128)(2,1)S(1)} %pad_maximum_fusion.3.rest_0_), channel_id=1, source_target_pairs={{0,32},{4,36},{8,40},{12,44},{16,48},{20,52},{24,56},{28,60},{32,6... | collective-permute-start | bytes 786440 | tf_op jit(solution)/shard_map/ppermute | solution.py:234
  19.8 2.2 %collective-permute-start.8 = (bf16[4,64,512]{2,1,0:T(8,128)(2,1)S(1)}, bf16[4,64,512]{2,1,0:T(8,128)(2,1)S(1)}, u32[]{:S(2)}, u32[]{:S(2)}) collective-permute-start(bf16[4,64,512]{2,1,0:T(8,128)(2,1)S(1)} %pad_maximum_fusion.3.rest_0_), channel_id=1, source_target_pairs={{0,96},{4,100},{8,104},{12,108},{16,112},{20,116},{24,120},{28,124... | collective-permute-start | bytes 786440 | tf_op jit(solution)/shard_map/ppermute | solution.py:234
  22.0 1.8 %collective-permute-start.9 = (bf16[4,64,512]{2,1,0:T(8,128)(2,1)S(1)}, bf16[4,64,512]{2,1,0:T(8,128)(2,1)S(1)}, u32[]{:S(2)}, u32[]{:S(2)}) collective-permute-start(bf16[4,64,512]{2,1,0:T(8,128)(2,1)S(1)} %pad_maximum_fusion.3.rest_0_), channel_id=1, source_target_pairs={{0,64},{4,68},{8,72},{12,76},{16,80},{20,84},{24,88},{28,92},{32,9... | collective-permute-start | bytes 786440 | tf_op jit(solution)/shard_map/ppermute | solution.py:234
  23.8 2.4 %convolution_convert_fusion = bf16[1536,256]{1,0:T(8,128)(2,1)} fusion(bf16[320,256]{1,0:T(8,128)(2,1)} %get-tuple-element.35, s32[320]{0:T(512)S(1)} %multiply_add_fusion), kind=kOutput, calls=%fused_computation | convolution fusion | flops 252542976 | bytes 951552 | tf_op jit(solution)/shard_map/dot_general | solution.py:263
  26.2 5.0 %all-to-all-start = ((bf16[32,48,256]{2,1,0:T(8,128)(2,1)}), bf16[32,48,256]{2,1,0:T(8,128)(2,1)}, u32[]{:S(2)}, u32[]{:S(2)}) async-start(bf16[32,48,256]{2,1,0:T(8,128)(2,1)} %bitcast.9), calls=%async_computation | async-start | bytes 1572864 | tf_op jit(solution)/shard_map/all_to_all | solution.py:258
  31.2 10.3 %near.1 = (bf16[1280,256]{1,0:T(8,128)(2,1)}, f32[1280,256]{1,0:T(8,128)}, f32[1280,128]{1,0:T(8,128)}) custom-call(bf16[320,256]{1,0:T(8,128)(2,1)} %get-tuple-element.28.q_ref, bf16[3136,1024]{1,0:T(8,128)(2,1)} %x_ref.3, bf16[1024,256]{1,0:T(8,128)(2,1)} %wk_ref.3, bf16[1024,256]{1,0:T(8,128)(2,1)} %wv_ref.3, bf16[320,80]{1,0:T(8,128)(2,1)} %constant.126.clone.spread_ref), custom_call_target="tpu_custom_call" | custom-call | flops 5000000000 | bytes 10000000 | tf_op jit(solution)/shard_map/near/pallas_call | solution.py:271
  43.7 1.7 %collective-permute-start.4 = (bf16[128,1024]{1,0:T(8,128)(2,1)}, bf16[128,1024]{1,0:T(8,128)(2,1)}, u32[]{:S(2)}, u32[]{:S(2)}) collective-permute-start(bf16[128,1024]{1,0:T(8,128)(2,1)} %constant_dynamic-slice_fusion), channel_id=1, source_target_pairs={{0,3},{1,0},{2,1},{3,2},{4,7},{5,4},{6,5},{7,6},{8,11},{9,8},{10,9... | collective-permute-start | bytes 786440 | tf_op jit(solution)/shard_map/ppermute | solution.py:321
  45.5 1.8 %collective-permute-start.5 = (bf16[128,1024]{1,0:T(8,128)(2,1)}, bf16[128,1024]{1,0:T(8,128)(2,1)}, u32[]{:S(2)}, u32[]{:S(2)}) collective-permute-start(bf16[128,1024]{1,0:T(8,128)(2,1)} %constant_dynamic-slice_fusion), channel_id=1, source_target_pairs={{0,2},{1,3},{2,0},{3,1},{4,6},{5,7},{6,4},{7,5},{8,10},{9,11},{10,... | collective-permute-start | bytes 786440 | tf_op jit(solution)/shard_map/ppermute | solution.py:321
  48.3 3.9 %collective-permute-done.3 = bf16[128,1024]{1,0:T(8,128)(2,1)} collective-permute-done((bf16[128,1024]{1,0:T(8,128)(2,1)}, bf16[128,1024]{1,0:T(8,128)(2,1)}, u32[]{:S(2)}, u32[]{:S(2)}) %collective-permute-start.3) | collective-permute-done | bytes 262176 | tf_op jit(solution)/shard_map/ppermute | solution.py:321
  52.2 4.9 %collective-permute-done.4 = bf16[128,1024]{1,0:T(8,128)(2,1)} collective-permute-done((bf16[128,1024]{1,0:T(8,128)(2,1)}, bf16[128,1024]{1,0:T(8,128)(2,1)}, u32[]{:S(2)}, u32[]{:S(2)}) %collective-permute-start.4) | collective-permute-done | bytes 262176 | tf_op jit(solution)/shard_map/ppermute | solution.py:321
  57.1 1.7 %collective-permute-done.5 = bf16[128,1024]{1,0:T(8,128)(2,1)} collective-permute-done((bf16[128,1024]{1,0:T(8,128)(2,1)}, bf16[128,1024]{1,0:T(8,128)(2,1)}, u32[]{:S(2)}, u32[]{:S(2)}) %collective-permute-start.5) | collective-permute-done | bytes 262176 | tf_op jit(solution)/shard_map/ppermute | solution.py:321
  58.8 2.2 %pad_maximum_fusion.1 = bf16[4,128,1024]{2,1,0:T(8,128)(2,1)} fusion(bf16[1,128,1024]{2,1,0:T(8,128)(2,1)} %bitcast.8, bf16[1,128,1024]{2,1,0:T(8,128)(2,1)} %bitcast.7, bf16[1,128,1024]{2,1,0:T(8,128)(2,1)} %bitcast.6, bf16[1,128,1024]{2,1,0:T(8,128)(2,1)S(1)} %fusion.20), kind=kLoop, calls=%fused_computation.14 | loop fusion | flops 1572864 | bytes 2097152 | tf_op jit(solution)/shard_map/stack | solution.py:324
  64.4 7.1 %far.1 = bf16[32,48,256]{2,1,0:T(8,128)(2,1)} custom-call(bf16[1280,256]{1,0:T(8,128)(2,1)S(1)} %copy-done.5, f32[1280,256]{1,0:T(8,128)S(1)} %copy-done.4, f32[1280,128]{1,0:T(8,128)S(1)} %copy-done.6, s32[16,512]{1,0:T(8,128)S(1)} %copy-done.1, bf16[1280,16]{1,0:T(8,128)(2,1)S(1)} %copy-done.3, s32[1,512]{1,0:T(1,128)S(1)} %add.112.where_ref, ...), custom_call_target="tpu_custom_call" | custom-call | flops 4000000000 | bytes 4000000 | tf_op jit(solution)/shard_map/far/pallas_call | solution.py:299
  71.5 7.6 %all-to-all-start.1 = ((bf16[32,48,256]{2,1,0:T(8,128)(2,1)}), bf16[32,48,256]{2,1,0:T(8,128)(2,1)}, u32[]{:S(2)}, u32[]{:S(2)}) async-start(bf16[32,48,256]{2,1,0:T(8,128)(2,1)} %far.1), calls=%async_computation.1 | async-start | bytes 1572864 | tf_op jit(solution)/shard_map/all_to_all | solution.py:258
  82.6 2.1 %collective-permute-start.18 = (bf16[320,512]{1,0:T(8,128)(2,1)S(1)}, bf16[320,512]{1,0:T(8,128)(2,1)S(1)}, u32[]{:S(2)}, u32[]{:S(2)}) collective-permute-start(bf16[320,512]{1,0:T(8,128)(2,1)S(1)} %pad_maximum_fusion.2.rest_4_), channel_id=1, source_target_pairs={{0,3},{1,0},{2,1},{3,2},{4,7},{5,4},{6,5},{7,6},{8,11},{9,8},{10,9... | collective-permute-start | bytes 983048 | tf_op jit(solution)/shard_map/ppermute | solution.py:321
  85.3 2.6 %broadcast_select_fusion.1 = (bf16[4,128,1024]{2,1,0:T(8,128)(2,1)S(1)}, bf16[4,128,1024]{2,1,0:T(8,128)(2,1)}) fusion(bf16[4,128,1024]{2,1,0:T(8,128)(2,1)} %collective-permute-done.6, pred[]{:T(512)S(6)} %eq.71, bf16[1,128,1024]{2,1,0:T(8,128)(2,1)} %bitcast.8, bf16[1,128,1024]{2,1,0:T(8,128)(2,1)} %bitcast.7, bf16[1,128,1024]{2,1,0:T(8,128)(2,1)} %bitcast.6, ...), kind=kLoop, calls=%fused_computation.16 | loop fusion | flops 2621440 | bytes 4194305 | tf_op jit(solution)/shard_map/jit(_where)/select_n | solution.py:327
  88.0 5.7 %all-to-all-done.1 = bf16[32,48,256]{2,1,0:T(8,128)(2,1)} async-done(((bf16[32,48,256]{2,1,0:T(8,128)(2,1)}), bf16[32,48,256]{2,1,0:T(8,128)(2,1)}, u32[]{:S(2)}, u32[]{:S(2)}) %all-to-all-start.1) | async-done | bytes 786464 | tf_op jit(solution)/shard_map/all_to_all | solution.py:258
  96.5 2.1 %collective-permute-start.15 = (bf16[320,256]{1,0:T(8,128)(2,1)S(1)}, bf16[320,256]{1,0:T(8,128)(2,1)S(1)}, u32[]{:S(2)}, u32[]{:S(2)}) collective-permute-start(bf16[320,256]{1,0:T(8,128)(2,1)S(1)} %fusion.4.rest_0_), channel_id=1, source_target_pairs={{0,3},{1,0},{2,1},{3,2},{4,7},{5,4},{6,5},{7,6},{8,11},{9,8},{10,9... | collective-permute-start | bytes 491528 | tf_op jit(solution)/shard_map/ppermute | solution.py:321
  100.5 3.8 %collective-permute-done.14.rest_1_ = bf16[320,256]{1,0:T(8,128)(2,1)S(1)} collective-permute-done((bf16[320,256]{1,0:T(8,128)(2,1)S(1)}, bf16[320,256]{1,0:T(8,128)(2,1)S(1)}, u32[]{:S(2)}, u32[]{:S(2)}) %collective-permute-start.14) | collective-permute-done | bytes 163872 | tf_op jit(solution)/shard_map/ppermute | solution.py:321
  107.2 2.3 %final.1 = (bf16[320,256]{1,0:T(8,128)(2,1)}, f32[1,320]{1,0:T(1,128)S(1)}) custom-call(s32[1]{0:T(128)} %bitcast.head_ref, bf16[4,256,1024]{2,1,0:T(8,128)(2,1)S(1)} %pad_maximum_fusion.wo_ref, bf16[320,256]{1,0:T(8,128)(2,1)S(1)} %fusion.4.rest_0_, bf16[320,256]{1,0:T(8,128)(2,1)S(1)} %collective-permute-done.14.rest_1_, ...), custom_call_target="tpu_custom_call" | custom-call | flops 1000000000 | bytes 4000000 | tf_op jit(solution)/shard_map/final/pallas_call | solution.py:330
  (76 shorter events, 22.5 us)
Async XLA Ops:
  0.6 40.9 %copy-start = (bf16[256,1024]{1,0:T(8,128)(2,1)S(1)}, bf16[256,1024]{1,0:T(8,128)(2,1)}, u32[]{:S(2)}) copy-start(bf16[256,1024]{1,0:T(8,128)(2,1)} %param.21) | copy-start | bytes 1572868
  7.7 6.6 %collective-permute-start = (bf16[64,512]{1,0:T(8,128)(2,1)}, bf16[64,512]{1,0:T(8,128)(2,1)S(1)}, u32[]{:S(2)}, u32[]{:S(2)}) collective-permute-start(bf16[64,512]{1,0:T(8,128)(2,1)} %get-tuple-element.25), channel_id=1, source_target_pairs={{0,8},{4,12},{8,16},{12,20},{16,24},{20,28},{24,0},{28,4},{32,40},... | collective-permute-start | bytes 196616 | tf_op jit(solution)/shard_map/ppermute | solution.py:232
  9.3 4.9 %collective-permute-start.1 = (bf16[64,512]{1,0:T(8,128)(2,1)}, bf16[64,512]{1,0:T(8,128)(2,1)S(1)}, u32[]{:S(2)}, u32[]{:S(2)}) collective-permute-start(bf16[64,512]{1,0:T(8,128)(2,1)} %get-tuple-element.25), channel_id=1, source_target_pairs={{0,24},{4,28},{8,0},{12,4},{16,8},{20,12},{24,16},{28,20},{32,56},... | collective-permute-start | bytes 196616 | tf_op jit(solution)/shard_map/ppermute | solution.py:232
  10.9 6.0 %collective-permute-start.2 = (bf16[64,512]{1,0:T(8,128)(2,1)}, bf16[64,512]{1,0:T(8,128)(2,1)S(1)}, u32[]{:S(2)}, u32[]{:S(2)}) collective-permute-start(bf16[64,512]{1,0:T(8,128)(2,1)} %get-tuple-element.25), channel_id=1, source_target_pairs={{0,16},{4,20},{8,24},{12,28},{16,0},{20,4},{24,8},{28,12},{32,48},... | collective-permute-start | bytes 196616 | tf_op jit(solution)/shard_map/ppermute | solution.py:232
  17.8 27.7 %collective-permute-start.7 = (bf16[4,64,512]{2,1,0:T(8,128)(2,1)S(1)}, bf16[4,64,512]{2,1,0:T(8,128)(2,1)S(1)}, u32[]{:S(2)}, u32[]{:S(2)}) collective-permute-start(bf16[4,64,512]{2,1,0:T(8,128)(2,1)S(1)} %pad_maximum_fusion.3.rest_0_), channel_id=1, source_target_pairs={{0,32},{4,36},{8,40},{12,44},{16,48},{20,52},{24,56},{28,60},{32,6... | collective-permute-start | bytes 786440 | tf_op jit(solution)/shard_map/ppermute | solution.py:234
  19.8 27.8 %collective-permute-start.8 = (bf16[4,64,512]{2,1,0:T(8,128)(2,1)S(1)}, bf16[4,64,512]{2,1,0:T(8,128)(2,1)S(1)}, u32[]{:S(2)}, u32[]{:S(2)}) collective-permute-start(bf16[4,64,512]{2,1,0:T(8,128)(2,1)S(1)} %pad_maximum_fusion.3.rest_0_), channel_id=1, source_target_pairs={{0,96},{4,100},{8,104},{12,108},{16,112},{20,116},{24,120},{28,124... | collective-permute-start | bytes 786440 | tf_op jit(solution)/shard_map/ppermute | solution.py:234
  22.0 25.6 %collective-permute-start.9 = (bf16[4,64,512]{2,1,0:T(8,128)(2,1)S(1)}, bf16[4,64,512]{2,1,0:T(8,128)(2,1)S(1)}, u32[]{:S(2)}, u32[]{:S(2)}) collective-permute-start(bf16[4,64,512]{2,1,0:T(8,128)(2,1)S(1)} %pad_maximum_fusion.3.rest_0_), channel_id=1, source_target_pairs={{0,64},{4,68},{8,72},{12,76},{16,80},{20,84},{24,88},{28,92},{32,9... | collective-permute-start | bytes 786440 | tf_op jit(solution)/shard_map/ppermute | solution.py:234
  26.2 21.5 %all-to-all-start = ((bf16[32,48,256]{2,1,0:T(8,128)(2,1)}), bf16[32,48,256]{2,1,0:T(8,128)(2,1)}, u32[]{:S(2)}, u32[]{:S(2)}) async-start(bf16[32,48,256]{2,1,0:T(8,128)(2,1)} %bitcast.9), calls=%async_computation | async-start | bytes 1572864 | tf_op jit(solution)/shard_map/all_to_all | solution.py:258
  41.5 20.7 %copy-start.3 = (bf16[1280,16]{1,0:T(8,128)(2,1)S(1)}, bf16[1280,16]{1,0:T(8,128)(2,1)}, u32[]{:S(2)}) copy-start(bf16[1280,16]{1,0:T(8,128)(2,1)} %constant.127.clone.pick_ref) | copy-start | bytes 122884
  42.2 9.9 %collective-permute-start.3 = (bf16[128,1024]{1,0:T(8,128)(2,1)}, bf16[128,1024]{1,0:T(8,128)(2,1)}, u32[]{:S(2)}, u32[]{:S(2)}) collective-permute-start(bf16[128,1024]{1,0:T(8,128)(2,1)} %constant_dynamic-slice_fusion), channel_id=1, source_target_pairs={{0,1},{1,2},{2,3},{3,0},{4,5},{5,6},{6,7},{7,4},{8,9},{9,10},{10,1... | collective-permute-start | bytes 786440 | tf_op jit(solution)/shard_map/ppermute | solution.py:321
  43.7 13.4 %collective-permute-start.4 = (bf16[128,1024]{1,0:T(8,128)(2,1)}, bf16[128,1024]{1,0:T(8,128)(2,1)}, u32[]{:S(2)}, u32[]{:S(2)}) collective-permute-start(bf16[128,1024]{1,0:T(8,128)(2,1)} %constant_dynamic-slice_fusion), channel_id=1, source_target_pairs={{0,3},{1,0},{2,1},{3,2},{4,7},{5,4},{6,5},{7,6},{8,11},{9,8},{10,9... | collective-permute-start | bytes 786440 | tf_op jit(solution)/shard_map/ppermute | solution.py:321
  45.5 13.3 %collective-permute-start.5 = (bf16[128,1024]{1,0:T(8,128)(2,1)}, bf16[128,1024]{1,0:T(8,128)(2,1)}, u32[]{:S(2)}, u32[]{:S(2)}) collective-permute-start(bf16[128,1024]{1,0:T(8,128)(2,1)} %constant_dynamic-slice_fusion), channel_id=1, source_target_pairs={{0,2},{1,3},{2,0},{3,1},{4,6},{5,7},{6,4},{7,5},{8,10},{9,11},{10,... | collective-permute-start | bytes 786440 | tf_op jit(solution)/shard_map/ppermute | solution.py:321
  47.7 14.4 %collective-permute-start.10 = (bf16[4,64,512]{2,1,0:T(8,128)(2,1)S(1)}, bf16[4,64,512]{2,1,0:T(8,128)(2,1)S(1)}, u32[]{:S(2)}, u32[]{:S(2)}) collective-permute-start(bf16[4,64,512]{2,1,0:T(8,128)(2,1)S(1)} %pad_maximum_fusion.3.rest_0_), channel_id=1, source_target_pairs={{0,4},{4,0},{8,12},{12,8},{16,20},{20,16},{24,28},{28,24},{32,36},... | collective-permute-start | bytes 786440 | tf_op jit(solution)/shard_map/ppermute | solution.py:298
  47.8 14.3 %collective-permute-start.11 = (bf16[4,64,512]{2,1,0:T(8,128)(2,1)S(1)}, bf16[4,64,512]{2,1,0:T(8,128)(2,1)S(1)}, u32[]{:S(2)}, u32[]{:S(2)}) collective-permute-start(bf16[4,64,512]{2,1,0:T(8,128)(2,1)S(1)} %collective-permute-done.7.rest_1_), channel_id=1, source_target_pairs={{0,4},{4,0},{8,12},{12,8},{16,20},{20,16},{24,28},{28,24},{32,36},... | collective-permute-start | bytes 786440 | tf_op jit(solution)/shard_map/ppermute | solution.py:298
  52.2 10.0 %collective-permute-start.12 = (bf16[4,64,512]{2,1,0:T(8,128)(2,1)S(1)}, bf16[4,64,512]{2,1,0:T(8,128)(2,1)S(1)}, u32[]{:S(2)}, u32[]{:S(2)}) collective-permute-start(bf16[4,64,512]{2,1,0:T(8,128)(2,1)S(1)} %collective-permute-done.8.rest_2_), channel_id=1, source_target_pairs={{0,4},{4,0},{8,12},{12,8},{16,20},{20,16},{24,28},{28,24},{32,36},... | collective-permute-start | bytes 786440 | tf_op jit(solution)/shard_map/ppermute | solution.py:298
  57.1 5.1 %collective-permute-start.13 = (bf16[4,64,512]{2,1,0:T(8,128)(2,1)S(1)}, bf16[4,64,512]{2,1,0:T(8,128)(2,1)S(1)}, u32[]{:S(2)}, u32[]{:S(2)}) collective-permute-start(bf16[4,64,512]{2,1,0:T(8,128)(2,1)S(1)} %collective-permute-done.9.rest_3_), channel_id=1, source_target_pairs={{0,4},{4,0},{8,12},{12,8},{16,20},{20,16},{24,28},{28,24},{32,36},... | collective-permute-start | bytes 786440 | tf_op jit(solution)/shard_map/ppermute | solution.py:298
  61.0 24.3 %collective-permute-start.6 = (bf16[4,128,1024]{2,1,0:T(8,128)(2,1)}, bf16[4,128,1024]{2,1,0:T(8,128)(2,1)}, u32[]{:S(2)}, u32[]{:S(2)}) collective-permute-start(bf16[4,128,1024]{2,1,0:T(8,128)(2,1)} %pad_maximum_fusion.1), channel_id=1, source_target_pairs={{0,4},{4,0},{8,12},{12,8},{16,20},{20,16},{24,28},{28,24},{32,36},... | collective-permute-start | bytes 3145736 | tf_op jit(solution)/shard_map/ppermute | solution.py:325
  71.5 22.2 %all-to-all-start.1 = ((bf16[32,48,256]{2,1,0:T(8,128)(2,1)}), bf16[32,48,256]{2,1,0:T(8,128)(2,1)}, u32[]{:S(2)}, u32[]{:S(2)}) async-start(bf16[32,48,256]{2,1,0:T(8,128)(2,1)} %far.1), calls=%async_computation.1 | async-start | bytes 1572864 | tf_op jit(solution)/shard_map/all_to_all | solution.py:258
  81.4 17.2 %collective-permute-start.17 = (bf16[320,512]{1,0:T(8,128)(2,1)S(1)}, bf16[320,512]{1,0:T(8,128)(2,1)S(1)}, u32[]{:S(2)}, u32[]{:S(2)}) collective-permute-start(bf16[320,512]{1,0:T(8,128)(2,1)S(1)} %pad_maximum_fusion.2.rest_4_), channel_id=1, source_target_pairs={{0,1},{1,2},{2,3},{3,0},{4,5},{5,6},{6,7},{7,4},{8,9},{9,10},{10,1... | collective-permute-start | bytes 983048 | tf_op jit(solution)/shard_map/ppermute | solution.py:321
  82.6 16.9 %collective-permute-start.18 = (bf16[320,512]{1,0:T(8,128)(2,1)S(1)}, bf16[320,512]{1,0:T(8,128)(2,1)S(1)}, u32[]{:S(2)}, u32[]{:S(2)}) collective-permute-start(bf16[320,512]{1,0:T(8,128)(2,1)S(1)} %pad_maximum_fusion.2.rest_4_), channel_id=1, source_target_pairs={{0,3},{1,0},{2,1},{3,2},{4,7},{5,4},{6,5},{7,6},{8,11},{9,8},{10,9... | collective-permute-start | bytes 983048 | tf_op jit(solution)/shard_map/ppermute | solution.py:321
  84.7 15.8 %collective-permute-start.19 = (bf16[320,512]{1,0:T(8,128)(2,1)S(1)}, bf16[320,512]{1,0:T(8,128)(2,1)S(1)}, u32[]{:S(2)}, u32[]{:S(2)}) collective-permute-start(bf16[320,512]{1,0:T(8,128)(2,1)S(1)} %pad_maximum_fusion.2.rest_4_), channel_id=1, source_target_pairs={{0,2},{1,3},{2,0},{3,1},{4,6},{5,7},{6,4},{7,5},{8,10},{9,11},{10,... | collective-permute-start | bytes 983048 | tf_op jit(solution)/shard_map/ppermute | solution.py:321
  95.3 8.9 %collective-permute-start.14 = (bf16[320,256]{1,0:T(8,128)(2,1)S(1)}, bf16[320,256]{1,0:T(8,128)(2,1)S(1)}, u32[]{:S(2)}, u32[]{:S(2)}) collective-permute-start(bf16[320,256]{1,0:T(8,128)(2,1)S(1)} %fusion.4.rest_0_), channel_id=1, source_target_pairs={{0,1},{1,2},{2,3},{3,0},{4,5},{5,6},{6,7},{7,4},{8,9},{9,10},{10,1... | collective-permute-start | bytes 491528 | tf_op jit(solution)/shard_map/ppermute | solution.py:321
  96.5 9.4 %collective-permute-start.15 = (bf16[320,256]{1,0:T(8,128)(2,1)S(1)}, bf16[320,256]{1,0:T(8,128)(2,1)S(1)}, u32[]{:S(2)}, u32[]{:S(2)}) collective-permute-start(bf16[320,256]{1,0:T(8,128)(2,1)S(1)} %fusion.4.rest_0_), channel_id=1, source_target_pairs={{0,3},{1,0},{2,1},{3,2},{4,7},{5,4},{6,5},{7,6},{8,11},{9,8},{10,9... | collective-permute-start | bytes 491528 | tf_op jit(solution)/shard_map/ppermute | solution.py:321
  98.6 8.5 %collective-permute-start.16 = (bf16[320,256]{1,0:T(8,128)(2,1)S(1)}, bf16[320,256]{1,0:T(8,128)(2,1)S(1)}, u32[]{:S(2)}, u32[]{:S(2)}) collective-permute-start(bf16[320,256]{1,0:T(8,128)(2,1)S(1)} %fusion.4.rest_0_), channel_id=1, source_target_pairs={{0,2},{1,3},{2,0},{3,1},{4,6},{5,7},{6,4},{7,5},{8,10},{9,11},{10,... | collective-permute-start | bytes 491528 | tf_op jit(solution)/shard_map/ppermute | solution.py:321
  (10 other events, 105.4 us)

commit v4 on v3

v4 whole, which is shorter than its diff:
```python
import numpy as np

import jax
import jax.numpy as jnp
from jax import lax
from jax.experimental import pallas as pl
from jax.experimental.pallas import tpu as pltpu
from jax.sharding import PartitionSpec as P

HEAD_DIM = 64
PATCHES = 196
CAP = 48
NEG = -1e30
EPS = 1e-06
BF = jnp.bfloat16
F32 = jnp.float32


def nt(a, b):
    return lax.dot_general(a, b, (((1,), (1,)), ((), ())), preferred_element_type=F32)


def nn(a, b):
    return lax.dot_general(a, b, (((1,), (0,)), ((), ())), preferred_element_type=F32)


def fetch(pairs, sem):
    copies = [pltpu.make_async_copy(source, target, sem.at[i]) for i, (source, target) in enumerate(pairs)]
    for copy in copies:
        copy.start()
    return copies


def row_blocks(ref, count):
    size = ref.shape[0] // count
    return [ref.at[pl.ds(i * size, size)] for i in range(count)]


def gather_kernel(
    head_ref, x_hbm, wq_hbm, wk_hbm, wv_hbm, pool_ref, vis_ref, order_ref, chunk_ref, q_ref, t_ref, x_ref, wq_ref, wk_ref, wv_ref, sums, rows_in, sem
):
    steps = vis_ref.shape[0] // 4
    pairs = list(zip(row_blocks(x_hbm, steps), row_blocks(x_ref, steps)))
    copies = fetch(pairs + [(wk_hbm, wk_ref), (wv_hbm, wv_ref), (wq_hbm, wq_ref)], sem)
    rows = x_ref.shape[0] // steps
    frames, keep = vis_ref.shape
    count = 4 * keep
    cols = wk_ref.shape[1]
    r = lax.broadcasted_iota(jnp.int32, (count, 1), 0)
    frame = sum((r >= keep * i).astype(jnp.int32) for i in (1, 2, 3))
    spot = lax.broadcasted_iota(jnp.int32, (count, keep), 1) == r - keep * frame
    for step in range(steps):
        mine = (lax.broadcasted_iota(jnp.int32, (count, frames), 1) == frame + step * 4).astype(F32).astype(BF)
        seen = nn(mine, vis_ref[...].astype(F32).astype(BF))
        pos = jnp.sum(jnp.where(spot, seen, 0.0), axis=1, keepdims=True).astype(jnp.int32) + frame * PATCHES
        pick = (pos == lax.broadcasted_iota(jnp.int32, (count, rows), 1)).astype(F32).astype(BF)
        choose = jnp.concatenate([pool_ref[...], pick], axis=0)
        copies[step].wait()
        both = nn(choose, x_ref[step * rows : (step + 1) * rows, :])
        sums[step * 16 : (step + 1) * 16, :] = both[:16]
        rows_in[step * count : (step + 1) * count, :] = both[16:].astype(BF)
    total = sums[...]
    count = total.shape[0]
    high = total.astype(BF)
    low = (total - high.astype(F32)).astype(BF)
    pair = jnp.concatenate([high, low], axis=0)
    order = order_ref[...]
    for i, w_ref in enumerate((wk_ref, wv_ref)):
        copies[steps + i].wait()
        field = nn(pair, w_ref[...])
        pooled = ((field[:count] + field[count:]) / 7.0).astype(BF)
        chunk_ref[:, i * cols : (i + 1) * cols] = nn(order, pooled).astype(BF)
    copies[steps + 2].wait()
    q = nn(rows_in[...], wq_ref[...]).astype(BF).astype(F32) * HEAD_DIM ** -0.5
    q_ref[...] = q.astype(BF)
    t_ref[...] = rows_in[:, pl.ds(pl.multiple_of(head_ref[0] * cols, 128), cols)]


def stacked(q, spread, keep, heads):
    rows, cols = spread.shape[0], q.shape[1]
    r = lax.broadcasted_iota(jnp.int32, (rows, cols), 0)
    lane = lax.broadcasted_iota(jnp.int32, (rows, cols), 1)
    mine = lane // HEAD_DIM == r // keep % heads
    return mine, jnp.where(mine, nn(spread, q), 0.0).astype(BF)


def near_kernel(q_ref, x_hbm, wk_hbm, wv_hbm, spread_ref, out_ref, x_ref, wk_ref, wv_ref, sem):
    heads = wk_ref.shape[1] // HEAD_DIM
    chunk = spread_ref.shape[1]
    steps = q_ref.shape[0] // chunk
    pairs = list(zip(row_blocks(x_hbm, steps), row_blocks(x_ref, steps)))
    copies = fetch([(wk_hbm, wk_ref), (wv_hbm, wv_ref)] + pairs, sem)
    size = x_ref.shape[0] // steps
    keep = chunk // 4
    cols = q_ref.shape[1]
    rows = keep * heads
    span = 208
    lane = lax.broadcasted_iota(jnp.int32, (rows, 128), 1)
    copies[0].wait()
    copies[1].wait()
    for step in range(steps):
        copies[2 + step].wait()
        x = x_ref[step * size : (step + 1) * size, :]
        k = nn(x, wk_ref[...]).astype(BF)
        v = nn(x, wv_ref[...]).astype(BF)
        _, stack = stacked(q_ref[step * chunk : (step + 1) * chunk, :], spread_ref[...], keep, heads)
        for f in range(4):
            start = f * PATCHES // 16 * 16
            part = slice((step * 4 + f) * rows, (step * 4 + f + 1) * rows)
            c = lax.broadcasted_iota(jnp.int32, (rows, span), 1) + (start - f * PATCHES)
            s = jnp.where((c >= 0) & (c < PATCHES), nt(stack[f * rows : (f + 1) * rows], k[start : start + span]), NEG)
            m = jnp.max(s, axis=1, keepdims=True)
            e = jnp.exp(s - m)
            total = jnp.sum(e, axis=1, keepdims=True)
            level = m + jnp.log(total)
            high = level.astype(BF).astype(F32)
            middle = (level - high).astype(BF).astype(F32)
            side = jnp.where(lane == 0, high, jnp.where(lane == 1, middle, level - high - middle))
            out_ref[part, :cols] = (nn(e.astype(BF), v[start : start + span]) / total).astype(BF)
            out_ref[part, cols:] = side.astype(BF)


def far_kernel(q_ref, near_ref, allow_ref, pick_ref, where_ref, spread_ref, pack_ref, *rest):
    parts, (out_ref, key, value) = rest[:8], rest[8:]
    cols = q_ref.shape[1]
    heads = cols // HEAD_DIM
    chunk = spread_ref.shape[1]
    each = parts[0].shape[0] * 16
    count = each * len(parts)
    for i, ref in enumerate(parts):
        spot = slice(i * each, (i + 1) * each)
        for u in range(4):
            key[u, spot, :] = ref[:, u * 16 : (u + 1) * 16, :cols].reshape(each, cols)
            value[u, spot, :] = ref[:, u * 16 : (u + 1) * 16, cols:].reshape(each, cols)
    allowed = allow_ref[...].astype(F32).astype(BF)
    order = (lax.broadcasted_iota(jnp.int32, (allowed.shape[1], count), 0) == where_ref[...]).astype(F32).astype(BF)
    wall = jnp.where(nn(allowed, order) > 0.5, 0.0, NEG).astype(BF)
    rows = spread_ref.shape[0]
    outs = []
    for g in range(q_ref.shape[0] // chunk):
        part = slice(g * rows, (g + 1) * rows)
        mine, q = stacked(q_ref[g * chunk : (g + 1) * chunk, :], spread_ref[...], chunk // 4, heads)
        block = nn(pick_ref[part, :], wall)
        level = sum(near_ref[part, cols + i : cols + i + 1].astype(F32) for i in range(3))
        top = level
        scores = []
        for u in range(4):
            s = nt(q, key[u]) + block
            top = jnp.maximum(top, jnp.max(s, axis=1, keepdims=True))
            scores.append(s)
        total = jnp.exp(level - top)
        acc = total * near_ref[part, :cols].astype(F32)
        for u in range(4):
            e = jnp.exp(scores[u] - top)
            total = total + jnp.sum(e, axis=1, keepdims=True)
            acc = acc + nn(e.astype(BF), value[u])
        done = jnp.where(mine, acc / total, 0.0).astype(BF)
        outs.append(lax.dot_general(spread_ref[...], done, (((0,), (0,)), ((), ())), preferred_element_type=F32).astype(BF))
    out = jnp.concatenate(outs, axis=0)
    out_ref[...] = nn(pack_ref[...], out).astype(BF).reshape(out_ref.shape)


def final_kernel(at_ref, *rest):
    att, side, own_half, other_half, (target_ref, loss_ref, raw) = rest[:4], rest[4:8], rest[8:12], rest[12:16], rest[16:]
    head, core = at_ref[0], at_ref[1]
    rows, cols = att[0].shape
    half = cols // 2
    width = raw.shape[1]
    here = pl.ds(pl.multiple_of(core * half, 128), half)
    there = pl.ds(pl.multiple_of((1 - core) * half, 128), half)
    raw[...] = sum(nn(att[i][:, here], own_half[i][...]) + nn(att[i][:, there], other_half[i][...]) for i in range(4))
    spots = [pl.ds(pl.multiple_of(lax.rem(head + 4 - d, 4) * cols, 128), cols) for d in DISTANCES]
    for i in range(4):
        raw[:, spots[i]] += side[i][:, :cols].astype(F32)
    full = raw[...]
    mean = jnp.sum(full, axis=1, keepdims=True) / width
    var = jnp.sum(full * full, axis=1, keepdims=True) / width - mean * mean
    scale = lax.rsqrt(var + EPS)
    loss = jnp.zeros((rows, 1), F32)
    for i in range(4):
        normed = (raw[:, spots[i]] - mean) * scale
        if i == 0:
            target_ref[...] = normed.astype(BF)
        gap = side[i][:, cols:].astype(F32) - normed
        loss = loss + jnp.sum(gap * gap, axis=1, keepdims=True)
    loss_ref[...] = jnp.broadcast_to(loss / width, (rows, 128)).T[:1]


def whole(n):
    return [pl.BlockSpec(memory_space=pltpu.VMEM) for _ in range(n)]


def params(mib):
    return pltpu.CompilerParams(vmem_limit_bytes=mib * 2**20)


def tm_index(z, y, c):
    return ((z % 4) * 4 + y % 4) * 2 + c


DISTANCES = (0, 1, 3, 2)
PLACES = [(z, y, c) for z in range(4) for y in range(4) for c in range(2)]
SMEM = pl.BlockSpec(memory_space=pltpu.SMEM)
HBM = pl.BlockSpec(memory_space=pl.ANY)


def along_y(d):
    return [(tm_index(z, y, c), tm_index(z, y + d, c)) for z, y, c in PLACES]


def along_z(d):
    return [(tm_index(z, y, c), tm_index(z + d, y, c)) for z, y, c in PLACES]


OTHER_CORE = [(t, t ^ 1) for t in range(32)]


def body(tokens, w_query, w_key, w_value, w_out, pattern, visible, slot, pred):
    n_peers = lax.axis_size("tm")
    me = lax.axis_index("tm")
    head = lax.axis_index("head")
    n_heads = lax.axis_size("head")
    frames, keep = visible.shape
    width = tokens.shape[1]
    cols = w_query.shape[1]
    own = frames * keep
    steps = frames // 4
    block = 4 * PATCHES
    chunk = 4 * keep
    my_z, my_y, my_core = me // 8, me // 2 % 4, me % 2
    at = jnp.stack([head, my_core]).astype(jnp.int32)

    r = np.arange(block)
    p = r % PATCHES
    quadrant = 2 * (p // 14 >= 7) + (p % 14 >= 7)
    pool = np.zeros((16, block), np.float32)
    pool[r // PATCHES * 4 + quadrant, r] = 1.0
    n = np.arange(4 * frames)
    order = np.zeros((4 * frames, 4 * frames), np.float32)
    order[n, n % frames * 4 + n // frames] = 1.0

    mine, q, tok = pl.pallas_call(
        gather_kernel,
        in_specs=[SMEM] + [HBM] * 4 + whole(3),
        out_specs=whole(3),
        out_shape=[
            jax.ShapeDtypeStruct((4 * frames, 2 * cols), BF),
            jax.ShapeDtypeStruct((own, cols), BF),
            jax.ShapeDtypeStruct((own, cols), BF),
        ],
        scratch_shapes=[pltpu.VMEM((frames * PATCHES, width), BF)]
        + [pltpu.VMEM((width, cols), BF)] * 3
        + [pltpu.VMEM((4 * frames, width), F32), pltpu.VMEM((own, width), BF), pltpu.SemaphoreType.DMA((steps + 3,))],
        compiler_params=params(56),
        cost_estimate=pl.CostEstimate(flops=2 * 10**9, bytes_accessed=10**7, transcendentals=0),
        name="gather",
    )(at, tokens, w_query, w_key, w_value, jnp.asarray(pool, BF), visible, jnp.asarray(order, BF))

    plane = jnp.stack([mine] + [lax.ppermute(mine, "tm", along_y(d)) for d in DISTANCES[1:]])
    plane, q, tok = lax.optimization_barrier((plane, q, tok))
    parts = [plane] + [lax.ppermute(plane, "tm", along_z(d)) for d in DISTANCES[1:]]
    gap = jnp.asarray(DISTANCES, jnp.int32)
    core_at = jnp.stack([my_core, 1 - my_core])[:, None, None, None]
    z_at = ((my_z - gap) % 4)[None, :, None, None]
    y_at = ((my_y - gap) % 4)[None, None, :, None]
    where = ((z_at * 4 + y_at) * 2 + core_at) * frames + jnp.arange(frames, dtype=jnp.int32)
    where = where.reshape(1, n_peers * frames)

    owner_all = slot // own
    my_slots = lax.dynamic_slice_in_dim(slot, me * own, own)
    my_owner = my_slots // own
    before = np.tril(np.ones((own, own), np.float32), -1)
    same = (my_owner[:, None] == my_owner[None, :]) & (before > 0)
    place = my_owner * CAP + jnp.sum(same, axis=1, dtype=jnp.int32)
    pack = (jnp.arange(n_peers * CAP, dtype=jnp.int32)[:, None] == place[None, :]).astype(BF)
    coming = (owner_all == me).reshape(n_peers, own)
    rank = jnp.dot(coming.astype(BF), jnp.asarray(before.T, BF), preferred_element_type=F32).astype(jnp.int32)
    rank = jnp.where(coming, rank, -1)
    hit = rank[:, None, :] == jnp.arange(CAP, dtype=jnp.int32)[None, :, None]
    student = jnp.max(jnp.where(hit, (slot % own).reshape(n_peers, 1, own), -1), axis=2)
    unpack = (jnp.arange(own, dtype=jnp.int32)[:, None] == student.reshape(1, -1)).astype(BF)

    def deliver(packed):
        return lax.all_to_all(packed, "tm", 0, 0, tiled=True)

    def arrange(got):
        return jnp.dot(unpack, got.reshape(n_peers * CAP, -1), preferred_element_type=F32).astype(BF)

    tok_got = deliver(jnp.dot(pack, tok, preferred_element_type=F32).astype(BF).reshape(n_peers, CAP, cols))

    heads = cols // HEAD_DIM
    n = np.arange(own * heads)
    n_frame, n_keep = n // (keep * heads), n % keep
    spread = jnp.asarray(n_frame[: chunk * heads, None] * keep + n_keep[: chunk * heads, None] == np.arange(chunk), BF)
    pick = jnp.asarray(n_frame[:, None] == np.arange(frames), BF)
    near = pl.pallas_call(
        near_kernel,
        in_specs=whole(1) + [HBM] * 3 + whole(1),
        out_specs=pl.BlockSpec(memory_space=pltpu.VMEM),
        out_shape=jax.ShapeDtypeStruct((own * heads, cols + 128), BF),
        scratch_shapes=[pltpu.VMEM((frames * PATCHES, width), BF)]
        + [pltpu.VMEM((width, cols), BF)] * 2
        + [pltpu.SemaphoreType.DMA((steps + 2,))],
        compiler_params=params(40),
        cost_estimate=pl.CostEstimate(flops=5 * 10**9, bytes_accessed=10**7, transcendentals=10**6),
        name="near",
    )(q, tokens, w_key, w_value, spread)

    *parts, q, near, tok_got = lax.optimization_barrier((*parts, q, near, tok_got))
    parts = parts + [lax.ppermute(part, "tm", OTHER_CORE) for part in parts]
    packed = pl.pallas_call(
        far_kernel,
        in_specs=whole(15),
        out_specs=pl.BlockSpec(memory_space=pltpu.VMEM),
        out_shape=jax.ShapeDtypeStruct((n_peers, CAP, cols), BF),
        scratch_shapes=[
            pltpu.VMEM((4, n_peers * frames, cols), BF),
            pltpu.VMEM((4, n_peers * frames, cols), BF),
        ],
        compiler_params=params(40),
        cost_estimate=pl.CostEstimate(flops=4 * 10**9, bytes_accessed=4 * 10**6, transcendentals=3 * 10**6),
        name="far",
    )(q, near, pattern, pick, where, spread, pack, *parts)
    packed, tok_got = lax.optimization_barrier((packed, tok_got))
    tok_own = arrange(tok_got)
    att = arrange(deliver(packed))

    def to(d):
        return [(h, (h + d) % n_heads) for h in range(n_heads)]

    def over_heads(x):
        return [x] + [lax.ppermute(x, "head", to(d)) for d in DISTANCES[1:]]

    half = cols // 2
    halves = over_heads(lax.dynamic_slice_in_dim(w_out, my_core * half, half, 0))
    other = [lax.ppermute(piece, "tm", OTHER_CORE) for piece in halves]
    side = over_heads(jnp.concatenate([tok_own, pred], axis=1))

    target, row_loss = pl.pallas_call(
        final_kernel,
        in_specs=[SMEM] + whole(16),
        out_specs=whole(2),
        out_shape=[jax.ShapeDtypeStruct((own, cols), BF), jax.ShapeDtypeStruct((1, own), F32)],
        scratch_shapes=[pltpu.VMEM((own, width), F32)],
        compiler_params=params(40),
        cost_estimate=pl.CostEstimate(flops=10**9, bytes_accessed=4 * 10**6, transcendentals=0),
        name="final",
    )(at, *over_heads(att), *side, *halves, *other)
    return target, row_loss.reshape(own)


def solution(mesh):
    return jax.shard_map(
        body,
        mesh=mesh,
        in_specs=(
            P("tm", None),
            P(None, "head"),
            P(None, "head"),
            P(None, "head"),
            P("head", None),
            P("tm", None),
            P("tm", None),
            P(),
            P("tm", "head"),
        ),
        out_specs=(P("tm", "head"), P("tm")),
        check_vma=False,
    )
```

time: 111 us -> 118 us (1.063); the launches traced: 110 us -> 116 us
  local copies, waits for them, and re-layouts: 3.33 us -> 16.6 us
  waiting for transfers between devices: 26.5 us -> 16.3 us
  starting transfers between devices: 37.4 us -> 41.1 us
  other arithmetic: 8.51 us -> 5.6 us
  Pallas kernels: 26.7 us -> 29.3 us
    unnamed x24 -> x54, local copies, waits for them, and re-layouts: 2.22 us -> 16.3 us
    ppermute x9, waiting for transfers between devices: 18.1 us -> 7.18 us  [over_heads(): return [x] + [lax.ppermute(x, 'head', to(d)) for d in DISTANCES[1:]]]
    pallas_call x4, Pallas kernels: 26.7 us -> 29.3 us  [the longest x1 10.6 us: body(): pl.pallas_call(far_kernel, in_specs=whole(15), out_specs=pl.BlockSpec(mem...]
    select_n x1 -> x0, other arithmetic: 2.62 us -> none  [body(): jnp.where(first, halves, other)]
    ppermute x3, waiting for transfers between devices: 0.01 us -> 2.19 us  [body(): lax.ppermute(plane, 'tm', along_z(d))]
    ppermute x9, starting transfers between devices: 12.8 us -> 14.9 us  [over_heads(): return [x] + [lax.ppermute(x, 'head', to(d)) for d in DISTANCES[1:]]]
    another operation x1, other arithmetic: 2.23 us -> 0.67 us  [body(): at = jnp.stack([head, my_core]).astype(jnp.int32)]
    ppermute x3, waiting for transfers between devices: 2.67 us -> 1.3 us  [body(): lax.ppermute(mine, 'tm', along_y(d))]
  transfers between devices with their start and end apart: 22 -> 25, of which waited for: 9 -> 6; matrix products, arithmetic and copies ran while one was open for 14% -> 9% of each run, Pallas kernels for 16% -> 16%
where the time goes in v4:
time: 118 us; the launch traced here: 116 us
  starting transfers between devices  41.1 us (35%)
  Pallas kernels  29.3 us (25%)
  local copies, waits for them, and re-layouts  16.6 us (14%)
  waiting for transfers between devices  16.3 us (14%)
  matrix products  5.73 us (5%)
  other arithmetic  5.6 us (5%)
    unnamed x54, local copies, waits for them, and re-layouts  16.3 us
    ppermute x9, starting transfers between devices, over_heads(): return [x] + [lax.ppermute(x, 'head', to(d)) for d in DISTANCES[1:]]  14.9 us
    all_to_all x2, starting transfers between devices, deliver(): return lax.all_to_all(packed, 'tm', 0, 0, tiled=True)  13.7 us
    pallas_call x1, Pallas kernels, body(): pl.pallas_call(far_kernel, in_specs=whole(15), out_specs=pl.BlockSpec(mem...  10.6 us
    pallas_call x1, Pallas kernels, body(): pl.pallas_call(near_kernel, in_specs=whole(1) + [HBM] * 3 + whole(1), out...  8.37 us
    ppermute x9, waiting for transfers between devices, over_heads(): return [x] + [lax.ppermute(x, 'head', to(d)) for d in DISTANCES[1:]]  7.18 us
    pallas_call x1, Pallas kernels, body(): pl.pallas_call(gather_kernel, in_specs=[SMEM] + [HBM] * 4 + whole(3), out...  6.35 us
    all_to_all x2, waiting for transfers between devices, deliver(): return lax.all_to_all(packed, 'tm', 0, 0, tiled=True)  5.58 us
  transfers between devices with their start and end apart: 25, of which 6 were waited for; matrix products, arithmetic and copies ran while one was open for 9% of the time, Pallas kernels for 16%

profile of v4, /device:TPU:0, one launch (start us, length us, event | category | flops | bytes accessed | tf_op | source)
XLA Modules:
  0.0 115.6 jit_solution(7005829201954120922)
XLA Ops:
  1.3 6.4 %gather.1 = (bf16[64,512]{1,0:T(8,128)(2,1)}, bf16[320,256]{1,0:T(8,128)(2,1)}, bf16[320,256]{1,0:T(8,128)(2,1)}) custom-call(s32[2]{0:T(128)} %pad_add_fusion.head_ref.at_ref, bf16[3136,1024]{1,0:T(8,128)(2,1)} %x_hbm.3, bf16[1024,256]{1,0:T(8,128)(2,1)} %wq_hbm.1, bf16[1024,256]{1,0:T(8,128)(2,1)} %wk_hbm.3, bf16[1024,256]{1,0:T(8,128)(2,1)} %wv_hbm.3, ...), custom_call_target="tpu_custom_call" | custom-call | flops 2000000000 | bytes 10000000 | tf_op jit(solution)/shard_map/gather/pallas_call | solution.py:242
  7.7 1.7 %collective-permute-start = (bf16[64,512]{1,0:T(8,128)(2,1)}, bf16[64,512]{1,0:T(8,128)(2,1)S(1)}, u32[]{:S(2)}, u32[]{:S(2)}) collective-permute-start(bf16[64,512]{1,0:T(8,128)(2,1)} %get-tuple-element.19), channel_id=1, source_target_pairs={{0,8},{4,12},{8,16},{12,20},{16,24},{20,28},{24,0},{28,4},{32,40},... | collective-permute-start | bytes 196616 | tf_op jit(solution)/shard_map/ppermute | solution.py:259
  9.4 1.6 %collective-permute-start.1 = (bf16[64,512]{1,0:T(8,128)(2,1)}, bf16[64,512]{1,0:T(8,128)(2,1)S(1)}, u32[]{:S(2)}, u32[]{:S(2)}) collective-permute-start(bf16[64,512]{1,0:T(8,128)(2,1)} %get-tuple-element.19), channel_id=1, source_target_pairs={{0,24},{4,28},{8,0},{12,4},{16,8},{20,12},{24,16},{28,20},{32,56},... | collective-permute-start | bytes 196616 | tf_op jit(solution)/shard_map/ppermute | solution.py:259
  11.0 2.1 %collective-permute-start.2 = (bf16[64,512]{1,0:T(8,128)(2,1)}, bf16[64,512]{1,0:T(8,128)(2,1)S(1)}, u32[]{:S(2)}, u32[]{:S(2)}) collective-permute-start(bf16[64,512]{1,0:T(8,128)(2,1)} %get-tuple-element.19), channel_id=1, source_target_pairs={{0,16},{4,20},{8,24},{12,28},{16,0},{20,4},{24,8},{28,12},{32,48},... | collective-permute-start | bytes 196616 | tf_op jit(solution)/shard_map/ppermute | solution.py:259
  13.1 1.6 %collective-permute-start.16 = (bf16[128,1024]{1,0:T(8,128)(2,1)S(1)}, bf16[128,1024]{1,0:T(8,128)(2,1)S(1)}, u32[]{:S(2)}, u32[]{:S(2)}) collective-permute-start(bf16[128,1024]{1,0:T(8,128)(2,1)S(1)} %constant_dynamic-slice_fusion.rest_8_), channel_id=1, source_target_pairs={{0,1},{1,2},{2,3},{3,0},{4,5},{5,6},{6,7},{7,4},{8,9},{9,10},{10,1... | collective-permute-start | bytes 786440 | tf_op jit(solution)/shard_map/ppermute | solution.py:332
  18.0 2.5 %convolution_convert_fusion = bf16[1536,256]{1,0:T(8,128)(2,1)} fusion(bf16[320,256]{1,0:T(8,128)(2,1)} %get-tuple-element.24, s32[320]{0:T(512)S(1)} %multiply_add_fusion), kind=kOutput, calls=%fused_computation | convolution fusion | flops 252542976 | bytes 951552 | tf_op jit(solution)/shard_map/dot_general | solution.py:289
  20.4 7.3 %all-to-all-start = ((bf16[32,48,256]{2,1,0:T(8,128)(2,1)}), bf16[32,48,256]{2,1,0:T(8,128)(2,1)}, u32[]{:S(2)}, u32[]{:S(2)}) async-start(bf16[32,48,256]{2,1,0:T(8,128)(2,1)} %bitcast.6), calls=%async_computation | async-start | bytes 1572864 | tf_op jit(solution)/shard_map/all_to_all | solution.py:284
  28.9 1.8 %collective-permute-start.3 = (bf16[4,64,512]{2,1,0:T(8,128)(2,1)S(1)}, bf16[4,64,512]{2,1,0:T(8,128)(2,1)S(1)}, u32[]{:S(2)}, u32[]{:S(2)}) collective-permute-start(bf16[4,64,512]{2,1,0:T(8,128)(2,1)S(1)} %pad_maximum_fusion.1.rest_0_), channel_id=1, source_target_pairs={{0,32},{4,36},{8,40},{12,44},{16,48},{20,52},{24,56},{28,60},{32,6... | collective-permute-start | bytes 786440 | tf_op jit(solution)/shard_map/ppermute | solution.py:261
  32.2 2.0 %collective-permute-start.5 = (bf16[4,64,512]{2,1,0:T(8,128)(2,1)S(1)}, bf16[4,64,512]{2,1,0:T(8,128)(2,1)}, u32[]{:S(2)}, u32[]{:S(2)}) collective-permute-start(bf16[4,64,512]{2,1,0:T(8,128)(2,1)S(1)} %pad_maximum_fusion.1.rest_0_), channel_id=1, source_target_pairs={{0,64},{4,68},{8,72},{12,76},{16,80},{20,84},{24,88},{28,92},{32,9... | collective-permute-start | bytes 786440 | tf_op jit(solution)/shard_map/ppermute | solution.py:261
  34.3 2.8 %copy-done.1 = bf16[3136,1024]{1,0:T(8,128)(2,1)S(1)} copy-done((bf16[3136,1024]{1,0:T(8,128)(2,1)S(1)}, bf16[3136,1024]{1,0:T(8,128)(2,1)}, u32[]{:S(2)}) %copy-start.1) | copy-done | bytes 6422552
  38.9 8.4 %near.1.near_ref = bf16[1280,384]{1,0:T(8,128)(2,1)S(1)} custom-call(bf16[320,256]{1,0:T(8,128)(2,1)S(1)} %copy-done.13, bf16[3136,1024]{1,0:T(8,128)(2,1)S(1)} %copy-done.1, bf16[1024,256]{1,0:T(8,128)(2,1)S(1)} %copy-done.2, bf16[1024,256]{1,0:T(8,128)(2,1)S(1)} %copy-done.3, bf16[320,80]{1,0:T(8,128)(2,1)S(1)} %copy-done.17), custom_call_target="tpu_custom_call" | custom-call | flops 5000000000 | bytes 10000000 | tf_op jit(solution)/shard_map/near/pallas_call | solution.py:296
  49.6 2.2 %collective-permute-done.5.rest_3_ = bf16[4,64,512]{2,1,0:T(8,128)(2,1)} collective-permute-done((bf16[4,64,512]{2,1,0:T(8,128)(2,1)S(1)}, bf16[4,64,512]{2,1,0:T(8,128)(2,1)}, u32[]{:S(2)}, u32[]{:S(2)}) %collective-permute-start.5) | collective-permute-done | bytes 262176 | tf_op jit(solution)/shard_map/ppermute | solution.py:261
  53.7 2.8 %collective-permute-start.17 = (bf16[128,1024]{1,0:T(8,128)(2,1)S(1)}, bf16[128,1024]{1,0:T(8,128)(2,1)S(1)}, u32[]{:S(2)}, u32[]{:S(2)}) collective-permute-start(bf16[128,1024]{1,0:T(8,128)(2,1)S(1)} %constant_dynamic-slice_fusion.rest_8_), channel_id=1, source_target_pairs={{0,3},{1,0},{2,1},{3,2},{4,7},{5,4},{6,5},{7,6},{8,11},{9,8},{10,9... | collective-permute-start | bytes 786440 | tf_op jit(solution)/shard_map/ppermute | solution.py:332
  64.9 10.6 %far.1 = bf16[32,48,256]{2,1,0:T(8,128)(2,1)} custom-call(bf16[320,256]{1,0:T(8,128)(2,1)S(1)} %copy-done.14, bf16[1280,384]{1,0:T(8,128)(2,1)S(1)} %copy-done.20, s32[16,512]{1,0:T(8,128)S(1)} %copy-done.15, bf16[1280,16]{1,0:T(8,128)(2,1)S(1)} %copy-done.16, s32[1,512]{1,0:T(1,128)S(1)} %add.111.where_ref, bf16[320,80]{1,0:T(8,128)(2,1)S(1)} %copy-done.18, ...), custom_call_target="tpu_custom_call" | custom-call | flops 4000000000 | bytes 4000000 | tf_op jit(solution)/shard_map/far/pallas_call | solution.py:311
  75.5 6.4 %all-to-all-start.1 = ((bf16[32,48,256]{2,1,0:T(8,128)(2,1)}), bf16[32,48,256]{2,1,0:T(8,128)(2,1)}, u32[]{:S(2)}, u32[]{:S(2)}) async-start(bf16[32,48,256]{2,1,0:T(8,128)(2,1)} %far.1), calls=%async_computation.1 | async-start | bytes 1572864 | tf_op jit(solution)/shard_map/all_to_all | solution.py:284
  83.1 1.6 %fusion.5 = bf16[320,256]{1,0:T(8,128)(2,1)S(1)} fusion(bf16[1536,256]{1,0:T(8,128)(2,1)} %bitcast.9, s32[1536]{0:T(1024)S(1)} %eq.74), kind=kOutput, calls=%fused_computation.10 | convolution fusion | flops 252231680 | bytes 956416 | tf_op jit(solution)/shard_map/dot_general | solution.py:287
  86.2 2.3 %collective-permute-start.14 = (bf16[320,512]{1,0:T(8,128)(2,1)S(1)}, bf16[320,512]{1,0:T(8,128)(2,1)S(1)}, u32[]{:S(2)}, u32[]{:S(2)}) collective-permute-start(bf16[320,512]{1,0:T(8,128)(2,1)S(1)} %pad_maximum_fusion.rest_4_), channel_id=1, source_target_pairs={{0,3},{1,0},{2,1},{3,2},{4,7},{5,4},{6,5},{7,6},{8,11},{9,8},{10,9... | collective-permute-start | bytes 983048 | tf_op jit(solution)/shard_map/ppermute | solution.py:332
  90.8 5.6 %all-to-all-done.1 = bf16[32,48,256]{2,1,0:T(8,128)(2,1)} async-done(((bf16[32,48,256]{2,1,0:T(8,128)(2,1)}), bf16[32,48,256]{2,1,0:T(8,128)(2,1)}, u32[]{:S(2)}, u32[]{:S(2)}) %all-to-all-start.1) | async-done | bytes 786464 | tf_op jit(solution)/shard_map/all_to_all | solution.py:284
  96.4 1.6 %fusion.4.rest_0_ = bf16[320,256]{1,0:T(8,128)(2,1)S(1)} fusion(bf16[1536,256]{1,0:T(8,128)(2,1)} %bitcast.8, s32[1536]{0:T(1024)S(1)} %eq.74), kind=kOutput, calls=%fused_computation.9 | convolution fusion | flops 252231680 | bytes 956416 | tf_op jit(solution)/shard_map/dot_general | solution.py:287
  99.0 2.3 %collective-permute-start.11 = (bf16[320,256]{1,0:T(8,128)(2,1)S(1)}, bf16[320,256]{1,0:T(8,128)(2,1)S(1)}, u32[]{:S(2)}, u32[]{:S(2)}) collective-permute-start(bf16[320,256]{1,0:T(8,128)(2,1)S(1)} %fusion.4.rest_0_), channel_id=1, source_target_pairs={{0,3},{1,0},{2,1},{3,2},{4,7},{5,4},{6,5},{7,6},{8,11},{9,8},{10,9... | collective-permute-start | bytes 491528 | tf_op jit(solution)/shard_map/ppermute | solution.py:332
  101.3 1.6 %collective-permute-done.13.rest_5_ = bf16[320,512]{1,0:T(8,128)(2,1)S(1)} collective-permute-done((bf16[320,512]{1,0:T(8,128)(2,1)S(1)}, bf16[320,512]{1,0:T(8,128)(2,1)S(1)}, u32[]{:S(2)}, u32[]{:S(2)}) %collective-permute-start.13) | collective-permute-done | bytes 327712 | tf_op jit(solution)/shard_map/ppermute | solution.py:332
  102.9 1.6 %collective-permute-start.12 = (bf16[320,256]{1,0:T(8,128)(2,1)S(1)}, bf16[320,256]{1,0:T(8,128)(2,1)S(1)}, u32[]{:S(2)}, u32[]{:S(2)}) collective-permute-start(bf16[320,256]{1,0:T(8,128)(2,1)S(1)} %fusion.4.rest_0_), channel_id=1, source_target_pairs={{0,2},{1,3},{2,0},{3,1},{4,6},{5,7},{6,4},{7,5},{8,10},{9,11},{10,... | collective-permute-start | bytes 491528 | tf_op jit(solution)/shard_map/ppermute | solution.py:332
  104.5 5.5 %collective-permute-done.10.rest_1_ = bf16[320,256]{1,0:T(8,128)(2,1)S(1)} collective-permute-done((bf16[320,256]{1,0:T(8,128)(2,1)S(1)}, bf16[320,256]{1,0:T(8,128)(2,1)S(1)}, u32[]{:S(2)}, u32[]{:S(2)}) %collective-permute-start.10) | collective-permute-done | bytes 163872 | tf_op jit(solution)/shard_map/ppermute | solution.py:332
  111.0 4.0 %final.1 = (bf16[320,256]{1,0:T(8,128)(2,1)}, f32[1,320]{1,0:T(1,128)S(1)}) custom-call(s32[2]{0:T(128)S(1)} %copy-done.8, bf16[320,256]{1,0:T(8,128)(2,1)S(1)} %fusion.4.rest_0_, bf16[320,256]{1,0:T(8,128)(2,1)S(1)} %collective-permute-done.10.rest_1_, bf16[320,256]{1,0:T(8,128)(2,1)S(1)} %collective-permute-done.11.rest_2_, ...), custom_call_target="tpu_custom_call" | custom-call | flops 1000000000 | bytes 4000000 | tf_op jit(solution)/shard_map/final/pallas_call | solution.py:339
  (109 shorter events, 28.6 us)
Async XLA Ops:
  7.7 8.0 %collective-permute-start = (bf16[64,512]{1,0:T(8,128)(2,1)}, bf16[64,512]{1,0:T(8,128)(2,1)S(1)}, u32[]{:S(2)}, u32[]{:S(2)}) collective-permute-start(bf16[64,512]{1,0:T(8,128)(2,1)} %get-tuple-element.19), channel_id=1, source_target_pairs={{0,8},{4,12},{8,16},{12,20},{16,24},{20,28},{24,0},{28,4},{32,40},... | collective-permute-start | bytes 196616 | tf_op jit(solution)/shard_map/ppermute | solution.py:259
  9.4 6.3 %collective-permute-start.1 = (bf16[64,512]{1,0:T(8,128)(2,1)}, bf16[64,512]{1,0:T(8,128)(2,1)S(1)}, u32[]{:S(2)}, u32[]{:S(2)}) collective-permute-start(bf16[64,512]{1,0:T(8,128)(2,1)} %get-tuple-element.19), channel_id=1, source_target_pairs={{0,24},{4,28},{8,0},{12,4},{16,8},{20,12},{24,16},{28,20},{32,56},... | collective-permute-start | bytes 196616 | tf_op jit(solution)/shard_map/ppermute | solution.py:259
  11.0 6.0 %collective-permute-start.2 = (bf16[64,512]{1,0:T(8,128)(2,1)}, bf16[64,512]{1,0:T(8,128)(2,1)S(1)}, u32[]{:S(2)}, u32[]{:S(2)}) collective-permute-start(bf16[64,512]{1,0:T(8,128)(2,1)} %get-tuple-element.19), channel_id=1, source_target_pairs={{0,16},{4,20},{8,24},{12,28},{16,0},{20,4},{24,8},{28,12},{32,48},... | collective-permute-start | bytes 196616 | tf_op jit(solution)/shard_map/ppermute | solution.py:259
  13.1 69.7 %collective-permute-start.16 = (bf16[128,1024]{1,0:T(8,128)(2,1)S(1)}, bf16[128,1024]{1,0:T(8,128)(2,1)S(1)}, u32[]{:S(2)}, u32[]{:S(2)}) collective-permute-start(bf16[128,1024]{1,0:T(8,128)(2,1)S(1)} %constant_dynamic-slice_fusion.rest_8_), channel_id=1, source_target_pairs={{0,1},{1,2},{2,3},{3,0},{4,5},{5,6},{6,7},{7,4},{8,9},{9,10},{10,1... | collective-permute-start | bytes 786440 | tf_op jit(solution)/shard_map/ppermute | solution.py:332
  20.4 31.4 %all-to-all-start = ((bf16[32,48,256]{2,1,0:T(8,128)(2,1)}), bf16[32,48,256]{2,1,0:T(8,128)(2,1)}, u32[]{:S(2)}, u32[]{:S(2)}) async-start(bf16[32,48,256]{2,1,0:T(8,128)(2,1)} %bitcast.6), calls=%async_computation | async-start | bytes 1572864 | tf_op jit(solution)/shard_map/all_to_all | solution.py:284
  28.9 19.3 %collective-permute-start.3 = (bf16[4,64,512]{2,1,0:T(8,128)(2,1)S(1)}, bf16[4,64,512]{2,1,0:T(8,128)(2,1)S(1)}, u32[]{:S(2)}, u32[]{:S(2)}) collective-permute-start(bf16[4,64,512]{2,1,0:T(8,128)(2,1)S(1)} %pad_maximum_fusion.1.rest_0_), channel_id=1, source_target_pairs={{0,32},{4,36},{8,40},{12,44},{16,48},{20,52},{24,56},{28,60},{32,6... | collective-permute-start | bytes 786440 | tf_op jit(solution)/shard_map/ppermute | solution.py:261
  30.7 17.5 %collective-permute-start.4 = (bf16[4,64,512]{2,1,0:T(8,128)(2,1)S(1)}, bf16[4,64,512]{2,1,0:T(8,128)(2,1)S(1)}, u32[]{:S(2)}, u32[]{:S(2)}) collective-permute-start(bf16[4,64,512]{2,1,0:T(8,128)(2,1)S(1)} %pad_maximum_fusion.1.rest_0_), channel_id=1, source_target_pairs={{0,96},{4,100},{8,104},{12,108},{16,112},{20,116},{24,120},{28,124... | collective-permute-start | bytes 786440 | tf_op jit(solution)/shard_map/ppermute | solution.py:261
  32.2 19.6 %collective-permute-start.5 = (bf16[4,64,512]{2,1,0:T(8,128)(2,1)S(1)}, bf16[4,64,512]{2,1,0:T(8,128)(2,1)}, u32[]{:S(2)}, u32[]{:S(2)}) collective-permute-start(bf16[4,64,512]{2,1,0:T(8,128)(2,1)S(1)} %pad_maximum_fusion.1.rest_0_), channel_id=1, source_target_pairs={{0,64},{4,68},{8,72},{12,76},{16,80},{20,84},{24,88},{28,92},{32,9... | collective-permute-start | bytes 786440 | tf_op jit(solution)/shard_map/ppermute | solution.py:261
  51.8 4.6 %collective-permute-start.7 = (bf16[4,64,512]{2,1,0:T(8,128)(2,1)}, bf16[4,64,512]{2,1,0:T(8,128)(2,1)S(1)}, u32[]{:S(2)}, u32[]{:S(2)}) collective-permute-start(bf16[4,64,512]{2,1,0:T(8,128)(2,1)} %copy-done.9), channel_id=1, source_target_pairs={{0,4},{4,0},{8,12},{12,8},{16,20},{20,16},{24,28},{28,24},{32,36},... | collective-permute-start | bytes 786440 | tf_op jit(solution)/shard_map/ppermute | solution.py:310
  52.3 4.9 %collective-permute-start.8 = (bf16[4,64,512]{2,1,0:T(8,128)(2,1)}, bf16[4,64,512]{2,1,0:T(8,128)(2,1)S(1)}, u32[]{:S(2)}, u32[]{:S(2)}) collective-permute-start(bf16[4,64,512]{2,1,0:T(8,128)(2,1)} %copy-done.11), channel_id=1, source_target_pairs={{0,4},{4,0},{8,12},{12,8},{16,20},{20,16},{24,28},{28,24},{32,36},... | collective-permute-start | bytes 786440 | tf_op jit(solution)/shard_map/ppermute | solution.py:310
  52.6 4.7 %collective-permute-start.9 = (bf16[4,64,512]{2,1,0:T(8,128)(2,1)}, bf16[4,64,512]{2,1,0:T(8,128)(2,1)S(1)}, u32[]{:S(2)}, u32[]{:S(2)}) collective-permute-start(bf16[4,64,512]{2,1,0:T(8,128)(2,1)} %collective-permute-done.5.rest_3_), channel_id=1, source_target_pairs={{0,4},{4,0},{8,12},{12,8},{16,20},{20,16},{24,28},{28,24},{32,36},... | collective-permute-start | bytes 786440 | tf_op jit(solution)/shard_map/ppermute | solution.py:310
  53.7 32.0 %collective-permute-start.17 = (bf16[128,1024]{1,0:T(8,128)(2,1)S(1)}, bf16[128,1024]{1,0:T(8,128)(2,1)S(1)}, u32[]{:S(2)}, u32[]{:S(2)}) collective-permute-start(bf16[128,1024]{1,0:T(8,128)(2,1)S(1)} %constant_dynamic-slice_fusion.rest_8_), channel_id=1, source_target_pairs={{0,3},{1,0},{2,1},{3,2},{4,7},{5,4},{6,5},{7,6},{8,11},{9,8},{10,9... | collective-permute-start | bytes 786440 | tf_op jit(solution)/shard_map/ppermute | solution.py:332
  56.5 29.2 %collective-permute-start.18 = (bf16[128,1024]{1,0:T(8,128)(2,1)S(1)}, bf16[128,1024]{1,0:T(8,128)(2,1)S(1)}, u32[]{:S(2)}, u32[]{:S(2)}) collective-permute-start(bf16[128,1024]{1,0:T(8,128)(2,1)S(1)} %constant_dynamic-slice_fusion.rest_8_), channel_id=1, source_target_pairs={{0,2},{1,3},{2,0},{3,1},{4,6},{5,7},{6,4},{7,5},{8,10},{9,11},{10,... | collective-permute-start | bytes 786440 | tf_op jit(solution)/shard_map/ppermute | solution.py:332
  57.3 28.9 %collective-permute-start.19 = (bf16[128,1024]{1,0:T(8,128)(2,1)S(1)}, bf16[128,1024]{1,0:T(8,128)(2,1)S(1)}, u32[]{:S(2)}, u32[]{:S(2)}) collective-permute-start(bf16[128,1024]{1,0:T(8,128)(2,1)S(1)} %constant_dynamic-slice_fusion.rest_8_), channel_id=1, source_target_pairs={{0,4},{4,0},{8,12},{12,8},{16,20},{20,16},{24,28},{28,24},{32,36},... | collective-permute-start | bytes 786440 | tf_op jit(solution)/shard_map/ppermute | solution.py:336
  75.5 20.9 %all-to-all-start.1 = ((bf16[32,48,256]{2,1,0:T(8,128)(2,1)}), bf16[32,48,256]{2,1,0:T(8,128)(2,1)}, u32[]{:S(2)}, u32[]{:S(2)}) async-start(bf16[32,48,256]{2,1,0:T(8,128)(2,1)} %far.1), calls=%async_computation.1 | async-start | bytes 1572864 | tf_op jit(solution)/shard_map/all_to_all | solution.py:284
  82.8 5.7 %collective-permute-start.20 = (bf16[128,1024]{1,0:T(8,128)(2,1)S(1)}, bf16[128,1024]{1,0:T(8,128)(2,1)S(1)}, u32[]{:S(2)}, u32[]{:S(2)}) collective-permute-start(bf16[128,1024]{1,0:T(8,128)(2,1)S(1)} %collective-permute-done.16.rest_9_), channel_id=1, source_target_pairs={{0,4},{4,0},{8,12},{12,8},{16,20},{20,16},{24,28},{28,24},{32,36},... | collective-permute-start | bytes 786440 | tf_op jit(solution)/shard_map/ppermute | solution.py:336
  84.7 18.1 %collective-permute-start.13 = (bf16[320,512]{1,0:T(8,128)(2,1)S(1)}, bf16[320,512]{1,0:T(8,128)(2,1)S(1)}, u32[]{:S(2)}, u32[]{:S(2)}) collective-permute-start(bf16[320,512]{1,0:T(8,128)(2,1)S(1)} %pad_maximum_fusion.rest_4_), channel_id=1, source_target_pairs={{0,1},{1,2},{2,3},{3,0},{4,5},{5,6},{6,7},{7,4},{8,9},{9,10},{10,1... | collective-permute-start | bytes 983048 | tf_op jit(solution)/shard_map/ppermute | solution.py:332
  85.7 12.3 %collective-permute-start.21 = (bf16[128,1024]{1,0:T(8,128)(2,1)S(1)}, bf16[128,1024]{1,0:T(8,128)(2,1)}, u32[]{:S(2)}, u32[]{:S(2)}) collective-permute-start(bf16[128,1024]{1,0:T(8,128)(2,1)S(1)} %collective-permute-done.17.rest_10_), channel_id=1, source_target_pairs={{0,4},{4,0},{8,12},{12,8},{16,20},{20,16},{24,28},{28,24},{32,36},... | collective-permute-start | bytes 786440 | tf_op jit(solution)/shard_map/ppermute | solution.py:336
  85.7 13.2 %collective-permute-start.22 = (bf16[128,1024]{1,0:T(8,128)(2,1)S(1)}, bf16[128,1024]{1,0:T(8,128)(2,1)}, u32[]{:S(2)}, u32[]{:S(2)}) collective-permute-start(bf16[128,1024]{1,0:T(8,128)(2,1)S(1)} %collective-permute-done.18.rest_11_), channel_id=1, source_target_pairs={{0,4},{4,0},{8,12},{12,8},{16,20},{20,16},{24,28},{28,24},{32,36},... | collective-permute-start | bytes 786440 | tf_op jit(solution)/shard_map/ppermute | solution.py:336
  86.2 18.2 %collective-permute-start.14 = (bf16[320,512]{1,0:T(8,128)(2,1)S(1)}, bf16[320,512]{1,0:T(8,128)(2,1)S(1)}, u32[]{:S(2)}, u32[]{:S(2)}) collective-permute-start(bf16[320,512]{1,0:T(8,128)(2,1)S(1)} %pad_maximum_fusion.rest_4_), channel_id=1, source_target_pairs={{0,3},{1,0},{2,1},{3,2},{4,7},{5,4},{6,5},{7,6},{8,11},{9,8},{10,9... | collective-permute-start | bytes 983048 | tf_op jit(solution)/shard_map/ppermute | solution.py:332
  89.3 15.2 %collective-permute-start.15 = (bf16[320,512]{1,0:T(8,128)(2,1)S(1)}, bf16[320,512]{1,0:T(8,128)(2,1)S(1)}, u32[]{:S(2)}, u32[]{:S(2)}) collective-permute-start(bf16[320,512]{1,0:T(8,128)(2,1)S(1)} %pad_maximum_fusion.rest_4_), channel_id=1, source_target_pairs={{0,2},{1,3},{2,0},{3,1},{4,6},{5,7},{6,4},{7,5},{8,10},{9,11},{10,... | collective-permute-start | bytes 983048 | tf_op jit(solution)/shard_map/ppermute | solution.py:332
  98.0 12.0 %collective-permute-start.10 = (bf16[320,256]{1,0:T(8,128)(2,1)S(1)}, bf16[320,256]{1,0:T(8,128)(2,1)S(1)}, u32[]{:S(2)}, u32[]{:S(2)}) collective-permute-start(bf16[320,256]{1,0:T(8,128)(2,1)S(1)} %fusion.4.rest_0_), channel_id=1, source_target_pairs={{0,1},{1,2},{2,3},{3,0},{4,5},{5,6},{6,7},{7,4},{8,9},{9,10},{10,1... | collective-permute-start | bytes 491528 | tf_op jit(solution)/shard_map/ppermute | solution.py:332
  99.0 11.1 %collective-permute-start.11 = (bf16[320,256]{1,0:T(8,128)(2,1)S(1)}, bf16[320,256]{1,0:T(8,128)(2,1)S(1)}, u32[]{:S(2)}, u32[]{:S(2)}) collective-permute-start(bf16[320,256]{1,0:T(8,128)(2,1)S(1)} %fusion.4.rest_0_), channel_id=1, source_target_pairs={{0,3},{1,0},{2,1},{3,2},{4,7},{5,4},{6,5},{7,6},{8,11},{9,8},{10,9... | collective-permute-start | bytes 491528 | tf_op jit(solution)/shard_map/ppermute | solution.py:332
  102.9 7.2 %collective-permute-start.12 = (bf16[320,256]{1,0:T(8,128)(2,1)S(1)}, bf16[320,256]{1,0:T(8,128)(2,1)S(1)}, u32[]{:S(2)}, u32[]{:S(2)}) collective-permute-start(bf16[320,256]{1,0:T(8,128)(2,1)S(1)} %fusion.4.rest_0_), channel_id=1, source_target_pairs={{0,2},{1,3},{2,0},{3,1},{4,6},{5,7},{6,4},{7,5},{8,10},{9,11},{10,... | collective-permute-start | bytes 491528 | tf_op jit(solution)/shard_map/ppermute | solution.py:332
  (28 other events, 199.0 us)

commit v5 on v4

--- a/solution.py
+++ b/solution.py
@@ -37,7 +37,7 @@
 
 
 def gather_kernel(
-    head_ref, x_hbm, wq_hbm, wk_hbm, wv_hbm, pool_ref, vis_ref, order_ref, chunk_ref, q_ref, t_ref, x_ref, wq_ref, wk_ref, wv_ref, sums, rows_in, sem
+    x_hbm, wq_hbm, wk_hbm, wv_hbm, pool_ref, vis_ref, order_ref, chunk_ref, q_ref, t_ref, x_ref, wq_ref, wk_ref, wv_ref, sums, rows_in, sem
 ):
     steps = vis_ref.shape[0] // 4
     pairs = list(zip(row_blocks(x_hbm, steps), row_blocks(x_ref, steps)))
@@ -73,29 +73,37 @@
     copies[steps + 2].wait()
     q = nn(rows_in[...], wq_ref[...]).astype(BF).astype(F32) * HEAD_DIM ** -0.5
     q_ref[...] = q.astype(BF)
-    t_ref[...] = rows_in[:, pl.ds(pl.multiple_of(head_ref[0] * cols, 128), cols)]
-
-
-def stacked(q, spread, keep, heads):
-    rows, cols = spread.shape[0], q.shape[1]
-    r = lax.broadcasted_iota(jnp.int32, (rows, cols), 0)
-    lane = lax.broadcasted_iota(jnp.int32, (rows, cols), 1)
-    mine = lane // HEAD_DIM == r // keep % heads
-    return mine, jnp.where(mine, nn(spread, q), 0.0).astype(BF)
-
-
-def near_kernel(q_ref, x_hbm, wk_hbm, wv_hbm, spread_ref, out_ref, x_ref, wk_ref, wv_ref, sem):
+    t_ref[...] = rows_in[:, pl.ds(pl.multiple_of(lax.axis_index("head") * cols, 128), cols)]
+
+
+def spreading(keep, heads):
+    shape = (4 * keep * heads, 4 * keep)
+    r = lax.broadcasted_iota(jnp.int32, shape, 0)
+    source = r // (keep * heads) * keep + r % keep
+    return (source == lax.broadcasted_iota(jnp.int32, shape, 1)).astype(F32).astype(BF)
+
+
+def own_lanes(keep, heads):
+    shape = (4 * keep * heads, heads * HEAD_DIM)
+    r = lax.broadcasted_iota(jnp.int32, shape, 0)
+    return lax.broadcasted_iota(jnp.int32, shape, 1) // HEAD_DIM == r // keep % heads
+
+
+def near_kernel(q_hbm, x_hbm, wk_hbm, wv_hbm, out_ref, q_ref, x_ref, wk_ref, wv_ref, sem):
     heads = wk_ref.shape[1] // HEAD_DIM
-    chunk = spread_ref.shape[1]
-    steps = q_ref.shape[0] // chunk
+    steps = x_ref.shape[0] // (4 * PATCHES)
+    chunk = q_ref.shape[0] // steps
     pairs = list(zip(row_blocks(x_hbm, steps), row_blocks(x_ref, steps)))
-    copies = fetch([(wk_hbm, wk_ref), (wv_hbm, wv_ref)] + pairs, sem)
+    copies = fetch([(wk_hbm, wk_ref), (wv_hbm, wv_ref)] + pairs + [(q_hbm, q_ref)], sem)
     size = x_ref.shape[0] // steps
     keep = chunk // 4
     cols = q_ref.shape[1]
     rows = keep * heads
     span = 208
     lane = lax.broadcasted_iota(jnp.int32, (rows, 128), 1)
+    spread = spreading(keep, heads)
+    mine = own_lanes(keep, heads)
+    copies[-1].wait()
     copies[0].wait()
     copies[1].wait()
     for step in range(steps):
@@ -103,7 +111,7 @@
         x = x_ref[step * size : (step + 1) * size, :]
         k = nn(x, wk_ref[...]).astype(BF)
         v = nn(x, wv_ref[...]).astype(BF)
-        _, stack = stacked(q_ref[step * chunk : (step + 1) * chunk, :], spread_ref[...], keep, heads)
+        stack = jnp.where(mine, nn(spread, q_ref[step * chunk : (step + 1) * chunk, :]), 0.0).astype(BF)
         for f in range(4):
             start = f * PATCHES // 16 * 16
             part = slice((step * 4 + f) * rows, (step * 4 + f + 1) * rows)
@@ -115,37 +123,48 @@
             level = m + jnp.log(total)
             high = level.astype(BF).astype(F32)
             middle = (level - high).astype(BF).astype(F32)
-            side = jnp.where(lane == 0, high, jnp.where(lane == 1, middle, level - high - middle))
+            side = jnp.where(lane == 0, high, jnp.where(lane == 1, middle, jnp.where(lane == 2, level - high - middle, 0.0)))
             out_ref[part, :cols] = (nn(e.astype(BF), v[start : start + span]) / total).astype(BF)
             out_ref[part, cols:] = side.astype(BF)
 
 
-def far_kernel(q_ref, near_ref, allow_ref, pick_ref, where_ref, spread_ref, pack_ref, *rest):
-    parts, (out_ref, key, value) = rest[:8], rest[8:]
+def far_kernel(q_hbm, near_hbm, allow_hbm, pack_hbm, _, *rest):
+    parts, (out_ref, far_ref, q_ref, near_ref, allow_ref, pack_ref, sem) = rest[:8], rest[8:]
+    pairs = [(allow_hbm, allow_ref), (q_hbm, q_ref)] + [(part, far_ref.at[i]) for i, part in enumerate(parts)]
+    copies = fetch(pairs + [(near_hbm, near_ref), (pack_hbm, pack_ref)], sem)
     cols = q_ref.shape[1]
     heads = cols // HEAD_DIM
-    chunk = spread_ref.shape[1]
-    each = parts[0].shape[0] * 16
-    count = each * len(parts)
-    for i, ref in enumerate(parts):
-        spot = slice(i * each, (i + 1) * each)
-        for u in range(4):
-            key[u, spot, :] = ref[:, u * 16 : (u + 1) * 16, :cols].reshape(each, cols)
-            value[u, spot, :] = ref[:, u * 16 : (u + 1) * 16, cols:].reshape(each, cols)
-    allowed = allow_ref[...].astype(F32).astype(BF)
-    order = (lax.broadcasted_iota(jnp.int32, (allowed.shape[1], count), 0) == where_ref[...]).astype(F32).astype(BF)
-    wall = jnp.where(nn(allowed, order) > 0.5, 0.0, NEG).astype(BF)
-    rows = spread_ref.shape[0]
+    frames, total_frames = allow_ref.shape
+    groups = frames // 4
+    chunk = q_ref.shape[0] // groups
+    keep = chunk // 4
+    rows = chunk * heads
+    spread = spreading(keep, heads)
+    mine = own_lanes(keep, heads)
+    me = lax.axis_index("tm")
+    n = lax.broadcasted_iota(jnp.int32, (1, total_frames), 1)
+    i, j = (n >> 6) & 3, (n >> 4) & 3
+    z = ((me >> 3) - (i ^ (i >> 1))) & 3
+    y = ((me >> 1) - (j ^ (j >> 1))) & 3
+    where = ((z * 4 + y) * 2 + (me & 1 ^ (n >> 8))) * 16 + (n & 15)
+    order = (lax.broadcasted_iota(jnp.int32, (total_frames, total_frames), 0) == where).astype(F32).astype(BF)
+    copies[0].wait()
+    wall = jnp.where(nn(allow_ref[...].astype(F32).astype(BF), order) > 0.5, 0.0, NEG).astype(BF)
+    for copy in copies[1:-1]:
+        copy.wait()
+    frame = lax.broadcasted_iota(jnp.int32, (rows, frames), 0) // (keep * heads)
+    column = lax.broadcasted_iota(jnp.int32, (rows, frames), 1)
     outs = []
-    for g in range(q_ref.shape[0] // chunk):
+    for g in range(groups):
         part = slice(g * rows, (g + 1) * rows)
-        mine, q = stacked(q_ref[g * chunk : (g + 1) * chunk, :], spread_ref[...], chunk // 4, heads)
-        block = nn(pick_ref[part, :], wall)
-        level = sum(near_ref[part, cols + i : cols + i + 1].astype(F32) for i in range(3))
+        q = jnp.where(mine, nn(spread, q_ref[g * chunk : (g + 1) * chunk, :]), 0.0).astype(BF)
+        block = nn((column == frame + 4 * g).astype(F32).astype(BF), wall)
+        level = jnp.sum(near_ref[part, cols:].astype(F32), axis=1, keepdims=True)
         top = level
         scores = []
         for u in range(4):
-            s = nt(q, key[u]) + block
+            key = far_ref[:, :, u * 16 : (u + 1) * 16, :cols].reshape(total_frames, cols)
+            s = nt(q, key) + block
             top = jnp.maximum(top, jnp.max(s, axis=1, keepdims=True))
             scores.append(s)
         total = jnp.exp(level - top)
@@ -153,25 +172,31 @@
         for u in range(4):
             e = jnp.exp(scores[u] - top)
             total = total + jnp.sum(e, axis=1, keepdims=True)
-            acc = acc + nn(e.astype(BF), value[u])
+            value = far_ref[:, :, u * 16 : (u + 1) * 16, cols:].reshape(total_frames, cols)
+            acc = acc + nn(e.astype(BF), value)
         done = jnp.where(mine, acc / total, 0.0).astype(BF)
-        outs.append(lax.dot_general(spread_ref[...], done, (((0,), (0,)), ((), ())), preferred_element_type=F32).astype(BF))
+        outs.append(lax.dot_general(spread, done, (((0,), (0,)), ((), ())), preferred_element_type=F32).astype(BF))
     out = jnp.concatenate(outs, axis=0)
+    copies[-1].wait()
     out_ref[...] = nn(pack_ref[...], out).astype(BF).reshape(out_ref.shape)
 
 
-def final_kernel(at_ref, *rest):
-    att, side, own_half, other_half, (target_ref, loss_ref, raw) = rest[:4], rest[4:8], rest[8:12], rest[12:16], rest[16:]
-    head, core = at_ref[0], at_ref[1]
-    rows, cols = att[0].shape
+def final_kernel(*refs):
+    sources, (target_ref, loss_ref, att, side, wo, raw, sem) = refs[:16], refs[16:]
+    head, core = lax.axis_index("head"), lax.axis_index("tm") & 1
+    rows, cols = att.shape[1:]
     half = cols // 2
     width = raw.shape[1]
     here = pl.ds(pl.multiple_of(core * half, 128), half)
     there = pl.ds(pl.multiple_of((1 - core) * half, 128), half)
-    raw[...] = sum(nn(att[i][:, here], own_half[i][...]) + nn(att[i][:, there], other_half[i][...]) for i in range(4))
+    targets = [att.at[i] for i in range(4)] + [side.at[i] for i in range(4)]
+    targets += [wo.at[i, here] for i in range(4)] + [wo.at[i, there] for i in range(4)]
+    for copy in fetch(list(zip(sources, targets)), sem):
+        copy.wait()
+    raw[...] = sum(nn(att[i], wo[i]) for i in range(4))
     spots = [pl.ds(pl.multiple_of(lax.rem(head + 4 - d, 4) * cols, 128), cols) for d in DISTANCES]
     for i in range(4):
-        raw[:, spots[i]] += side[i][:, :cols].astype(F32)
+        raw[:, spots[i]] += side[i, :, :cols].astype(F32)
     full = raw[...]
     mean = jnp.sum(full, axis=1, keepdims=True) / width
     var = jnp.sum(full * full, axis=1, keepdims=True) / width - mean * mean
@@ -181,7 +206,7 @@
         normed = (raw[:, spots[i]] - mean) * scale
         if i == 0:
             target_ref[...] = normed.astype(BF)
-        gap = side[i][:, cols:].astype(F32) - normed
+        gap = side[i, :, cols:].astype(F32) - normed
         loss = loss + jnp.sum(gap * gap, axis=1, keepdims=True)
     loss_ref[...] = jnp.broadcast_to(loss / width, (rows, 128)).T[:1]
 
@@ -200,8 +225,8 @@
 
 DISTANCES = (0, 1, 3, 2)
 PLACES = [(z, y, c) for z in range(4) for y in range(4) for c in range(2)]
-SMEM = pl.BlockSpec(memory_space=pltpu.SMEM)
-HBM = pl.BlockSpec(memory_space=pl.ANY)
+FREE = pl.BlockSpec(memory_space=pl.ANY)
+HBM = pl.BlockSpec(memory_space=pltpu.HBM)
 
 
 def along_y(d):
@@ -227,8 +252,7 @@
     steps = frames // 4
     block = 4 * PATCHES
     chunk = 4 * keep
-    my_z, my_y, my_core = me // 8, me // 2 % 4, me % 2
-    at = jnp.stack([head, my_core]).astype(jnp.int32)
+    my_core = me % 2
 
     r = np.arange(block)
     p = r % PATCHES
@@ -241,7 +265,7 @@
 
     mine, q, tok = pl.pallas_call(
         gather_kernel,
-        in_specs=[SMEM] + [HBM] * 4 + whole(3),
+        in_specs=[HBM] * 4 + whole(3),
         out_specs=whole(3),
         out_shape=[
             jax.ShapeDtypeStruct((4 * frames, 2 * cols), BF),
@@ -251,21 +275,14 @@
         scratch_shapes=[pltpu.VMEM((frames * PATCHES, width), BF)]
         + [pltpu.VMEM((width, cols), BF)] * 3
         + [pltpu.VMEM((4 * frames, width), F32), pltpu.VMEM((own, width), BF), pltpu.SemaphoreType.DMA((steps + 3,))],
-        compiler_params=params(56),
+        compiler_params=params(60),
         cost_estimate=pl.CostEstimate(flops=2 * 10**9, bytes_accessed=10**7, transcendentals=0),
         name="gather",
-    )(at, tokens, w_query, w_key, w_value, jnp.asarray(pool, BF), visible, jnp.asarray(order, BF))
+    )(tokens, w_query, w_key, w_value, jnp.asarray(pool, BF), visible, jnp.asarray(order, BF))
 
     plane = jnp.stack([mine] + [lax.ppermute(mine, "tm", along_y(d)) for d in DISTANCES[1:]])
     plane, q, tok = lax.optimization_barrier((plane, q, tok))
     parts = [plane] + [lax.ppermute(plane, "tm", along_z(d)) for d in DISTANCES[1:]]
-    gap = jnp.asarray(DISTANCES, jnp.int32)
-    core_at = jnp.stack([my_core, 1 - my_core])[:, None, None, None]
-    z_at = ((my_z - gap) % 4)[None, :, None, None]
-    y_at = ((my_y - gap) % 4)[None, None, :, None]
-    where = ((z_at * 4 + y_at) * 2 + core_at) * frames + jnp.arange(frames, dtype=jnp.int32)
-    where = where.reshape(1, n_peers * frames)
-
     owner_all = slot // own
     my_slots = lax.dynamic_slice_in_dim(slot, me * own, own)
     my_owner = my_slots // own
@@ -289,39 +306,38 @@
     tok_got = deliver(jnp.dot(pack, tok, preferred_element_type=F32).astype(BF).reshape(n_peers, CAP, cols))
 
     heads = cols // HEAD_DIM
-    n = np.arange(own * heads)
-    n_frame, n_keep = n // (keep * heads), n % keep
-    spread = jnp.asarray(n_frame[: chunk * heads, None] * keep + n_keep[: chunk * heads, None] == np.arange(chunk), BF)
-    pick = jnp.asarray(n_frame[:, None] == np.arange(frames), BF)
     near = pl.pallas_call(
         near_kernel,
-        in_specs=whole(1) + [HBM] * 3 + whole(1),
+        in_specs=[HBM] * 4,
         out_specs=pl.BlockSpec(memory_space=pltpu.VMEM),
         out_shape=jax.ShapeDtypeStruct((own * heads, cols + 128), BF),
-        scratch_shapes=[pltpu.VMEM((frames * PATCHES, width), BF)]
+        scratch_shapes=[pltpu.VMEM((own, cols), BF), pltpu.VMEM((frames * PATCHES, width), BF)]
         + [pltpu.VMEM((width, cols), BF)] * 2
-        + [pltpu.SemaphoreType.DMA((steps + 2,))],
-        compiler_params=params(40),
+        + [pltpu.SemaphoreType.DMA((steps + 3,))],
+        compiler_params=params(60),
         cost_estimate=pl.CostEstimate(flops=5 * 10**9, bytes_accessed=10**7, transcendentals=10**6),
         name="near",
-    )(q, tokens, w_key, w_value, spread)
-
-    *parts, q, near, tok_got = lax.optimization_barrier((*parts, q, near, tok_got))
-    parts = parts + [lax.ppermute(part, "tm", OTHER_CORE) for part in parts]
+    )(q, tokens, w_key, w_value)
+
+    plane, near = lax.optimization_barrier((plane, near))
+    parts = parts + [lax.ppermute(part, "tm", OTHER_CORE) for part in [plane] + parts[1:]]
     packed = pl.pallas_call(
         far_kernel,
-        in_specs=whole(15),
+        in_specs=[HBM] * 13,
         out_specs=pl.BlockSpec(memory_space=pltpu.VMEM),
         out_shape=jax.ShapeDtypeStruct((n_peers, CAP, cols), BF),
         scratch_shapes=[
-            pltpu.VMEM((4, n_peers * frames, cols), BF),
-            pltpu.VMEM((4, n_peers * frames, cols), BF),
+            pltpu.VMEM((8, 4, 4 * frames, 2 * cols), BF),
+            pltpu.VMEM((own, cols), BF),
+            pltpu.VMEM((own * heads, cols + 128), BF),
+            pltpu.VMEM(pattern.shape, jnp.int32),
+            pltpu.VMEM(pack.shape, BF),
+            pltpu.SemaphoreType.DMA((12,)),
         ],
-        compiler_params=params(40),
+        compiler_params=params(60),
         cost_estimate=pl.CostEstimate(flops=4 * 10**9, bytes_accessed=4 * 10**6, transcendentals=3 * 10**6),
         name="far",
-    )(q, near, pattern, pick, where, spread, pack, *parts)
-    packed, tok_got = lax.optimization_barrier((packed, tok_got))
+    )(q, near, pattern, pack, tok_got, *parts)
     tok_own = arrange(tok_got)
     att = arrange(deliver(packed))
 
@@ -338,14 +354,20 @@
 
     target, row_loss = pl.pallas_call(
         final_kernel,
-        in_specs=[SMEM] + whole(16),
+        in_specs=[HBM] * 16,
         out_specs=whole(2),
         out_shape=[jax.ShapeDtypeStruct((own, cols), BF), jax.ShapeDtypeStruct((1, own), F32)],
-        scratch_shapes=[pltpu.VMEM((own, width), F32)],
-        compiler_params=params(40),
+        scratch_shapes=[
+            pltpu.VMEM((4, own, cols), BF),
+            pltpu.VMEM((4, own, 2 * cols), BF),
+            pltpu.VMEM((4, cols, width), BF),
+            pltpu.VMEM((own, width), F32),
+            pltpu.SemaphoreType.DMA((16,)),
+        ],
+        compiler_params=params(16),
         cost_estimate=pl.CostEstimate(flops=10**9, bytes_accessed=4 * 10**6, transcendentals=0),
         name="final",
-    )(at, *over_heads(att), *side, *halves, *other)
+    )(*over_heads(att), *side, *halves, *other)
     return target, row_loss.reshape(own)
 
 

time: 118 us -> 102 us (0.86); the launches traced: 116 us -> 101 us
  local copies, waits for them, and re-layouts: 16.6 us -> 1.83 us
  Pallas kernels: 29.3 us -> 34.3 us
  waiting for transfers between devices: 16.3 us -> 14.2 us
  other arithmetic: 5.6 us -> 4.09 us
    unnamed x54 -> x22, local copies, waits for them, and re-layouts: 16.3 us -> 1.57 us
    pallas_call x4, Pallas kernels: 29.3 us -> 34.3 us  [the longest x1 11.8 us: body(): pl.pallas_call(near_kernel, in_specs=[HBM] * 4, out_specs=pl.BlockSpec(me...]
    ppermute x3, waiting for transfers between devices: 2.19 us -> 0.01 us  [body(): lax.ppermute(plane, 'tm', along_z(d))]
    all_to_all x2, starting transfers between devices: 13.7 us -> 12.5 us  [deliver(): return lax.all_to_all(packed, 'tm', 0, 0, tiled=True)]
  transfers between devices with their start and end apart: 25 -> 25, of which waited for: 6 -> 5; matrix products, arithmetic and copies ran while one was open for 9% -> 8% of each run, Pallas kernels for 16% -> 23%
where the time goes in v5:
time: 102 us; the launch traced here: 101 us
  starting transfers between devices  40.8 us (40%)
  Pallas kernels  34.3 us (34%)
  waiting for transfers between devices  14.2 us (14%)
  matrix products  4.74 us (5%)
  other arithmetic  4.09 us (4%)
  local copies, waits for them, and re-layouts  1.83 us (2%)
    ppermute x9, starting transfers between devices, over_heads(): return [x] + [lax.ppermute(x, 'head', to(d)) for d in DISTANCES[1:]]  14.8 us
    all_to_all x2, starting transfers between devices, deliver(): return lax.all_to_all(packed, 'tm', 0, 0, tiled=True)  12.5 us
    pallas_call x1, Pallas kernels, body(): pl.pallas_call(near_kernel, in_specs=[HBM] * 4, out_specs=pl.BlockSpec(me...  11.8 us
    pallas_call x1, Pallas kernels, body(): pl.pallas_call(far_kernel, in_specs=[HBM] * 13, out_specs=pl.BlockSpec(me...  11.2 us
    ppermute x9, waiting for transfers between devices, over_heads(): return [x] + [lax.ppermute(x, 'head', to(d)) for d in DISTANCES[1:]]  7.1 us
    pallas_call x1, Pallas kernels, body(): pl.pallas_call(gather_kernel, in_specs=[HBM] * 4 + whole(3), out_specs=wh...  6.38 us
    all_to_all x2, waiting for transfers between devices, deliver(): return lax.all_to_all(packed, 'tm', 0, 0, tiled=True)  6.32 us
    ppermute x3, starting transfers between devices, body(): lax.ppermute(plane, 'tm', along_z(d))  6.05 us
  transfers between devices with their start and end apart: 25, of which 5 were waited for; matrix products, arithmetic and copies ran while one was open for 8% of the time, Pallas kernels for 23%

profile of v5, /device:TPU:0, one launch (start us, length us, event | category | flops | bytes accessed | tf_op | source)
XLA Modules:
  0.0 100.9 jit_solution(11588717648694354744)
XLA Ops:
  0.7 6.4 %gather.1 = (bf16[64,512]{1,0:T(8,128)(2,1)}, bf16[320,256]{1,0:T(8,128)(2,1)}, bf16[320,256]{1,0:T(8,128)(2,1)}) custom-call(bf16[3136,1024]{1,0:T(8,128)(2,1)} %x_hbm.3, bf16[1024,256]{1,0:T(8,128)(2,1)} %wq_hbm.1, bf16[1024,256]{1,0:T(8,128)(2,1)} %wk_hbm.3, bf16[1024,256]{1,0:T(8,128)(2,1)} %wv_hbm.3, bf16[16,784]{1,0:T(8,128)(2,1)} %constant.62.clone.pool_ref, ...), custom_call_target="tpu_custom_call" | custom-call | flops 2000000000 | bytes 10000000 | tf_op jit(solution)/shard_map/gather/pallas_call | solution.py:266
  7.1 1.7 %collective-permute-start = (bf16[64,512]{1,0:T(8,128)(2,1)}, bf16[64,512]{1,0:T(8,128)(2,1)S(1)}, u32[]{:S(2)}, u32[]{:S(2)}) collective-permute-start(bf16[64,512]{1,0:T(8,128)(2,1)} %get-tuple-element.12), channel_id=1, source_target_pairs={{0,8},{4,12},{8,16},{12,20},{16,24},{20,28},{24,0},{28,4},{32,40},... | collective-permute-start | bytes 196616 | tf_op jit(solution)/shard_map/ppermute | solution.py:283
  8.8 1.6 %collective-permute-start.1 = (bf16[64,512]{1,0:T(8,128)(2,1)}, bf16[64,512]{1,0:T(8,128)(2,1)S(1)}, u32[]{:S(2)}, u32[]{:S(2)}) collective-permute-start(bf16[64,512]{1,0:T(8,128)(2,1)} %get-tuple-element.12), channel_id=1, source_target_pairs={{0,24},{4,28},{8,0},{12,4},{16,8},{20,12},{24,16},{28,20},{32,56},... | collective-permute-start | bytes 196616 | tf_op jit(solution)/shard_map/ppermute | solution.py:283
  10.4 2.1 %collective-permute-start.2 = (bf16[64,512]{1,0:T(8,128)(2,1)}, bf16[64,512]{1,0:T(8,128)(2,1)S(1)}, u32[]{:S(2)}, u32[]{:S(2)}) collective-permute-start(bf16[64,512]{1,0:T(8,128)(2,1)} %get-tuple-element.12), channel_id=1, source_target_pairs={{0,16},{4,20},{8,24},{12,28},{16,0},{20,4},{24,8},{28,12},{32,48},... | collective-permute-start | bytes 196616 | tf_op jit(solution)/shard_map/ppermute | solution.py:283
  12.5 1.6 %collective-permute-start.16 = (bf16[128,1024]{1,0:T(8,128)(2,1)S(1)}, bf16[128,1024]{1,0:T(8,128)(2,1)S(1)}, u32[]{:S(2)}, u32[]{:S(2)}) collective-permute-start(bf16[128,1024]{1,0:T(8,128)(2,1)S(1)} %constant_dynamic-slice_fusion.refs_8_), channel_id=1, source_target_pairs={{0,1},{1,2},{2,3},{3,0},{4,5},{5,6},{6,7},{7,4},{8,9},{9,10},{10,1... | collective-permute-start | bytes 786440 | tf_op jit(solution)/shard_map/ppermute | solution.py:348
  14.5 1.5 %fusion.pack_hbm = bf16[1536,320]{1,0:T(8,128)(2,1)} fusion(s32[320]{0:T(512)S(1)} %multiply_add_fusion), kind=kLoop, calls=%fused_computation.2 | loop fusion | flops 983040 | bytes 984320 | tf_op jit(solution)/shard_map/convert_element_type | solution.py:292
  17.2 2.1 %collective-permute-start.3 = (bf16[4,64,512]{2,1,0:T(8,128)(2,1)S(1)}, bf16[4,64,512]{2,1,0:T(8,128)(2,1)S(1)}, u32[]{:S(2)}, u32[]{:S(2)}) collective-permute-start(bf16[4,64,512]{2,1,0:T(8,128)(2,1)S(1)} %pad_maximum_fusion.1.rest_0_), channel_id=1, source_target_pairs={{0,32},{4,36},{8,40},{12,44},{16,48},{20,52},{24,56},{28,60},{32,6... | collective-permute-start | bytes 786440 | tf_op jit(solution)/shard_map/ppermute | solution.py:285
  19.3 2.2 %collective-permute-start.4 = (bf16[4,64,512]{2,1,0:T(8,128)(2,1)S(1)}, bf16[4,64,512]{2,1,0:T(8,128)(2,1)S(1)}, u32[]{:S(2)}, u32[]{:S(2)}) collective-permute-start(bf16[4,64,512]{2,1,0:T(8,128)(2,1)S(1)} %pad_maximum_fusion.1.rest_0_), channel_id=1, source_target_pairs={{0,96},{4,100},{8,104},{12,108},{16,112},{20,116},{24,120},{28,124... | collective-permute-start | bytes 786440 | tf_op jit(solution)/shard_map/ppermute | solution.py:285
  21.5 1.8 %collective-permute-start.5 = (bf16[4,64,512]{2,1,0:T(8,128)(2,1)S(1)}, bf16[4,64,512]{2,1,0:T(8,128)(2,1)}, u32[]{:S(2)}, u32[]{:S(2)}) collective-permute-start(bf16[4,64,512]{2,1,0:T(8,128)(2,1)S(1)} %pad_maximum_fusion.1.rest_0_), channel_id=1, source_target_pairs={{0,64},{4,68},{8,72},{12,76},{16,80},{20,84},{24,88},{28,92},{32,9... | collective-permute-start | bytes 786440 | tf_op jit(solution)/shard_map/ppermute | solution.py:285
  24.8 4.8 %all-to-all-start = ((bf16[32,48,256]{2,1,0:T(8,128)(2,1)}), bf16[32,48,256]{2,1,0:T(8,128)(2,1)S(1)}, u32[]{:S(2)}, u32[]{:S(2)}) async-start(bf16[32,48,256]{2,1,0:T(8,128)(2,1)} %bitcast.4), calls=%async_computation | async-start | bytes 1572864 | tf_op jit(solution)/shard_map/all_to_all | solution.py:301
  29.6 11.8 %near.1.near_hbm = bf16[1280,384]{1,0:T(8,128)(2,1)} custom-call(bf16[320,256]{1,0:T(8,128)(2,1)} %get-tuple-element.15.q_hbm, bf16[3136,1024]{1,0:T(8,128)(2,1)} %x_hbm.3, bf16[1024,256]{1,0:T(8,128)(2,1)} %wk_hbm.3, bf16[1024,256]{1,0:T(8,128)(2,1)} %wv_hbm.3), custom_call_target="tpu_custom_call" | custom-call | flops 5000000000 | bytes 10000000 | tf_op jit(solution)/shard_map/near/pallas_call | solution.py:309
  43.1 2.8 %collective-permute-start.17 = (bf16[128,1024]{1,0:T(8,128)(2,1)S(1)}, bf16[128,1024]{1,0:T(8,128)(2,1)S(1)}, u32[]{:S(2)}, u32[]{:S(2)}) collective-permute-start(bf16[128,1024]{1,0:T(8,128)(2,1)S(1)} %constant_dynamic-slice_fusion.refs_8_), channel_id=1, source_target_pairs={{0,3},{1,0},{2,1},{3,2},{4,7},{5,4},{6,5},{7,6},{8,11},{9,8},{10,9... | collective-permute-start | bytes 786440 | tf_op jit(solution)/shard_map/ppermute | solution.py:348
  48.3 11.2 %far.1 = bf16[32,48,256]{2,1,0:T(8,128)(2,1)} custom-call(bf16[320,256]{1,0:T(8,128)(2,1)} %get-tuple-element.15.q_hbm, bf16[1280,384]{1,0:T(8,128)(2,1)} %near.1.near_hbm, s32[16,512]{1,0:T(8,128)} %allow_hbm.1, bf16[1536,320]{1,0:T(8,128)(2,1)} %fusion.pack_hbm, bf16[32,48,256]{2,1,0:T(8,128)(2,1)} %copy-done.1, bf16[4,64,512]{2,1,0:T(8,128)(2,1)} %copy-done.2, ...), custom_call_target="tpu_custom_call" | custom-call | flops 4000000000 | bytes 4000000 | tf_op jit(solution)/shard_map/far/pallas_call | solution.py:324
  59.5 7.6 %all-to-all-start.1 = ((bf16[32,48,256]{2,1,0:T(8,128)(2,1)}), bf16[32,48,256]{2,1,0:T(8,128)(2,1)}, u32[]{:S(2)}, u32[]{:S(2)}) async-start(bf16[32,48,256]{2,1,0:T(8,128)(2,1)} %far.1), calls=%async_computation.1 | async-start | bytes 1572864 | tf_op jit(solution)/shard_map/all_to_all | solution.py:301
  68.4 1.6 %fusion.5 = bf16[320,256]{1,0:T(8,128)(2,1)S(1)} fusion(bf16[1536,256]{1,0:T(8,128)(2,1)} %bitcast.12, s32[1536]{0:T(1024)S(1)} %eq.70), kind=kOutput, calls=%fused_computation.10 | convolution fusion | flops 252231680 | bytes 956416 | tf_op jit(solution)/shard_map/dot_general | solution.py:304
  71.5 2.3 %collective-permute-start.14 = (bf16[320,512]{1,0:T(8,128)(2,1)S(1)}, bf16[320,512]{1,0:T(8,128)(2,1)S(1)}, u32[]{:S(2)}, u32[]{:S(2)}) collective-permute-start(bf16[320,512]{1,0:T(8,128)(2,1)S(1)} %pad_maximum_fusion.refs_4_), channel_id=1, source_target_pairs={{0,3},{1,0},{2,1},{3,2},{4,7},{5,4},{6,5},{7,6},{8,11},{9,8},{10,9... | collective-permute-start | bytes 983048 | tf_op jit(solution)/shard_map/ppermute | solution.py:348
  73.9 1.5 %collective-permute-start.15 = (bf16[320,512]{1,0:T(8,128)(2,1)S(1)}, bf16[320,512]{1,0:T(8,128)(2,1)S(1)}, u32[]{:S(2)}, u32[]{:S(2)}) collective-permute-start(bf16[320,512]{1,0:T(8,128)(2,1)S(1)} %pad_maximum_fusion.refs_4_), channel_id=1, source_target_pairs={{0,2},{1,3},{2,0},{3,1},{4,6},{5,7},{6,4},{7,5},{8,10},{9,11},{10,... | collective-permute-start | bytes 983048 | tf_op jit(solution)/shard_map/ppermute | solution.py:348
  75.4 6.3 %all-to-all-done.1 = bf16[32,48,256]{2,1,0:T(8,128)(2,1)} async-done(((bf16[32,48,256]{2,1,0:T(8,128)(2,1)}), bf16[32,48,256]{2,1,0:T(8,128)(2,1)}, u32[]{:S(2)}, u32[]{:S(2)}) %all-to-all-start.1) | async-done | bytes 786464 | tf_op jit(solution)/shard_map/all_to_all | solution.py:301
  81.7 1.6 %fusion.4.refs_0_ = bf16[320,256]{1,0:T(8,128)(2,1)S(1)} fusion(bf16[1536,256]{1,0:T(8,128)(2,1)} %bitcast.5, s32[1536]{0:T(1024)S(1)} %eq.70), kind=kOutput, calls=%fused_computation.9 | convolution fusion | flops 252231680 | bytes 956416 | tf_op jit(solution)/shard_map/dot_general | solution.py:304
  84.3 2.3 %collective-permute-start.11 = (bf16[320,256]{1,0:T(8,128)(2,1)S(1)}, bf16[320,256]{1,0:T(8,128)(2,1)S(1)}, u32[]{:S(2)}, u32[]{:S(2)}) collective-permute-start(bf16[320,256]{1,0:T(8,128)(2,1)S(1)} %fusion.4.refs_0_), channel_id=1, source_target_pairs={{0,3},{1,0},{2,1},{3,2},{4,7},{5,4},{6,5},{7,6},{8,11},{9,8},{10,9... | collective-permute-start | bytes 491528 | tf_op jit(solution)/shard_map/ppermute | solution.py:348
  86.6 1.6 %collective-permute-done.13.refs_5_ = bf16[320,512]{1,0:T(8,128)(2,1)S(1)} collective-permute-done((bf16[320,512]{1,0:T(8,128)(2,1)S(1)}, bf16[320,512]{1,0:T(8,128)(2,1)S(1)}, u32[]{:S(2)}, u32[]{:S(2)}) %collective-permute-start.13) | collective-permute-done | bytes 327712 | tf_op jit(solution)/shard_map/ppermute | solution.py:348
  88.2 1.6 %collective-permute-start.12 = (bf16[320,256]{1,0:T(8,128)(2,1)S(1)}, bf16[320,256]{1,0:T(8,128)(2,1)S(1)}, u32[]{:S(2)}, u32[]{:S(2)}) collective-permute-start(bf16[320,256]{1,0:T(8,128)(2,1)S(1)} %fusion.4.refs_0_), channel_id=1, source_target_pairs={{0,2},{1,3},{2,0},{3,1},{4,6},{5,7},{6,4},{7,5},{8,10},{9,11},{10,... | collective-permute-start | bytes 491528 | tf_op jit(solution)/shard_map/ppermute | solution.py:348
  89.8 5.5 %collective-permute-done.10.refs_1_ = bf16[320,256]{1,0:T(8,128)(2,1)S(1)} collective-permute-done((bf16[320,256]{1,0:T(8,128)(2,1)S(1)}, bf16[320,256]{1,0:T(8,128)(2,1)S(1)}, u32[]{:S(2)}, u32[]{:S(2)}) %collective-permute-start.10) | collective-permute-done | bytes 163872 | tf_op jit(solution)/shard_map/ppermute | solution.py:348
  95.3 5.0 %final.1 = (bf16[320,256]{1,0:T(8,128)(2,1)}, f32[1,320]{1,0:T(1,128)S(1)}) custom-call(bf16[320,256]{1,0:T(8,128)(2,1)S(1)} %fusion.4.refs_0_, bf16[320,256]{1,0:T(8,128)(2,1)S(1)} %collective-permute-done.10.refs_1_, bf16[320,256]{1,0:T(8,128)(2,1)S(1)} %collective-permute-done.11.refs_2_, bf16[320,256]{1,0:T(8,128)(2,1)S(1)} %collective-permute-done.12.refs_3_, ...), custom_call_target="tpu_custom_call" | custom-call | flops 1000000000 | bytes 4000000 | tf_op jit(solution)/shard_map/final/pallas_call | solution.py:355
  (70 shorter events, 11.7 us)
Async XLA Ops:
  7.1 9.0 %collective-permute-start = (bf16[64,512]{1,0:T(8,128)(2,1)}, bf16[64,512]{1,0:T(8,128)(2,1)S(1)}, u32[]{:S(2)}, u32[]{:S(2)}) collective-permute-start(bf16[64,512]{1,0:T(8,128)(2,1)} %get-tuple-element.12), channel_id=1, source_target_pairs={{0,8},{4,12},{8,16},{12,20},{16,24},{20,28},{24,0},{28,4},{32,40},... | collective-permute-start | bytes 196616 | tf_op jit(solution)/shard_map/ppermute | solution.py:283
  8.8 7.3 %collective-permute-start.1 = (bf16[64,512]{1,0:T(8,128)(2,1)}, bf16[64,512]{1,0:T(8,128)(2,1)S(1)}, u32[]{:S(2)}, u32[]{:S(2)}) collective-permute-start(bf16[64,512]{1,0:T(8,128)(2,1)} %get-tuple-element.12), channel_id=1, source_target_pairs={{0,24},{4,28},{8,0},{12,4},{16,8},{20,12},{24,16},{28,20},{32,56},... | collective-permute-start | bytes 196616 | tf_op jit(solution)/shard_map/ppermute | solution.py:283
  10.4 6.0 %collective-permute-start.2 = (bf16[64,512]{1,0:T(8,128)(2,1)}, bf16[64,512]{1,0:T(8,128)(2,1)S(1)}, u32[]{:S(2)}, u32[]{:S(2)}) collective-permute-start(bf16[64,512]{1,0:T(8,128)(2,1)} %get-tuple-element.12), channel_id=1, source_target_pairs={{0,16},{4,20},{8,24},{12,28},{16,0},{20,4},{24,8},{28,12},{32,48},... | collective-permute-start | bytes 196616 | tf_op jit(solution)/shard_map/ppermute | solution.py:283
  12.5 55.7 %collective-permute-start.16 = (bf16[128,1024]{1,0:T(8,128)(2,1)S(1)}, bf16[128,1024]{1,0:T(8,128)(2,1)S(1)}, u32[]{:S(2)}, u32[]{:S(2)}) collective-permute-start(bf16[128,1024]{1,0:T(8,128)(2,1)S(1)} %constant_dynamic-slice_fusion.refs_8_), channel_id=1, source_target_pairs={{0,1},{1,2},{2,3},{3,0},{4,5},{5,6},{6,7},{7,4},{8,9},{9,10},{10,1... | collective-permute-start | bytes 786440 | tf_op jit(solution)/shard_map/ppermute | solution.py:348
  17.2 24.5 %collective-permute-start.3 = (bf16[4,64,512]{2,1,0:T(8,128)(2,1)S(1)}, bf16[4,64,512]{2,1,0:T(8,128)(2,1)S(1)}, u32[]{:S(2)}, u32[]{:S(2)}) collective-permute-start(bf16[4,64,512]{2,1,0:T(8,128)(2,1)S(1)} %pad_maximum_fusion.1.rest_0_), channel_id=1, source_target_pairs={{0,32},{4,36},{8,40},{12,44},{16,48},{20,52},{24,56},{28,60},{32,6... | collective-permute-start | bytes 786440 | tf_op jit(solution)/shard_map/ppermute | solution.py:285
  19.3 22.7 %collective-permute-start.4 = (bf16[4,64,512]{2,1,0:T(8,128)(2,1)S(1)}, bf16[4,64,512]{2,1,0:T(8,128)(2,1)S(1)}, u32[]{:S(2)}, u32[]{:S(2)}) collective-permute-start(bf16[4,64,512]{2,1,0:T(8,128)(2,1)S(1)} %pad_maximum_fusion.1.rest_0_), channel_id=1, source_target_pairs={{0,96},{4,100},{8,104},{12,108},{16,112},{20,116},{24,120},{28,124... | collective-permute-start | bytes 786440 | tf_op jit(solution)/shard_map/ppermute | solution.py:285
  21.5 20.8 %collective-permute-start.5 = (bf16[4,64,512]{2,1,0:T(8,128)(2,1)S(1)}, bf16[4,64,512]{2,1,0:T(8,128)(2,1)}, u32[]{:S(2)}, u32[]{:S(2)}) collective-permute-start(bf16[4,64,512]{2,1,0:T(8,128)(2,1)S(1)} %pad_maximum_fusion.1.rest_0_), channel_id=1, source_target_pairs={{0,64},{4,68},{8,72},{12,76},{16,80},{20,84},{24,88},{28,92},{32,9... | collective-permute-start | bytes 786440 | tf_op jit(solution)/shard_map/ppermute | solution.py:285
  24.8 22.6 %all-to-all-start = ((bf16[32,48,256]{2,1,0:T(8,128)(2,1)}), bf16[32,48,256]{2,1,0:T(8,128)(2,1)S(1)}, u32[]{:S(2)}, u32[]{:S(2)}) async-start(bf16[32,48,256]{2,1,0:T(8,128)(2,1)} %bitcast.4), calls=%async_computation | async-start | bytes 1572864 | tf_op jit(solution)/shard_map/all_to_all | solution.py:301
  41.7 4.1 %collective-permute-start.7 = (bf16[4,64,512]{2,1,0:T(8,128)(2,1)S(1)}, bf16[4,64,512]{2,1,0:T(8,128)(2,1)}, u32[]{:S(2)}, u32[]{:S(2)}) collective-permute-start(bf16[4,64,512]{2,1,0:T(8,128)(2,1)S(1)} %collective-permute-done.3.rest_1_), channel_id=1, source_target_pairs={{0,4},{4,0},{8,12},{12,8},{16,20},{20,16},{24,28},{28,24},{32,36},... | collective-permute-start | bytes 786440 | tf_op jit(solution)/shard_map/ppermute | solution.py:323
  42.0 4.7 %collective-permute-start.8 = (bf16[4,64,512]{2,1,0:T(8,128)(2,1)S(1)}, bf16[4,64,512]{2,1,0:T(8,128)(2,1)S(1)}, u32[]{:S(2)}, u32[]{:S(2)}) collective-permute-start(bf16[4,64,512]{2,1,0:T(8,128)(2,1)S(1)} %collective-permute-done.4.rest_2_), channel_id=1, source_target_pairs={{0,4},{4,0},{8,12},{12,8},{16,20},{20,16},{24,28},{28,24},{32,36},... | collective-permute-start | bytes 786440 | tf_op jit(solution)/shard_map/ppermute | solution.py:323
  42.3 5.1 %collective-permute-start.9 = (bf16[4,64,512]{2,1,0:T(8,128)(2,1)}, bf16[4,64,512]{2,1,0:T(8,128)(2,1)}, u32[]{:S(2)}, u32[]{:S(2)}) collective-permute-start(bf16[4,64,512]{2,1,0:T(8,128)(2,1)} %collective-permute-done.5.rest_3_), channel_id=1, source_target_pairs={{0,4},{4,0},{8,12},{12,8},{16,20},{20,16},{24,28},{28,24},{32,36},... | collective-permute-start | bytes 786440 | tf_op jit(solution)/shard_map/ppermute | solution.py:323
  43.1 27.9 %collective-permute-start.17 = (bf16[128,1024]{1,0:T(8,128)(2,1)S(1)}, bf16[128,1024]{1,0:T(8,128)(2,1)S(1)}, u32[]{:S(2)}, u32[]{:S(2)}) collective-permute-start(bf16[128,1024]{1,0:T(8,128)(2,1)S(1)} %constant_dynamic-slice_fusion.refs_8_), channel_id=1, source_target_pairs={{0,3},{1,0},{2,1},{3,2},{4,7},{5,4},{6,5},{7,6},{8,11},{9,8},{10,9... | collective-permute-start | bytes 786440 | tf_op jit(solution)/shard_map/ppermute | solution.py:348
  45.9 25.1 %collective-permute-start.18 = (bf16[128,1024]{1,0:T(8,128)(2,1)S(1)}, bf16[128,1024]{1,0:T(8,128)(2,1)S(1)}, u32[]{:S(2)}, u32[]{:S(2)}) collective-permute-start(bf16[128,1024]{1,0:T(8,128)(2,1)S(1)} %constant_dynamic-slice_fusion.refs_8_), channel_id=1, source_target_pairs={{0,2},{1,3},{2,0},{3,1},{4,6},{5,7},{6,4},{7,5},{8,10},{9,11},{10,... | collective-permute-start | bytes 786440 | tf_op jit(solution)/shard_map/ppermute | solution.py:348
  46.7 24.8 %collective-permute-start.19 = (bf16[128,1024]{1,0:T(8,128)(2,1)S(1)}, bf16[128,1024]{1,0:T(8,128)(2,1)S(1)}, u32[]{:S(2)}, u32[]{:S(2)}) collective-permute-start(bf16[128,1024]{1,0:T(8,128)(2,1)S(1)} %constant_dynamic-slice_fusion.refs_8_), channel_id=1, source_target_pairs={{0,4},{4,0},{8,12},{12,8},{16,20},{20,16},{24,28},{28,24},{32,36},... | collective-permute-start | bytes 786440 | tf_op jit(solution)/shard_map/ppermute | solution.py:352
  59.5 22.2 %all-to-all-start.1 = ((bf16[32,48,256]{2,1,0:T(8,128)(2,1)}), bf16[32,48,256]{2,1,0:T(8,128)(2,1)}, u32[]{:S(2)}, u32[]{:S(2)}) async-start(bf16[32,48,256]{2,1,0:T(8,128)(2,1)} %far.1), calls=%async_computation.1 | async-start | bytes 1572864 | tf_op jit(solution)/shard_map/all_to_all | solution.py:301
  68.1 5.7 %collective-permute-start.20 = (bf16[128,1024]{1,0:T(8,128)(2,1)S(1)}, bf16[128,1024]{1,0:T(8,128)(2,1)S(1)}, u32[]{:S(2)}, u32[]{:S(2)}) collective-permute-start(bf16[128,1024]{1,0:T(8,128)(2,1)S(1)} %collective-permute-done.16.refs_9_), channel_id=1, source_target_pairs={{0,4},{4,0},{8,12},{12,8},{16,20},{20,16},{24,28},{28,24},{32,36},... | collective-permute-start | bytes 786440 | tf_op jit(solution)/shard_map/ppermute | solution.py:352
  70.0 18.2 %collective-permute-start.13 = (bf16[320,512]{1,0:T(8,128)(2,1)S(1)}, bf16[320,512]{1,0:T(8,128)(2,1)S(1)}, u32[]{:S(2)}, u32[]{:S(2)}) collective-permute-start(bf16[320,512]{1,0:T(8,128)(2,1)S(1)} %pad_maximum_fusion.refs_4_), channel_id=1, source_target_pairs={{0,1},{1,2},{2,3},{3,0},{4,5},{5,6},{6,7},{7,4},{8,9},{9,10},{10,1... | collective-permute-start | bytes 983048 | tf_op jit(solution)/shard_map/ppermute | solution.py:348
  71.0 12.3 %collective-permute-start.21 = (bf16[128,1024]{1,0:T(8,128)(2,1)S(1)}, bf16[128,1024]{1,0:T(8,128)(2,1)}, u32[]{:S(2)}, u32[]{:S(2)}) collective-permute-start(bf16[128,1024]{1,0:T(8,128)(2,1)S(1)} %collective-permute-done.17.refs_10_), channel_id=1, source_target_pairs={{0,4},{4,0},{8,12},{12,8},{16,20},{20,16},{24,28},{28,24},{32,36},... | collective-permute-start | bytes 786440 | tf_op jit(solution)/shard_map/ppermute | solution.py:352
  71.0 13.2 %collective-permute-start.22 = (bf16[128,1024]{1,0:T(8,128)(2,1)S(1)}, bf16[128,1024]{1,0:T(8,128)(2,1)}, u32[]{:S(2)}, u32[]{:S(2)}) collective-permute-start(bf16[128,1024]{1,0:T(8,128)(2,1)S(1)} %collective-permute-done.18.refs_11_), channel_id=1, source_target_pairs={{0,4},{4,0},{8,12},{12,8},{16,20},{20,16},{24,28},{28,24},{32,36},... | collective-permute-start | bytes 786440 | tf_op jit(solution)/shard_map/ppermute | solution.py:352
  71.5 18.2 %collective-permute-start.14 = (bf16[320,512]{1,0:T(8,128)(2,1)S(1)}, bf16[320,512]{1,0:T(8,128)(2,1)S(1)}, u32[]{:S(2)}, u32[]{:S(2)}) collective-permute-start(bf16[320,512]{1,0:T(8,128)(2,1)S(1)} %pad_maximum_fusion.refs_4_), channel_id=1, source_target_pairs={{0,3},{1,0},{2,1},{3,2},{4,7},{5,4},{6,5},{7,6},{8,11},{9,8},{10,9... | collective-permute-start | bytes 983048 | tf_op jit(solution)/shard_map/ppermute | solution.py:348
  73.9 15.9 %collective-permute-start.15 = (bf16[320,512]{1,0:T(8,128)(2,1)S(1)}, bf16[320,512]{1,0:T(8,128)(2,1)S(1)}, u32[]{:S(2)}, u32[]{:S(2)}) collective-permute-start(bf16[320,512]{1,0:T(8,128)(2,1)S(1)} %pad_maximum_fusion.refs_4_), channel_id=1, source_target_pairs={{0,2},{1,3},{2,0},{3,1},{4,6},{5,7},{6,4},{7,5},{8,10},{9,11},{10,... | collective-permute-start | bytes 983048 | tf_op jit(solution)/shard_map/ppermute | solution.py:348
  83.3 12.0 %collective-permute-start.10 = (bf16[320,256]{1,0:T(8,128)(2,1)S(1)}, bf16[320,256]{1,0:T(8,128)(2,1)S(1)}, u32[]{:S(2)}, u32[]{:S(2)}) collective-permute-start(bf16[320,256]{1,0:T(8,128)(2,1)S(1)} %fusion.4.refs_0_), channel_id=1, source_target_pairs={{0,1},{1,2},{2,3},{3,0},{4,5},{5,6},{6,7},{7,4},{8,9},{9,10},{10,1... | collective-permute-start | bytes 491528 | tf_op jit(solution)/shard_map/ppermute | solution.py:348
  84.3 11.0 %collective-permute-start.11 = (bf16[320,256]{1,0:T(8,128)(2,1)S(1)}, bf16[320,256]{1,0:T(8,128)(2,1)S(1)}, u32[]{:S(2)}, u32[]{:S(2)}) collective-permute-start(bf16[320,256]{1,0:T(8,128)(2,1)S(1)} %fusion.4.refs_0_), channel_id=1, source_target_pairs={{0,3},{1,0},{2,1},{3,2},{4,7},{5,4},{6,5},{7,6},{8,11},{9,8},{10,9... | collective-permute-start | bytes 491528 | tf_op jit(solution)/shard_map/ppermute | solution.py:348
  88.2 7.1 %collective-permute-start.12 = (bf16[320,256]{1,0:T(8,128)(2,1)S(1)}, bf16[320,256]{1,0:T(8,128)(2,1)S(1)}, u32[]{:S(2)}, u32[]{:S(2)}) collective-permute-start(bf16[320,256]{1,0:T(8,128)(2,1)S(1)} %fusion.4.refs_0_), channel_id=1, source_target_pairs={{0,2},{1,3},{2,0},{3,1},{4,6},{5,7},{6,4},{7,5},{8,10},{9,11},{10,... | collective-permute-start | bytes 491528 | tf_op jit(solution)/shard_map/ppermute | solution.py:348
  (12 other events, 127.8 us)

commit v6 on v5

--- a/solution.py
+++ b/solution.py
@@ -73,20 +73,25 @@
     copies[steps + 2].wait()
     q = nn(rows_in[...], wq_ref[...]).astype(BF).astype(F32) * HEAD_DIM ** -0.5
     q_ref[...] = q.astype(BF)
-    t_ref[...] = rows_in[:, pl.ds(pl.multiple_of(lax.axis_index("head") * cols, 128), cols)]
-
-
-def spreading(keep, heads):
-    shape = (4 * keep * heads, 4 * keep)
-    r = lax.broadcasted_iota(jnp.int32, shape, 0)
-    source = r // (keep * heads) * keep + r % keep
-    return (source == lax.broadcasted_iota(jnp.int32, shape, 1)).astype(F32).astype(BF)
-
-
-def own_lanes(keep, heads):
-    shape = (4 * keep * heads, heads * HEAD_DIM)
-    r = lax.broadcasted_iota(jnp.int32, shape, 0)
-    return lax.broadcasted_iota(jnp.int32, shape, 1) // HEAD_DIM == r // keep % heads
+    t_ref[q_ref.shape[0] :, :] = jnp.zeros((t_ref.shape[0] - q_ref.shape[0], cols), BF)
+    t_ref[: q_ref.shape[0], :] = rows_in[:, pl.ds(pl.multiple_of(lax.axis_index("head") * cols, 128), cols)]
+
+
+def row_order(keep, heads):
+    rows, chunk, cols = 4 * keep * heads, 4 * keep, heads * HEAD_DIM
+
+    def split(r):
+        frame = sum((r >= keep * heads * i).astype(jnp.int32) for i in (1, 2, 3))
+        r = r - frame * keep * heads
+        head = sum((r >= keep * i).astype(jnp.int32) for i in range(1, heads))
+        return frame * keep + r - head * keep, head
+
+    source, head = split(lax.broadcasted_iota(jnp.int32, (rows, 1), 0))
+    spread = (source == lax.broadcasted_iota(jnp.int32, (rows, chunk), 1)).astype(F32).astype(BF)
+    lanes = (head == lax.broadcasted_iota(jnp.int32, (rows, cols), 1) >> 6).astype(F32).astype(BF)
+    source, _ = split(lax.broadcasted_iota(jnp.int32, (1, rows), 1))
+    join = (source == lax.broadcasted_iota(jnp.int32, (chunk, rows), 0)).astype(F32).astype(BF)
+    return spread, lanes, join
 
 
 def near_kernel(q_hbm, x_hbm, wk_hbm, wv_hbm, out_ref, q_ref, x_ref, wk_ref, wv_ref, sem):
@@ -94,53 +99,60 @@
     steps = x_ref.shape[0] // (4 * PATCHES)
     chunk = q_ref.shape[0] // steps
     pairs = list(zip(row_blocks(x_hbm, steps), row_blocks(x_ref, steps)))
-    copies = fetch([(wk_hbm, wk_ref), (wv_hbm, wv_ref)] + pairs + [(q_hbm, q_ref)], sem)
+    copies = fetch([(wk_hbm, wk_ref)] + pairs[:1] + [(wv_hbm, wv_ref), (q_hbm, q_ref)] + pairs[1:], sem)
     size = x_ref.shape[0] // steps
-    keep = chunk // 4
     cols = q_ref.shape[1]
-    rows = keep * heads
+    rows = chunk // 4 * heads
     span = 208
-    lane = lax.broadcasted_iota(jnp.int32, (rows, 128), 1)
-    spread = spreading(keep, heads)
-    mine = own_lanes(keep, heads)
-    copies[-1].wait()
-    copies[0].wait()
-    copies[1].wait()
+    starts = [f * PATCHES // 16 * 16 for f in range(4)]
+    c = lax.broadcasted_iota(jnp.int32, (rows, span), 1)
+    walls = [jnp.where((c >= f * PATCHES - starts[f]) & (c < (f + 1) * PATCHES - starts[f]), 0.0, NEG) for f in range(4)]
+    lane = lax.broadcasted_iota(jnp.int32, (4 * rows, 128), 1)
+    spread, lanes, _ = row_order(chunk // 4, heads)
+    for copy in copies[:4]:
+        copy.wait()
     for step in range(steps):
-        copies[2 + step].wait()
+        if step:
+            copies[3 + step].wait()
         x = x_ref[step * size : (step + 1) * size, :]
         k = nn(x, wk_ref[...]).astype(BF)
         v = nn(x, wv_ref[...]).astype(BF)
-        stack = jnp.where(mine, nn(spread, q_ref[step * chunk : (step + 1) * chunk, :]), 0.0).astype(BF)
-        for f in range(4):
-            start = f * PATCHES // 16 * 16
-            part = slice((step * 4 + f) * rows, (step * 4 + f + 1) * rows)
-            c = lax.broadcasted_iota(jnp.int32, (rows, span), 1) + (start - f * PATCHES)
-            s = jnp.where((c >= 0) & (c < PATCHES), nt(stack[f * rows : (f + 1) * rows], k[start : start + span]), NEG)
-            m = jnp.max(s, axis=1, keepdims=True)
-            e = jnp.exp(s - m)
-            total = jnp.sum(e, axis=1, keepdims=True)
-            level = m + jnp.log(total)
-            high = level.astype(BF).astype(F32)
-            middle = (level - high).astype(BF).astype(F32)
-            side = jnp.where(lane == 0, high, jnp.where(lane == 1, middle, jnp.where(lane == 2, level - high - middle, 0.0)))
-            out_ref[part, :cols] = (nn(e.astype(BF), v[start : start + span]) / total).astype(BF)
-            out_ref[part, cols:] = side.astype(BF)
+        stack = nn(spread, q_ref[step * chunk : (step + 1) * chunk, :]).astype(BF) * lanes
+        s = jnp.concatenate(
+            [nt(stack[f * rows : (f + 1) * rows], k[starts[f] : starts[f] + span]) + walls[f] for f in range(4)], axis=0
+        )
+        m = jnp.max(s, axis=1, keepdims=True)
+        e = jnp.exp(s - m)
+        total = jnp.sum(e, axis=1, keepdims=True)
+        e = e.astype(BF)
+        o = jnp.concatenate(
+            [nn(e[f * rows : (f + 1) * rows], v[starts[f] : starts[f] + span]) for f in range(4)], axis=0
+        )
+        level = m + jnp.log(total)
+        high = level.astype(BF).astype(F32)
+        middle = (level - high).astype(BF).astype(F32)
+        side = jnp.where(lane == 0, high, jnp.where(lane == 1, middle, jnp.where(lane == 2, level - high - middle, 0.0)))
+        part = slice(step * 4 * rows, (step + 1) * 4 * rows)
+        out_ref[part, :cols] = (o * (1.0 / total)).astype(BF)
+        out_ref[part, cols:] = side.astype(BF)
 
 
 def far_kernel(q_hbm, near_hbm, allow_hbm, pack_hbm, _, *rest):
-    parts, (out_ref, far_ref, q_ref, near_ref, allow_ref, pack_ref, sem) = rest[:8], rest[8:]
-    pairs = [(allow_hbm, allow_ref), (q_hbm, q_ref)] + [(part, far_ref.at[i]) for i, part in enumerate(parts)]
-    copies = fetch(pairs + [(near_hbm, near_ref), (pack_hbm, pack_ref)], sem)
+    parts, rest = rest[:8], rest[8:]
+    out_ref, far_ref, key, value, q_ref, near_ref, allow_ref, pack_ref, sem = rest
+    pairs = [(allow_hbm, allow_ref)] + [(part, far_ref.at[i]) for i, part in enumerate(parts)]
+    copies = fetch(pairs + [(q_hbm, q_ref), (near_hbm, near_ref), (pack_hbm, pack_ref)], sem)
     cols = q_ref.shape[1]
-    heads = cols // HEAD_DIM
     frames, total_frames = allow_ref.shape
     groups = frames // 4
     chunk = q_ref.shape[0] // groups
     keep = chunk // 4
+    heads = cols // HEAD_DIM
     rows = chunk * heads
-    spread = spreading(keep, heads)
-    mine = own_lanes(keep, heads)
+    spread, lanes, join = row_order(keep, heads)
+    column = lax.broadcasted_iota(jnp.int32, (rows, frames), 1)
+    r = lax.broadcasted_iota(jnp.int32, (rows, frames), 0)
+    frame = sum((r >= keep * heads * i).astype(jnp.int32) for i in (1, 2, 3))
     me = lax.axis_index("tm")
     n = lax.broadcasted_iota(jnp.int32, (1, total_frames), 1)
     i, j = (n >> 6) & 3, (n >> 4) & 3
@@ -150,21 +162,24 @@
     order = (lax.broadcasted_iota(jnp.int32, (total_frames, total_frames), 0) == where).astype(F32).astype(BF)
     copies[0].wait()
     wall = jnp.where(nn(allow_ref[...].astype(F32).astype(BF), order) > 0.5, 0.0, NEG).astype(BF)
-    for copy in copies[1:-1]:
-        copy.wait()
-    frame = lax.broadcasted_iota(jnp.int32, (rows, frames), 0) // (keep * heads)
-    column = lax.broadcasted_iota(jnp.int32, (rows, frames), 1)
+    for p in range(8):
+        copies[1 + p].wait()
+        spot = slice(p * 64, (p + 1) * 64)
+        for u in range(4):
+            key[u, spot, :] = far_ref[p, :, u * 16 : (u + 1) * 16, :cols].reshape(64, cols)
+            value[u, spot, :] = far_ref[p, :, u * 16 : (u + 1) * 16, cols:].reshape(64, cols)
+    copies[9].wait()
+    copies[10].wait()
     outs = []
     for g in range(groups):
         part = slice(g * rows, (g + 1) * rows)
-        q = jnp.where(mine, nn(spread, q_ref[g * chunk : (g + 1) * chunk, :]), 0.0).astype(BF)
+        q = nn(spread, q_ref[g * chunk : (g + 1) * chunk, :]).astype(BF) * lanes
         block = nn((column == frame + 4 * g).astype(F32).astype(BF), wall)
         level = jnp.sum(near_ref[part, cols:].astype(F32), axis=1, keepdims=True)
         top = level
         scores = []
         for u in range(4):
-            key = far_ref[:, :, u * 16 : (u + 1) * 16, :cols].reshape(total_frames, cols)
-            s = nt(q, key) + block
+            s = nt(q, key[u]) + block
             top = jnp.maximum(top, jnp.max(s, axis=1, keepdims=True))
             scores.append(s)
         total = jnp.exp(level - top)
@@ -172,12 +187,12 @@
         for u in range(4):
             e = jnp.exp(scores[u] - top)
             total = total + jnp.sum(e, axis=1, keepdims=True)
-            value = far_ref[:, :, u * 16 : (u + 1) * 16, cols:].reshape(total_frames, cols)
-            acc = acc + nn(e.astype(BF), value)
-        done = jnp.where(mine, acc / total, 0.0).astype(BF)
-        outs.append(lax.dot_general(spread, done, (((0,), (0,)), ((), ())), preferred_element_type=F32).astype(BF))
+            acc = acc + nn(e.astype(BF), value[u])
+        outs.append((acc * (1.0 / total)).astype(BF) * lanes)
+    outs = [nn(join, done).astype(BF) for done in outs]
+    outs.append(jnp.zeros((pack_ref.shape[1] - chunk * groups, cols), BF))
     out = jnp.concatenate(outs, axis=0)
-    copies[-1].wait()
+    copies[11].wait()
     out_ref[...] = nn(pack_ref[...], out).astype(BF).reshape(out_ref.shape)
 
 
@@ -191,10 +206,13 @@
     there = pl.ds(pl.multiple_of((1 - core) * half, 128), half)
     targets = [att.at[i] for i in range(4)] + [side.at[i] for i in range(4)]
     targets += [wo.at[i, here] for i in range(4)] + [wo.at[i, there] for i in range(4)]
-    for copy in fetch(list(zip(sources, targets)), sem):
+    copies = fetch(list(zip(sources, targets)), sem)
+    for copy in copies[:4] + copies[8:]:
         copy.wait()
     raw[...] = sum(nn(att[i], wo[i]) for i in range(4))
     spots = [pl.ds(pl.multiple_of(lax.rem(head + 4 - d, 4) * cols, 128), cols) for d in DISTANCES]
+    for copy in copies[4:8]:
+        copy.wait()
     for i in range(4):
         raw[:, spots[i]] += side[i, :, :cols].astype(F32)
     full = raw[...]
@@ -252,6 +270,7 @@
     steps = frames // 4
     block = 4 * PATCHES
     chunk = 4 * keep
+    padded = -(-own // 128) * 128
     my_core = me % 2
 
     r = np.arange(block)
@@ -270,7 +289,7 @@
         out_shape=[
             jax.ShapeDtypeStruct((4 * frames, 2 * cols), BF),
             jax.ShapeDtypeStruct((own, cols), BF),
-            jax.ShapeDtypeStruct((own, cols), BF),
+            jax.ShapeDtypeStruct((padded, cols), BF),
         ],
         scratch_shapes=[pltpu.VMEM((frames * PATCHES, width), BF)]
         + [pltpu.VMEM((width, cols), BF)] * 3
@@ -289,6 +308,7 @@
     before = np.tril(np.ones((own, own), np.float32), -1)
     same = (my_owner[:, None] == my_owner[None, :]) & (before > 0)
     place = my_owner * CAP + jnp.sum(same, axis=1, dtype=jnp.int32)
+    place = jnp.pad(place, (0, padded - own), constant_values=-1)
     pack = (jnp.arange(n_peers * CAP, dtype=jnp.int32)[:, None] == place[None, :]).astype(BF)
     coming = (owner_all == me).reshape(n_peers, own)
     rank = jnp.dot(coming.astype(BF), jnp.asarray(before.T, BF), preferred_element_type=F32).astype(jnp.int32)
@@ -328,6 +348,8 @@
         out_shape=jax.ShapeDtypeStruct((n_peers, CAP, cols), BF),
         scratch_shapes=[
             pltpu.VMEM((8, 4, 4 * frames, 2 * cols), BF),
+            pltpu.VMEM((4, n_peers * frames, cols), BF),
+            pltpu.VMEM((4, n_peers * frames, cols), BF),
             pltpu.VMEM((own, cols), BF),
             pltpu.VMEM((own * heads, cols + 128), BF),
             pltpu.VMEM(pattern.shape, jnp.int32),

time: 102 us -> 96.4 us (0.945)
  Pallas kernels: 34.3 us -> 28.4 us
    pallas_call x1, Pallas kernels: 11.8 us -> 8.68 us  [body(): pl.pallas_call(near_kernel, in_specs=[HBM] * 4, out_specs=pl.BlockSpec(me...]
    pallas_call x1, Pallas kernels: 11.2 us -> 8.56 us  [body(): pl.pallas_call(far_kernel, in_specs=[HBM] * 13, out_specs=pl.BlockSpec(me...]
  transfers between devices with their start and end apart: 25 -> 25, of which waited for: 5 -> 5; matrix products, arithmetic and copies ran while one was open for 8% -> 9% of each run, Pallas kernels for 23% -> 18%
where the time goes in v6:
time: 96.4 us; the launch traced here: 94.9 us
  starting transfers between devices  40.7 us (42%)
  Pallas kernels  28.4 us (29%)
  waiting for transfers between devices  14.3 us (15%)
  matrix products  4.74 us (5%)
  other arithmetic  4.09 us (4%)
  local copies, waits for them, and re-layouts  1.84 us (2%)
    ppermute x9, starting transfers between devices, over_heads(): return [x] + [lax.ppermute(x, 'head', to(d)) for d in DISTANCES[1:]]  14.8 us
    all_to_all x2, starting transfers between devices, deliver(): return lax.all_to_all(packed, 'tm', 0, 0, tiled=True)  12.5 us
    pallas_call x1, Pallas kernels, body(): pl.pallas_call(near_kernel, in_specs=[HBM] * 4, out_specs=pl.BlockSpec(me...  8.68 us
    pallas_call x1, Pallas kernels, body(): pl.pallas_call(far_kernel, in_specs=[HBM] * 13, out_specs=pl.BlockSpec(me...  8.56 us
    ppermute x9, waiting for transfers between devices, over_heads(): return [x] + [lax.ppermute(x, 'head', to(d)) for d in DISTANCES[1:]]  7.11 us
    pallas_call x1, Pallas kernels, body(): pl.pallas_call(gather_kernel, in_specs=[HBM] * 4 + whole(3), out_specs=wh...  6.39 us
    all_to_all x2, waiting for transfers between devices, deliver(): return lax.all_to_all(packed, 'tm', 0, 0, tiled=True)  6.33 us
    ppermute x3, starting transfers between devices, body(): lax.ppermute(plane, 'tm', along_z(d))  6.06 us
  transfers between devices with their start and end apart: 25, of which 5 were waited for; matrix products, arithmetic and copies ran while one was open for 9% of the time, Pallas kernels for 18%

profile of v6, /device:TPU:0, one launch (start us, length us, event | category | flops | bytes accessed | tf_op | source)
XLA Modules:
  0.0 94.9 jit_solution(1223358776405944117)
XLA Ops:
  0.7 6.4 %gather.1 = (bf16[64,512]{1,0:T(8,128)(2,1)}, bf16[320,256]{1,0:T(8,128)(2,1)}, bf16[384,256]{1,0:T(8,128)(2,1)}) custom-call(bf16[3136,1024]{1,0:T(8,128)(2,1)} %x_hbm.3, bf16[1024,256]{1,0:T(8,128)(2,1)} %wq_hbm.1, bf16[1024,256]{1,0:T(8,128)(2,1)} %wk_hbm.3, bf16[1024,256]{1,0:T(8,128)(2,1)} %wv_hbm.3, bf16[16,784]{1,0:T(8,128)(2,1)} %constant.62.clone.pool_ref, ...), custom_call_target="tpu_custom_call" | custom-call | flops 2000000000 | bytes 10000000 | tf_op jit(solution)/shard_map/gather/pallas_call | solution.py:285
  7.1 1.7 %collective-permute-start = (bf16[64,512]{1,0:T(8,128)(2,1)}, bf16[64,512]{1,0:T(8,128)(2,1)S(1)}, u32[]{:S(2)}, u32[]{:S(2)}) collective-permute-start(bf16[64,512]{1,0:T(8,128)(2,1)} %get-tuple-element.12), channel_id=1, source_target_pairs={{0,8},{4,12},{8,16},{12,20},{16,24},{20,28},{24,0},{28,4},{32,40},... | collective-permute-start | bytes 196616 | tf_op jit(solution)/shard_map/ppermute | solution.py:302
  8.8 1.6 %collective-permute-start.1 = (bf16[64,512]{1,0:T(8,128)(2,1)}, bf16[64,512]{1,0:T(8,128)(2,1)S(1)}, u32[]{:S(2)}, u32[]{:S(2)}) collective-permute-start(bf16[64,512]{1,0:T(8,128)(2,1)} %get-tuple-element.12), channel_id=1, source_target_pairs={{0,24},{4,28},{8,0},{12,4},{16,8},{20,12},{24,16},{28,20},{32,56},... | collective-permute-start | bytes 196616 | tf_op jit(solution)/shard_map/ppermute | solution.py:302
  10.4 2.1 %collective-permute-start.2 = (bf16[64,512]{1,0:T(8,128)(2,1)}, bf16[64,512]{1,0:T(8,128)(2,1)S(1)}, u32[]{:S(2)}, u32[]{:S(2)}) collective-permute-start(bf16[64,512]{1,0:T(8,128)(2,1)} %get-tuple-element.12), channel_id=1, source_target_pairs={{0,16},{4,20},{8,24},{12,28},{16,0},{20,4},{24,8},{28,12},{32,48},... | collective-permute-start | bytes 196616 | tf_op jit(solution)/shard_map/ppermute | solution.py:302
  12.5 1.6 %collective-permute-start.16 = (bf16[128,1024]{1,0:T(8,128)(2,1)S(1)}, bf16[128,1024]{1,0:T(8,128)(2,1)S(1)}, u32[]{:S(2)}, u32[]{:S(2)}) collective-permute-start(bf16[128,1024]{1,0:T(8,128)(2,1)S(1)} %constant_dynamic-slice_fusion.refs_8_), channel_id=1, source_target_pairs={{0,1},{1,2},{2,3},{3,0},{4,5},{5,6},{6,7},{7,4},{8,9},{9,10},{10,1... | collective-permute-start | bytes 786440 | tf_op jit(solution)/shard_map/ppermute | solution.py:370
  14.5 1.5 %fusion.pack_hbm = bf16[1536,384]{1,0:T(8,128)(2,1)} fusion(s32[384]{0:T(512)S(1)} %pad.4), kind=kLoop, calls=%fused_computation.2 | loop fusion | flops 1179648 | bytes 1181184 | tf_op jit(solution)/shard_map/convert_element_type | solution.py:312
  17.3 2.1 %collective-permute-start.3 = (bf16[4,64,512]{2,1,0:T(8,128)(2,1)S(1)}, bf16[4,64,512]{2,1,0:T(8,128)(2,1)S(1)}, u32[]{:S(2)}, u32[]{:S(2)}) collective-permute-start(bf16[4,64,512]{2,1,0:T(8,128)(2,1)S(1)} %pad_maximum_fusion.1.rest_0_), channel_id=1, source_target_pairs={{0,32},{4,36},{8,40},{12,44},{16,48},{20,52},{24,56},{28,60},{32,6... | collective-permute-start | bytes 786440 | tf_op jit(solution)/shard_map/ppermute | solution.py:304
  19.3 2.2 %collective-permute-start.4 = (bf16[4,64,512]{2,1,0:T(8,128)(2,1)S(1)}, bf16[4,64,512]{2,1,0:T(8,128)(2,1)S(1)}, u32[]{:S(2)}, u32[]{:S(2)}) collective-permute-start(bf16[4,64,512]{2,1,0:T(8,128)(2,1)S(1)} %pad_maximum_fusion.1.rest_0_), channel_id=1, source_target_pairs={{0,96},{4,100},{8,104},{12,108},{16,112},{20,116},{24,120},{28,124... | collective-permute-start | bytes 786440 | tf_op jit(solution)/shard_map/ppermute | solution.py:304
  21.5 1.8 %collective-permute-start.5 = (bf16[4,64,512]{2,1,0:T(8,128)(2,1)S(1)}, bf16[4,64,512]{2,1,0:T(8,128)(2,1)}, u32[]{:S(2)}, u32[]{:S(2)}) collective-permute-start(bf16[4,64,512]{2,1,0:T(8,128)(2,1)S(1)} %pad_maximum_fusion.1.rest_0_), channel_id=1, source_target_pairs={{0,64},{4,68},{8,72},{12,76},{16,80},{20,84},{24,88},{28,92},{32,9... | collective-permute-start | bytes 786440 | tf_op jit(solution)/shard_map/ppermute | solution.py:304
  24.8 4.8 %all-to-all-start = ((bf16[32,48,256]{2,1,0:T(8,128)(2,1)}), bf16[32,48,256]{2,1,0:T(8,128)(2,1)S(1)}, u32[]{:S(2)}, u32[]{:S(2)}) async-start(bf16[32,48,256]{2,1,0:T(8,128)(2,1)} %bitcast.4), calls=%async_computation | async-start | bytes 1572864 | tf_op jit(solution)/shard_map/all_to_all | solution.py:321
  29.6 8.7 %near.1.near_hbm = bf16[1280,384]{1,0:T(8,128)(2,1)} custom-call(bf16[320,256]{1,0:T(8,128)(2,1)} %get-tuple-element.15.q_hbm, bf16[3136,1024]{1,0:T(8,128)(2,1)} %x_hbm.3, bf16[1024,256]{1,0:T(8,128)(2,1)} %wk_hbm.3, bf16[1024,256]{1,0:T(8,128)(2,1)} %wv_hbm.3), custom_call_target="tpu_custom_call" | custom-call | flops 5000000000 | bytes 10000000 | tf_op jit(solution)/shard_map/near/pallas_call | solution.py:329
  40.1 2.8 %collective-permute-start.17 = (bf16[128,1024]{1,0:T(8,128)(2,1)S(1)}, bf16[128,1024]{1,0:T(8,128)(2,1)S(1)}, u32[]{:S(2)}, u32[]{:S(2)}) collective-permute-start(bf16[128,1024]{1,0:T(8,128)(2,1)S(1)} %constant_dynamic-slice_fusion.refs_8_), channel_id=1, source_target_pairs={{0,3},{1,0},{2,1},{3,2},{4,7},{5,4},{6,5},{7,6},{8,11},{9,8},{10,9... | collective-permute-start | bytes 786440 | tf_op jit(solution)/shard_map/ppermute | solution.py:370
  45.3 8.6 %far.1 = bf16[32,48,256]{2,1,0:T(8,128)(2,1)} custom-call(bf16[320,256]{1,0:T(8,128)(2,1)} %get-tuple-element.15.q_hbm, bf16[1280,384]{1,0:T(8,128)(2,1)} %near.1.near_hbm, s32[16,512]{1,0:T(8,128)} %allow_hbm.1, bf16[1536,384]{1,0:T(8,128)(2,1)} %fusion.pack_hbm, bf16[32,48,256]{2,1,0:T(8,128)(2,1)} %copy-done.1, bf16[4,64,512]{2,1,0:T(8,128)(2,1)} %copy-done.2, ...), custom_call_target="tpu_custom_call" | custom-call | flops 4000000000 | bytes 4000000 | tf_op jit(solution)/shard_map/far/pallas_call | solution.py:344
  53.8 7.6 %all-to-all-start.1 = ((bf16[32,48,256]{2,1,0:T(8,128)(2,1)}), bf16[32,48,256]{2,1,0:T(8,128)(2,1)}, u32[]{:S(2)}, u32[]{:S(2)}) async-start(bf16[32,48,256]{2,1,0:T(8,128)(2,1)} %far.1), calls=%async_computation.1 | async-start | bytes 1572864 | tf_op jit(solution)/shard_map/all_to_all | solution.py:321
  62.7 1.6 %fusion.5 = bf16[320,256]{1,0:T(8,128)(2,1)S(1)} fusion(bf16[1536,256]{1,0:T(8,128)(2,1)} %bitcast.12, s32[1536]{0:T(1024)S(1)} %eq.70), kind=kOutput, calls=%fused_computation.10 | convolution fusion | flops 252231680 | bytes 956416 | tf_op jit(solution)/shard_map/dot_general | solution.py:324
  65.8 2.3 %collective-permute-start.14 = (bf16[320,512]{1,0:T(8,128)(2,1)S(1)}, bf16[320,512]{1,0:T(8,128)(2,1)S(1)}, u32[]{:S(2)}, u32[]{:S(2)}) collective-permute-start(bf16[320,512]{1,0:T(8,128)(2,1)S(1)} %pad_maximum_fusion.refs_4_), channel_id=1, source_target_pairs={{0,3},{1,0},{2,1},{3,2},{4,7},{5,4},{6,5},{7,6},{8,11},{9,8},{10,9... | collective-permute-start | bytes 983048 | tf_op jit(solution)/shard_map/ppermute | solution.py:370
  68.2 1.5 %collective-permute-start.15 = (bf16[320,512]{1,0:T(8,128)(2,1)S(1)}, bf16[320,512]{1,0:T(8,128)(2,1)S(1)}, u32[]{:S(2)}, u32[]{:S(2)}) collective-permute-start(bf16[320,512]{1,0:T(8,128)(2,1)S(1)} %pad_maximum_fusion.refs_4_), channel_id=1, source_target_pairs={{0,2},{1,3},{2,0},{3,1},{4,6},{5,7},{6,4},{7,5},{8,10},{9,11},{10,... | collective-permute-start | bytes 983048 | tf_op jit(solution)/shard_map/ppermute | solution.py:370
  69.7 6.3 %all-to-all-done.1 = bf16[32,48,256]{2,1,0:T(8,128)(2,1)} async-done(((bf16[32,48,256]{2,1,0:T(8,128)(2,1)}), bf16[32,48,256]{2,1,0:T(8,128)(2,1)}, u32[]{:S(2)}, u32[]{:S(2)}) %all-to-all-start.1) | async-done | bytes 786464 | tf_op jit(solution)/shard_map/all_to_all | solution.py:321
  76.0 1.6 %fusion.4.refs_0_ = bf16[320,256]{1,0:T(8,128)(2,1)S(1)} fusion(bf16[1536,256]{1,0:T(8,128)(2,1)} %bitcast.5, s32[1536]{0:T(1024)S(1)} %eq.70), kind=kOutput, calls=%fused_computation.9 | convolution fusion | flops 252231680 | bytes 956416 | tf_op jit(solution)/shard_map/dot_general | solution.py:324
  78.6 2.3 %collective-permute-start.11 = (bf16[320,256]{1,0:T(8,128)(2,1)S(1)}, bf16[320,256]{1,0:T(8,128)(2,1)S(1)}, u32[]{:S(2)}, u32[]{:S(2)}) collective-permute-start(bf16[320,256]{1,0:T(8,128)(2,1)S(1)} %fusion.4.refs_0_), channel_id=1, source_target_pairs={{0,3},{1,0},{2,1},{3,2},{4,7},{5,4},{6,5},{7,6},{8,11},{9,8},{10,9... | collective-permute-start | bytes 491528 | tf_op jit(solution)/shard_map/ppermute | solution.py:370
  80.9 1.6 %collective-permute-done.13.refs_5_ = bf16[320,512]{1,0:T(8,128)(2,1)S(1)} collective-permute-done((bf16[320,512]{1,0:T(8,128)(2,1)S(1)}, bf16[320,512]{1,0:T(8,128)(2,1)S(1)}, u32[]{:S(2)}, u32[]{:S(2)}) %collective-permute-start.13) | collective-permute-done | bytes 327712 | tf_op jit(solution)/shard_map/ppermute | solution.py:370
  82.5 1.6 %collective-permute-start.12 = (bf16[320,256]{1,0:T(8,128)(2,1)S(1)}, bf16[320,256]{1,0:T(8,128)(2,1)S(1)}, u32[]{:S(2)}, u32[]{:S(2)}) collective-permute-start(bf16[320,256]{1,0:T(8,128)(2,1)S(1)} %fusion.4.refs_0_), channel_id=1, source_target_pairs={{0,2},{1,3},{2,0},{3,1},{4,6},{5,7},{6,4},{7,5},{8,10},{9,11},{10,... | collective-permute-start | bytes 491528 | tf_op jit(solution)/shard_map/ppermute | solution.py:370
  84.1 5.5 %collective-permute-done.10.refs_1_ = bf16[320,256]{1,0:T(8,128)(2,1)S(1)} collective-permute-done((bf16[320,256]{1,0:T(8,128)(2,1)S(1)}, bf16[320,256]{1,0:T(8,128)(2,1)S(1)}, u32[]{:S(2)}, u32[]{:S(2)}) %collective-permute-start.10) | collective-permute-done | bytes 163872 | tf_op jit(solution)/shard_map/ppermute | solution.py:370
  89.6 4.7 %final.1 = (bf16[320,256]{1,0:T(8,128)(2,1)}, f32[1,320]{1,0:T(1,128)S(1)}) custom-call(bf16[320,256]{1,0:T(8,128)(2,1)S(1)} %fusion.4.refs_0_, bf16[320,256]{1,0:T(8,128)(2,1)S(1)} %collective-permute-done.10.refs_1_, bf16[320,256]{1,0:T(8,128)(2,1)S(1)} %collective-permute-done.11.refs_2_, bf16[320,256]{1,0:T(8,128)(2,1)S(1)} %collective-permute-done.12.refs_3_, ...), custom_call_target="tpu_custom_call" | custom-call | flops 1000000000 | bytes 4000000 | tf_op jit(solution)/shard_map/final/pallas_call | solution.py:377
  (71 shorter events, 11.6 us)
Async XLA Ops:
  7.1 9.0 %collective-permute-start = (bf16[64,512]{1,0:T(8,128)(2,1)}, bf16[64,512]{1,0:T(8,128)(2,1)S(1)}, u32[]{:S(2)}, u32[]{:S(2)}) collective-permute-start(bf16[64,512]{1,0:T(8,128)(2,1)} %get-tuple-element.12), channel_id=1, source_target_pairs={{0,8},{4,12},{8,16},{12,20},{16,24},{20,28},{24,0},{28,4},{32,40},... | collective-permute-start | bytes 196616 | tf_op jit(solution)/shard_map/ppermute | solution.py:302
  8.8 7.3 %collective-permute-start.1 = (bf16[64,512]{1,0:T(8,128)(2,1)}, bf16[64,512]{1,0:T(8,128)(2,1)S(1)}, u32[]{:S(2)}, u32[]{:S(2)}) collective-permute-start(bf16[64,512]{1,0:T(8,128)(2,1)} %get-tuple-element.12), channel_id=1, source_target_pairs={{0,24},{4,28},{8,0},{12,4},{16,8},{20,12},{24,16},{28,20},{32,56},... | collective-permute-start | bytes 196616 | tf_op jit(solution)/shard_map/ppermute | solution.py:302
  10.4 6.0 %collective-permute-start.2 = (bf16[64,512]{1,0:T(8,128)(2,1)}, bf16[64,512]{1,0:T(8,128)(2,1)S(1)}, u32[]{:S(2)}, u32[]{:S(2)}) collective-permute-start(bf16[64,512]{1,0:T(8,128)(2,1)} %get-tuple-element.12), channel_id=1, source_target_pairs={{0,16},{4,20},{8,24},{12,28},{16,0},{20,4},{24,8},{28,12},{32,48},... | collective-permute-start | bytes 196616 | tf_op jit(solution)/shard_map/ppermute | solution.py:302
  12.5 50.0 %collective-permute-start.16 = (bf16[128,1024]{1,0:T(8,128)(2,1)S(1)}, bf16[128,1024]{1,0:T(8,128)(2,1)S(1)}, u32[]{:S(2)}, u32[]{:S(2)}) collective-permute-start(bf16[128,1024]{1,0:T(8,128)(2,1)S(1)} %constant_dynamic-slice_fusion.refs_8_), channel_id=1, source_target_pairs={{0,1},{1,2},{2,3},{3,0},{4,5},{5,6},{6,7},{7,4},{8,9},{9,10},{10,1... | collective-permute-start | bytes 786440 | tf_op jit(solution)/shard_map/ppermute | solution.py:370
  17.3 21.4 %collective-permute-start.3 = (bf16[4,64,512]{2,1,0:T(8,128)(2,1)S(1)}, bf16[4,64,512]{2,1,0:T(8,128)(2,1)S(1)}, u32[]{:S(2)}, u32[]{:S(2)}) collective-permute-start(bf16[4,64,512]{2,1,0:T(8,128)(2,1)S(1)} %pad_maximum_fusion.1.rest_0_), channel_id=1, source_target_pairs={{0,32},{4,36},{8,40},{12,44},{16,48},{20,52},{24,56},{28,60},{32,6... | collective-permute-start | bytes 786440 | tf_op jit(solution)/shard_map/ppermute | solution.py:304
  19.3 19.6 %collective-permute-start.4 = (bf16[4,64,512]{2,1,0:T(8,128)(2,1)S(1)}, bf16[4,64,512]{2,1,0:T(8,128)(2,1)S(1)}, u32[]{:S(2)}, u32[]{:S(2)}) collective-permute-start(bf16[4,64,512]{2,1,0:T(8,128)(2,1)S(1)} %pad_maximum_fusion.1.rest_0_), channel_id=1, source_target_pairs={{0,96},{4,100},{8,104},{12,108},{16,112},{20,116},{24,120},{28,124... | collective-permute-start | bytes 786440 | tf_op jit(solution)/shard_map/ppermute | solution.py:304
  21.5 17.7 %collective-permute-start.5 = (bf16[4,64,512]{2,1,0:T(8,128)(2,1)S(1)}, bf16[4,64,512]{2,1,0:T(8,128)(2,1)}, u32[]{:S(2)}, u32[]{:S(2)}) collective-permute-start(bf16[4,64,512]{2,1,0:T(8,128)(2,1)S(1)} %pad_maximum_fusion.1.rest_0_), channel_id=1, source_target_pairs={{0,64},{4,68},{8,72},{12,76},{16,80},{20,84},{24,88},{28,92},{32,9... | collective-permute-start | bytes 786440 | tf_op jit(solution)/shard_map/ppermute | solution.py:304
  24.8 19.6 %all-to-all-start = ((bf16[32,48,256]{2,1,0:T(8,128)(2,1)}), bf16[32,48,256]{2,1,0:T(8,128)(2,1)S(1)}, u32[]{:S(2)}, u32[]{:S(2)}) async-start(bf16[32,48,256]{2,1,0:T(8,128)(2,1)} %bitcast.4), calls=%async_computation | async-start | bytes 1572864 | tf_op jit(solution)/shard_map/all_to_all | solution.py:321
  38.7 4.1 %collective-permute-start.7 = (bf16[4,64,512]{2,1,0:T(8,128)(2,1)S(1)}, bf16[4,64,512]{2,1,0:T(8,128)(2,1)}, u32[]{:S(2)}, u32[]{:S(2)}) collective-permute-start(bf16[4,64,512]{2,1,0:T(8,128)(2,1)S(1)} %collective-permute-done.3.rest_1_), channel_id=1, source_target_pairs={{0,4},{4,0},{8,12},{12,8},{16,20},{20,16},{24,28},{28,24},{32,36},... | collective-permute-start | bytes 786440 | tf_op jit(solution)/shard_map/ppermute | solution.py:343
  38.9 4.7 %collective-permute-start.8 = (bf16[4,64,512]{2,1,0:T(8,128)(2,1)S(1)}, bf16[4,64,512]{2,1,0:T(8,128)(2,1)S(1)}, u32[]{:S(2)}, u32[]{:S(2)}) collective-permute-start(bf16[4,64,512]{2,1,0:T(8,128)(2,1)S(1)} %collective-permute-done.4.rest_2_), channel_id=1, source_target_pairs={{0,4},{4,0},{8,12},{12,8},{16,20},{20,16},{24,28},{28,24},{32,36},... | collective-permute-start | bytes 786440 | tf_op jit(solution)/shard_map/ppermute | solution.py:343
  39.2 5.1 %collective-permute-start.9 = (bf16[4,64,512]{2,1,0:T(8,128)(2,1)}, bf16[4,64,512]{2,1,0:T(8,128)(2,1)}, u32[]{:S(2)}, u32[]{:S(2)}) collective-permute-start(bf16[4,64,512]{2,1,0:T(8,128)(2,1)} %collective-permute-done.5.rest_3_), channel_id=1, source_target_pairs={{0,4},{4,0},{8,12},{12,8},{16,20},{20,16},{24,28},{28,24},{32,36},... | collective-permute-start | bytes 786440 | tf_op jit(solution)/shard_map/ppermute | solution.py:343
  40.1 25.2 %collective-permute-start.17 = (bf16[128,1024]{1,0:T(8,128)(2,1)S(1)}, bf16[128,1024]{1,0:T(8,128)(2,1)S(1)}, u32[]{:S(2)}, u32[]{:S(2)}) collective-permute-start(bf16[128,1024]{1,0:T(8,128)(2,1)S(1)} %constant_dynamic-slice_fusion.refs_8_), channel_id=1, source_target_pairs={{0,3},{1,0},{2,1},{3,2},{4,7},{5,4},{6,5},{7,6},{8,11},{9,8},{10,9... | collective-permute-start | bytes 786440 | tf_op jit(solution)/shard_map/ppermute | solution.py:370
  42.8 22.5 %collective-permute-start.18 = (bf16[128,1024]{1,0:T(8,128)(2,1)S(1)}, bf16[128,1024]{1,0:T(8,128)(2,1)S(1)}, u32[]{:S(2)}, u32[]{:S(2)}) collective-permute-start(bf16[128,1024]{1,0:T(8,128)(2,1)S(1)} %constant_dynamic-slice_fusion.refs_8_), channel_id=1, source_target_pairs={{0,2},{1,3},{2,0},{3,1},{4,6},{5,7},{6,4},{7,5},{8,10},{9,11},{10,... | collective-permute-start | bytes 786440 | tf_op jit(solution)/shard_map/ppermute | solution.py:370
  43.6 22.2 %collective-permute-start.19 = (bf16[128,1024]{1,0:T(8,128)(2,1)S(1)}, bf16[128,1024]{1,0:T(8,128)(2,1)S(1)}, u32[]{:S(2)}, u32[]{:S(2)}) collective-permute-start(bf16[128,1024]{1,0:T(8,128)(2,1)S(1)} %constant_dynamic-slice_fusion.refs_8_), channel_id=1, source_target_pairs={{0,4},{4,0},{8,12},{12,8},{16,20},{20,16},{24,28},{28,24},{32,36},... | collective-permute-start | bytes 786440 | tf_op jit(solution)/shard_map/ppermute | solution.py:374
  53.8 22.2 %all-to-all-start.1 = ((bf16[32,48,256]{2,1,0:T(8,128)(2,1)}), bf16[32,48,256]{2,1,0:T(8,128)(2,1)}, u32[]{:S(2)}, u32[]{:S(2)}) async-start(bf16[32,48,256]{2,1,0:T(8,128)(2,1)} %far.1), calls=%async_computation.1 | async-start | bytes 1572864 | tf_op jit(solution)/shard_map/all_to_all | solution.py:321
  62.4 5.7 %collective-permute-start.20 = (bf16[128,1024]{1,0:T(8,128)(2,1)S(1)}, bf16[128,1024]{1,0:T(8,128)(2,1)S(1)}, u32[]{:S(2)}, u32[]{:S(2)}) collective-permute-start(bf16[128,1024]{1,0:T(8,128)(2,1)S(1)} %collective-permute-done.16.refs_9_), channel_id=1, source_target_pairs={{0,4},{4,0},{8,12},{12,8},{16,20},{20,16},{24,28},{28,24},{32,36},... | collective-permute-start | bytes 786440 | tf_op jit(solution)/shard_map/ppermute | solution.py:374
  64.3 18.2 %collective-permute-start.13 = (bf16[320,512]{1,0:T(8,128)(2,1)S(1)}, bf16[320,512]{1,0:T(8,128)(2,1)S(1)}, u32[]{:S(2)}, u32[]{:S(2)}) collective-permute-start(bf16[320,512]{1,0:T(8,128)(2,1)S(1)} %pad_maximum_fusion.refs_4_), channel_id=1, source_target_pairs={{0,1},{1,2},{2,3},{3,0},{4,5},{5,6},{6,7},{7,4},{8,9},{9,10},{10,1... | collective-permute-start | bytes 983048 | tf_op jit(solution)/shard_map/ppermute | solution.py:370
  65.3 12.3 %collective-permute-start.21 = (bf16[128,1024]{1,0:T(8,128)(2,1)S(1)}, bf16[128,1024]{1,0:T(8,128)(2,1)}, u32[]{:S(2)}, u32[]{:S(2)}) collective-permute-start(bf16[128,1024]{1,0:T(8,128)(2,1)S(1)} %collective-permute-done.17.refs_10_), channel_id=1, source_target_pairs={{0,4},{4,0},{8,12},{12,8},{16,20},{20,16},{24,28},{28,24},{32,36},... | collective-permute-start | bytes 786440 | tf_op jit(solution)/shard_map/ppermute | solution.py:374
  65.3 13.2 %collective-permute-start.22 = (bf16[128,1024]{1,0:T(8,128)(2,1)S(1)}, bf16[128,1024]{1,0:T(8,128)(2,1)}, u32[]{:S(2)}, u32[]{:S(2)}) collective-permute-start(bf16[128,1024]{1,0:T(8,128)(2,1)S(1)} %collective-permute-done.18.refs_11_), channel_id=1, source_target_pairs={{0,4},{4,0},{8,12},{12,8},{16,20},{20,16},{24,28},{28,24},{32,36},... | collective-permute-start | bytes 786440 | tf_op jit(solution)/shard_map/ppermute | solution.py:374
  65.8 18.3 %collective-permute-start.14 = (bf16[320,512]{1,0:T(8,128)(2,1)S(1)}, bf16[320,512]{1,0:T(8,128)(2,1)S(1)}, u32[]{:S(2)}, u32[]{:S(2)}) collective-permute-start(bf16[320,512]{1,0:T(8,128)(2,1)S(1)} %pad_maximum_fusion.refs_4_), channel_id=1, source_target_pairs={{0,3},{1,0},{2,1},{3,2},{4,7},{5,4},{6,5},{7,6},{8,11},{9,8},{10,9... | collective-permute-start | bytes 983048 | tf_op jit(solution)/shard_map/ppermute | solution.py:370
  68.2 15.9 %collective-permute-start.15 = (bf16[320,512]{1,0:T(8,128)(2,1)S(1)}, bf16[320,512]{1,0:T(8,128)(2,1)S(1)}, u32[]{:S(2)}, u32[]{:S(2)}) collective-permute-start(bf16[320,512]{1,0:T(8,128)(2,1)S(1)} %pad_maximum_fusion.refs_4_), channel_id=1, source_target_pairs={{0,2},{1,3},{2,0},{3,1},{4,6},{5,7},{6,4},{7,5},{8,10},{9,11},{10,... | collective-permute-start | bytes 983048 | tf_op jit(solution)/shard_map/ppermute | solution.py:370
  77.6 12.0 %collective-permute-start.10 = (bf16[320,256]{1,0:T(8,128)(2,1)S(1)}, bf16[320,256]{1,0:T(8,128)(2,1)S(1)}, u32[]{:S(2)}, u32[]{:S(2)}) collective-permute-start(bf16[320,256]{1,0:T(8,128)(2,1)S(1)} %fusion.4.refs_0_), channel_id=1, source_target_pairs={{0,1},{1,2},{2,3},{3,0},{4,5},{5,6},{6,7},{7,4},{8,9},{9,10},{10,1... | collective-permute-start | bytes 491528 | tf_op jit(solution)/shard_map/ppermute | solution.py:370
  78.6 11.0 %collective-permute-start.11 = (bf16[320,256]{1,0:T(8,128)(2,1)S(1)}, bf16[320,256]{1,0:T(8,128)(2,1)S(1)}, u32[]{:S(2)}, u32[]{:S(2)}) collective-permute-start(bf16[320,256]{1,0:T(8,128)(2,1)S(1)} %fusion.4.refs_0_), channel_id=1, source_target_pairs={{0,3},{1,0},{2,1},{3,2},{4,7},{5,4},{6,5},{7,6},{8,11},{9,8},{10,9... | collective-permute-start | bytes 491528 | tf_op jit(solution)/shard_map/ppermute | solution.py:370
  82.5 7.1 %collective-permute-start.12 = (bf16[320,256]{1,0:T(8,128)(2,1)S(1)}, bf16[320,256]{1,0:T(8,128)(2,1)S(1)}, u32[]{:S(2)}, u32[]{:S(2)}) collective-permute-start(bf16[320,256]{1,0:T(8,128)(2,1)S(1)} %fusion.4.refs_0_), channel_id=1, source_target_pairs={{0,2},{1,3},{2,0},{3,1},{4,6},{5,7},{6,4},{7,5},{8,10},{9,11},{10,... | collective-permute-start | bytes 491528 | tf_op jit(solution)/shard_map/ppermute | solution.py:370
  (12 other events, 122.3 us)

commit v7 on v6

--- a/solution.py
+++ b/solution.py
@@ -356,11 +356,12 @@
             pltpu.VMEM(pack.shape, BF),
             pltpu.SemaphoreType.DMA((12,)),
         ],
-        compiler_params=params(60),
+        compiler_params=params(50),
         cost_estimate=pl.CostEstimate(flops=4 * 10**9, bytes_accessed=4 * 10**6, transcendentals=3 * 10**6),
         name="far",
     )(q, near, pattern, pack, tok_got, *parts)
     tok_own = arrange(tok_got)
+    packed, w_out = lax.optimization_barrier((packed, w_out))
     att = arrange(deliver(packed))
 
     def to(d):

time: 96.4 us -> 106 us (1.100); the launches traced: 94.9 us -> 106 us
  waiting for transfers between devices: 14.3 us -> 31.1 us
  starting transfers between devices: 40.7 us -> 35.8 us
    ppermute x9, waiting for transfers between devices: 7.11 us -> 25.6 us  [over_heads(): return [x] + [lax.ppermute(x, 'head', to(d)) for d in DISTANCES[1:]]]
    all_to_all x2, waiting for transfers between devices: 6.33 us -> 3.11 us  [deliver(): return lax.all_to_all(packed, 'tm', 0, 0, tiled=True)]
    all_to_all x2, starting transfers between devices: 12.5 us -> 9.59 us  [deliver(): return lax.all_to_all(packed, 'tm', 0, 0, tiled=True)]
    ppermute x3, waiting for transfers between devices: 0.24 us -> 2.29 us  [body(): lax.ppermute(mine, 'tm', along_y(d))]
    ppermute x9, starting transfers between devices: 14.8 us -> 13 us  [over_heads(): return [x] + [lax.ppermute(x, 'head', to(d)) for d in DISTANCES[1:]]]
    dot_general x2, matrix products: 3.12 us -> 1.99 us  [arrange(): jnp.dot(unpack, got.reshape(n_peers * CAP, -1), preferred_element_type=F32)]
  transfers between devices with their start and end apart: 25 -> 25, of which waited for: 5 -> 9; matrix products, arithmetic and copies ran while one was open for 9% -> 7% of each run, Pallas kernels for 18% -> 8%
where the time goes in v7:
time: 106 us
  starting transfers between devices  35.8 us (34%)
  waiting for transfers between devices  31.1 us (29%)
  Pallas kernels  28 us (26%)
  matrix products  4.53 us (4%)
  other arithmetic  4.12 us (4%)
  local copies, waits for them, and re-layouts  1.23 us (1%)
    ppermute x9, waiting for transfers between devices, over_heads(): return [x] + [lax.ppermute(x, 'head', to(d)) for d in DISTANCES[1:]]  25.6 us
    ppermute x9, starting transfers between devices, over_heads(): return [x] + [lax.ppermute(x, 'head', to(d)) for d in DISTANCES[1:]]  13 us
    all_to_all x2, starting transfers between devices, deliver(): return lax.all_to_all(packed, 'tm', 0, 0, tiled=True)  9.59 us
    pallas_call x1, Pallas kernels, body(): pl.pallas_call(near_kernel, in_specs=[HBM] * 4, out_specs=pl.BlockSpec(me...  8.69 us
    pallas_call x1, Pallas kernels, body(): pl.pallas_call(far_kernel, in_specs=[HBM] * 13, out_specs=pl.BlockSpec(me...  8.24 us
    pallas_call x1, Pallas kernels, body(): pl.pallas_call(gather_kernel, in_specs=[HBM] * 4 + whole(3), out_specs=wh...  6.39 us
    ppermute x3, starting transfers between devices, body(): lax.ppermute(plane, 'tm', along_z(d))  6.07 us
    ppermute x3, starting transfers between devices, body(): lax.ppermute(mine, 'tm', along_y(d))  5.39 us
  transfers between devices with their start and end apart: 25, of which 9 were waited for; matrix products, arithmetic and copies ran while one was open for 7% of the time, Pallas kernels for 8%

profile of v7, /device:TPU:0, one launch (start us, length us, event | category | flops | bytes accessed | tf_op | source)
XLA Modules:
  0.0 105.6 jit_solution(8451649201829204043)
XLA Ops:
  0.7 6.4 %gather.1 = (bf16[64,512]{1,0:T(8,128)(2,1)}, bf16[320,256]{1,0:T(8,128)(2,1)}, bf16[384,256]{1,0:T(8,128)(2,1)}) custom-call(bf16[3136,1024]{1,0:T(8,128)(2,1)} %x_hbm.3, bf16[1024,256]{1,0:T(8,128)(2,1)} %wq_hbm.1, bf16[1024,256]{1,0:T(8,128)(2,1)} %wk_hbm.3, bf16[1024,256]{1,0:T(8,128)(2,1)} %wv_hbm.3, bf16[16,784]{1,0:T(8,128)(2,1)} %constant.62.clone.pool_ref, ...), custom_call_target="tpu_custom_call" | custom-call | flops 2000000000 | bytes 10000000 | tf_op jit(solution)/shard_map/gather/pallas_call | solution.py:285
  7.1 1.7 %collective-permute-start = (bf16[64,512]{1,0:T(8,128)(2,1)}, bf16[64,512]{1,0:T(8,128)(2,1)S(1)}, u32[]{:S(2)}, u32[]{:S(2)}) collective-permute-start(bf16[64,512]{1,0:T(8,128)(2,1)} %get-tuple-element.14), channel_id=1, source_target_pairs={{0,8},{4,12},{8,16},{12,20},{16,24},{20,28},{24,0},{28,4},{32,40},... | collective-permute-start | bytes 196616 | tf_op jit(solution)/shard_map/ppermute | solution.py:302
  8.8 1.6 %collective-permute-start.1 = (bf16[64,512]{1,0:T(8,128)(2,1)}, bf16[64,512]{1,0:T(8,128)(2,1)S(1)}, u32[]{:S(2)}, u32[]{:S(2)}) collective-permute-start(bf16[64,512]{1,0:T(8,128)(2,1)} %get-tuple-element.14), channel_id=1, source_target_pairs={{0,24},{4,28},{8,0},{12,4},{16,8},{20,12},{24,16},{28,20},{32,56},... | collective-permute-start | bytes 196616 | tf_op jit(solution)/shard_map/ppermute | solution.py:302
  10.4 2.1 %collective-permute-start.2 = (bf16[64,512]{1,0:T(8,128)(2,1)}, bf16[64,512]{1,0:T(8,128)(2,1)S(1)}, u32[]{:S(2)}, u32[]{:S(2)}) collective-permute-start(bf16[64,512]{1,0:T(8,128)(2,1)} %get-tuple-element.14), channel_id=1, source_target_pairs={{0,16},{4,20},{8,24},{12,28},{16,0},{20,4},{24,8},{28,12},{32,48},... | collective-permute-start | bytes 196616 | tf_op jit(solution)/shard_map/ppermute | solution.py:302
  14.1 2.3 %collective-permute-done.2 = bf16[64,512]{1,0:T(8,128)(2,1)S(1)} collective-permute-done((bf16[64,512]{1,0:T(8,128)(2,1)}, bf16[64,512]{1,0:T(8,128)(2,1)S(1)}, u32[]{:S(2)}, u32[]{:S(2)}) %collective-permute-start.2) | collective-permute-done | bytes 65568 | tf_op jit(solution)/shard_map/ppermute | solution.py:302
  17.2 2.1 %collective-permute-start.3 = (bf16[4,64,512]{2,1,0:T(8,128)(2,1)S(1)}, bf16[4,64,512]{2,1,0:T(8,128)(2,1)S(1)}, u32[]{:S(2)}, u32[]{:S(2)}) collective-permute-start(bf16[4,64,512]{2,1,0:T(8,128)(2,1)S(1)} %pad_maximum_fusion.1.rest_0_), channel_id=1, source_target_pairs={{0,32},{4,36},{8,40},{12,44},{16,48},{20,52},{24,56},{28,60},{32,6... | collective-permute-start | bytes 786440 | tf_op jit(solution)/shard_map/ppermute | solution.py:304
  19.3 2.2 %collective-permute-start.4 = (bf16[4,64,512]{2,1,0:T(8,128)(2,1)S(1)}, bf16[4,64,512]{2,1,0:T(8,128)(2,1)S(1)}, u32[]{:S(2)}, u32[]{:S(2)}) collective-permute-start(bf16[4,64,512]{2,1,0:T(8,128)(2,1)S(1)} %pad_maximum_fusion.1.rest_0_), channel_id=1, source_target_pairs={{0,96},{4,100},{8,104},{12,108},{16,112},{20,116},{24,120},{28,124... | collective-permute-start | bytes 786440 | tf_op jit(solution)/shard_map/ppermute | solution.py:304
  21.5 1.8 %collective-permute-start.5 = (bf16[4,64,512]{2,1,0:T(8,128)(2,1)S(1)}, bf16[4,64,512]{2,1,0:T(8,128)(2,1)S(1)}, u32[]{:S(2)}, u32[]{:S(2)}) collective-permute-start(bf16[4,64,512]{2,1,0:T(8,128)(2,1)S(1)} %pad_maximum_fusion.1.rest_0_), channel_id=1, source_target_pairs={{0,64},{4,68},{8,72},{12,76},{16,80},{20,84},{24,88},{28,92},{32,9... | collective-permute-start | bytes 786440 | tf_op jit(solution)/shard_map/ppermute | solution.py:304
  23.3 2.4 %convolution_convert_fusion = bf16[1536,256]{1,0:T(8,128)(2,1)} fusion(bf16[384,256]{1,0:T(8,128)(2,1)} %get-tuple-element.20, s32[384]{0:T(512)S(1)} %pad.4), kind=kOutput, calls=%fused_computation | convolution fusion | flops 302972928 | bytes 984576 | tf_op jit(solution)/shard_map/dot_general | solution.py:326
  25.7 4.8 %all-to-all-start = ((bf16[32,48,256]{2,1,0:T(8,128)(2,1)}), bf16[32,48,256]{2,1,0:T(8,128)(2,1)S(1)}, u32[]{:S(2)}, u32[]{:S(2)}) async-start(bf16[32,48,256]{2,1,0:T(8,128)(2,1)} %bitcast.4), calls=%async_computation | async-start | bytes 1572864 | tf_op jit(solution)/shard_map/all_to_all | solution.py:321
  30.5 8.7 %near.1.near_hbm = bf16[1280,384]{1,0:T(8,128)(2,1)} custom-call(bf16[320,256]{1,0:T(8,128)(2,1)} %get-tuple-element.17.q_hbm, bf16[3136,1024]{1,0:T(8,128)(2,1)} %x_hbm.3, bf16[1024,256]{1,0:T(8,128)(2,1)} %wk_hbm.3, bf16[1024,256]{1,0:T(8,128)(2,1)} %wv_hbm.3), custom_call_target="tpu_custom_call" | custom-call | flops 5000000000 | bytes 10000000 | tf_op jit(solution)/shard_map/near/pallas_call | solution.py:329
  42.0 3.1 %all-to-all-done._ = bf16[32,48,256]{2,1,0:T(8,128)(2,1)S(1)} async-done(((bf16[32,48,256]{2,1,0:T(8,128)(2,1)}), bf16[32,48,256]{2,1,0:T(8,128)(2,1)S(1)}, u32[]{:S(2)}, u32[]{:S(2)}) %all-to-all-start) | async-done | bytes 786464 | tf_op jit(solution)/shard_map/all_to_all | solution.py:321
  46.0 8.2 %far.1 = bf16[32,48,256]{2,1,0:T(8,128)(2,1)} custom-call(bf16[320,256]{1,0:T(8,128)(2,1)S(1)} %copy-done.1, bf16[1280,384]{1,0:T(8,128)(2,1)} %near.1.near_hbm, s32[16,512]{1,0:T(8,128)S(1)} %copy-done.2, bf16[1536,384]{1,0:T(8,128)(2,1)} %fusion.pack_hbm, bf16[32,48,256]{2,1,0:T(8,128)(2,1)S(1)} %all-to-all-done._, ...), custom_call_target="tpu_custom_call" | custom-call | flops 4000000000 | bytes 4000000 | tf_op jit(solution)/shard_map/far/pallas_call | solution.py:344
  54.3 4.8 %all-to-all-start.1 = ((bf16[32,48,256]{2,1,0:T(8,128)(2,1)}), bf16[32,48,256]{2,1,0:T(8,128)(2,1)}, u32[]{:S(2)}, u32[]{:S(2)}) async-start(bf16[32,48,256]{2,1,0:T(8,128)(2,1)} %far.1), calls=%async_computation.1 | async-start | bytes 1572864 | tf_op jit(solution)/shard_map/all_to_all | solution.py:321
  60.7 1.7 %collective-permute-start.17 = (bf16[128,1024]{1,0:T(8,128)(2,1)S(1)}, bf16[128,1024]{1,0:T(8,128)(2,1)S(1)}, u32[]{:S(2)}, u32[]{:S(2)}) collective-permute-start(bf16[128,1024]{1,0:T(8,128)(2,1)S(1)} %constant_dynamic-slice_fusion.refs_8_), channel_id=1, source_target_pairs={{0,3},{1,0},{2,1},{3,2},{4,7},{5,4},{6,5},{7,6},{8,11},{9,8},{10,9... | collective-permute-start | bytes 786440 | tf_op jit(solution)/shard_map/ppermute | solution.py:371
  63.2 2.7 %collective-permute-start.18 = (bf16[128,1024]{1,0:T(8,128)(2,1)S(1)}, bf16[128,1024]{1,0:T(8,128)(2,1)S(1)}, u32[]{:S(2)}, u32[]{:S(2)}) collective-permute-start(bf16[128,1024]{1,0:T(8,128)(2,1)S(1)} %constant_dynamic-slice_fusion.refs_8_), channel_id=1, source_target_pairs={{0,2},{1,3},{2,0},{3,1},{4,6},{5,7},{6,4},{7,5},{8,10},{9,11},{10,... | collective-permute-start | bytes 786440 | tf_op jit(solution)/shard_map/ppermute | solution.py:371
  65.9 3.6 %collective-permute-done.16.refs_9_ = bf16[128,1024]{1,0:T(8,128)(2,1)S(1)} collective-permute-done((bf16[128,1024]{1,0:T(8,128)(2,1)S(1)}, bf16[128,1024]{1,0:T(8,128)(2,1)S(1)}, u32[]{:S(2)}, u32[]{:S(2)}) %collective-permute-start.16) | collective-permute-done | bytes 262176 | tf_op jit(solution)/shard_map/ppermute | solution.py:371
  72.6 10.6 %collective-permute-done.18.refs_11_ = bf16[128,1024]{1,0:T(8,128)(2,1)S(1)} collective-permute-done((bf16[128,1024]{1,0:T(8,128)(2,1)S(1)}, bf16[128,1024]{1,0:T(8,128)(2,1)S(1)}, u32[]{:S(2)}, u32[]{:S(2)}) %collective-permute-start.18) | collective-permute-done | bytes 262176 | tf_op jit(solution)/shard_map/ppermute | solution.py:371
  85.4 3.9 %collective-permute-done.15.refs_7_ = bf16[320,512]{1,0:T(8,128)(2,1)S(1)} collective-permute-done((bf16[320,512]{1,0:T(8,128)(2,1)S(1)}, bf16[320,512]{1,0:T(8,128)(2,1)S(1)}, u32[]{:S(2)}, u32[]{:S(2)}) %collective-permute-start.15) | collective-permute-done | bytes 327712 | tf_op jit(solution)/shard_map/ppermute | solution.py:371
  89.3 2.0 %collective-permute-start.11 = (bf16[320,256]{1,0:T(8,128)(2,1)S(1)}, bf16[320,256]{1,0:T(8,128)(2,1)S(1)}, u32[]{:S(2)}, u32[]{:S(2)}) collective-permute-start(bf16[320,256]{1,0:T(8,128)(2,1)S(1)} %fusion.4.refs_0_), channel_id=1, source_target_pairs={{0,3},{1,0},{2,1},{3,2},{4,7},{5,4},{6,5},{7,6},{8,11},{9,8},{10,9... | collective-permute-start | bytes 491528 | tf_op jit(solution)/shard_map/ppermute | solution.py:371
  92.9 2.8 %collective-permute-done.10.refs_1_ = bf16[320,256]{1,0:T(8,128)(2,1)S(1)} collective-permute-done((bf16[320,256]{1,0:T(8,128)(2,1)S(1)}, bf16[320,256]{1,0:T(8,128)(2,1)S(1)}, u32[]{:S(2)}, u32[]{:S(2)}) %collective-permute-start.10) | collective-permute-done | bytes 163872 | tf_op jit(solution)/shard_map/ppermute | solution.py:371
  95.7 2.8 %collective-permute-done.11.refs_2_ = bf16[320,256]{1,0:T(8,128)(2,1)S(1)} collective-permute-done((bf16[320,256]{1,0:T(8,128)(2,1)S(1)}, bf16[320,256]{1,0:T(8,128)(2,1)S(1)}, u32[]{:S(2)}, u32[]{:S(2)}) %collective-permute-start.11) | collective-permute-done | bytes 163872 | tf_op jit(solution)/shard_map/ppermute | solution.py:371
  98.5 1.9 %collective-permute-done.12.refs_3_ = bf16[320,256]{1,0:T(8,128)(2,1)S(1)} collective-permute-done((bf16[320,256]{1,0:T(8,128)(2,1)S(1)}, bf16[320,256]{1,0:T(8,128)(2,1)S(1)}, u32[]{:S(2)}, u32[]{:S(2)}) %collective-permute-start.12) | collective-permute-done | bytes 163872 | tf_op jit(solution)/shard_map/ppermute | solution.py:371
  100.3 4.7 %final.1 = (bf16[320,256]{1,0:T(8,128)(2,1)}, f32[1,320]{1,0:T(1,128)S(1)}) custom-call(bf16[320,256]{1,0:T(8,128)(2,1)S(1)} %fusion.4.refs_0_, bf16[320,256]{1,0:T(8,128)(2,1)S(1)} %collective-permute-done.10.refs_1_, bf16[320,256]{1,0:T(8,128)(2,1)S(1)} %collective-permute-done.11.refs_2_, bf16[320,256]{1,0:T(8,128)(2,1)S(1)} %collective-permute-done.12.refs_3_, ...), custom_call_target="tpu_custom_call" | custom-call | flops 1000000000 | bytes 4000000 | tf_op jit(solution)/shard_map/final/pallas_call | solution.py:378
  (63 shorter events, 15.9 us)
Async XLA Ops:
  7.1 7.0 %collective-permute-start = (bf16[64,512]{1,0:T(8,128)(2,1)}, bf16[64,512]{1,0:T(8,128)(2,1)S(1)}, u32[]{:S(2)}, u32[]{:S(2)}) collective-permute-start(bf16[64,512]{1,0:T(8,128)(2,1)} %get-tuple-element.14), channel_id=1, source_target_pairs={{0,8},{4,12},{8,16},{12,20},{16,24},{20,28},{24,0},{28,4},{32,40},... | collective-permute-start | bytes 196616 | tf_op jit(solution)/shard_map/ppermute | solution.py:302
  8.8 5.3 %collective-permute-start.1 = (bf16[64,512]{1,0:T(8,128)(2,1)}, bf16[64,512]{1,0:T(8,128)(2,1)S(1)}, u32[]{:S(2)}, u32[]{:S(2)}) collective-permute-start(bf16[64,512]{1,0:T(8,128)(2,1)} %get-tuple-element.14), channel_id=1, source_target_pairs={{0,24},{4,28},{8,0},{12,4},{16,8},{20,12},{24,16},{28,20},{32,56},... | collective-permute-start | bytes 196616 | tf_op jit(solution)/shard_map/ppermute | solution.py:302
  10.4 6.0 %collective-permute-start.2 = (bf16[64,512]{1,0:T(8,128)(2,1)}, bf16[64,512]{1,0:T(8,128)(2,1)S(1)}, u32[]{:S(2)}, u32[]{:S(2)}) collective-permute-start(bf16[64,512]{1,0:T(8,128)(2,1)} %get-tuple-element.14), channel_id=1, source_target_pairs={{0,16},{4,20},{8,24},{12,28},{16,0},{20,4},{24,8},{28,12},{32,48},... | collective-permute-start | bytes 196616 | tf_op jit(solution)/shard_map/ppermute | solution.py:302
  17.2 22.3 %collective-permute-start.3 = (bf16[4,64,512]{2,1,0:T(8,128)(2,1)S(1)}, bf16[4,64,512]{2,1,0:T(8,128)(2,1)S(1)}, u32[]{:S(2)}, u32[]{:S(2)}) collective-permute-start(bf16[4,64,512]{2,1,0:T(8,128)(2,1)S(1)} %pad_maximum_fusion.1.rest_0_), channel_id=1, source_target_pairs={{0,32},{4,36},{8,40},{12,44},{16,48},{20,52},{24,56},{28,60},{32,6... | collective-permute-start | bytes 786440 | tf_op jit(solution)/shard_map/ppermute | solution.py:304
  19.3 20.5 %collective-permute-start.4 = (bf16[4,64,512]{2,1,0:T(8,128)(2,1)S(1)}, bf16[4,64,512]{2,1,0:T(8,128)(2,1)S(1)}, u32[]{:S(2)}, u32[]{:S(2)}) collective-permute-start(bf16[4,64,512]{2,1,0:T(8,128)(2,1)S(1)} %pad_maximum_fusion.1.rest_0_), channel_id=1, source_target_pairs={{0,96},{4,100},{8,104},{12,108},{16,112},{20,116},{24,120},{28,124... | collective-permute-start | bytes 786440 | tf_op jit(solution)/shard_map/ppermute | solution.py:304
  21.5 18.6 %collective-permute-start.5 = (bf16[4,64,512]{2,1,0:T(8,128)(2,1)S(1)}, bf16[4,64,512]{2,1,0:T(8,128)(2,1)S(1)}, u32[]{:S(2)}, u32[]{:S(2)}) collective-permute-start(bf16[4,64,512]{2,1,0:T(8,128)(2,1)S(1)} %pad_maximum_fusion.1.rest_0_), channel_id=1, source_target_pairs={{0,64},{4,68},{8,72},{12,76},{16,80},{20,84},{24,88},{28,92},{32,9... | collective-permute-start | bytes 786440 | tf_op jit(solution)/shard_map/ppermute | solution.py:304
  25.7 19.4 %all-to-all-start = ((bf16[32,48,256]{2,1,0:T(8,128)(2,1)}), bf16[32,48,256]{2,1,0:T(8,128)(2,1)S(1)}, u32[]{:S(2)}, u32[]{:S(2)}) async-start(bf16[32,48,256]{2,1,0:T(8,128)(2,1)} %bitcast.4), calls=%async_computation | async-start | bytes 1572864 | tf_op jit(solution)/shard_map/all_to_all | solution.py:321
  39.2 2.6 %collective-permute-start.6 = (bf16[4,64,512]{2,1,0:T(8,128)(2,1)S(1)}, bf16[4,64,512]{2,1,0:T(8,128)(2,1)S(1)}, u32[]{:S(2)}, u32[]{:S(2)}) collective-permute-start(bf16[4,64,512]{2,1,0:T(8,128)(2,1)S(1)} %pad_maximum_fusion.1.rest_0_), channel_id=1, source_target_pairs={{0,4},{4,0},{8,12},{12,8},{16,20},{20,16},{24,28},{28,24},{32,36},... | collective-permute-start | bytes 786440 | tf_op jit(solution)/shard_map/ppermute | solution.py:343
  39.6 2.3 %collective-permute-start.7 = (bf16[4,64,512]{2,1,0:T(8,128)(2,1)S(1)}, bf16[4,64,512]{2,1,0:T(8,128)(2,1)S(1)}, u32[]{:S(2)}, u32[]{:S(2)}) collective-permute-start(bf16[4,64,512]{2,1,0:T(8,128)(2,1)S(1)} %collective-permute-done.3.rest_1_), channel_id=1, source_target_pairs={{0,4},{4,0},{8,12},{12,8},{16,20},{20,16},{24,28},{28,24},{32,36},... | collective-permute-start | bytes 786440 | tf_op jit(solution)/shard_map/ppermute | solution.py:343
  39.8 2.1 %collective-permute-start.8 = (bf16[4,64,512]{2,1,0:T(8,128)(2,1)S(1)}, bf16[4,64,512]{2,1,0:T(8,128)(2,1)S(1)}, u32[]{:S(2)}, u32[]{:S(2)}) collective-permute-start(bf16[4,64,512]{2,1,0:T(8,128)(2,1)S(1)} %collective-permute-done.4.rest_2_), channel_id=1, source_target_pairs={{0,4},{4,0},{8,12},{12,8},{16,20},{20,16},{24,28},{28,24},{32,36},... | collective-permute-start | bytes 786440 | tf_op jit(solution)/shard_map/ppermute | solution.py:343
  54.3 29.5 %all-to-all-start.1 = ((bf16[32,48,256]{2,1,0:T(8,128)(2,1)}), bf16[32,48,256]{2,1,0:T(8,128)(2,1)}, u32[]{:S(2)}, u32[]{:S(2)}) async-start(bf16[32,48,256]{2,1,0:T(8,128)(2,1)} %far.1), calls=%async_computation.1 | async-start | bytes 1572864 | tf_op jit(solution)/shard_map/all_to_all | solution.py:321
  59.1 10.4 %collective-permute-start.16 = (bf16[128,1024]{1,0:T(8,128)(2,1)S(1)}, bf16[128,1024]{1,0:T(8,128)(2,1)S(1)}, u32[]{:S(2)}, u32[]{:S(2)}) collective-permute-start(bf16[128,1024]{1,0:T(8,128)(2,1)S(1)} %constant_dynamic-slice_fusion.refs_8_), channel_id=1, source_target_pairs={{0,1},{1,2},{2,3},{3,0},{4,5},{5,6},{6,7},{7,4},{8,9},{9,10},{10,1... | collective-permute-start | bytes 786440 | tf_op jit(solution)/shard_map/ppermute | solution.py:371
  60.7 10.4 %collective-permute-start.17 = (bf16[128,1024]{1,0:T(8,128)(2,1)S(1)}, bf16[128,1024]{1,0:T(8,128)(2,1)S(1)}, u32[]{:S(2)}, u32[]{:S(2)}) collective-permute-start(bf16[128,1024]{1,0:T(8,128)(2,1)S(1)} %constant_dynamic-slice_fusion.refs_8_), channel_id=1, source_target_pairs={{0,3},{1,0},{2,1},{3,2},{4,7},{5,4},{6,5},{7,6},{8,11},{9,8},{10,9... | collective-permute-start | bytes 786440 | tf_op jit(solution)/shard_map/ppermute | solution.py:371
  62.9 20.8 %collective-permute-start.13 = (bf16[320,512]{1,0:T(8,128)(2,1)S(1)}, bf16[320,512]{1,0:T(8,128)(2,1)S(1)}, u32[]{:S(2)}, u32[]{:S(2)}) collective-permute-start(bf16[320,512]{1,0:T(8,128)(2,1)S(1)} %pad_maximum_fusion.refs_4_), channel_id=1, source_target_pairs={{0,1},{1,2},{2,3},{3,0},{4,5},{5,6},{6,7},{7,4},{8,9},{9,10},{10,1... | collective-permute-start | bytes 983048 | tf_op jit(solution)/shard_map/ppermute | solution.py:371
  63.2 19.9 %collective-permute-start.18 = (bf16[128,1024]{1,0:T(8,128)(2,1)S(1)}, bf16[128,1024]{1,0:T(8,128)(2,1)S(1)}, u32[]{:S(2)}, u32[]{:S(2)}) collective-permute-start(bf16[128,1024]{1,0:T(8,128)(2,1)S(1)} %constant_dynamic-slice_fusion.refs_8_), channel_id=1, source_target_pairs={{0,2},{1,3},{2,0},{3,1},{4,6},{5,7},{6,4},{7,5},{8,10},{9,11},{10,... | collective-permute-start | bytes 786440 | tf_op jit(solution)/shard_map/ppermute | solution.py:371
  65.9 17.2 %collective-permute-start.19 = (bf16[128,1024]{1,0:T(8,128)(2,1)S(1)}, bf16[128,1024]{1,0:T(8,128)(2,1)S(1)}, u32[]{:S(2)}, u32[]{:S(2)}) collective-permute-start(bf16[128,1024]{1,0:T(8,128)(2,1)S(1)} %constant_dynamic-slice_fusion.refs_8_), channel_id=1, source_target_pairs={{0,4},{4,0},{8,12},{12,8},{16,20},{20,16},{24,28},{28,24},{32,36},... | collective-permute-start | bytes 786440 | tf_op jit(solution)/shard_map/ppermute | solution.py:375
  69.5 15.8 %collective-permute-start.14 = (bf16[320,512]{1,0:T(8,128)(2,1)S(1)}, bf16[320,512]{1,0:T(8,128)(2,1)S(1)}, u32[]{:S(2)}, u32[]{:S(2)}) collective-permute-start(bf16[320,512]{1,0:T(8,128)(2,1)S(1)} %pad_maximum_fusion.refs_4_), channel_id=1, source_target_pairs={{0,3},{1,0},{2,1},{3,2},{4,7},{5,4},{6,5},{7,6},{8,11},{9,8},{10,9... | collective-permute-start | bytes 983048 | tf_op jit(solution)/shard_map/ppermute | solution.py:371
  71.1 18.2 %collective-permute-start.15 = (bf16[320,512]{1,0:T(8,128)(2,1)S(1)}, bf16[320,512]{1,0:T(8,128)(2,1)S(1)}, u32[]{:S(2)}, u32[]{:S(2)}) collective-permute-start(bf16[320,512]{1,0:T(8,128)(2,1)S(1)} %pad_maximum_fusion.refs_4_), channel_id=1, source_target_pairs={{0,2},{1,3},{2,0},{3,1},{4,6},{5,7},{6,4},{7,5},{8,10},{9,11},{10,... | collective-permute-start | bytes 983048 | tf_op jit(solution)/shard_map/ppermute | solution.py:371
  83.1 8.2 %collective-permute-start.20 = (bf16[128,1024]{1,0:T(8,128)(2,1)S(1)}, bf16[128,1024]{1,0:T(8,128)(2,1)S(1)}, u32[]{:S(2)}, u32[]{:S(2)}) collective-permute-start(bf16[128,1024]{1,0:T(8,128)(2,1)S(1)} %collective-permute-done.16.refs_9_), channel_id=1, source_target_pairs={{0,4},{4,0},{8,12},{12,8},{16,20},{20,16},{24,28},{28,24},{32,36},... | collective-permute-start | bytes 786440 | tf_op jit(solution)/shard_map/ppermute | solution.py:375
  83.2 9.7 %collective-permute-start.21 = (bf16[128,1024]{1,0:T(8,128)(2,1)S(1)}, bf16[128,1024]{1,0:T(8,128)(2,1)}, u32[]{:S(2)}, u32[]{:S(2)}) collective-permute-start(bf16[128,1024]{1,0:T(8,128)(2,1)S(1)} %collective-permute-done.17.refs_10_), channel_id=1, source_target_pairs={{0,4},{4,0},{8,12},{12,8},{16,20},{20,16},{24,28},{28,24},{32,36},... | collective-permute-start | bytes 786440 | tf_op jit(solution)/shard_map/ppermute | solution.py:375
  83.7 9.2 %collective-permute-start.22 = (bf16[128,1024]{1,0:T(8,128)(2,1)S(1)}, bf16[128,1024]{1,0:T(8,128)(2,1)}, u32[]{:S(2)}, u32[]{:S(2)}) collective-permute-start(bf16[128,1024]{1,0:T(8,128)(2,1)S(1)} %collective-permute-done.18.refs_11_), channel_id=1, source_target_pairs={{0,4},{4,0},{8,12},{12,8},{16,20},{20,16},{24,28},{28,24},{32,36},... | collective-permute-start | bytes 786440 | tf_op jit(solution)/shard_map/ppermute | solution.py:375
  85.3 10.3 %collective-permute-start.10 = (bf16[320,256]{1,0:T(8,128)(2,1)S(1)}, bf16[320,256]{1,0:T(8,128)(2,1)S(1)}, u32[]{:S(2)}, u32[]{:S(2)}) collective-permute-start(bf16[320,256]{1,0:T(8,128)(2,1)S(1)} %fusion.4.refs_0_), channel_id=1, source_target_pairs={{0,1},{1,2},{2,3},{3,0},{4,5},{5,6},{6,7},{7,4},{8,9},{9,10},{10,1... | collective-permute-start | bytes 491528 | tf_op jit(solution)/shard_map/ppermute | solution.py:371
  89.3 9.1 %collective-permute-start.11 = (bf16[320,256]{1,0:T(8,128)(2,1)S(1)}, bf16[320,256]{1,0:T(8,128)(2,1)S(1)}, u32[]{:S(2)}, u32[]{:S(2)}) collective-permute-start(bf16[320,256]{1,0:T(8,128)(2,1)S(1)} %fusion.4.refs_0_), channel_id=1, source_target_pairs={{0,3},{1,0},{2,1},{3,2},{4,7},{5,4},{6,5},{7,6},{8,11},{9,8},{10,9... | collective-permute-start | bytes 491528 | tf_op jit(solution)/shard_map/ppermute | solution.py:371
  91.3 9.0 %collective-permute-start.12 = (bf16[320,256]{1,0:T(8,128)(2,1)S(1)}, bf16[320,256]{1,0:T(8,128)(2,1)S(1)}, u32[]{:S(2)}, u32[]{:S(2)}) collective-permute-start(bf16[320,256]{1,0:T(8,128)(2,1)S(1)} %fusion.4.refs_0_), channel_id=1, source_target_pairs={{0,2},{1,3},{2,0},{3,1},{4,6},{5,7},{6,4},{7,5},{8,10},{9,11},{10,... | collective-permute-start | bytes 491528 | tf_op jit(solution)/shard_map/ppermute | solution.py:371
  (8 other events, 120.6 us)

commit v8 on v6

--- a/solution.py
+++ b/solution.py
@@ -197,24 +197,21 @@
 
 
 def final_kernel(*refs):
-    sources, (target_ref, loss_ref, att, side, wo, raw, sem) = refs[:16], refs[16:]
+    att, side, sources, (target_ref, loss_ref, wo, raw, sem) = refs[:4], refs[4:8], refs[8:16], refs[16:]
     head, core = lax.axis_index("head"), lax.axis_index("tm") & 1
-    rows, cols = att.shape[1:]
+    rows, cols = att[0].shape
     half = cols // 2
     width = raw.shape[1]
     here = pl.ds(pl.multiple_of(core * half, 128), half)
     there = pl.ds(pl.multiple_of((1 - core) * half, 128), half)
-    targets = [att.at[i] for i in range(4)] + [side.at[i] for i in range(4)]
-    targets += [wo.at[i, here] for i in range(4)] + [wo.at[i, there] for i in range(4)]
+    targets = [wo.at[i, here] for i in range(4)] + [wo.at[i, there] for i in range(4)]
     copies = fetch(list(zip(sources, targets)), sem)
-    for copy in copies[:4] + copies[8:]:
+    for copy in copies:
         copy.wait()
-    raw[...] = sum(nn(att[i], wo[i]) for i in range(4))
+    raw[...] = sum(nn(att[i][...], wo[i]) for i in range(4))
     spots = [pl.ds(pl.multiple_of(lax.rem(head + 4 - d, 4) * cols, 128), cols) for d in DISTANCES]
-    for copy in copies[4:8]:
-        copy.wait()
     for i in range(4):
-        raw[:, spots[i]] += side[i, :, :cols].astype(F32)
+        raw[:, spots[i]] += side[i][:, :cols].astype(F32)
     full = raw[...]
     mean = jnp.sum(full, axis=1, keepdims=True) / width
     var = jnp.sum(full * full, axis=1, keepdims=True) / width - mean * mean
@@ -224,9 +221,9 @@
         normed = (raw[:, spots[i]] - mean) * scale
         if i == 0:
             target_ref[...] = normed.astype(BF)
-        gap = side[i, :, cols:].astype(F32) - normed
+        gap = side[i][:, cols:].astype(F32) - normed
         loss = loss + jnp.sum(gap * gap, axis=1, keepdims=True)
-    loss_ref[...] = jnp.broadcast_to(loss / width, (rows, 128)).T[:1]
+    loss_ref[...] = jnp.broadcast_to(loss / width, (rows, 128)).T[0]
 
 
 def whole(n):
@@ -359,7 +356,7 @@
         compiler_params=params(60),
         cost_estimate=pl.CostEstimate(flops=4 * 10**9, bytes_accessed=4 * 10**6, transcendentals=3 * 10**6),
         name="far",
-    )(q, near, pattern, pack, tok_got, *parts)
+    )(q, near, pattern, pack, tok_got[0, :16, :128], *parts)
     tok_own = arrange(tok_got)
     att = arrange(deliver(packed))
 
@@ -376,21 +373,19 @@
 
     target, row_loss = pl.pallas_call(
         final_kernel,
-        in_specs=[HBM] * 16,
+        in_specs=whole(8) + [HBM] * 8,
         out_specs=whole(2),
-        out_shape=[jax.ShapeDtypeStruct((own, cols), BF), jax.ShapeDtypeStruct((1, own), F32)],
+        out_shape=[jax.ShapeDtypeStruct((own, cols), BF), jax.ShapeDtypeStruct((own,), F32)],
         scratch_shapes=[
-            pltpu.VMEM((4, own, cols), BF),
-            pltpu.VMEM((4, own, 2 * cols), BF),
             pltpu.VMEM((4, cols, width), BF),
             pltpu.VMEM((own, width), F32),
-            pltpu.SemaphoreType.DMA((16,)),
+            pltpu.SemaphoreType.DMA((8,)),
         ],
         compiler_params=params(16),
         cost_estimate=pl.CostEstimate(flops=10**9, bytes_accessed=4 * 10**6, transcendentals=0),
         name="final",
     )(*over_heads(att), *side, *halves, *other)
-    return target, row_loss.reshape(own)
+    return target, row_loss
 
 
 def solution(mesh):

time: 96.4 us -> 93.7 us (0.972)
  waiting for transfers between devices: 14.3 us -> 18.4 us
  starting transfers between devices: 40.7 us -> 37.8 us
  matrix products: 4.74 us -> 3.6 us
  Pallas kernels: 28.4 us -> 27.3 us
    all_to_all x2, waiting for transfers between devices: 6.33 us -> 12 us  [deliver(): return lax.all_to_all(packed, 'tm', 0, 0, tiled=True)]
    all_to_all x2, starting transfers between devices: 12.5 us -> 9.6 us  [deliver(): return lax.all_to_all(packed, 'tm', 0, 0, tiled=True)]
    unnamed x22 -> x18, local copies, waits for them, and re-layouts: 1.57 us -> 0.05 us
    dot_general x2, matrix products: 3.12 us -> 1.99 us  [arrange(): jnp.dot(unpack, got.reshape(n_peers * CAP, -1), preferred_element_type=F32)]
    pallas_call x1, Pallas kernels: 4.73 us -> 3.61 us  [body(): pl.pallas_call(final_kernel, in_specs=whole(8) + [HBM] * 8, out_specs=who...]
    ppermute x9, waiting for transfers between devices: 7.11 us -> 6.02 us  [over_heads(): return [x] + [lax.ppermute(x, 'head', to(d)) for d in DISTANCES[1:]]]
  transfers between devices with their start and end apart: 25 -> 25, of which waited for: 5 -> 5; matrix products, arithmetic and copies ran while one was open for 9% -> 9% of each run, Pallas kernels for 18% -> 19%
where the time goes in v8:
time: 93.7 us; the launch traced here: 92.5 us
  starting transfers between devices  37.8 us (40%)
  Pallas kernels  27.3 us (29%)
  waiting for transfers between devices  18.4 us (20%)
  matrix products  3.6 us (4%)
  other arithmetic  3.49 us (4%)
  between operations  1.03 us (1%)
    ppermute x9, starting transfers between devices, over_heads(): return [x] + [lax.ppermute(x, 'head', to(d)) for d in DISTANCES[1:]]  14.8 us
    all_to_all x2, waiting for transfers between devices, deliver(): return lax.all_to_all(packed, 'tm', 0, 0, tiled=True)  12 us
    all_to_all x2, starting transfers between devices, deliver(): return lax.all_to_all(packed, 'tm', 0, 0, tiled=True)  9.6 us
    pallas_call x1, Pallas kernels, body(): pl.pallas_call(near_kernel, in_specs=[HBM] * 4, out_specs=pl.BlockSpec(me...  8.68 us
    pallas_call x1, Pallas kernels, body(): pl.pallas_call(far_kernel, in_specs=[HBM] * 13, out_specs=pl.BlockSpec(me...  8.57 us
    pallas_call x1, Pallas kernels, body(): pl.pallas_call(gather_kernel, in_specs=[HBM] * 4 + whole(3), out_specs=wh...  6.39 us
    ppermute x3, starting transfers between devices, body(): lax.ppermute(plane, 'tm', along_z(d))  6.06 us
    ppermute x9, waiting for transfers between devices, over_heads(): return [x] + [lax.ppermute(x, 'head', to(d)) for d in DISTANCES[1:]]  6.02 us
  transfers between devices with their start and end apart: 25, of which 5 were waited for; matrix products, arithmetic and copies ran while one was open for 9% of the time, Pallas kernels for 19%

profile of v8, /device:TPU:0, one launch (start us, length us, event | category | flops | bytes accessed | tf_op | source)
XLA Modules:
  0.0 92.5 jit_solution(10841535071829548966)
XLA Ops:
  0.7 6.4 %gather.1 = (bf16[64,512]{1,0:T(8,128)(2,1)}, bf16[320,256]{1,0:T(8,128)(2,1)}, bf16[384,256]{1,0:T(8,128)(2,1)}) custom-call(bf16[3136,1024]{1,0:T(8,128)(2,1)} %x_hbm.3, bf16[1024,256]{1,0:T(8,128)(2,1)} %wq_hbm.1, bf16[1024,256]{1,0:T(8,128)(2,1)} %wk_hbm.3, bf16[1024,256]{1,0:T(8,128)(2,1)} %wv_hbm.3, bf16[16,784]{1,0:T(8,128)(2,1)} %constant.62.clone.pool_ref, ...), custom_call_target="tpu_custom_call" | custom-call | flops 2000000000 | bytes 10000000 | tf_op jit(solution)/shard_map/gather/pallas_call | solution.py:282
  7.1 1.7 %collective-permute-start = (bf16[64,512]{1,0:T(8,128)(2,1)}, bf16[64,512]{1,0:T(8,128)(2,1)S(1)}, u32[]{:S(2)}, u32[]{:S(2)}) collective-permute-start(bf16[64,512]{1,0:T(8,128)(2,1)} %get-tuple-element.10), channel_id=1, source_target_pairs={{0,8},{4,12},{8,16},{12,20},{16,24},{20,28},{24,0},{28,4},{32,40},... | collective-permute-start | bytes 196616 | tf_op jit(solution)/shard_map/ppermute | solution.py:299
  8.8 1.6 %collective-permute-start.1 = (bf16[64,512]{1,0:T(8,128)(2,1)}, bf16[64,512]{1,0:T(8,128)(2,1)S(1)}, u32[]{:S(2)}, u32[]{:S(2)}) collective-permute-start(bf16[64,512]{1,0:T(8,128)(2,1)} %get-tuple-element.10), channel_id=1, source_target_pairs={{0,24},{4,28},{8,0},{12,4},{16,8},{20,12},{24,16},{28,20},{32,56},... | collective-permute-start | bytes 196616 | tf_op jit(solution)/shard_map/ppermute | solution.py:299
  10.4 2.1 %collective-permute-start.2 = (bf16[64,512]{1,0:T(8,128)(2,1)}, bf16[64,512]{1,0:T(8,128)(2,1)S(1)}, u32[]{:S(2)}, u32[]{:S(2)}) collective-permute-start(bf16[64,512]{1,0:T(8,128)(2,1)} %get-tuple-element.10), channel_id=1, source_target_pairs={{0,16},{4,20},{8,24},{12,28},{16,0},{20,4},{24,8},{28,12},{32,48},... | collective-permute-start | bytes 196616 | tf_op jit(solution)/shard_map/ppermute | solution.py:299
  12.5 1.6 %collective-permute-start.16 = (bf16[128,1024]{1,0:T(8,128)(2,1)S(1)}, bf16[128,1024]{1,0:T(8,128)(2,1)S(1)}, u32[]{:S(2)}, u32[]{:S(2)}) collective-permute-start(bf16[128,1024]{1,0:T(8,128)(2,1)S(1)} %constant_dynamic-slice_fusion.refs_8_), channel_id=1, source_target_pairs={{0,1},{1,2},{2,3},{3,0},{4,5},{5,6},{6,7},{7,4},{8,9},{9,10},{10,1... | collective-permute-start | bytes 786440 | tf_op jit(solution)/shard_map/ppermute | solution.py:367
  14.5 1.5 %fusion.pack_hbm = bf16[1536,384]{1,0:T(8,128)(2,1)} fusion(s32[384]{0:T(512)S(1)} %pad.4), kind=kLoop, calls=%fused_computation.2 | loop fusion | flops 1179648 | bytes 1181184 | tf_op jit(solution)/shard_map/convert_element_type | solution.py:309
  17.3 2.1 %collective-permute-start.3 = (bf16[4,64,512]{2,1,0:T(8,128)(2,1)S(1)}, bf16[4,64,512]{2,1,0:T(8,128)(2,1)S(1)}, u32[]{:S(2)}, u32[]{:S(2)}) collective-permute-start(bf16[4,64,512]{2,1,0:T(8,128)(2,1)S(1)} %pad_maximum_fusion.1.rest_0_), channel_id=1, source_target_pairs={{0,32},{4,36},{8,40},{12,44},{16,48},{20,52},{24,56},{28,60},{32,6... | collective-permute-start | bytes 786440 | tf_op jit(solution)/shard_map/ppermute | solution.py:301
  19.3 2.2 %collective-permute-start.4 = (bf16[4,64,512]{2,1,0:T(8,128)(2,1)S(1)}, bf16[4,64,512]{2,1,0:T(8,128)(2,1)S(1)}, u32[]{:S(2)}, u32[]{:S(2)}) collective-permute-start(bf16[4,64,512]{2,1,0:T(8,128)(2,1)S(1)} %pad_maximum_fusion.1.rest_0_), channel_id=1, source_target_pairs={{0,96},{4,100},{8,104},{12,108},{16,112},{20,116},{24,120},{28,124... | collective-permute-start | bytes 786440 | tf_op jit(solution)/shard_map/ppermute | solution.py:301
  21.5 1.8 %collective-permute-start.5 = (bf16[4,64,512]{2,1,0:T(8,128)(2,1)S(1)}, bf16[4,64,512]{2,1,0:T(8,128)(2,1)}, u32[]{:S(2)}, u32[]{:S(2)}) collective-permute-start(bf16[4,64,512]{2,1,0:T(8,128)(2,1)S(1)} %pad_maximum_fusion.1.rest_0_), channel_id=1, source_target_pairs={{0,64},{4,68},{8,72},{12,76},{16,80},{20,84},{24,88},{28,92},{32,9... | collective-permute-start | bytes 786440 | tf_op jit(solution)/shard_map/ppermute | solution.py:301
  23.3 1.5 %convolution_convert_fusion = bf16[1536,256]{1,0:T(8,128)(2,1)} fusion(bf16[384,256]{1,0:T(8,128)(2,1)S(1)} %copy-done.8, s32[384]{0:T(512)S(1)} %pad.4), kind=kOutput, calls=%fused_computation | convolution fusion | flops 302972928 | bytes 984576 | tf_op jit(solution)/shard_map/dot_general | solution.py:323
  24.8 4.8 %all-to-all-start = ((bf16[32,48,256]{2,1,0:T(8,128)(2,1)}), bf16[32,48,256]{2,1,0:T(8,128)(2,1)S(1)}, u32[]{:S(2)}, u32[]{:S(2)}) async-start(bf16[32,48,256]{2,1,0:T(8,128)(2,1)} %bitcast.4), calls=%async_computation | async-start | bytes 1572864 | tf_op jit(solution)/shard_map/all_to_all | solution.py:318
  29.6 8.7 %near.1.near_hbm = bf16[1280,384]{1,0:T(8,128)(2,1)} custom-call(bf16[320,256]{1,0:T(8,128)(2,1)} %get-tuple-element.13.q_hbm, bf16[3136,1024]{1,0:T(8,128)(2,1)} %x_hbm.3, bf16[1024,256]{1,0:T(8,128)(2,1)} %wk_hbm.3, bf16[1024,256]{1,0:T(8,128)(2,1)} %wv_hbm.3), custom_call_target="tpu_custom_call" | custom-call | flops 5000000000 | bytes 10000000 | tf_op jit(solution)/shard_map/near/pallas_call | solution.py:326
  39.6 4.6 %all-to-all-done = bf16[32,48,256]{2,1,0:T(8,128)(2,1)S(1)} async-done(((bf16[32,48,256]{2,1,0:T(8,128)(2,1)}), bf16[32,48,256]{2,1,0:T(8,128)(2,1)S(1)}, u32[]{:S(2)}, u32[]{:S(2)}) %all-to-all-start) | async-done | bytes 786464 | tf_op jit(solution)/shard_map/all_to_all | solution.py:318
  44.8 2.8 %collective-permute-start.17 = (bf16[128,1024]{1,0:T(8,128)(2,1)S(1)}, bf16[128,1024]{1,0:T(8,128)(2,1)S(1)}, u32[]{:S(2)}, u32[]{:S(2)}) collective-permute-start(bf16[128,1024]{1,0:T(8,128)(2,1)S(1)} %constant_dynamic-slice_fusion.refs_8_), channel_id=1, source_target_pairs={{0,3},{1,0},{2,1},{3,2},{4,7},{5,4},{6,5},{7,6},{8,11},{9,8},{10,9... | collective-permute-start | bytes 786440 | tf_op jit(solution)/shard_map/ppermute | solution.py:367
  48.4 8.6 %far.1 = bf16[32,48,256]{2,1,0:T(8,128)(2,1)} custom-call(bf16[320,256]{1,0:T(8,128)(2,1)} %get-tuple-element.13.q_hbm, bf16[1280,384]{1,0:T(8,128)(2,1)} %near.1.near_hbm, s32[16,512]{1,0:T(8,128)} %allow_hbm.1, bf16[1536,384]{1,0:T(8,128)(2,1)} %fusion.pack_hbm, bf16[16,128]{1,0:T(8,128)(2,1)} %slice_bitcast_fusion._, bf16[4,64,512]{2,1,0:T(8,128)(2,1)} %copy-done.1, ...), custom_call_target="tpu_custom_call" | custom-call | flops 4000000000 | bytes 4000000 | tf_op jit(solution)/shard_map/far/pallas_call | solution.py:341
  56.9 4.8 %all-to-all-start.1 = ((bf16[32,48,256]{2,1,0:T(8,128)(2,1)}), bf16[32,48,256]{2,1,0:T(8,128)(2,1)}, u32[]{:S(2)}, u32[]{:S(2)}) async-start(bf16[32,48,256]{2,1,0:T(8,128)(2,1)} %far.1), calls=%async_computation.1 | async-start | bytes 1572864 | tf_op jit(solution)/shard_map/all_to_all | solution.py:318
  65.0 2.3 %collective-permute-start.14 = (bf16[320,512]{1,0:T(8,128)(2,1)S(1)}, bf16[320,512]{1,0:T(8,128)(2,1)S(1)}, u32[]{:S(2)}, u32[]{:S(2)}) collective-permute-start(bf16[320,512]{1,0:T(8,128)(2,1)S(1)} %pad_maximum_fusion.refs_4_), channel_id=1, source_target_pairs={{0,3},{1,0},{2,1},{3,2},{4,7},{5,4},{6,5},{7,6},{8,11},{9,8},{10,9... | collective-permute-start | bytes 983048 | tf_op jit(solution)/shard_map/ppermute | solution.py:367
  67.4 1.5 %collective-permute-start.15 = (bf16[320,512]{1,0:T(8,128)(2,1)S(1)}, bf16[320,512]{1,0:T(8,128)(2,1)S(1)}, u32[]{:S(2)}, u32[]{:S(2)}) collective-permute-start(bf16[320,512]{1,0:T(8,128)(2,1)S(1)} %pad_maximum_fusion.refs_4_), channel_id=1, source_target_pairs={{0,2},{1,3},{2,0},{3,1},{4,6},{5,7},{6,4},{7,5},{8,10},{9,11},{10,... | collective-permute-start | bytes 983048 | tf_op jit(solution)/shard_map/ppermute | solution.py:367
  68.9 7.4 %all-to-all-done.1 = bf16[32,48,256]{2,1,0:T(8,128)(2,1)} async-done(((bf16[32,48,256]{2,1,0:T(8,128)(2,1)}), bf16[32,48,256]{2,1,0:T(8,128)(2,1)}, u32[]{:S(2)}, u32[]{:S(2)}) %all-to-all-start.1) | async-done | bytes 786464 | tf_op jit(solution)/shard_map/all_to_all | solution.py:318
  76.3 1.6 %fusion.4.refs_0_ = bf16[320,256]{1,0:T(8,128)(2,1)S(1)} fusion(bf16[1536,256]{1,0:T(8,128)(2,1)} %bitcast.6, s32[1536]{0:T(1024)S(1)} %eq.70), kind=kOutput, calls=%fused_computation.9 | convolution fusion | flops 252231680 | bytes 956416 | tf_op jit(solution)/shard_map/dot_general | solution.py:321
  78.8 2.3 %collective-permute-start.11 = (bf16[320,256]{1,0:T(8,128)(2,1)S(1)}, bf16[320,256]{1,0:T(8,128)(2,1)S(1)}, u32[]{:S(2)}, u32[]{:S(2)}) collective-permute-start(bf16[320,256]{1,0:T(8,128)(2,1)S(1)} %fusion.4.refs_0_), channel_id=1, source_target_pairs={{0,3},{1,0},{2,1},{3,2},{4,7},{5,4},{6,5},{7,6},{8,11},{9,8},{10,9... | collective-permute-start | bytes 491528 | tf_op jit(solution)/shard_map/ppermute | solution.py:367
  81.7 1.5 %collective-permute-start.12 = (bf16[320,256]{1,0:T(8,128)(2,1)S(1)}, bf16[320,256]{1,0:T(8,128)(2,1)S(1)}, u32[]{:S(2)}, u32[]{:S(2)}) collective-permute-start(bf16[320,256]{1,0:T(8,128)(2,1)S(1)} %fusion.4.refs_0_), channel_id=1, source_target_pairs={{0,2},{1,3},{2,0},{3,1},{4,6},{5,7},{6,4},{7,5},{8,10},{9,11},{10,... | collective-permute-start | bytes 491528 | tf_op jit(solution)/shard_map/ppermute | solution.py:367
  83.2 5.5 %collective-permute-done.10.refs_1_ = bf16[320,256]{1,0:T(8,128)(2,1)S(1)} collective-permute-done((bf16[320,256]{1,0:T(8,128)(2,1)S(1)}, bf16[320,256]{1,0:T(8,128)(2,1)S(1)}, u32[]{:S(2)}, u32[]{:S(2)}) %collective-permute-start.10) | collective-permute-done | bytes 163872 | tf_op jit(solution)/shard_map/ppermute | solution.py:367
  88.7 3.6 %final.1 = (bf16[320,256]{1,0:T(8,128)(2,1)}, f32[320]{0:T(512)}) custom-call(bf16[320,256]{1,0:T(8,128)(2,1)S(1)} %fusion.4.refs_0_, bf16[320,256]{1,0:T(8,128)(2,1)S(1)} %collective-permute-done.10.refs_1_, bf16[320,256]{1,0:T(8,128)(2,1)S(1)} %collective-permute-done.11.refs_2_, bf16[320,256]{1,0:T(8,128)(2,1)S(1)} %collective-permute-done.12.refs_3_, ...), custom_call_target="tpu_custom_call" | custom-call | flops 1000000000 | bytes 4000000 | tf_op jit(solution)/shard_map/final/pallas_call | solution.py:374
  (67 shorter events, 9.1 us)
Async XLA Ops:
  7.1 8.9 %collective-permute-start = (bf16[64,512]{1,0:T(8,128)(2,1)}, bf16[64,512]{1,0:T(8,128)(2,1)S(1)}, u32[]{:S(2)}, u32[]{:S(2)}) collective-permute-start(bf16[64,512]{1,0:T(8,128)(2,1)} %get-tuple-element.10), channel_id=1, source_target_pairs={{0,8},{4,12},{8,16},{12,20},{16,24},{20,28},{24,0},{28,4},{32,40},... | collective-permute-start | bytes 196616 | tf_op jit(solution)/shard_map/ppermute | solution.py:299
  8.8 7.2 %collective-permute-start.1 = (bf16[64,512]{1,0:T(8,128)(2,1)}, bf16[64,512]{1,0:T(8,128)(2,1)S(1)}, u32[]{:S(2)}, u32[]{:S(2)}) collective-permute-start(bf16[64,512]{1,0:T(8,128)(2,1)} %get-tuple-element.10), channel_id=1, source_target_pairs={{0,24},{4,28},{8,0},{12,4},{16,8},{20,12},{24,16},{28,20},{32,56},... | collective-permute-start | bytes 196616 | tf_op jit(solution)/shard_map/ppermute | solution.py:299
  10.4 6.0 %collective-permute-start.2 = (bf16[64,512]{1,0:T(8,128)(2,1)}, bf16[64,512]{1,0:T(8,128)(2,1)S(1)}, u32[]{:S(2)}, u32[]{:S(2)}) collective-permute-start(bf16[64,512]{1,0:T(8,128)(2,1)} %get-tuple-element.10), channel_id=1, source_target_pairs={{0,16},{4,20},{8,24},{12,28},{16,0},{20,4},{24,8},{28,12},{32,48},... | collective-permute-start | bytes 196616 | tf_op jit(solution)/shard_map/ppermute | solution.py:299
  12.5 50.2 %collective-permute-start.16 = (bf16[128,1024]{1,0:T(8,128)(2,1)S(1)}, bf16[128,1024]{1,0:T(8,128)(2,1)S(1)}, u32[]{:S(2)}, u32[]{:S(2)}) collective-permute-start(bf16[128,1024]{1,0:T(8,128)(2,1)S(1)} %constant_dynamic-slice_fusion.refs_8_), channel_id=1, source_target_pairs={{0,1},{1,2},{2,3},{3,0},{4,5},{5,6},{6,7},{7,4},{8,9},{9,10},{10,1... | collective-permute-start | bytes 786440 | tf_op jit(solution)/shard_map/ppermute | solution.py:367
  17.3 21.4 %collective-permute-start.3 = (bf16[4,64,512]{2,1,0:T(8,128)(2,1)S(1)}, bf16[4,64,512]{2,1,0:T(8,128)(2,1)S(1)}, u32[]{:S(2)}, u32[]{:S(2)}) collective-permute-start(bf16[4,64,512]{2,1,0:T(8,128)(2,1)S(1)} %pad_maximum_fusion.1.rest_0_), channel_id=1, source_target_pairs={{0,32},{4,36},{8,40},{12,44},{16,48},{20,52},{24,56},{28,60},{32,6... | collective-permute-start | bytes 786440 | tf_op jit(solution)/shard_map/ppermute | solution.py:301
  19.3 19.6 %collective-permute-start.4 = (bf16[4,64,512]{2,1,0:T(8,128)(2,1)S(1)}, bf16[4,64,512]{2,1,0:T(8,128)(2,1)S(1)}, u32[]{:S(2)}, u32[]{:S(2)}) collective-permute-start(bf16[4,64,512]{2,1,0:T(8,128)(2,1)S(1)} %pad_maximum_fusion.1.rest_0_), channel_id=1, source_target_pairs={{0,96},{4,100},{8,104},{12,108},{16,112},{20,116},{24,120},{28,124... | collective-permute-start | bytes 786440 | tf_op jit(solution)/shard_map/ppermute | solution.py:301
  21.5 17.7 %collective-permute-start.5 = (bf16[4,64,512]{2,1,0:T(8,128)(2,1)S(1)}, bf16[4,64,512]{2,1,0:T(8,128)(2,1)}, u32[]{:S(2)}, u32[]{:S(2)}) collective-permute-start(bf16[4,64,512]{2,1,0:T(8,128)(2,1)S(1)} %pad_maximum_fusion.1.rest_0_), channel_id=1, source_target_pairs={{0,64},{4,68},{8,72},{12,76},{16,80},{20,84},{24,88},{28,92},{32,9... | collective-permute-start | bytes 786440 | tf_op jit(solution)/shard_map/ppermute | solution.py:301
  24.8 19.4 %all-to-all-start = ((bf16[32,48,256]{2,1,0:T(8,128)(2,1)}), bf16[32,48,256]{2,1,0:T(8,128)(2,1)S(1)}, u32[]{:S(2)}, u32[]{:S(2)}) async-start(bf16[32,48,256]{2,1,0:T(8,128)(2,1)} %bitcast.4), calls=%async_computation | async-start | bytes 1572864 | tf_op jit(solution)/shard_map/all_to_all | solution.py:318
  38.3 6.5 %collective-permute-start.6 = (bf16[4,64,512]{2,1,0:T(8,128)(2,1)S(1)}, bf16[4,64,512]{2,1,0:T(8,128)(2,1)}, u32[]{:S(2)}, u32[]{:S(2)}) collective-permute-start(bf16[4,64,512]{2,1,0:T(8,128)(2,1)S(1)} %pad_maximum_fusion.1.rest_0_), channel_id=1, source_target_pairs={{0,4},{4,0},{8,12},{12,8},{16,20},{20,16},{24,28},{28,24},{32,36},... | collective-permute-start | bytes 786440 | tf_op jit(solution)/shard_map/ppermute | solution.py:340
  38.7 8.9 %collective-permute-start.7 = (bf16[4,64,512]{2,1,0:T(8,128)(2,1)S(1)}, bf16[4,64,512]{2,1,0:T(8,128)(2,1)}, u32[]{:S(2)}, u32[]{:S(2)}) collective-permute-start(bf16[4,64,512]{2,1,0:T(8,128)(2,1)S(1)} %collective-permute-done.3.rest_1_), channel_id=1, source_target_pairs={{0,4},{4,0},{8,12},{12,8},{16,20},{20,16},{24,28},{28,24},{32,36},... | collective-permute-start | bytes 786440 | tf_op jit(solution)/shard_map/ppermute | solution.py:340
  38.9 9.4 %collective-permute-start.8 = (bf16[4,64,512]{2,1,0:T(8,128)(2,1)S(1)}, bf16[4,64,512]{2,1,0:T(8,128)(2,1)}, u32[]{:S(2)}, u32[]{:S(2)}) collective-permute-start(bf16[4,64,512]{2,1,0:T(8,128)(2,1)S(1)} %collective-permute-done.4.rest_2_), channel_id=1, source_target_pairs={{0,4},{4,0},{8,12},{12,8},{16,20},{20,16},{24,28},{28,24},{32,36},... | collective-permute-start | bytes 786440 | tf_op jit(solution)/shard_map/ppermute | solution.py:340
  39.2 9.1 %collective-permute-start.9 = (bf16[4,64,512]{2,1,0:T(8,128)(2,1)}, bf16[4,64,512]{2,1,0:T(8,128)(2,1)}, u32[]{:S(2)}, u32[]{:S(2)}) collective-permute-start(bf16[4,64,512]{2,1,0:T(8,128)(2,1)} %collective-permute-done.5.rest_3_), channel_id=1, source_target_pairs={{0,4},{4,0},{8,12},{12,8},{16,20},{20,16},{24,28},{28,24},{32,36},... | collective-permute-start | bytes 786440 | tf_op jit(solution)/shard_map/ppermute | solution.py:340
  44.8 19.7 %collective-permute-start.17 = (bf16[128,1024]{1,0:T(8,128)(2,1)S(1)}, bf16[128,1024]{1,0:T(8,128)(2,1)S(1)}, u32[]{:S(2)}, u32[]{:S(2)}) collective-permute-start(bf16[128,1024]{1,0:T(8,128)(2,1)S(1)} %constant_dynamic-slice_fusion.refs_8_), channel_id=1, source_target_pairs={{0,3},{1,0},{2,1},{3,2},{4,7},{5,4},{6,5},{7,6},{8,11},{9,8},{10,9... | collective-permute-start | bytes 786440 | tf_op jit(solution)/shard_map/ppermute | solution.py:367
  47.5 17.0 %collective-permute-start.18 = (bf16[128,1024]{1,0:T(8,128)(2,1)S(1)}, bf16[128,1024]{1,0:T(8,128)(2,1)S(1)}, u32[]{:S(2)}, u32[]{:S(2)}) collective-permute-start(bf16[128,1024]{1,0:T(8,128)(2,1)S(1)} %constant_dynamic-slice_fusion.refs_8_), channel_id=1, source_target_pairs={{0,2},{1,3},{2,0},{3,1},{4,6},{5,7},{6,4},{7,5},{8,10},{9,11},{10,... | collective-permute-start | bytes 786440 | tf_op jit(solution)/shard_map/ppermute | solution.py:367
  48.3 16.7 %collective-permute-start.19 = (bf16[128,1024]{1,0:T(8,128)(2,1)S(1)}, bf16[128,1024]{1,0:T(8,128)(2,1)S(1)}, u32[]{:S(2)}, u32[]{:S(2)}) collective-permute-start(bf16[128,1024]{1,0:T(8,128)(2,1)S(1)} %constant_dynamic-slice_fusion.refs_8_), channel_id=1, source_target_pairs={{0,4},{4,0},{8,12},{12,8},{16,20},{20,16},{24,28},{28,24},{32,36},... | collective-permute-start | bytes 786440 | tf_op jit(solution)/shard_map/ppermute | solution.py:371
  56.9 19.3 %all-to-all-start.1 = ((bf16[32,48,256]{2,1,0:T(8,128)(2,1)}), bf16[32,48,256]{2,1,0:T(8,128)(2,1)}, u32[]{:S(2)}, u32[]{:S(2)}) async-start(bf16[32,48,256]{2,1,0:T(8,128)(2,1)} %far.1), calls=%async_computation.1 | async-start | bytes 1572864 | tf_op jit(solution)/shard_map/all_to_all | solution.py:318
  63.5 18.1 %collective-permute-start.13 = (bf16[320,512]{1,0:T(8,128)(2,1)S(1)}, bf16[320,512]{1,0:T(8,128)(2,1)S(1)}, u32[]{:S(2)}, u32[]{:S(2)}) collective-permute-start(bf16[320,512]{1,0:T(8,128)(2,1)S(1)} %pad_maximum_fusion.refs_4_), channel_id=1, source_target_pairs={{0,1},{1,2},{2,3},{3,0},{4,5},{5,6},{6,7},{7,4},{8,9},{9,10},{10,1... | collective-permute-start | bytes 983048 | tf_op jit(solution)/shard_map/ppermute | solution.py:367
  64.5 13.3 %collective-permute-start.21 = (bf16[128,1024]{1,0:T(8,128)(2,1)S(1)}, bf16[128,1024]{1,0:T(8,128)(2,1)}, u32[]{:S(2)}, u32[]{:S(2)}) collective-permute-start(bf16[128,1024]{1,0:T(8,128)(2,1)S(1)} %collective-permute-done.17.refs_10_), channel_id=1, source_target_pairs={{0,4},{4,0},{8,12},{12,8},{16,20},{20,16},{24,28},{28,24},{32,36},... | collective-permute-start | bytes 786440 | tf_op jit(solution)/shard_map/ppermute | solution.py:371
  64.5 14.3 %collective-permute-start.22 = (bf16[128,1024]{1,0:T(8,128)(2,1)S(1)}, bf16[128,1024]{1,0:T(8,128)(2,1)}, u32[]{:S(2)}, u32[]{:S(2)}) collective-permute-start(bf16[128,1024]{1,0:T(8,128)(2,1)S(1)} %collective-permute-done.18.refs_11_), channel_id=1, source_target_pairs={{0,4},{4,0},{8,12},{12,8},{16,20},{20,16},{24,28},{28,24},{32,36},... | collective-permute-start | bytes 786440 | tf_op jit(solution)/shard_map/ppermute | solution.py:371
  65.0 18.2 %collective-permute-start.14 = (bf16[320,512]{1,0:T(8,128)(2,1)S(1)}, bf16[320,512]{1,0:T(8,128)(2,1)S(1)}, u32[]{:S(2)}, u32[]{:S(2)}) collective-permute-start(bf16[320,512]{1,0:T(8,128)(2,1)S(1)} %pad_maximum_fusion.refs_4_), channel_id=1, source_target_pairs={{0,3},{1,0},{2,1},{3,2},{4,7},{5,4},{6,5},{7,6},{8,11},{9,8},{10,9... | collective-permute-start | bytes 983048 | tf_op jit(solution)/shard_map/ppermute | solution.py:367
  67.4 15.8 %collective-permute-start.15 = (bf16[320,512]{1,0:T(8,128)(2,1)S(1)}, bf16[320,512]{1,0:T(8,128)(2,1)S(1)}, u32[]{:S(2)}, u32[]{:S(2)}) collective-permute-start(bf16[320,512]{1,0:T(8,128)(2,1)S(1)} %pad_maximum_fusion.refs_4_), channel_id=1, source_target_pairs={{0,2},{1,3},{2,0},{3,1},{4,6},{5,7},{6,4},{7,5},{8,10},{9,11},{10,... | collective-permute-start | bytes 983048 | tf_op jit(solution)/shard_map/ppermute | solution.py:367
  77.8 10.8 %collective-permute-start.10 = (bf16[320,256]{1,0:T(8,128)(2,1)S(1)}, bf16[320,256]{1,0:T(8,128)(2,1)S(1)}, u32[]{:S(2)}, u32[]{:S(2)}) collective-permute-start(bf16[320,256]{1,0:T(8,128)(2,1)S(1)} %fusion.4.refs_0_), channel_id=1, source_target_pairs={{0,1},{1,2},{2,3},{3,0},{4,5},{5,6},{6,7},{7,4},{8,9},{9,10},{10,1... | collective-permute-start | bytes 491528 | tf_op jit(solution)/shard_map/ppermute | solution.py:367
  78.8 9.9 %collective-permute-start.11 = (bf16[320,256]{1,0:T(8,128)(2,1)S(1)}, bf16[320,256]{1,0:T(8,128)(2,1)S(1)}, u32[]{:S(2)}, u32[]{:S(2)}) collective-permute-start(bf16[320,256]{1,0:T(8,128)(2,1)S(1)} %fusion.4.refs_0_), channel_id=1, source_target_pairs={{0,3},{1,0},{2,1},{3,2},{4,7},{5,4},{6,5},{7,6},{8,11},{9,8},{10,9... | collective-permute-start | bytes 491528 | tf_op jit(solution)/shard_map/ppermute | solution.py:367
  81.7 7.0 %collective-permute-start.12 = (bf16[320,256]{1,0:T(8,128)(2,1)S(1)}, bf16[320,256]{1,0:T(8,128)(2,1)S(1)}, u32[]{:S(2)}, u32[]{:S(2)}) collective-permute-start(bf16[320,256]{1,0:T(8,128)(2,1)S(1)} %fusion.4.refs_0_), channel_id=1, source_target_pairs={{0,2},{1,3},{2,0},{3,1},{4,6},{5,7},{6,4},{7,5},{8,10},{9,11},{10,... | collective-permute-start | bytes 491528 | tf_op jit(solution)/shard_map/ppermute | solution.py:367
  (10 other events, 122.5 us)

commit v9 on v8

--- a/solution.py
+++ b/solution.py
@@ -137,7 +137,7 @@
         out_ref[part, cols:] = side.astype(BF)
 
 
-def far_kernel(q_hbm, near_hbm, allow_hbm, pack_hbm, _, *rest):
+def far_kernel(q_hbm, near_hbm, allow_hbm, pack_hbm, *rest):
     parts, rest = rest[:8], rest[8:]
     out_ref, far_ref, key, value, q_ref, near_ref, allow_ref, pack_ref, sem = rest
     pairs = [(allow_hbm, allow_ref)] + [(part, far_ref.at[i]) for i, part in enumerate(parts)]
@@ -340,7 +340,7 @@
     parts = parts + [lax.ppermute(part, "tm", OTHER_CORE) for part in [plane] + parts[1:]]
     packed = pl.pallas_call(
         far_kernel,
-        in_specs=[HBM] * 13,
+        in_specs=[HBM] * 12,
         out_specs=pl.BlockSpec(memory_space=pltpu.VMEM),
         out_shape=jax.ShapeDtypeStruct((n_peers, CAP, cols), BF),
         scratch_shapes=[
@@ -354,9 +354,10 @@
             pltpu.SemaphoreType.DMA((12,)),
         ],
         compiler_params=params(60),
-        cost_estimate=pl.CostEstimate(flops=4 * 10**9, bytes_accessed=4 * 10**6, transcendentals=3 * 10**6),
+        cost_estimate=pl.CostEstimate(flops=10**6, bytes_accessed=10**4, transcendentals=0),
         name="far",
-    )(q, near, pattern, pack, tok_got[0, :16, :128], *parts)
+    )(q, near, pattern, pack, *parts)
+    packed, tok_got = lax.optimization_barrier((packed, tok_got))
     tok_own = arrange(tok_got)
     att = arrange(deliver(packed))
 

time: 93.7 us -> 91.9 us (0.981)
  waiting for transfers between devices: 18.4 us -> 14.2 us
  starting transfers between devices: 37.8 us -> 40.7 us
    all_to_all x2, waiting for transfers between devices: 12 us -> 7.45 us  [deliver(): return lax.all_to_all(packed, 'tm', 0, 0, tiled=True)]
    all_to_all x2, starting transfers between devices: 9.6 us -> 12.6 us  [deliver(): return lax.all_to_all(packed, 'tm', 0, 0, tiled=True)]
  transfers between devices with their start and end apart: 25 -> 25, of which waited for: 5 -> 5; matrix products, arithmetic and copies ran while one was open for 9% -> 8% of each run, Pallas kernels for 19% -> 19%
where the time goes in v9:
time: 91.9 us; the launch traced here: 90.6 us
  starting transfers between devices  40.7 us (44%)
  Pallas kernels  27.3 us (30%)
  waiting for transfers between devices  14.2 us (15%)
  matrix products  3.6 us (4%)
  other arithmetic  3.5 us (4%)
  between operations  1.06 us (1%)
    ppermute x9, starting transfers between devices, over_heads(): return [x] + [lax.ppermute(x, 'head', to(d)) for d in DISTANCES[1:]]  14.8 us
    all_to_all x2, starting transfers between devices, deliver(): return lax.all_to_all(packed, 'tm', 0, 0, tiled=True)  12.6 us
    pallas_call x1, Pallas kernels, body(): pl.pallas_call(near_kernel, in_specs=[HBM] * 4, out_specs=pl.BlockSpec(me...  8.69 us
    pallas_call x1, Pallas kernels, body(): pl.pallas_call(far_kernel, in_specs=[HBM] * 12, out_specs=pl.BlockSpec(me...  8.57 us
    all_to_all x2, waiting for transfers between devices, deliver(): return lax.all_to_all(packed, 'tm', 0, 0, tiled=True)  7.45 us
    pallas_call x1, Pallas kernels, body(): pl.pallas_call(gather_kernel, in_specs=[HBM] * 4 + whole(3), out_specs=wh...  6.38 us
    ppermute x3, starting transfers between devices, body(): lax.ppermute(plane, 'tm', along_z(d))  6.06 us
    ppermute x9, waiting for transfers between devices, over_heads(): return [x] + [lax.ppermute(x, 'head', to(d)) for d in DISTANCES[1:]]  6.02 us
  transfers between devices with their start and end apart: 25, of which 5 were waited for; matrix products, arithmetic and copies ran while one was open for 8% of the time, Pallas kernels for 19%

profile of v9, /device:TPU:0, one launch (start us, length us, event | category | flops | bytes accessed | tf_op | source)
XLA Modules:
  0.0 90.6 jit_solution(5515017307934084459)
XLA Ops:
  0.7 6.4 %gather.1 = (bf16[64,512]{1,0:T(8,128)(2,1)}, bf16[320,256]{1,0:T(8,128)(2,1)}, bf16[384,256]{1,0:T(8,128)(2,1)}) custom-call(bf16[3136,1024]{1,0:T(8,128)(2,1)} %x_hbm.3, bf16[1024,256]{1,0:T(8,128)(2,1)} %wq_hbm.1, bf16[1024,256]{1,0:T(8,128)(2,1)} %wk_hbm.3, bf16[1024,256]{1,0:T(8,128)(2,1)} %wv_hbm.3, bf16[16,784]{1,0:T(8,128)(2,1)} %constant.62.clone.pool_ref, ...), custom_call_target="tpu_custom_call" | custom-call | flops 2000000000 | bytes 10000000 | tf_op jit(solution)/shard_map/gather/pallas_call | solution.py:282
  7.1 1.7 %collective-permute-start = (bf16[64,512]{1,0:T(8,128)(2,1)}, bf16[64,512]{1,0:T(8,128)(2,1)S(1)}, u32[]{:S(2)}, u32[]{:S(2)}) collective-permute-start(bf16[64,512]{1,0:T(8,128)(2,1)} %get-tuple-element.12), channel_id=1, source_target_pairs={{0,8},{4,12},{8,16},{12,20},{16,24},{20,28},{24,0},{28,4},{32,40},... | collective-permute-start | bytes 196616 | tf_op jit(solution)/shard_map/ppermute | solution.py:299
  8.8 1.6 %collective-permute-start.1 = (bf16[64,512]{1,0:T(8,128)(2,1)}, bf16[64,512]{1,0:T(8,128)(2,1)S(1)}, u32[]{:S(2)}, u32[]{:S(2)}) collective-permute-start(bf16[64,512]{1,0:T(8,128)(2,1)} %get-tuple-element.12), channel_id=1, source_target_pairs={{0,24},{4,28},{8,0},{12,4},{16,8},{20,12},{24,16},{28,20},{32,56},... | collective-permute-start | bytes 196616 | tf_op jit(solution)/shard_map/ppermute | solution.py:299
  10.4 2.1 %collective-permute-start.2 = (bf16[64,512]{1,0:T(8,128)(2,1)}, bf16[64,512]{1,0:T(8,128)(2,1)S(1)}, u32[]{:S(2)}, u32[]{:S(2)}) collective-permute-start(bf16[64,512]{1,0:T(8,128)(2,1)} %get-tuple-element.12), channel_id=1, source_target_pairs={{0,16},{4,20},{8,24},{12,28},{16,0},{20,4},{24,8},{28,12},{32,48},... | collective-permute-start | bytes 196616 | tf_op jit(solution)/shard_map/ppermute | solution.py:299
  12.5 1.6 %collective-permute-start.16 = (bf16[128,1024]{1,0:T(8,128)(2,1)S(1)}, bf16[128,1024]{1,0:T(8,128)(2,1)S(1)}, u32[]{:S(2)}, u32[]{:S(2)}) collective-permute-start(bf16[128,1024]{1,0:T(8,128)(2,1)S(1)} %constant_dynamic-slice_fusion.refs_8_), channel_id=1, source_target_pairs={{0,1},{1,2},{2,3},{3,0},{4,5},{5,6},{6,7},{7,4},{8,9},{9,10},{10,1... | collective-permute-start | bytes 786440 | tf_op jit(solution)/shard_map/ppermute | solution.py:368
  14.5 1.5 %fusion.pack_hbm = bf16[1536,384]{1,0:T(8,128)(2,1)} fusion(s32[384]{0:T(512)S(1)} %pad.4), kind=kLoop, calls=%fused_computation.2 | loop fusion | flops 1179648 | bytes 1181184 | tf_op jit(solution)/shard_map/convert_element_type | solution.py:309
  17.2 2.1 %collective-permute-start.3 = (bf16[4,64,512]{2,1,0:T(8,128)(2,1)S(1)}, bf16[4,64,512]{2,1,0:T(8,128)(2,1)S(1)}, u32[]{:S(2)}, u32[]{:S(2)}) collective-permute-start(bf16[4,64,512]{2,1,0:T(8,128)(2,1)S(1)} %pad_maximum_fusion.1.rest_0_), channel_id=1, source_target_pairs={{0,32},{4,36},{8,40},{12,44},{16,48},{20,52},{24,56},{28,60},{32,6... | collective-permute-start | bytes 786440 | tf_op jit(solution)/shard_map/ppermute | solution.py:301
  19.3 2.2 %collective-permute-start.4 = (bf16[4,64,512]{2,1,0:T(8,128)(2,1)S(1)}, bf16[4,64,512]{2,1,0:T(8,128)(2,1)S(1)}, u32[]{:S(2)}, u32[]{:S(2)}) collective-permute-start(bf16[4,64,512]{2,1,0:T(8,128)(2,1)S(1)} %pad_maximum_fusion.1.rest_0_), channel_id=1, source_target_pairs={{0,96},{4,100},{8,104},{12,108},{16,112},{20,116},{24,120},{28,124... | collective-permute-start | bytes 786440 | tf_op jit(solution)/shard_map/ppermute | solution.py:301
  21.5 1.8 %collective-permute-start.5 = (bf16[4,64,512]{2,1,0:T(8,128)(2,1)S(1)}, bf16[4,64,512]{2,1,0:T(8,128)(2,1)}, u32[]{:S(2)}, u32[]{:S(2)}) collective-permute-start(bf16[4,64,512]{2,1,0:T(8,128)(2,1)S(1)} %pad_maximum_fusion.1.rest_0_), channel_id=1, source_target_pairs={{0,64},{4,68},{8,72},{12,76},{16,80},{20,84},{24,88},{28,92},{32,9... | collective-permute-start | bytes 786440 | tf_op jit(solution)/shard_map/ppermute | solution.py:301
  23.3 1.5 %convolution_convert_fusion = bf16[1536,256]{1,0:T(8,128)(2,1)} fusion(bf16[384,256]{1,0:T(8,128)(2,1)S(1)} %copy-done.10, s32[384]{0:T(512)S(1)} %pad.4), kind=kOutput, calls=%fused_computation | convolution fusion | flops 302972928 | bytes 984576 | tf_op jit(solution)/shard_map/dot_general | solution.py:323
  24.8 4.8 %all-to-all-start = ((bf16[32,48,256]{2,1,0:T(8,128)(2,1)}), bf16[32,48,256]{2,1,0:T(8,128)(2,1)S(1)}, u32[]{:S(2)}, u32[]{:S(2)}) async-start(bf16[32,48,256]{2,1,0:T(8,128)(2,1)} %bitcast.4), calls=%async_computation | async-start | bytes 1572864 | tf_op jit(solution)/shard_map/all_to_all | solution.py:318
  29.6 8.7 %near.1.near_hbm = bf16[1280,384]{1,0:T(8,128)(2,1)} custom-call(bf16[320,256]{1,0:T(8,128)(2,1)} %get-tuple-element.15.q_hbm, bf16[3136,1024]{1,0:T(8,128)(2,1)} %x_hbm.3, bf16[1024,256]{1,0:T(8,128)(2,1)} %wk_hbm.3, bf16[1024,256]{1,0:T(8,128)(2,1)} %wv_hbm.3), custom_call_target="tpu_custom_call" | custom-call | flops 5000000000 | bytes 10000000 | tf_op jit(solution)/shard_map/near/pallas_call | solution.py:326
  39.9 2.7 %collective-permute-start.17 = (bf16[128,1024]{1,0:T(8,128)(2,1)S(1)}, bf16[128,1024]{1,0:T(8,128)(2,1)S(1)}, u32[]{:S(2)}, u32[]{:S(2)}) collective-permute-start(bf16[128,1024]{1,0:T(8,128)(2,1)S(1)} %constant_dynamic-slice_fusion.refs_8_), channel_id=1, source_target_pairs={{0,3},{1,0},{2,1},{3,2},{4,7},{5,4},{6,5},{7,6},{8,11},{9,8},{10,9... | collective-permute-start | bytes 786440 | tf_op jit(solution)/shard_map/ppermute | solution.py:368
  43.5 8.6 %far.1 = bf16[32,48,256]{2,1,0:T(8,128)(2,1)} custom-call(bf16[320,256]{1,0:T(8,128)(2,1)} %get-tuple-element.15.q_hbm, bf16[1280,384]{1,0:T(8,128)(2,1)} %near.1.near_hbm, s32[16,512]{1,0:T(8,128)} %allow_hbm.1, bf16[1536,384]{1,0:T(8,128)(2,1)} %fusion.pack_hbm, bf16[4,64,512]{2,1,0:T(8,128)(2,1)} %copy-done.1, bf16[4,64,512]{2,1,0:T(8,128)(2,1)} %copy-done.2, ...), custom_call_target="tpu_custom_call" | custom-call | flops 1000000 | bytes 10000 | tf_op jit(solution)/shard_map/far/pallas_call | solution.py:341
  52.1 7.7 %all-to-all-start.1 = ((bf16[32,48,256]{2,1,0:T(8,128)(2,1)}), bf16[32,48,256]{2,1,0:T(8,128)(2,1)}, u32[]{:S(2)}, u32[]{:S(2)}) async-start(bf16[32,48,256]{2,1,0:T(8,128)(2,1)} %far.1), calls=%async_computation.1 | async-start | bytes 1572864 | tf_op jit(solution)/shard_map/all_to_all | solution.py:318
  61.6 1.0 %collective-permute-start.13 = (bf16[320,512]{1,0:T(8,128)(2,1)S(1)}, bf16[320,512]{1,0:T(8,128)(2,1)S(1)}, u32[]{:S(2)}, u32[]{:S(2)}) collective-permute-start(bf16[320,512]{1,0:T(8,128)(2,1)S(1)} %pad_maximum_fusion.refs_4_), channel_id=1, source_target_pairs={{0,1},{1,2},{2,3},{3,0},{4,5},{5,6},{6,7},{7,4},{8,9},{9,10},{10,1... | collective-permute-start | bytes 983048 | tf_op jit(solution)/shard_map/ppermute | solution.py:368
  63.1 2.3 %collective-permute-start.14 = (bf16[320,512]{1,0:T(8,128)(2,1)S(1)}, bf16[320,512]{1,0:T(8,128)(2,1)S(1)}, u32[]{:S(2)}, u32[]{:S(2)}) collective-permute-start(bf16[320,512]{1,0:T(8,128)(2,1)S(1)} %pad_maximum_fusion.refs_4_), channel_id=1, source_target_pairs={{0,3},{1,0},{2,1},{3,2},{4,7},{5,4},{6,5},{7,6},{8,11},{9,8},{10,9... | collective-permute-start | bytes 983048 | tf_op jit(solution)/shard_map/ppermute | solution.py:368
  65.4 1.5 %collective-permute-start.15 = (bf16[320,512]{1,0:T(8,128)(2,1)S(1)}, bf16[320,512]{1,0:T(8,128)(2,1)S(1)}, u32[]{:S(2)}, u32[]{:S(2)}) collective-permute-start(bf16[320,512]{1,0:T(8,128)(2,1)S(1)} %pad_maximum_fusion.refs_4_), channel_id=1, source_target_pairs={{0,2},{1,3},{2,0},{3,1},{4,6},{5,7},{6,4},{7,5},{8,10},{9,11},{10,... | collective-permute-start | bytes 983048 | tf_op jit(solution)/shard_map/ppermute | solution.py:368
  67.0 7.5 %all-to-all-done.1 = bf16[32,48,256]{2,1,0:T(8,128)(2,1)} async-done(((bf16[32,48,256]{2,1,0:T(8,128)(2,1)}), bf16[32,48,256]{2,1,0:T(8,128)(2,1)}, u32[]{:S(2)}, u32[]{:S(2)}) %all-to-all-start.1) | async-done | bytes 786464 | tf_op jit(solution)/shard_map/all_to_all | solution.py:318
  74.4 1.6 %fusion.4.refs_0_ = bf16[320,256]{1,0:T(8,128)(2,1)S(1)} fusion(bf16[1536,256]{1,0:T(8,128)(2,1)} %bitcast.5, s32[1536]{0:T(1024)S(1)} %eq.70), kind=kOutput, calls=%fused_computation.9 | convolution fusion | flops 252231680 | bytes 956416 | tf_op jit(solution)/shard_map/dot_general | solution.py:321
  77.0 2.3 %collective-permute-start.11 = (bf16[320,256]{1,0:T(8,128)(2,1)S(1)}, bf16[320,256]{1,0:T(8,128)(2,1)S(1)}, u32[]{:S(2)}, u32[]{:S(2)}) collective-permute-start(bf16[320,256]{1,0:T(8,128)(2,1)S(1)} %fusion.4.refs_0_), channel_id=1, source_target_pairs={{0,3},{1,0},{2,1},{3,2},{4,7},{5,4},{6,5},{7,6},{8,11},{9,8},{10,9... | collective-permute-start | bytes 491528 | tf_op jit(solution)/shard_map/ppermute | solution.py:368
  79.8 1.5 %collective-permute-start.12 = (bf16[320,256]{1,0:T(8,128)(2,1)S(1)}, bf16[320,256]{1,0:T(8,128)(2,1)S(1)}, u32[]{:S(2)}, u32[]{:S(2)}) collective-permute-start(bf16[320,256]{1,0:T(8,128)(2,1)S(1)} %fusion.4.refs_0_), channel_id=1, source_target_pairs={{0,2},{1,3},{2,0},{3,1},{4,6},{5,7},{6,4},{7,5},{8,10},{9,11},{10,... | collective-permute-start | bytes 491528 | tf_op jit(solution)/shard_map/ppermute | solution.py:368
  81.4 5.5 %collective-permute-done.10.refs_1_ = bf16[320,256]{1,0:T(8,128)(2,1)S(1)} collective-permute-done((bf16[320,256]{1,0:T(8,128)(2,1)S(1)}, bf16[320,256]{1,0:T(8,128)(2,1)S(1)}, u32[]{:S(2)}, u32[]{:S(2)}) %collective-permute-start.10) | collective-permute-done | bytes 163872 | tf_op jit(solution)/shard_map/ppermute | solution.py:368
  86.9 3.6 %final.1 = (bf16[320,256]{1,0:T(8,128)(2,1)}, f32[320]{0:T(512)}) custom-call(bf16[320,256]{1,0:T(8,128)(2,1)S(1)} %fusion.4.refs_0_, bf16[320,256]{1,0:T(8,128)(2,1)S(1)} %collective-permute-done.10.refs_1_, bf16[320,256]{1,0:T(8,128)(2,1)S(1)} %collective-permute-done.11.refs_2_, bf16[320,256]{1,0:T(8,128)(2,1)S(1)} %collective-permute-done.12.refs_3_, ...), custom_call_target="tpu_custom_call" | custom-call | flops 1000000000 | bytes 4000000 | tf_op jit(solution)/shard_map/final/pallas_call | solution.py:375
  (70 shorter events, 7.8 us)
Async XLA Ops:
  7.1 9.0 %collective-permute-start = (bf16[64,512]{1,0:T(8,128)(2,1)}, bf16[64,512]{1,0:T(8,128)(2,1)S(1)}, u32[]{:S(2)}, u32[]{:S(2)}) collective-permute-start(bf16[64,512]{1,0:T(8,128)(2,1)} %get-tuple-element.12), channel_id=1, source_target_pairs={{0,8},{4,12},{8,16},{12,20},{16,24},{20,28},{24,0},{28,4},{32,40},... | collective-permute-start | bytes 196616 | tf_op jit(solution)/shard_map/ppermute | solution.py:299
  8.8 7.3 %collective-permute-start.1 = (bf16[64,512]{1,0:T(8,128)(2,1)}, bf16[64,512]{1,0:T(8,128)(2,1)S(1)}, u32[]{:S(2)}, u32[]{:S(2)}) collective-permute-start(bf16[64,512]{1,0:T(8,128)(2,1)} %get-tuple-element.12), channel_id=1, source_target_pairs={{0,24},{4,28},{8,0},{12,4},{16,8},{20,12},{24,16},{28,20},{32,56},... | collective-permute-start | bytes 196616 | tf_op jit(solution)/shard_map/ppermute | solution.py:299
  10.4 6.0 %collective-permute-start.2 = (bf16[64,512]{1,0:T(8,128)(2,1)}, bf16[64,512]{1,0:T(8,128)(2,1)S(1)}, u32[]{:S(2)}, u32[]{:S(2)}) collective-permute-start(bf16[64,512]{1,0:T(8,128)(2,1)} %get-tuple-element.12), channel_id=1, source_target_pairs={{0,16},{4,20},{8,24},{12,28},{16,0},{20,4},{24,8},{28,12},{32,48},... | collective-permute-start | bytes 196616 | tf_op jit(solution)/shard_map/ppermute | solution.py:299
  12.5 48.4 %collective-permute-start.16 = (bf16[128,1024]{1,0:T(8,128)(2,1)S(1)}, bf16[128,1024]{1,0:T(8,128)(2,1)S(1)}, u32[]{:S(2)}, u32[]{:S(2)}) collective-permute-start(bf16[128,1024]{1,0:T(8,128)(2,1)S(1)} %constant_dynamic-slice_fusion.refs_8_), channel_id=1, source_target_pairs={{0,1},{1,2},{2,3},{3,0},{4,5},{5,6},{6,7},{7,4},{8,9},{9,10},{10,1... | collective-permute-start | bytes 786440 | tf_op jit(solution)/shard_map/ppermute | solution.py:368
  17.2 21.4 %collective-permute-start.3 = (bf16[4,64,512]{2,1,0:T(8,128)(2,1)S(1)}, bf16[4,64,512]{2,1,0:T(8,128)(2,1)S(1)}, u32[]{:S(2)}, u32[]{:S(2)}) collective-permute-start(bf16[4,64,512]{2,1,0:T(8,128)(2,1)S(1)} %pad_maximum_fusion.1.rest_0_), channel_id=1, source_target_pairs={{0,32},{4,36},{8,40},{12,44},{16,48},{20,52},{24,56},{28,60},{32,6... | collective-permute-start | bytes 786440 | tf_op jit(solution)/shard_map/ppermute | solution.py:301
  19.3 19.6 %collective-permute-start.4 = (bf16[4,64,512]{2,1,0:T(8,128)(2,1)S(1)}, bf16[4,64,512]{2,1,0:T(8,128)(2,1)S(1)}, u32[]{:S(2)}, u32[]{:S(2)}) collective-permute-start(bf16[4,64,512]{2,1,0:T(8,128)(2,1)S(1)} %pad_maximum_fusion.1.rest_0_), channel_id=1, source_target_pairs={{0,96},{4,100},{8,104},{12,108},{16,112},{20,116},{24,120},{28,124... | collective-permute-start | bytes 786440 | tf_op jit(solution)/shard_map/ppermute | solution.py:301
  21.5 17.7 %collective-permute-start.5 = (bf16[4,64,512]{2,1,0:T(8,128)(2,1)S(1)}, bf16[4,64,512]{2,1,0:T(8,128)(2,1)}, u32[]{:S(2)}, u32[]{:S(2)}) collective-permute-start(bf16[4,64,512]{2,1,0:T(8,128)(2,1)S(1)} %pad_maximum_fusion.1.rest_0_), channel_id=1, source_target_pairs={{0,64},{4,68},{8,72},{12,76},{16,80},{20,84},{24,88},{28,92},{32,9... | collective-permute-start | bytes 786440 | tf_op jit(solution)/shard_map/ppermute | solution.py:301
  24.8 27.4 %all-to-all-start = ((bf16[32,48,256]{2,1,0:T(8,128)(2,1)}), bf16[32,48,256]{2,1,0:T(8,128)(2,1)S(1)}, u32[]{:S(2)}, u32[]{:S(2)}) async-start(bf16[32,48,256]{2,1,0:T(8,128)(2,1)} %bitcast.4), calls=%async_computation | async-start | bytes 1572864 | tf_op jit(solution)/shard_map/all_to_all | solution.py:318
  38.7 4.0 %collective-permute-start.7 = (bf16[4,64,512]{2,1,0:T(8,128)(2,1)S(1)}, bf16[4,64,512]{2,1,0:T(8,128)(2,1)S(1)}, u32[]{:S(2)}, u32[]{:S(2)}) collective-permute-start(bf16[4,64,512]{2,1,0:T(8,128)(2,1)S(1)} %collective-permute-done.3.rest_1_), channel_id=1, source_target_pairs={{0,4},{4,0},{8,12},{12,8},{16,20},{20,16},{24,28},{28,24},{32,36},... | collective-permute-start | bytes 786440 | tf_op jit(solution)/shard_map/ppermute | solution.py:340
  38.9 4.6 %collective-permute-start.8 = (bf16[4,64,512]{2,1,0:T(8,128)(2,1)S(1)}, bf16[4,64,512]{2,1,0:T(8,128)(2,1)}, u32[]{:S(2)}, u32[]{:S(2)}) collective-permute-start(bf16[4,64,512]{2,1,0:T(8,128)(2,1)S(1)} %collective-permute-done.4.rest_2_), channel_id=1, source_target_pairs={{0,4},{4,0},{8,12},{12,8},{16,20},{20,16},{24,28},{28,24},{32,36},... | collective-permute-start | bytes 786440 | tf_op jit(solution)/shard_map/ppermute | solution.py:340
  39.2 4.3 %collective-permute-start.9 = (bf16[4,64,512]{2,1,0:T(8,128)(2,1)}, bf16[4,64,512]{2,1,0:T(8,128)(2,1)}, u32[]{:S(2)}, u32[]{:S(2)}) collective-permute-start(bf16[4,64,512]{2,1,0:T(8,128)(2,1)} %collective-permute-done.5.rest_3_), channel_id=1, source_target_pairs={{0,4},{4,0},{8,12},{12,8},{16,20},{20,16},{24,28},{28,24},{32,36},... | collective-permute-start | bytes 786440 | tf_op jit(solution)/shard_map/ppermute | solution.py:340
  39.9 22.6 %collective-permute-start.17 = (bf16[128,1024]{1,0:T(8,128)(2,1)S(1)}, bf16[128,1024]{1,0:T(8,128)(2,1)S(1)}, u32[]{:S(2)}, u32[]{:S(2)}) collective-permute-start(bf16[128,1024]{1,0:T(8,128)(2,1)S(1)} %constant_dynamic-slice_fusion.refs_8_), channel_id=1, source_target_pairs={{0,3},{1,0},{2,1},{3,2},{4,7},{5,4},{6,5},{7,6},{8,11},{9,8},{10,9... | collective-permute-start | bytes 786440 | tf_op jit(solution)/shard_map/ppermute | solution.py:368
  42.7 19.9 %collective-permute-start.18 = (bf16[128,1024]{1,0:T(8,128)(2,1)S(1)}, bf16[128,1024]{1,0:T(8,128)(2,1)S(1)}, u32[]{:S(2)}, u32[]{:S(2)}) collective-permute-start(bf16[128,1024]{1,0:T(8,128)(2,1)S(1)} %constant_dynamic-slice_fusion.refs_8_), channel_id=1, source_target_pairs={{0,2},{1,3},{2,0},{3,1},{4,6},{5,7},{6,4},{7,5},{8,10},{9,11},{10,... | collective-permute-start | bytes 786440 | tf_op jit(solution)/shard_map/ppermute | solution.py:368
  43.5 19.6 %collective-permute-start.19 = (bf16[128,1024]{1,0:T(8,128)(2,1)S(1)}, bf16[128,1024]{1,0:T(8,128)(2,1)S(1)}, u32[]{:S(2)}, u32[]{:S(2)}) collective-permute-start(bf16[128,1024]{1,0:T(8,128)(2,1)S(1)} %constant_dynamic-slice_fusion.refs_8_), channel_id=1, source_target_pairs={{0,4},{4,0},{8,12},{12,8},{16,20},{20,16},{24,28},{28,24},{32,36},... | collective-permute-start | bytes 786440 | tf_op jit(solution)/shard_map/ppermute | solution.py:372
  52.1 22.3 %all-to-all-start.1 = ((bf16[32,48,256]{2,1,0:T(8,128)(2,1)}), bf16[32,48,256]{2,1,0:T(8,128)(2,1)}, u32[]{:S(2)}, u32[]{:S(2)}) async-start(bf16[32,48,256]{2,1,0:T(8,128)(2,1)} %far.1), calls=%async_computation.1 | async-start | bytes 1572864 | tf_op jit(solution)/shard_map/all_to_all | solution.py:318
  60.9 4.6 %collective-permute-start.20 = (bf16[128,1024]{1,0:T(8,128)(2,1)S(1)}, bf16[128,1024]{1,0:T(8,128)(2,1)S(1)}, u32[]{:S(2)}, u32[]{:S(2)}) collective-permute-start(bf16[128,1024]{1,0:T(8,128)(2,1)S(1)} %collective-permute-done.16.refs_9_), channel_id=1, source_target_pairs={{0,4},{4,0},{8,12},{12,8},{16,20},{20,16},{24,28},{28,24},{32,36},... | collective-permute-start | bytes 786440 | tf_op jit(solution)/shard_map/ppermute | solution.py:372
  61.6 18.2 %collective-permute-start.13 = (bf16[320,512]{1,0:T(8,128)(2,1)S(1)}, bf16[320,512]{1,0:T(8,128)(2,1)S(1)}, u32[]{:S(2)}, u32[]{:S(2)}) collective-permute-start(bf16[320,512]{1,0:T(8,128)(2,1)S(1)} %pad_maximum_fusion.refs_4_), channel_id=1, source_target_pairs={{0,1},{1,2},{2,3},{3,0},{4,5},{5,6},{6,7},{7,4},{8,9},{9,10},{10,1... | collective-permute-start | bytes 983048 | tf_op jit(solution)/shard_map/ppermute | solution.py:368
  62.6 13.4 %collective-permute-start.21 = (bf16[128,1024]{1,0:T(8,128)(2,1)S(1)}, bf16[128,1024]{1,0:T(8,128)(2,1)}, u32[]{:S(2)}, u32[]{:S(2)}) collective-permute-start(bf16[128,1024]{1,0:T(8,128)(2,1)S(1)} %collective-permute-done.17.refs_10_), channel_id=1, source_target_pairs={{0,4},{4,0},{8,12},{12,8},{16,20},{20,16},{24,28},{28,24},{32,36},... | collective-permute-start | bytes 786440 | tf_op jit(solution)/shard_map/ppermute | solution.py:372
  62.6 14.4 %collective-permute-start.22 = (bf16[128,1024]{1,0:T(8,128)(2,1)S(1)}, bf16[128,1024]{1,0:T(8,128)(2,1)}, u32[]{:S(2)}, u32[]{:S(2)}) collective-permute-start(bf16[128,1024]{1,0:T(8,128)(2,1)S(1)} %collective-permute-done.18.refs_11_), channel_id=1, source_target_pairs={{0,4},{4,0},{8,12},{12,8},{16,20},{20,16},{24,28},{28,24},{32,36},... | collective-permute-start | bytes 786440 | tf_op jit(solution)/shard_map/ppermute | solution.py:372
  63.1 18.3 %collective-permute-start.14 = (bf16[320,512]{1,0:T(8,128)(2,1)S(1)}, bf16[320,512]{1,0:T(8,128)(2,1)S(1)}, u32[]{:S(2)}, u32[]{:S(2)}) collective-permute-start(bf16[320,512]{1,0:T(8,128)(2,1)S(1)} %pad_maximum_fusion.refs_4_), channel_id=1, source_target_pairs={{0,3},{1,0},{2,1},{3,2},{4,7},{5,4},{6,5},{7,6},{8,11},{9,8},{10,9... | collective-permute-start | bytes 983048 | tf_op jit(solution)/shard_map/ppermute | solution.py:368
  65.4 15.9 %collective-permute-start.15 = (bf16[320,512]{1,0:T(8,128)(2,1)S(1)}, bf16[320,512]{1,0:T(8,128)(2,1)S(1)}, u32[]{:S(2)}, u32[]{:S(2)}) collective-permute-start(bf16[320,512]{1,0:T(8,128)(2,1)S(1)} %pad_maximum_fusion.refs_4_), channel_id=1, source_target_pairs={{0,2},{1,3},{2,0},{3,1},{4,6},{5,7},{6,4},{7,5},{8,10},{9,11},{10,... | collective-permute-start | bytes 983048 | tf_op jit(solution)/shard_map/ppermute | solution.py:368
  76.0 10.8 %collective-permute-start.10 = (bf16[320,256]{1,0:T(8,128)(2,1)S(1)}, bf16[320,256]{1,0:T(8,128)(2,1)S(1)}, u32[]{:S(2)}, u32[]{:S(2)}) collective-permute-start(bf16[320,256]{1,0:T(8,128)(2,1)S(1)} %fusion.4.refs_0_), channel_id=1, source_target_pairs={{0,1},{1,2},{2,3},{3,0},{4,5},{5,6},{6,7},{7,4},{8,9},{9,10},{10,1... | collective-permute-start | bytes 491528 | tf_op jit(solution)/shard_map/ppermute | solution.py:368
  77.0 9.9 %collective-permute-start.11 = (bf16[320,256]{1,0:T(8,128)(2,1)S(1)}, bf16[320,256]{1,0:T(8,128)(2,1)S(1)}, u32[]{:S(2)}, u32[]{:S(2)}) collective-permute-start(bf16[320,256]{1,0:T(8,128)(2,1)S(1)} %fusion.4.refs_0_), channel_id=1, source_target_pairs={{0,3},{1,0},{2,1},{3,2},{4,7},{5,4},{6,5},{7,6},{8,11},{9,8},{10,9... | collective-permute-start | bytes 491528 | tf_op jit(solution)/shard_map/ppermute | solution.py:368
  79.8 7.0 %collective-permute-start.12 = (bf16[320,256]{1,0:T(8,128)(2,1)S(1)}, bf16[320,256]{1,0:T(8,128)(2,1)S(1)}, u32[]{:S(2)}, u32[]{:S(2)}) collective-permute-start(bf16[320,256]{1,0:T(8,128)(2,1)S(1)} %fusion.4.refs_0_), channel_id=1, source_target_pairs={{0,2},{1,3},{2,0},{3,1},{4,6},{5,7},{6,4},{7,5},{8,10},{9,11},{10,... | collective-permute-start | bytes 491528 | tf_op jit(solution)/shard_map/ppermute | solution.py:368
  (12 other events, 120.9 us)

commit v10 on v9

--- a/solution.py
+++ b/solution.py
@@ -37,11 +37,11 @@
 
 
 def gather_kernel(
-    x_hbm, wq_hbm, wk_hbm, wv_hbm, pool_ref, vis_ref, order_ref, chunk_ref, q_ref, t_ref, x_ref, wq_ref, wk_ref, wv_ref, sums, rows_in, sem
+    x_hbm, wq_hbm, wk_hbm, wv_hbm, vis_hbm, chunk_ref, q_ref, t_ref, x_ref, wq_ref, wk_ref, wv_ref, vis_ref, sums, rows_in, sem
 ):
     steps = vis_ref.shape[0] // 4
     pairs = list(zip(row_blocks(x_hbm, steps), row_blocks(x_ref, steps)))
-    copies = fetch(pairs + [(wk_hbm, wk_ref), (wv_hbm, wv_ref), (wq_hbm, wq_ref)], sem)
+    copies = fetch([(vis_hbm, vis_ref)] + pairs + [(wk_hbm, wk_ref), (wv_hbm, wv_ref), (wq_hbm, wq_ref)], sem)
     rows = x_ref.shape[0] // steps
     frames, keep = vis_ref.shape
     count = 4 * keep
@@ -49,13 +49,19 @@
     r = lax.broadcasted_iota(jnp.int32, (count, 1), 0)
     frame = sum((r >= keep * i).astype(jnp.int32) for i in (1, 2, 3))
     spot = lax.broadcasted_iota(jnp.int32, (count, keep), 1) == r - keep * frame
+    c = lax.broadcasted_iota(jnp.int32, (1, rows), 1)
+    f = sum((c >= PATCHES * i).astype(jnp.int32) for i in (1, 2, 3))
+    p = c - f * PATCHES
+    quadrant = 4 * f + 2 * (p >= 98).astype(jnp.int32) + (p - p // 14 * 14 >= 7).astype(jnp.int32)
+    pool = (lax.broadcasted_iota(jnp.int32, (16, rows), 0) == quadrant).astype(F32).astype(BF)
+    copies[0].wait()
     for step in range(steps):
         mine = (lax.broadcasted_iota(jnp.int32, (count, frames), 1) == frame + step * 4).astype(F32).astype(BF)
         seen = nn(mine, vis_ref[...].astype(F32).astype(BF))
         pos = jnp.sum(jnp.where(spot, seen, 0.0), axis=1, keepdims=True).astype(jnp.int32) + frame * PATCHES
         pick = (pos == lax.broadcasted_iota(jnp.int32, (count, rows), 1)).astype(F32).astype(BF)
-        choose = jnp.concatenate([pool_ref[...], pick], axis=0)
-        copies[step].wait()
+        choose = jnp.concatenate([pool, pick], axis=0)
+        copies[1 + step].wait()
         both = nn(choose, x_ref[step * rows : (step + 1) * rows, :])
         sums[step * 16 : (step + 1) * 16, :] = both[:16]
         rows_in[step * count : (step + 1) * count, :] = both[16:].astype(BF)
@@ -64,13 +70,15 @@
     high = total.astype(BF)
     low = (total - high.astype(F32)).astype(BF)
     pair = jnp.concatenate([high, low], axis=0)
-    order = order_ref[...]
+    r = lax.broadcasted_iota(jnp.int32, (count, count), 0)
+    source = (r - r // frames * frames) * 4 + r // frames
+    order = (source == lax.broadcasted_iota(jnp.int32, (count, count), 1)).astype(F32).astype(BF)
     for i, w_ref in enumerate((wk_ref, wv_ref)):
-        copies[steps + i].wait()
+        copies[1 + steps + i].wait()
         field = nn(pair, w_ref[...])
         pooled = ((field[:count] + field[count:]) / 7.0).astype(BF)
         chunk_ref[:, i * cols : (i + 1) * cols] = nn(order, pooled).astype(BF)
-    copies[steps + 2].wait()
+    copies[steps + 3].wait()
     q = nn(rows_in[...], wq_ref[...]).astype(BF).astype(F32) * HEAD_DIM ** -0.5
     q_ref[...] = q.astype(BF)
     t_ref[q_ref.shape[0] :, :] = jnp.zeros((t_ref.shape[0] - q_ref.shape[0], cols), BF)
@@ -270,18 +278,9 @@
     padded = -(-own // 128) * 128
     my_core = me % 2
 
-    r = np.arange(block)
-    p = r % PATCHES
-    quadrant = 2 * (p // 14 >= 7) + (p % 14 >= 7)
-    pool = np.zeros((16, block), np.float32)
-    pool[r // PATCHES * 4 + quadrant, r] = 1.0
-    n = np.arange(4 * frames)
-    order = np.zeros((4 * frames, 4 * frames), np.float32)
-    order[n, n % frames * 4 + n // frames] = 1.0
-
     mine, q, tok = pl.pallas_call(
         gather_kernel,
-        in_specs=[HBM] * 4 + whole(3),
+        in_specs=[HBM] * 5,
         out_specs=whole(3),
         out_shape=[
             jax.ShapeDtypeStruct((4 * frames, 2 * cols), BF),
@@ -290,11 +289,12 @@
         ],
         scratch_shapes=[pltpu.VMEM((frames * PATCHES, width), BF)]
         + [pltpu.VMEM((width, cols), BF)] * 3
-        + [pltpu.VMEM((4 * frames, width), F32), pltpu.VMEM((own, width), BF), pltpu.SemaphoreType.DMA((steps + 3,))],
+        + [pltpu.VMEM((frames, keep), jnp.int32), pltpu.VMEM((4 * frames, width), F32), pltpu.VMEM((own, width), BF)]
+        + [pltpu.SemaphoreType.DMA((steps + 4,))],
         compiler_params=params(60),
         cost_estimate=pl.CostEstimate(flops=2 * 10**9, bytes_accessed=10**7, transcendentals=0),
         name="gather",
-    )(tokens, w_query, w_key, w_value, jnp.asarray(pool, BF), visible, jnp.asarray(order, BF))
+    )(tokens, w_query, w_key, w_value, visible)
 
     plane = jnp.stack([mine] + [lax.ppermute(mine, "tm", along_y(d)) for d in DISTANCES[1:]])
     plane, q, tok = lax.optimization_barrier((plane, q, tok))

time: 91.9 us -> 91.1 us (level)
  no operation moved by 1% of the time
where the time goes in v10:
time: 91.1 us; the launch traced here: 89.9 us
  starting transfers between devices  40.7 us (45%)
  Pallas kernels  26.5 us (29%)
  waiting for transfers between devices  14.2 us (16%)
  matrix products  3.6 us (4%)
  other arithmetic  3.5 us (4%)
  between operations  1.06 us (1%)
    ppermute x9, starting transfers between devices, over_heads(): return [x] + [lax.ppermute(x, 'head', to(d)) for d in DISTANCES[1:]]  14.8 us
    all_to_all x2, starting transfers between devices, deliver(): return lax.all_to_all(packed, 'tm', 0, 0, tiled=True)  12.6 us
    pallas_call x1, Pallas kernels, body(): pl.pallas_call(near_kernel, in_specs=[HBM] * 4, out_specs=pl.BlockSpec(me...  8.68 us
    pallas_call x1, Pallas kernels, body(): pl.pallas_call(far_kernel, in_specs=[HBM] * 12, out_specs=pl.BlockSpec(me...  8.58 us
    all_to_all x2, waiting for transfers between devices, deliver(): return lax.all_to_all(packed, 'tm', 0, 0, tiled=True)  7.46 us
    ppermute x3, starting transfers between devices, body(): lax.ppermute(plane, 'tm', along_z(d))  6.06 us
    ppermute x9, waiting for transfers between devices, over_heads(): return [x] + [lax.ppermute(x, 'head', to(d)) for d in DISTANCES[1:]]  6.02 us
    pallas_call x1, Pallas kernels, body(): pl.pallas_call(gather_kernel, in_specs=[HBM] * 5, out_specs=whole(3), out...  5.64 us
  transfers between devices with their start and end apart: 25, of which 5 were waited for; matrix products, arithmetic and copies ran while one was open for 8% of the time, Pallas kernels for 19%

profile of v10, /device:TPU:0, one launch (start us, length us, event | category | flops | bytes accessed | tf_op | source)
XLA Modules:
  0.0 89.9 jit_solution(3560854642243330027)
XLA Ops:
  0.7 5.6 %gather.1 = (bf16[64,512]{1,0:T(8,128)(2,1)}, bf16[320,256]{1,0:T(8,128)(2,1)}, bf16[384,256]{1,0:T(8,128)(2,1)}) custom-call(bf16[3136,1024]{1,0:T(8,128)(2,1)} %x_hbm.3, bf16[1024,256]{1,0:T(8,128)(2,1)} %wq_hbm.1, bf16[1024,256]{1,0:T(8,128)(2,1)} %wk_hbm.3, bf16[1024,256]{1,0:T(8,128)(2,1)} %wv_hbm.3, s32[16,20]{1,0:T(8,128)} %vis_hbm.1), custom_call_target="tpu_custom_call" | custom-call | flops 2000000000 | bytes 10000000 | tf_op jit(solution)/shard_map/gather/pallas_call | solution.py:281
  6.3 1.7 %collective-permute-start = (bf16[64,512]{1,0:T(8,128)(2,1)}, bf16[64,512]{1,0:T(8,128)(2,1)S(1)}, u32[]{:S(2)}, u32[]{:S(2)}) collective-permute-start(bf16[64,512]{1,0:T(8,128)(2,1)} %get-tuple-element.12), channel_id=1, source_target_pairs={{0,8},{4,12},{8,16},{12,20},{16,24},{20,28},{24,0},{28,4},{32,40},... | collective-permute-start | bytes 196616 | tf_op jit(solution)/shard_map/ppermute | solution.py:299
  8.1 1.6 %collective-permute-start.1 = (bf16[64,512]{1,0:T(8,128)(2,1)}, bf16[64,512]{1,0:T(8,128)(2,1)S(1)}, u32[]{:S(2)}, u32[]{:S(2)}) collective-permute-start(bf16[64,512]{1,0:T(8,128)(2,1)} %get-tuple-element.12), channel_id=1, source_target_pairs={{0,24},{4,28},{8,0},{12,4},{16,8},{20,12},{24,16},{28,20},{32,56},... | collective-permute-start | bytes 196616 | tf_op jit(solution)/shard_map/ppermute | solution.py:299
  9.6 2.1 %collective-permute-start.2 = (bf16[64,512]{1,0:T(8,128)(2,1)}, bf16[64,512]{1,0:T(8,128)(2,1)S(1)}, u32[]{:S(2)}, u32[]{:S(2)}) collective-permute-start(bf16[64,512]{1,0:T(8,128)(2,1)} %get-tuple-element.12), channel_id=1, source_target_pairs={{0,16},{4,20},{8,24},{12,28},{16,0},{20,4},{24,8},{28,12},{32,48},... | collective-permute-start | bytes 196616 | tf_op jit(solution)/shard_map/ppermute | solution.py:299
  11.7 1.6 %collective-permute-start.16 = (bf16[128,1024]{1,0:T(8,128)(2,1)S(1)}, bf16[128,1024]{1,0:T(8,128)(2,1)S(1)}, u32[]{:S(2)}, u32[]{:S(2)}) collective-permute-start(bf16[128,1024]{1,0:T(8,128)(2,1)S(1)} %constant_dynamic-slice_fusion.refs_8_), channel_id=1, source_target_pairs={{0,1},{1,2},{2,3},{3,0},{4,5},{5,6},{6,7},{7,4},{8,9},{9,10},{10,1... | collective-permute-start | bytes 786440 | tf_op jit(solution)/shard_map/ppermute | solution.py:368
  13.7 1.5 %fusion.pack_hbm = bf16[1536,384]{1,0:T(8,128)(2,1)} fusion(s32[384]{0:T(512)S(1)} %pad.4), kind=kLoop, calls=%fused_computation.2 | loop fusion | flops 1179648 | bytes 1181184 | tf_op jit(solution)/shard_map/convert_element_type | solution.py:309
  16.5 2.1 %collective-permute-start.3 = (bf16[4,64,512]{2,1,0:T(8,128)(2,1)S(1)}, bf16[4,64,512]{2,1,0:T(8,128)(2,1)S(1)}, u32[]{:S(2)}, u32[]{:S(2)}) collective-permute-start(bf16[4,64,512]{2,1,0:T(8,128)(2,1)S(1)} %pad_maximum_fusion.1.rest_0_), channel_id=1, source_target_pairs={{0,32},{4,36},{8,40},{12,44},{16,48},{20,52},{24,56},{28,60},{32,6... | collective-permute-start | bytes 786440 | tf_op jit(solution)/shard_map/ppermute | solution.py:301
  18.6 2.2 %collective-permute-start.4 = (bf16[4,64,512]{2,1,0:T(8,128)(2,1)S(1)}, bf16[4,64,512]{2,1,0:T(8,128)(2,1)S(1)}, u32[]{:S(2)}, u32[]{:S(2)}) collective-permute-start(bf16[4,64,512]{2,1,0:T(8,128)(2,1)S(1)} %pad_maximum_fusion.1.rest_0_), channel_id=1, source_target_pairs={{0,96},{4,100},{8,104},{12,108},{16,112},{20,116},{24,120},{28,124... | collective-permute-start | bytes 786440 | tf_op jit(solution)/shard_map/ppermute | solution.py:301
  20.8 1.8 %collective-permute-start.5 = (bf16[4,64,512]{2,1,0:T(8,128)(2,1)S(1)}, bf16[4,64,512]{2,1,0:T(8,128)(2,1)}, u32[]{:S(2)}, u32[]{:S(2)}) collective-permute-start(bf16[4,64,512]{2,1,0:T(8,128)(2,1)S(1)} %pad_maximum_fusion.1.rest_0_), channel_id=1, source_target_pairs={{0,64},{4,68},{8,72},{12,76},{16,80},{20,84},{24,88},{28,92},{32,9... | collective-permute-start | bytes 786440 | tf_op jit(solution)/shard_map/ppermute | solution.py:301
  22.6 1.5 %convolution_convert_fusion = bf16[1536,256]{1,0:T(8,128)(2,1)} fusion(bf16[384,256]{1,0:T(8,128)(2,1)S(1)} %copy-done.10, s32[384]{0:T(512)S(1)} %pad.4), kind=kOutput, calls=%fused_computation | convolution fusion | flops 302972928 | bytes 984576 | tf_op jit(solution)/shard_map/dot_general | solution.py:323
  24.0 4.8 %all-to-all-start = ((bf16[32,48,256]{2,1,0:T(8,128)(2,1)}), bf16[32,48,256]{2,1,0:T(8,128)(2,1)S(1)}, u32[]{:S(2)}, u32[]{:S(2)}) async-start(bf16[32,48,256]{2,1,0:T(8,128)(2,1)} %bitcast.4), calls=%async_computation | async-start | bytes 1572864 | tf_op jit(solution)/shard_map/all_to_all | solution.py:318
  28.9 8.7 %near.1.near_hbm = bf16[1280,384]{1,0:T(8,128)(2,1)} custom-call(bf16[320,256]{1,0:T(8,128)(2,1)} %get-tuple-element.15.q_hbm, bf16[3136,1024]{1,0:T(8,128)(2,1)} %x_hbm.3, bf16[1024,256]{1,0:T(8,128)(2,1)} %wk_hbm.3, bf16[1024,256]{1,0:T(8,128)(2,1)} %wv_hbm.3), custom_call_target="tpu_custom_call" | custom-call | flops 5000000000 | bytes 10000000 | tf_op jit(solution)/shard_map/near/pallas_call | solution.py:326
  39.2 2.8 %collective-permute-start.17 = (bf16[128,1024]{1,0:T(8,128)(2,1)S(1)}, bf16[128,1024]{1,0:T(8,128)(2,1)S(1)}, u32[]{:S(2)}, u32[]{:S(2)}) collective-permute-start(bf16[128,1024]{1,0:T(8,128)(2,1)S(1)} %constant_dynamic-slice_fusion.refs_8_), channel_id=1, source_target_pairs={{0,3},{1,0},{2,1},{3,2},{4,7},{5,4},{6,5},{7,6},{8,11},{9,8},{10,9... | collective-permute-start | bytes 786440 | tf_op jit(solution)/shard_map/ppermute | solution.py:368
  42.8 8.6 %far.1 = bf16[32,48,256]{2,1,0:T(8,128)(2,1)} custom-call(bf16[320,256]{1,0:T(8,128)(2,1)} %get-tuple-element.15.q_hbm, bf16[1280,384]{1,0:T(8,128)(2,1)} %near.1.near_hbm, s32[16,512]{1,0:T(8,128)} %allow_hbm.1, bf16[1536,384]{1,0:T(8,128)(2,1)} %fusion.pack_hbm, bf16[4,64,512]{2,1,0:T(8,128)(2,1)} %copy-done.1, bf16[4,64,512]{2,1,0:T(8,128)(2,1)} %copy-done.2, ...), custom_call_target="tpu_custom_call" | custom-call | flops 1000000 | bytes 10000 | tf_op jit(solution)/shard_map/far/pallas_call | solution.py:341
  51.4 7.7 %all-to-all-start.1 = ((bf16[32,48,256]{2,1,0:T(8,128)(2,1)}), bf16[32,48,256]{2,1,0:T(8,128)(2,1)}, u32[]{:S(2)}, u32[]{:S(2)}) async-start(bf16[32,48,256]{2,1,0:T(8,128)(2,1)} %far.1), calls=%async_computation.1 | async-start | bytes 1572864 | tf_op jit(solution)/shard_map/all_to_all | solution.py:318
  60.9 1.0 %collective-permute-start.13 = (bf16[320,512]{1,0:T(8,128)(2,1)S(1)}, bf16[320,512]{1,0:T(8,128)(2,1)S(1)}, u32[]{:S(2)}, u32[]{:S(2)}) collective-permute-start(bf16[320,512]{1,0:T(8,128)(2,1)S(1)} %pad_maximum_fusion.refs_4_), channel_id=1, source_target_pairs={{0,1},{1,2},{2,3},{3,0},{4,5},{5,6},{6,7},{7,4},{8,9},{9,10},{10,1... | collective-permute-start | bytes 983048 | tf_op jit(solution)/shard_map/ppermute | solution.py:368
  62.4 2.3 %collective-permute-start.14 = (bf16[320,512]{1,0:T(8,128)(2,1)S(1)}, bf16[320,512]{1,0:T(8,128)(2,1)S(1)}, u32[]{:S(2)}, u32[]{:S(2)}) collective-permute-start(bf16[320,512]{1,0:T(8,128)(2,1)S(1)} %pad_maximum_fusion.refs_4_), channel_id=1, source_target_pairs={{0,3},{1,0},{2,1},{3,2},{4,7},{5,4},{6,5},{7,6},{8,11},{9,8},{10,9... | collective-permute-start | bytes 983048 | tf_op jit(solution)/shard_map/ppermute | solution.py:368
  64.7 1.5 %collective-permute-start.15 = (bf16[320,512]{1,0:T(8,128)(2,1)S(1)}, bf16[320,512]{1,0:T(8,128)(2,1)S(1)}, u32[]{:S(2)}, u32[]{:S(2)}) collective-permute-start(bf16[320,512]{1,0:T(8,128)(2,1)S(1)} %pad_maximum_fusion.refs_4_), channel_id=1, source_target_pairs={{0,2},{1,3},{2,0},{3,1},{4,6},{5,7},{6,4},{7,5},{8,10},{9,11},{10,... | collective-permute-start | bytes 983048 | tf_op jit(solution)/shard_map/ppermute | solution.py:368
  66.2 7.5 %all-to-all-done.1 = bf16[32,48,256]{2,1,0:T(8,128)(2,1)} async-done(((bf16[32,48,256]{2,1,0:T(8,128)(2,1)}), bf16[32,48,256]{2,1,0:T(8,128)(2,1)}, u32[]{:S(2)}, u32[]{:S(2)}) %all-to-all-start.1) | async-done | bytes 786464 | tf_op jit(solution)/shard_map/all_to_all | solution.py:318
  73.7 1.6 %fusion.4.refs_0_ = bf16[320,256]{1,0:T(8,128)(2,1)S(1)} fusion(bf16[1536,256]{1,0:T(8,128)(2,1)} %bitcast.5, s32[1536]{0:T(1024)S(1)} %eq.70), kind=kOutput, calls=%fused_computation.9 | convolution fusion | flops 252231680 | bytes 956416 | tf_op jit(solution)/shard_map/dot_general | solution.py:321
  76.2 2.3 %collective-permute-start.11 = (bf16[320,256]{1,0:T(8,128)(2,1)S(1)}, bf16[320,256]{1,0:T(8,128)(2,1)S(1)}, u32[]{:S(2)}, u32[]{:S(2)}) collective-permute-start(bf16[320,256]{1,0:T(8,128)(2,1)S(1)} %fusion.4.refs_0_), channel_id=1, source_target_pairs={{0,3},{1,0},{2,1},{3,2},{4,7},{5,4},{6,5},{7,6},{8,11},{9,8},{10,9... | collective-permute-start | bytes 491528 | tf_op jit(solution)/shard_map/ppermute | solution.py:368
  79.1 1.5 %collective-permute-start.12 = (bf16[320,256]{1,0:T(8,128)(2,1)S(1)}, bf16[320,256]{1,0:T(8,128)(2,1)S(1)}, u32[]{:S(2)}, u32[]{:S(2)}) collective-permute-start(bf16[320,256]{1,0:T(8,128)(2,1)S(1)} %fusion.4.refs_0_), channel_id=1, source_target_pairs={{0,2},{1,3},{2,0},{3,1},{4,6},{5,7},{6,4},{7,5},{8,10},{9,11},{10,... | collective-permute-start | bytes 491528 | tf_op jit(solution)/shard_map/ppermute | solution.py:368
  80.6 5.5 %collective-permute-done.10.refs_1_ = bf16[320,256]{1,0:T(8,128)(2,1)S(1)} collective-permute-done((bf16[320,256]{1,0:T(8,128)(2,1)S(1)}, bf16[320,256]{1,0:T(8,128)(2,1)S(1)}, u32[]{:S(2)}, u32[]{:S(2)}) %collective-permute-start.10) | collective-permute-done | bytes 163872 | tf_op jit(solution)/shard_map/ppermute | solution.py:368
  86.1 3.6 %final.1 = (bf16[320,256]{1,0:T(8,128)(2,1)}, f32[320]{0:T(512)}) custom-call(bf16[320,256]{1,0:T(8,128)(2,1)S(1)} %fusion.4.refs_0_, bf16[320,256]{1,0:T(8,128)(2,1)S(1)} %collective-permute-done.10.refs_1_, bf16[320,256]{1,0:T(8,128)(2,1)S(1)} %collective-permute-done.11.refs_2_, bf16[320,256]{1,0:T(8,128)(2,1)S(1)} %collective-permute-done.12.refs_3_, ...), custom_call_target="tpu_custom_call" | custom-call | flops 1000000000 | bytes 4000000 | tf_op jit(solution)/shard_map/final/pallas_call | solution.py:375
  (70 shorter events, 7.8 us)
Async XLA Ops:
  6.3 9.0 %collective-permute-start = (bf16[64,512]{1,0:T(8,128)(2,1)}, bf16[64,512]{1,0:T(8,128)(2,1)S(1)}, u32[]{:S(2)}, u32[]{:S(2)}) collective-permute-start(bf16[64,512]{1,0:T(8,128)(2,1)} %get-tuple-element.12), channel_id=1, source_target_pairs={{0,8},{4,12},{8,16},{12,20},{16,24},{20,28},{24,0},{28,4},{32,40},... | collective-permute-start | bytes 196616 | tf_op jit(solution)/shard_map/ppermute | solution.py:299
  8.1 7.3 %collective-permute-start.1 = (bf16[64,512]{1,0:T(8,128)(2,1)}, bf16[64,512]{1,0:T(8,128)(2,1)S(1)}, u32[]{:S(2)}, u32[]{:S(2)}) collective-permute-start(bf16[64,512]{1,0:T(8,128)(2,1)} %get-tuple-element.12), channel_id=1, source_target_pairs={{0,24},{4,28},{8,0},{12,4},{16,8},{20,12},{24,16},{28,20},{32,56},... | collective-permute-start | bytes 196616 | tf_op jit(solution)/shard_map/ppermute | solution.py:299
  9.6 6.0 %collective-permute-start.2 = (bf16[64,512]{1,0:T(8,128)(2,1)}, bf16[64,512]{1,0:T(8,128)(2,1)S(1)}, u32[]{:S(2)}, u32[]{:S(2)}) collective-permute-start(bf16[64,512]{1,0:T(8,128)(2,1)} %get-tuple-element.12), channel_id=1, source_target_pairs={{0,16},{4,20},{8,24},{12,28},{16,0},{20,4},{24,8},{28,12},{32,48},... | collective-permute-start | bytes 196616 | tf_op jit(solution)/shard_map/ppermute | solution.py:299
  11.7 48.4 %collective-permute-start.16 = (bf16[128,1024]{1,0:T(8,128)(2,1)S(1)}, bf16[128,1024]{1,0:T(8,128)(2,1)S(1)}, u32[]{:S(2)}, u32[]{:S(2)}) collective-permute-start(bf16[128,1024]{1,0:T(8,128)(2,1)S(1)} %constant_dynamic-slice_fusion.refs_8_), channel_id=1, source_target_pairs={{0,1},{1,2},{2,3},{3,0},{4,5},{5,6},{6,7},{7,4},{8,9},{9,10},{10,1... | collective-permute-start | bytes 786440 | tf_op jit(solution)/shard_map/ppermute | solution.py:368
  16.5 21.4 %collective-permute-start.3 = (bf16[4,64,512]{2,1,0:T(8,128)(2,1)S(1)}, bf16[4,64,512]{2,1,0:T(8,128)(2,1)S(1)}, u32[]{:S(2)}, u32[]{:S(2)}) collective-permute-start(bf16[4,64,512]{2,1,0:T(8,128)(2,1)S(1)} %pad_maximum_fusion.1.rest_0_), channel_id=1, source_target_pairs={{0,32},{4,36},{8,40},{12,44},{16,48},{20,52},{24,56},{28,60},{32,6... | collective-permute-start | bytes 786440 | tf_op jit(solution)/shard_map/ppermute | solution.py:301
  18.6 19.6 %collective-permute-start.4 = (bf16[4,64,512]{2,1,0:T(8,128)(2,1)S(1)}, bf16[4,64,512]{2,1,0:T(8,128)(2,1)S(1)}, u32[]{:S(2)}, u32[]{:S(2)}) collective-permute-start(bf16[4,64,512]{2,1,0:T(8,128)(2,1)S(1)} %pad_maximum_fusion.1.rest_0_), channel_id=1, source_target_pairs={{0,96},{4,100},{8,104},{12,108},{16,112},{20,116},{24,120},{28,124... | collective-permute-start | bytes 786440 | tf_op jit(solution)/shard_map/ppermute | solution.py:301
  20.8 17.7 %collective-permute-start.5 = (bf16[4,64,512]{2,1,0:T(8,128)(2,1)S(1)}, bf16[4,64,512]{2,1,0:T(8,128)(2,1)}, u32[]{:S(2)}, u32[]{:S(2)}) collective-permute-start(bf16[4,64,512]{2,1,0:T(8,128)(2,1)S(1)} %pad_maximum_fusion.1.rest_0_), channel_id=1, source_target_pairs={{0,64},{4,68},{8,72},{12,76},{16,80},{20,84},{24,88},{28,92},{32,9... | collective-permute-start | bytes 786440 | tf_op jit(solution)/shard_map/ppermute | solution.py:301
  24.0 27.4 %all-to-all-start = ((bf16[32,48,256]{2,1,0:T(8,128)(2,1)}), bf16[32,48,256]{2,1,0:T(8,128)(2,1)S(1)}, u32[]{:S(2)}, u32[]{:S(2)}) async-start(bf16[32,48,256]{2,1,0:T(8,128)(2,1)} %bitcast.4), calls=%async_computation | async-start | bytes 1572864 | tf_op jit(solution)/shard_map/all_to_all | solution.py:318
  37.9 4.0 %collective-permute-start.7 = (bf16[4,64,512]{2,1,0:T(8,128)(2,1)S(1)}, bf16[4,64,512]{2,1,0:T(8,128)(2,1)S(1)}, u32[]{:S(2)}, u32[]{:S(2)}) collective-permute-start(bf16[4,64,512]{2,1,0:T(8,128)(2,1)S(1)} %collective-permute-done.3.rest_1_), channel_id=1, source_target_pairs={{0,4},{4,0},{8,12},{12,8},{16,20},{20,16},{24,28},{28,24},{32,36},... | collective-permute-start | bytes 786440 | tf_op jit(solution)/shard_map/ppermute | solution.py:340
  38.2 4.6 %collective-permute-start.8 = (bf16[4,64,512]{2,1,0:T(8,128)(2,1)S(1)}, bf16[4,64,512]{2,1,0:T(8,128)(2,1)}, u32[]{:S(2)}, u32[]{:S(2)}) collective-permute-start(bf16[4,64,512]{2,1,0:T(8,128)(2,1)S(1)} %collective-permute-done.4.rest_2_), channel_id=1, source_target_pairs={{0,4},{4,0},{8,12},{12,8},{16,20},{20,16},{24,28},{28,24},{32,36},... | collective-permute-start | bytes 786440 | tf_op jit(solution)/shard_map/ppermute | solution.py:340
  38.5 4.3 %collective-permute-start.9 = (bf16[4,64,512]{2,1,0:T(8,128)(2,1)}, bf16[4,64,512]{2,1,0:T(8,128)(2,1)}, u32[]{:S(2)}, u32[]{:S(2)}) collective-permute-start(bf16[4,64,512]{2,1,0:T(8,128)(2,1)} %collective-permute-done.5.rest_3_), channel_id=1, source_target_pairs={{0,4},{4,0},{8,12},{12,8},{16,20},{20,16},{24,28},{28,24},{32,36},... | collective-permute-start | bytes 786440 | tf_op jit(solution)/shard_map/ppermute | solution.py:340
  39.2 22.7 %collective-permute-start.17 = (bf16[128,1024]{1,0:T(8,128)(2,1)S(1)}, bf16[128,1024]{1,0:T(8,128)(2,1)S(1)}, u32[]{:S(2)}, u32[]{:S(2)}) collective-permute-start(bf16[128,1024]{1,0:T(8,128)(2,1)S(1)} %constant_dynamic-slice_fusion.refs_8_), channel_id=1, source_target_pairs={{0,3},{1,0},{2,1},{3,2},{4,7},{5,4},{6,5},{7,6},{8,11},{9,8},{10,9... | collective-permute-start | bytes 786440 | tf_op jit(solution)/shard_map/ppermute | solution.py:368
  42.0 19.9 %collective-permute-start.18 = (bf16[128,1024]{1,0:T(8,128)(2,1)S(1)}, bf16[128,1024]{1,0:T(8,128)(2,1)S(1)}, u32[]{:S(2)}, u32[]{:S(2)}) collective-permute-start(bf16[128,1024]{1,0:T(8,128)(2,1)S(1)} %constant_dynamic-slice_fusion.refs_8_), channel_id=1, source_target_pairs={{0,2},{1,3},{2,0},{3,1},{4,6},{5,7},{6,4},{7,5},{8,10},{9,11},{10,... | collective-permute-start | bytes 786440 | tf_op jit(solution)/shard_map/ppermute | solution.py:368
  42.8 19.6 %collective-permute-start.19 = (bf16[128,1024]{1,0:T(8,128)(2,1)S(1)}, bf16[128,1024]{1,0:T(8,128)(2,1)S(1)}, u32[]{:S(2)}, u32[]{:S(2)}) collective-permute-start(bf16[128,1024]{1,0:T(8,128)(2,1)S(1)} %constant_dynamic-slice_fusion.refs_8_), channel_id=1, source_target_pairs={{0,4},{4,0},{8,12},{12,8},{16,20},{20,16},{24,28},{28,24},{32,36},... | collective-permute-start | bytes 786440 | tf_op jit(solution)/shard_map/ppermute | solution.py:372
  51.4 22.3 %all-to-all-start.1 = ((bf16[32,48,256]{2,1,0:T(8,128)(2,1)}), bf16[32,48,256]{2,1,0:T(8,128)(2,1)}, u32[]{:S(2)}, u32[]{:S(2)}) async-start(bf16[32,48,256]{2,1,0:T(8,128)(2,1)} %far.1), calls=%async_computation.1 | async-start | bytes 1572864 | tf_op jit(solution)/shard_map/all_to_all | solution.py:318
  60.1 4.6 %collective-permute-start.20 = (bf16[128,1024]{1,0:T(8,128)(2,1)S(1)}, bf16[128,1024]{1,0:T(8,128)(2,1)S(1)}, u32[]{:S(2)}, u32[]{:S(2)}) collective-permute-start(bf16[128,1024]{1,0:T(8,128)(2,1)S(1)} %collective-permute-done.16.refs_9_), channel_id=1, source_target_pairs={{0,4},{4,0},{8,12},{12,8},{16,20},{20,16},{24,28},{28,24},{32,36},... | collective-permute-start | bytes 786440 | tf_op jit(solution)/shard_map/ppermute | solution.py:372
  60.9 18.2 %collective-permute-start.13 = (bf16[320,512]{1,0:T(8,128)(2,1)S(1)}, bf16[320,512]{1,0:T(8,128)(2,1)S(1)}, u32[]{:S(2)}, u32[]{:S(2)}) collective-permute-start(bf16[320,512]{1,0:T(8,128)(2,1)S(1)} %pad_maximum_fusion.refs_4_), channel_id=1, source_target_pairs={{0,1},{1,2},{2,3},{3,0},{4,5},{5,6},{6,7},{7,4},{8,9},{9,10},{10,1... | collective-permute-start | bytes 983048 | tf_op jit(solution)/shard_map/ppermute | solution.py:368
  61.9 13.4 %collective-permute-start.21 = (bf16[128,1024]{1,0:T(8,128)(2,1)S(1)}, bf16[128,1024]{1,0:T(8,128)(2,1)}, u32[]{:S(2)}, u32[]{:S(2)}) collective-permute-start(bf16[128,1024]{1,0:T(8,128)(2,1)S(1)} %collective-permute-done.17.refs_10_), channel_id=1, source_target_pairs={{0,4},{4,0},{8,12},{12,8},{16,20},{20,16},{24,28},{28,24},{32,36},... | collective-permute-start | bytes 786440 | tf_op jit(solution)/shard_map/ppermute | solution.py:372
  61.9 14.4 %collective-permute-start.22 = (bf16[128,1024]{1,0:T(8,128)(2,1)S(1)}, bf16[128,1024]{1,0:T(8,128)(2,1)}, u32[]{:S(2)}, u32[]{:S(2)}) collective-permute-start(bf16[128,1024]{1,0:T(8,128)(2,1)S(1)} %collective-permute-done.18.refs_11_), channel_id=1, source_target_pairs={{0,4},{4,0},{8,12},{12,8},{16,20},{20,16},{24,28},{28,24},{32,36},... | collective-permute-start | bytes 786440 | tf_op jit(solution)/shard_map/ppermute | solution.py:372
  62.4 18.3 %collective-permute-start.14 = (bf16[320,512]{1,0:T(8,128)(2,1)S(1)}, bf16[320,512]{1,0:T(8,128)(2,1)S(1)}, u32[]{:S(2)}, u32[]{:S(2)}) collective-permute-start(bf16[320,512]{1,0:T(8,128)(2,1)S(1)} %pad_maximum_fusion.refs_4_), channel_id=1, source_target_pairs={{0,3},{1,0},{2,1},{3,2},{4,7},{5,4},{6,5},{7,6},{8,11},{9,8},{10,9... | collective-permute-start | bytes 983048 | tf_op jit(solution)/shard_map/ppermute | solution.py:368
  64.7 15.9 %collective-permute-start.15 = (bf16[320,512]{1,0:T(8,128)(2,1)S(1)}, bf16[320,512]{1,0:T(8,128)(2,1)S(1)}, u32[]{:S(2)}, u32[]{:S(2)}) collective-permute-start(bf16[320,512]{1,0:T(8,128)(2,1)S(1)} %pad_maximum_fusion.refs_4_), channel_id=1, source_target_pairs={{0,2},{1,3},{2,0},{3,1},{4,6},{5,7},{6,4},{7,5},{8,10},{9,11},{10,... | collective-permute-start | bytes 983048 | tf_op jit(solution)/shard_map/ppermute | solution.py:368
  75.3 10.8 %collective-permute-start.10 = (bf16[320,256]{1,0:T(8,128)(2,1)S(1)}, bf16[320,256]{1,0:T(8,128)(2,1)S(1)}, u32[]{:S(2)}, u32[]{:S(2)}) collective-permute-start(bf16[320,256]{1,0:T(8,128)(2,1)S(1)} %fusion.4.refs_0_), channel_id=1, source_target_pairs={{0,1},{1,2},{2,3},{3,0},{4,5},{5,6},{6,7},{7,4},{8,9},{9,10},{10,1... | collective-permute-start | bytes 491528 | tf_op jit(solution)/shard_map/ppermute | solution.py:368
  76.2 9.9 %collective-permute-start.11 = (bf16[320,256]{1,0:T(8,128)(2,1)S(1)}, bf16[320,256]{1,0:T(8,128)(2,1)S(1)}, u32[]{:S(2)}, u32[]{:S(2)}) collective-permute-start(bf16[320,256]{1,0:T(8,128)(2,1)S(1)} %fusion.4.refs_0_), channel_id=1, source_target_pairs={{0,3},{1,0},{2,1},{3,2},{4,7},{5,4},{6,5},{7,6},{8,11},{9,8},{10,9... | collective-permute-start | bytes 491528 | tf_op jit(solution)/shard_map/ppermute | solution.py:368
  79.1 7.0 %collective-permute-start.12 = (bf16[320,256]{1,0:T(8,128)(2,1)S(1)}, bf16[320,256]{1,0:T(8,128)(2,1)S(1)}, u32[]{:S(2)}, u32[]{:S(2)}) collective-permute-start(bf16[320,256]{1,0:T(8,128)(2,1)S(1)} %fusion.4.refs_0_), channel_id=1, source_target_pairs={{0,2},{1,3},{2,0},{3,1},{4,6},{5,7},{6,4},{7,5},{8,10},{9,11},{10,... | collective-permute-start | bytes 491528 | tf_op jit(solution)/shard_map/ppermute | solution.py:368
  (12 other events, 118.7 us)
